TPU v7x, 128 devices: a whole 4x4x4 slice. The times are simulated.
128 devices in a mesh: dp: 4 (over x_lo, core), ctx: 32 (over z, x_hi, y).
Axes of the slice: x: 4 (x_hi: 2, x_lo: 2; x = x_hi * 2 + x_lo), y: 4, z: 4, core: 2. Of those that a mesh axis runs over, the one named last changes fastest.
Arguments:
- queries: bfloat16 [4, 6144, 2048], P('dp', 'ctx'), may hold values from -128 to 128
- keys: bfloat16 [4, 6144, 2048], P('dp', 'ctx'), may hold values from -4 to 4
- values: bfloat16 [4, 6144, 2048], P('dp', 'ctx'), may hold values from -6 to 6
- grad_out: bfloat16 [4, 6144, 2048], P('dp', 'ctx'), may hold values from -6 to 6
- lengths: int32 [4, 32], P('dp'), may hold values from 1 to 384, 6144 in all within a row
- image_flags: int32 [4, 32], P('dp'), may hold values 0 or 1
Outputs:
- grad_queries: bfloat16 [4, 6144, 2048], P('dp', 'ctx')
- grad_keys: bfloat16 [4, 6144, 2048], P('dp', 'ctx')
- grad_values: bfloat16 [4, 6144, 2048], P('dp', 'ctx')
Inputs may be any that keep to these rules, and one draw needn't show every extreme that they name: Each sample's 32 lengths sum to 6144, and the largest is 384.
All inputs are finite; a program needn't handle non-finite values. No bound on the sum of `image_flags` on one device may be relied on, other than what follows from the above.
Results may differ from a plain program's by a relative error of at most 0.027.
Values may be sent and summed in bfloat16 or wider, within the bound.
No kernel may reach another device: no remote copies, remote signals or barrier semaphores. Data moves between devices by JAX's collectives and lax.ppermute only.
A program may use at most 128 MiB of HBM per device.

v0:
```python
import jax
import jax.numpy as jnp
from jax import lax
from jax.sharding import PartitionSpec as P

HEAD = 128
STEPS = 4


def shifted(value, axis, steps):
    count = lax.axis_size(axis)
    pairs = [(source, (source + steps) % count) for source in range(count)]
    return lax.ppermute(value, axis, pairs)


def layout(device, stretch_rows, cycle_size, ending, flag_list):
    offsets = jnp.arange(stretch_rows, dtype=jnp.int32)
    first_pos = device * stretch_rows + offsets
    second_pos = (2 * cycle_size - 1 - device) * stretch_rows + offsets
    position = jnp.concatenate([first_pos, second_pos])
    segment = jnp.sum((position[:, None] >= ending[None, :]).astype(jnp.int32), axis=1)
    labels = jnp.arange(ending.shape[0], dtype=jnp.int32)
    is_image = jnp.sum(
        jnp.where(segment[:, None] == labels[None, :], flag_list[None, :], 0), axis=1
    )
    return (position, segment, is_image)


def visible(query_side, key_side):
    causal = key_side[0][None, :] <= query_side[0][:, None]
    within = (key_side[1][None, :] == query_side[1][:, None]) & (query_side[2][:, None] == 1)
    return causal | within


def shards(queries, keys, values, grad_out, lengths, image_flags):
    query_rows = queries[0]
    key_rows = keys[0]
    value_rows = values[0]
    row_count, width = query_rows.shape
    stretch_rows = row_count // 2
    cycle_size = lax.axis_size("ctx")
    device = lax.axis_index("ctx")
    ending = jnp.cumsum(lengths[0])
    flag_list = image_flags[0]
    scale = HEAD ** (-0.5)
    head_count = width // HEAD
    group_size = min(4, head_count)
    group_count = head_count // group_size
    group_width = group_size * HEAD
    own_side = layout(device, stretch_rows, cycle_size, ending, flag_list)
    text_rows = (1 - own_side[2]).astype(jnp.float32)
    text_count = lax.psum(jnp.sum(text_rows), ("dp", "ctx"))
    total_rows = float(row_count * cycle_size * lax.axis_size("dp"))
    weight = text_rows * (total_rows / text_count)
    weighted = (grad_out[0].astype(jnp.float32) * weight[:, None]).astype(jnp.bfloat16)
    key_blocks = [key_rows]
    value_blocks = [value_rows]
    carried = (key_rows, value_rows)
    for step_index in range(1, STEPS):
        carried = shifted((carried[0], carried[1]), "ctx", 1)
        key_blocks.append(carried[0])
        value_blocks.append(carried[1])
    window_keys = jnp.concatenate(key_blocks, axis=0)
    window_values = jnp.concatenate(value_blocks, axis=0)
    key_sides = [
        layout((device - step_index) % cycle_size, stretch_rows, cycle_size, ending, flag_list)
        for step_index in range(STEPS)
    ]
    window_side = (
        jnp.concatenate([side[0] for side in key_sides]),
        jnp.concatenate([side[1] for side in key_sides]),
    )
    allowed = visible(own_side, window_side)
    key_span = STEPS * row_count
    query_parts, key_parts, value_parts, lse_parts, delta_parts = ([], [], [], [], [])
    for head_group in range(group_count):
        lower = head_group * group_width
        upper = lower + group_width
        queries_grp = query_rows[:, lower:upper].reshape(row_count, group_size, HEAD)
        weighted_grp = weighted[:, lower:upper].reshape(row_count, group_size, HEAD)
        keys_grp = window_keys[:, lower:upper].reshape(-1, group_size, HEAD)
        values_grp = window_values[:, lower:upper].reshape(-1, group_size, HEAD)
        scores = (
            jnp.einsum("qhd,khd->hqk", queries_grp, keys_grp, preferred_element_type=jnp.float32)
            * scale
        )
        masked = jnp.where(allowed[None], scores, -jnp.inf)
        largest = jnp.max(masked, axis=-1)
        lse_grp = largest + jnp.log(jnp.sum(jnp.exp(masked - largest[:, :, None]), axis=-1))
        prob = jnp.exp(masked - lse_grp[:, :, None])
        prob_half = prob.astype(jnp.bfloat16)
        attended = jnp.einsum(
            "hqk,khd->qhd", prob_half, values_grp, preferred_element_type=jnp.float32
        ).astype(jnp.bfloat16)
        delta_grp = jnp.einsum(
            "qhd,qhd->hq", weighted_grp, attended, preferred_element_type=jnp.float32
        )
        dprob = jnp.einsum(
            "qhd,khd->hqk", weighted_grp, values_grp, preferred_element_type=jnp.float32
        )
        dscore = (prob * (dprob - delta_grp[:, :, None])).astype(jnp.bfloat16)
        grad_query = (
            jnp.einsum("hqk,khd->qhd", dscore, keys_grp, preferred_element_type=jnp.float32) * scale
        )
        grad_key = (
            jnp.einsum("hqk,qhd->khd", dscore, queries_grp, preferred_element_type=jnp.float32)
            * scale
        )
        grad_value = jnp.einsum(
            "hqk,qhd->khd", prob_half, weighted_grp, preferred_element_type=jnp.float32
        )
        query_parts.append(grad_query.astype(jnp.bfloat16).reshape(row_count, group_width))
        key_parts.append(grad_key.reshape(key_span, group_width))
        value_parts.append(grad_value.reshape(key_span, group_width))
        lse_parts.append(lse_grp)
        delta_parts.append(delta_grp)
    grad_queries = jnp.concatenate(query_parts, axis=1)
    key_terms = jnp.concatenate(key_parts, axis=1)
    value_terms = jnp.concatenate(value_parts, axis=1)
    start = (STEPS - 1) * row_count
    carried = (key_terms[start : start + row_count], value_terms[start : start + row_count])
    for step_index in range(STEPS - 2, -1, -1):
        carried = shifted((carried[0], carried[1]), "ctx", -1)
        start = step_index * row_count
        carried = (
            carried[0] + key_terms[start : start + row_count],
            carried[1] + value_terms[start : start + row_count],
        )
    grad_keys, grad_values = carried
    return (
        grad_queries[None],
        grad_keys.astype(jnp.bfloat16)[None],
        grad_values.astype(jnp.bfloat16)[None],
    )


def solution(mesh):
    in_specs = (
        P("dp", "ctx", None),
        P("dp", "ctx", None),
        P("dp", "ctx", None),
        P("dp", "ctx", None),
        P("dp", None),
        P("dp", None),
    )
    out_specs = (P("dp", "ctx", None), P("dp", "ctx", None), P("dp", "ctx", None))
    return jax.shard_map(shards, mesh=mesh, in_specs=in_specs, out_specs=out_specs, check_vma=False)
```

profile of v0, /device:TPU:0, one launch (start us, length us, event | category | flops | bytes accessed | tf_op | source)
XLA Modules:
  0.0 446.5 jit_solution(15666878563457120350)
XLA Ops:
  6.7 90.9 %psum.7 = f32[]{:T(128)} all-reduce(f32[]{:T(128)} %convert_reduce_fusion.5), channel_id=1, replica_groups=mesh['dp'=4,'ctx'=32] {'dp','ctx'}, use_global_device_ids=true, to_apply=%region_10.11 | all-reduce | flops 1 | bytes 8 | tf_op jit(solution)/shard_map/psum | solution.py:52
  108.2 19.4 %collective-permute-done.1 = bf16[192,2048]{1,0:T(8,128)(2,1)} collective-permute-done((bf16[192,2048]{1,0:T(8,128)(2,1)}, bf16[192,2048]{1,0:T(8,128)(2,1)}, u32[]{:S(2)}, u32[]{:S(2)}) %collective-permute-start.1) | collective-permute-done | bytes 786464 | tf_op jit(solution)/shard_map/ppermute | solution.py:13
  129.3 15.1 %collective-permute-done.4 = bf16[192,2048]{1,0:T(8,128)(2,1)} collective-permute-done((bf16[192,2048]{1,0:T(8,128)(2,1)S(1)}, bf16[192,2048]{1,0:T(8,128)(2,1)}, u32[]{:S(2)}, u32[]{:S(2)}) %collective-permute-start.4) | collective-permute-done | bytes 786464 | tf_op jit(solution)/shard_map/ppermute | solution.py:13
  148.9 2.2 copy.127
  151.1 10.2 %collective-permute-done.2 = bf16[192,2048]{1,0:T(8,128)(2,1)} collective-permute-done((bf16[192,2048]{1,0:T(8,128)(2,1)}, bf16[192,2048]{1,0:T(8,128)(2,1)}, u32[]{:S(2)}, u32[]{:S(2)}) %collective-permute-start.2) | collective-permute-done | bytes 786464 | tf_op jit(solution)/shard_map/ppermute | solution.py:13
  163.5 3.1 pad_maximum_fusion.2
  167.7 9.1 %collective-permute-done.5 = bf16[192,2048]{1,0:T(8,128)(2,1)} collective-permute-done((bf16[192,2048]{1,0:T(8,128)(2,1)}, bf16[192,2048]{1,0:T(8,128)(2,1)}, u32[]{:S(2)}, u32[]{:S(2)}) %collective-permute-start.5) | collective-permute-done | bytes 786464 | tf_op jit(solution)/shard_map/ppermute | solution.py:13
  176.8 2.2 copy.128
  179.0 3.7 pad_maximum_fusion.3
  188.9 3.0 copy.170
  193.6 3.0 copy.162
  201.3 3.5 copy.167
  204.7 2.5 convolution_multiply_fusion.3
  207.2 3.2 copy.159
  216.1 3.5 copy.169
  219.5 2.7 convolution_multiply_fusion.1
  222.3 3.1 copy.161
  231.0 3.5 copy.168
  234.4 3.1 pad_maximum_fusion.1
  237.6 2.6 copy-done
  243.1 3.2 copy.160
  246.3 3.3 pad_maximum_fusion
  249.8 29.4 %collective-permute-done.9 = f32[192,2048]{1,0:T(8,128)} collective-permute-done((f32[192,2048]{1,0:T(8,128)}, f32[192,2048]{1,0:T(8,128)}, u32[]{:S(2)}, u32[]{:S(2)}) %collective-permute-start.9) | collective-permute-done | bytes 1572896 | tf_op jit(solution)/shard_map/ppermute | solution.py:13
  280.8 5.8 %collective-permute-start.10 = (f32[192,2048]{1,0:T(8,128)S(1)}, f32[192,2048]{1,0:T(8,128)S(1)}, u32[]{:S(2)}, u32[]{:S(2)}) collective-permute-start(f32[192,2048]{1,0:T(8,128)S(1)} %slice_add_fusion.2), channel_id=1, source_target_pairs={{0,31},{1,0},{2,1},{3,2},{4,3},{5,4},{6,5},{7,6},{8,7},{9,8},{10,9... | collective-permute-start | bytes 4718600 | tf_op jit(solution)/shard_map/ppermute | solution.py:13
  286.6 26.2 %collective-permute-done.6 = f32[192,2048]{1,0:T(8,128)S(1)} collective-permute-done((f32[192,2048]{1,0:T(8,128)S(1)}, f32[192,2048]{1,0:T(8,128)S(1)}, u32[]{:S(2)}, u32[]{:S(2)}) %collective-permute-start.6) | collective-permute-done | bytes 1572896 | tf_op jit(solution)/shard_map/ppermute | solution.py:13
  313.0 5.8 %collective-permute-start.7 = (f32[192,2048]{1,0:T(8,128)S(1)}, f32[192,2048]{1,0:T(8,128)S(1)}, u32[]{:S(2)}, u32[]{:S(2)}) collective-permute-start(f32[192,2048]{1,0:T(8,128)S(1)} %slice_add_fusion.5), channel_id=1, source_target_pairs={{0,31},{1,0},{2,1},{3,2},{4,3},{5,4},{6,5},{7,6},{8,7},{9,8},{10,9... | collective-permute-start | bytes 4718600 | tf_op jit(solution)/shard_map/ppermute | solution.py:13
  318.8 27.7 %collective-permute-done.10 = f32[192,2048]{1,0:T(8,128)S(1)} collective-permute-done((f32[192,2048]{1,0:T(8,128)S(1)}, f32[192,2048]{1,0:T(8,128)S(1)}, u32[]{:S(2)}, u32[]{:S(2)}) %collective-permute-start.10) | collective-permute-done | bytes 1572896 | tf_op jit(solution)/shard_map/ppermute | solution.py:13
  346.7 5.8 %collective-permute-start.11 = (f32[192,2048]{1,0:T(8,128)S(1)}, f32[192,2048]{1,0:T(8,128)S(1)}, u32[]{:S(2)}, u32[]{:S(2)}) collective-permute-start(f32[192,2048]{1,0:T(8,128)S(1)} %slice_add_fusion.1), channel_id=1, source_target_pairs={{0,31},{1,0},{2,1},{3,2},{4,3},{5,4},{6,5},{7,6},{8,7},{9,8},{10,9... | collective-permute-start | bytes 4718600 | tf_op jit(solution)/shard_map/ppermute | solution.py:13
  352.5 27.7 %collective-permute-done.7 = f32[192,2048]{1,0:T(8,128)S(1)} collective-permute-done((f32[192,2048]{1,0:T(8,128)S(1)}, f32[192,2048]{1,0:T(8,128)S(1)}, u32[]{:S(2)}, u32[]{:S(2)}) %collective-permute-start.7) | collective-permute-done | bytes 1572896 | tf_op jit(solution)/shard_map/ppermute | solution.py:13
  380.5 5.8 %collective-permute-start.8 = (f32[192,2048]{1,0:T(8,128)S(1)}, f32[192,2048]{1,0:T(8,128)S(1)}, u32[]{:S(2)}, u32[]{:S(2)}) collective-permute-start(f32[192,2048]{1,0:T(8,128)S(1)} %slice_add_fusion.4), channel_id=1, source_target_pairs={{0,31},{1,0},{2,1},{3,2},{4,3},{5,4},{6,5},{7,6},{8,7},{9,8},{10,9... | collective-permute-start | bytes 4718600 | tf_op jit(solution)/shard_map/ppermute | solution.py:13
  389.8 24.1 %collective-permute-done.11 = f32[192,2048]{1,0:T(8,128)S(1)} collective-permute-done((f32[192,2048]{1,0:T(8,128)S(1)}, f32[192,2048]{1,0:T(8,128)S(1)}, u32[]{:S(2)}, u32[]{:S(2)}) %collective-permute-start.11) | collective-permute-done | bytes 1572896 | tf_op jit(solution)/shard_map/ppermute | solution.py:13
  415.0 30.4 %collective-permute-done.8 = f32[192,2048]{1,0:T(8,128)S(1)} collective-permute-done((f32[192,2048]{1,0:T(8,128)S(1)}, f32[192,2048]{1,0:T(8,128)S(1)}, u32[]{:S(2)}, u32[]{:S(2)}) %collective-permute-start.8) | collective-permute-done | bytes 1572896 | tf_op jit(solution)/shard_map/ppermute | solution.py:13
  (169 shorter events, 59.8 us)
Async XLA Ops:
  0.6 106.0 %collective-permute-start.3 = (bf16[192,2048]{1,0:T(8,128)(2,1)}, bf16[192,2048]{1,0:T(8,128)(2,1)S(1)}, u32[]{:S(2)}, u32[]{:S(2)}) collective-permute-start(bf16[192,2048]{1,0:T(8,128)(2,1)} %bitcast.245), channel_id=1, source_target_pairs={{0,1},{1,2},{2,3},{3,4},{4,5},{5,6},{6,7},{7,8},{8,9},{9,10},{10,1... | collective-permute-start | bytes 2359304 | tf_op jit(solution)/shard_map/ppermute | solution.py:13
  5.2 95.8 %collective-permute-start = (bf16[192,2048]{1,0:T(8,128)(2,1)}, bf16[192,2048]{1,0:T(8,128)(2,1)}, u32[]{:S(2)}, u32[]{:S(2)}) collective-permute-start(bf16[192,2048]{1,0:T(8,128)(2,1)} %bitcast.244), channel_id=1, source_target_pairs={{0,1},{1,2},{2,3},{3,4},{4,5},{5,6},{6,7},{7,8},{8,9},{9,10},{10,1... | collective-permute-start | bytes 2359304 | tf_op jit(solution)/shard_map/ppermute | solution.py:13
  98.4 3.6 copy-start.29
  99.8 2.7 copy-start.30
  101.0 26.6 %collective-permute-start.1 = (bf16[192,2048]{1,0:T(8,128)(2,1)}, bf16[192,2048]{1,0:T(8,128)(2,1)}, u32[]{:S(2)}, u32[]{:S(2)}) collective-permute-start(bf16[192,2048]{1,0:T(8,128)(2,1)} %collective-permute-done), channel_id=1, source_target_pairs={{0,1},{1,2},{2,3},{3,4},{4,5},{5,6},{6,7},{7,8},{8,9},{9,10},{10,1... | collective-permute-start | bytes 2359304 | tf_op jit(solution)/shard_map/ppermute | solution.py:13
  103.8 24.6 %copy-start.35 = (bf16[1,192,2048]{2,1,0:T(8,128)(2,1)S(1)}, bf16[1,192,2048]{2,1,0:T(8,128)(2,1)}, u32[]{:S(2)}) copy-start(bf16[1,192,2048]{2,1,0:T(8,128)(2,1)} %param.6) | copy-start | bytes 2359300
  106.6 37.8 %copy-start.31 = (bf16[192,2048]{1,0:T(8,128)(2,1)}, bf16[192,2048]{1,0:T(8,128)(2,1)S(1)}, u32[]{:S(2)}) copy-start(bf16[192,2048]{1,0:T(8,128)(2,1)S(1)} %collective-permute-done.3) | copy-start | bytes 2359300
  106.6 37.8 %collective-permute-start.4 = (bf16[192,2048]{1,0:T(8,128)(2,1)S(1)}, bf16[192,2048]{1,0:T(8,128)(2,1)}, u32[]{:S(2)}, u32[]{:S(2)}) collective-permute-start(bf16[192,2048]{1,0:T(8,128)(2,1)S(1)} %collective-permute-done.3), channel_id=1, source_target_pairs={{0,1},{1,2},{2,3},{3,4},{4,5},{5,6},{6,7},{7,8},{8,9},{9,10},{10,1... | collective-permute-start | bytes 2359304 | tf_op jit(solution)/shard_map/ppermute | solution.py:13
  127.6 33.7 %collective-permute-start.2 = (bf16[192,2048]{1,0:T(8,128)(2,1)}, bf16[192,2048]{1,0:T(8,128)(2,1)}, u32[]{:S(2)}, u32[]{:S(2)}) collective-permute-start(bf16[192,2048]{1,0:T(8,128)(2,1)} %collective-permute-done.1), channel_id=1, source_target_pairs={{0,1},{1,2},{2,3},{3,4},{4,5},{5,6},{6,7},{7,8},{8,9},{9,10},{10,1... | collective-permute-start | bytes 2359304 | tf_op jit(solution)/shard_map/ppermute | solution.py:13
  144.4 32.4 %collective-permute-start.5 = (bf16[192,2048]{1,0:T(8,128)(2,1)}, bf16[192,2048]{1,0:T(8,128)(2,1)}, u32[]{:S(2)}, u32[]{:S(2)}) collective-permute-start(bf16[192,2048]{1,0:T(8,128)(2,1)} %collective-permute-done.4), channel_id=1, source_target_pairs={{0,1},{1,2},{2,3},{3,4},{4,5},{5,6},{6,7},{7,8},{8,9},{9,10},{10,1... | collective-permute-start | bytes 2359304 | tf_op jit(solution)/shard_map/ppermute | solution.py:13
  167.7 16.5 %copy-start.13 = (bf16[768,512]{0,1:T(8,128)(2,1)}, bf16[768,512]{0,1:T(8,128)(2,1)S(1)}, u32[]{:S(2)}) copy-start(bf16[768,512]{0,1:T(8,128)(2,1)S(1)} %get-tuple-element.13) | copy-start | bytes 2359300
  167.7 28.9 %copy-start.11 = (bf16[768,512]{0,1:T(8,128)(2,1)}, bf16[768,512]{0,1:T(8,128)(2,1)S(1)}, u32[]{:S(2)}) copy-start(bf16[768,512]{0,1:T(8,128)(2,1)S(1)} %get-tuple-element.12) | copy-start | bytes 2359300
  167.7 57.6 %copy-start.7 = (bf16[768,512]{0,1:T(8,128)(2,1)}, bf16[768,512]{0,1:T(8,128)(2,1)S(1)}, u32[]{:S(2)}) copy-start(bf16[768,512]{0,1:T(8,128)(2,1)S(1)} %get-tuple-element.15) | copy-start | bytes 2359300
  192.0 4.6 %copy-start.23 = (bf16[24,4,8,128]{3,2,1,0:T(8,128)(2,1)S(1)}, bf16[24,4,8,128]{3,2,1,0:T(8,128)(2,1)}, u32[]{:S(2)}) copy-start(bf16[24,4,8,128]{3,2,1,0:T(8,128)(2,1)} %get-tuple-element.24) | copy-start | bytes 589828
  201.3 6.0 %copy-start.1 = (bf16[4,192,768]{2,1,0:T(8,128)(2,1)}, bf16[4,192,768]{2,1,0:T(8,128)(2,1)S(1)}, u32[]{:S(2)}) copy-start(bf16[4,192,768]{2,1,0:T(8,128)(2,1)S(1)} %multiply_convert_fusion.3) | copy-start | bytes 3538948
  207.2 3.2 copy-start.9
  216.1 6.2 %copy-start.3 = (bf16[4,192,768]{2,1,0:T(8,128)(2,1)}, bf16[4,192,768]{2,1,0:T(8,128)(2,1)S(1)}, u32[]{:S(2)}) copy-start(bf16[4,192,768]{2,1,0:T(8,128)(2,1)S(1)} %multiply_convert_fusion.1) | copy-start | bytes 3538948
  231.0 10.6 %copy-start.5 = (bf16[4,192,768]{2,1,0:T(8,128)(2,1)}, bf16[4,192,768]{2,1,0:T(8,128)(2,1)S(1)}, u32[]{:S(2)}) copy-start(bf16[4,192,768]{2,1,0:T(8,128)(2,1)S(1)} %multiply_convert_fusion.2) | copy-start | bytes 3538948
  237.6 2.7 copy-start
  241.6 37.6 %collective-permute-start.9 = (f32[192,2048]{1,0:T(8,128)}, f32[192,2048]{1,0:T(8,128)}, u32[]{:S(2)}, u32[]{:S(2)}) collective-permute-start(f32[192,2048]{1,0:T(8,128)} %slice.116), channel_id=1, source_target_pairs={{0,31},{1,0},{2,1},{3,2},{4,3},{5,4},{6,5},{7,6},{8,7},{9,8},{10,9... | collective-permute-start | bytes 4718600 | tf_op jit(solution)/shard_map/ppermute | solution.py:13
  243.1 36.1 %slice-start = ((s8[6291456]{0:T(1024)(128)(4,1)}), s8[2097152]{0:T(1024)(128)(4,1)S(1)}, s32[]{:S(2)}) async-start(s8[6291456]{0:T(1024)(128)(4,1)} %bitcast.216), calls=%async_computation | async-start | bytes 4194304
  246.3 32.9 %slice-start.1 = ((s8[6291456]{0:T(1024)(128)(4,1)}), s8[4194304]{0:T(1024)(128)(4,1)S(1)}, s32[]{:S(2)}) async-start(s8[6291456]{0:T(1024)(128)(4,1)} %bitcast.216), calls=%async_computation.1 | async-start | bytes 8388608
  249.7 63.1 %collective-permute-start.6 = (f32[192,2048]{1,0:T(8,128)S(1)}, f32[192,2048]{1,0:T(8,128)S(1)}, u32[]{:S(2)}, u32[]{:S(2)}) collective-permute-start(f32[192,2048]{1,0:T(8,128)S(1)} %slice.112), channel_id=1, source_target_pairs={{0,31},{1,0},{2,1},{3,2},{4,3},{5,4},{6,5},{7,6},{8,7},{9,8},{10,9... | collective-permute-start | bytes 4718600 | tf_op jit(solution)/shard_map/ppermute | solution.py:13
  280.8 65.7 %collective-permute-start.10 = (f32[192,2048]{1,0:T(8,128)S(1)}, f32[192,2048]{1,0:T(8,128)S(1)}, u32[]{:S(2)}, u32[]{:S(2)}) collective-permute-start(f32[192,2048]{1,0:T(8,128)S(1)} %slice_add_fusion.2), channel_id=1, source_target_pairs={{0,31},{1,0},{2,1},{3,2},{4,3},{5,4},{6,5},{7,6},{8,7},{9,8},{10,9... | collective-permute-start | bytes 4718600 | tf_op jit(solution)/shard_map/ppermute | solution.py:13
  313.0 67.2 %collective-permute-start.7 = (f32[192,2048]{1,0:T(8,128)S(1)}, f32[192,2048]{1,0:T(8,128)S(1)}, u32[]{:S(2)}, u32[]{:S(2)}) collective-permute-start(f32[192,2048]{1,0:T(8,128)S(1)} %slice_add_fusion.5), channel_id=1, source_target_pairs={{0,31},{1,0},{2,1},{3,2},{4,3},{5,4},{6,5},{7,6},{8,7},{9,8},{10,9... | collective-permute-start | bytes 4718600 | tf_op jit(solution)/shard_map/ppermute | solution.py:13
  346.7 39.5 %copy-start.14 = (bf16[768,512]{0,1:T(8,128)(2,1)S(1)}, bf16[768,512]{0,1:T(8,128)(2,1)}, u32[]{:S(2)}) copy-start(bf16[768,512]{0,1:T(8,128)(2,1)} %copy-done.13) | copy-start | bytes 2359300
  346.7 67.2 %collective-permute-start.11 = (f32[192,2048]{1,0:T(8,128)S(1)}, f32[192,2048]{1,0:T(8,128)S(1)}, u32[]{:S(2)}, u32[]{:S(2)}) collective-permute-start(f32[192,2048]{1,0:T(8,128)S(1)} %slice_add_fusion.1), channel_id=1, source_target_pairs={{0,31},{1,0},{2,1},{3,2},{4,3},{5,4},{6,5},{7,6},{8,7},{9,8},{10,9... | collective-permute-start | bytes 4718600 | tf_op jit(solution)/shard_map/ppermute | solution.py:13
  380.2 6.6 %copy-start.12 = (bf16[768,512]{0,1:T(8,128)(2,1)S(1)}, bf16[768,512]{0,1:T(8,128)(2,1)}, u32[]{:S(2)}) copy-start(bf16[768,512]{0,1:T(8,128)(2,1)} %copy-done.11) | copy-start | bytes 2359300
  380.5 6.4 %copy-start.2 = (bf16[4,192,768]{2,1,0:T(8,128)(2,1)S(1)}, bf16[4,192,768]{2,1,0:T(8,128)(2,1)}, u32[]{:S(2)}) copy-start(bf16[4,192,768]{2,1,0:T(8,128)(2,1)} %copy-done.1) | copy-start | bytes 3538948
  380.5 6.9 %copy-start.4 = (bf16[4,192,768]{2,1,0:T(8,128)(2,1)S(1)}, bf16[4,192,768]{2,1,0:T(8,128)(2,1)}, u32[]{:S(2)}) copy-start(bf16[4,192,768]{2,1,0:T(8,128)(2,1)} %copy-done.3) | copy-start | bytes 3538948
  380.5 6.9 %copy-start.10 = (bf16[768,512]{0,1:T(8,128)(2,1)S(1)}, bf16[768,512]{0,1:T(8,128)(2,1)}, u32[]{:S(2)}) copy-start(bf16[768,512]{0,1:T(8,128)(2,1)} %get-tuple-element.14) | copy-start | bytes 2359300
  380.5 64.9 %collective-permute-start.8 = (f32[192,2048]{1,0:T(8,128)S(1)}, f32[192,2048]{1,0:T(8,128)S(1)}, u32[]{:S(2)}, u32[]{:S(2)}) collective-permute-start(f32[192,2048]{1,0:T(8,128)S(1)} %slice_add_fusion.4), channel_id=1, source_target_pairs={{0,31},{1,0},{2,1},{3,2},{4,3},{5,4},{6,5},{7,6},{8,7},{9,8},{10,9... | collective-permute-start | bytes 4718600 | tf_op jit(solution)/shard_map/ppermute | solution.py:13
  (18 other events, 32.6 us)
where the time goes:
time: 447 us
  waiting for transfers between devices  219 us (49%)
  blocking collectives  90.9 us (20%)
  local copies, waits for them, and re-layouts  49.9 us (11%)
  other arithmetic  28.5 us (6%)
  starting transfers between devices  28.2 us (6%)
  matrix products  27.7 us (6%)
    ppermute x12, waiting for transfers between devices, shifted(): return lax.ppermute(value, axis, pairs)  219 us
    psum x1, blocking collectives, shards(): text_count = lax.psum(jnp.sum(text_rows), ('dp', 'ctx'))  90.9 us
    ppermute x12, starting transfers between devices, shifted(): return lax.ppermute(value, axis, pairs)  28.2 us
    reshape x4, local copies, waits for them, and re-layouts, shards(): value_parts.append(grad_value.reshape(key_span, group_width))  13.4 us
    reshape x4, local copies, waits for them, and re-layouts, shards(): key_parts.append(grad_key.reshape(key_span, group_width))  12.4 us
    ppermute x6, local copies, waits for them, and re-layouts, shifted(): return lax.ppermute(value, axis, pairs)  10.9 us
  transfers between devices with their start and end apart: 12, of which 10 were waited for; matrix products, arithmetic and copies ran while one was open for 9% of the time, Pallas kernels for 0%

commit v1 on v0

v1 whole, which is shorter than its diff:
```python
import functools

import jax
import jax.numpy as jnp
from jax import lax
from jax.experimental import pallas as pl
from jax.experimental.pallas import tpu as pltpu
from jax.sharding import PartitionSpec as P

HEAD = 128
STEPS = 4
GROUP = 4
CHUNKS = 2
LOG2E = 1.4426950408889634
MASKED = -1e30
VMEM = pl.BlockSpec(memory_space=pltpu.VMEM)
ANY = pl.BlockSpec(memory_space=pl.ANY)
LARGE = pltpu.CompilerParams(vmem_limit_bytes=60 * 1024 * 1024)
EDGE_COST = (0, 6000000000)
SETTLE_COST = 3000000000
SMALL = pltpu.CompilerParams(vmem_limit_bytes=10 * 1024 * 1024)


def columns(place, away, chunk, width):
    index = lax.rem(place + GROUP + away, GROUP)
    return pl.ds(pl.multiple_of((index * CHUNKS + chunk) * width, width), width)


def pack_kernel(chunk, first, second, after, one, two, three):
    width = one.shape[2]
    for away, message in ((1, one), (2, two), (3, three)):
        lanes = columns(lax.rem(lax.axis_index("ctx"), GROUP), away, chunk, width)
        message[0] = first[:, lanes]
        message[1] = second[:, lanes]


def first_pack_kernel(first, second, lengths, flags, one, two, three, text, sems):
    width = one.shape[2]
    place = lax.rem(lax.axis_index("ctx"), GROUP)
    copies = []
    for away, message in ((1, one), (2, two), (3, three)):
        lanes = columns(place, away, 0, width)
        for part, source in enumerate((first, second)):
            copies.append(
                pltpu.make_async_copy(source.at[:, lanes], message.at[part], sems.at[len(copies)])
            )
    for copy in copies:
        copy.start()
    text[...] = (lengths[...] * (1 - flags[...])).astype(jnp.float32)
    for copy in copies:
        copy.wait()


def pack(first, second, after, chunk):
    rows, total = first.shape
    width = total // (GROUP * CHUNKS)
    message = jax.ShapeDtypeStruct((2, rows, width), first.dtype)
    return pl.pallas_call(
        functools.partial(pack_kernel, chunk),
        out_shape=(message,) * (GROUP - 1),
        in_specs=[VMEM, VMEM, ANY],
        out_specs=(VMEM,) * (GROUP - 1),
        compiler_params=SMALL,
        cost_estimate=pl.CostEstimate(flops=0, bytes_accessed=12 * rows * width * 2, transcendentals=0),
        name="pack",
    )(first, second, after)


def first_pack(first, second, lengths, flags):
    rows, total = first.shape
    width = total // (GROUP * CHUNKS)
    message = jax.ShapeDtypeStruct((2, rows, width), first.dtype)
    *messages, text = pl.pallas_call(
        first_pack_kernel,
        out_shape=(message,) * (GROUP - 1) + (jax.ShapeDtypeStruct(lengths.shape, jnp.float32),),
        in_specs=[ANY, ANY, VMEM, VMEM],
        out_specs=(VMEM,) * GROUP,
        scratch_shapes=[pltpu.SemaphoreType.DMA((2 * (GROUP - 1),))],
        compiler_params=LARGE,
        cost_estimate=pl.CostEstimate(flops=0, bytes_accessed=12 * rows * width * 2, transcendentals=0),
        name="first_pack",
    )(first, second, lengths, flags)
    return messages, text


def edge_kernel(chunk, first, second, one, two, three, *refs):
    edge = refs[-1]
    rows = edge.shape[1] // (GROUP - 1)
    width = edge.shape[2]
    place = lax.rem(lax.axis_index("ctx"), GROUP)
    for away, message in enumerate((None, one, two, three)):
        index = lax.rem(place + GROUP - away, GROUP)

        @pl.when(index > 0)
        def put():
            at = pl.ds(pl.multiple_of((index - 1) * rows, rows), rows)
            if message is None:
                lanes = columns(place, 0, chunk, width)
                edge[0, at, :] = first[:, lanes]
                edge[1, at, :] = second[:, lanes]
            else:
                edge[:, at, :] = message[...]


def make_edge(first, second, blocks, afters, chunk, cost):
    _, rows, width = blocks[0].shape
    return pl.pallas_call(
        functools.partial(edge_kernel, chunk),
        out_shape=jax.ShapeDtypeStruct((2, (GROUP - 1) * rows, width), first.dtype),
        in_specs=[VMEM] * 5 + [ANY] * len(afters),
        out_specs=VMEM,
        compiler_params=SMALL,
        cost_estimate=pl.CostEstimate(flops=cost, bytes_accessed=0, transcendentals=0),
        name="edge",
    )(first, second, *blocks, *afters)


def sides_kernel(stretch_rows, cycle_size, bounds_ref, after, limit_ref, text_ref, key_ref):
    rows = 2 * stretch_rows
    device_here = lax.axis_index("ctx")
    start = device_here - lax.rem(device_here, GROUP)
    first = bounds_ref[0:1, :]
    ending = bounds_ref[1:2, :]
    flag = bounds_ref[2:3, :].astype(jnp.float32)
    last = ending.astype(jnp.float32)
    shape = (rows, HEAD)
    offset = lax.broadcasted_iota(jnp.int32, shape, 0)
    for block in range(GROUP):
        device = start + block
        position = jnp.where(
            offset < stretch_rows,
            device * stretch_rows + offset,
            (2 * cycle_size - 2 - device) * stretch_rows + offset,
        )
        inside = (position >= first) & (position < ending)
        image = jnp.sum(jnp.where(inside, flag, 0.0), axis=1, keepdims=True)
        final = jnp.sum(jnp.where(inside, last, 0.0), axis=1, keepdims=True).astype(jnp.int32) - 1
        limit_ref[block] = jnp.where(image > 0.5, final, position)
        text_ref[block] = jnp.broadcast_to(1.0 - image, shape)
        lane = lax.broadcasted_iota(jnp.int32, (8, STEPS * rows), 1)
        step = jnp.zeros_like(lane)
        for edge in range(1, STEPS):
            step = step + (lane >= edge * rows).astype(jnp.int32)
        owner = device - (STEPS - 1) + step
        owner = jnp.where(owner < 0, owner + cycle_size, owner)
        within = lane - step * rows
        key_ref[block] = jnp.where(
            within < stretch_rows,
            owner * stretch_rows + within,
            (2 * cycle_size - 2 - owner) * stretch_rows + within,
        )


def sides(bounds, after, stretch_rows, cycle_size):
    rows = 2 * stretch_rows
    return pl.pallas_call(
        functools.partial(sides_kernel, stretch_rows, cycle_size),
        out_shape=(
            jax.ShapeDtypeStruct((GROUP, rows, HEAD), jnp.int32),
            jax.ShapeDtypeStruct((GROUP, rows, HEAD), jnp.float32),
            jax.ShapeDtypeStruct((GROUP, 8, STEPS * rows), jnp.int32),
        ),
        in_specs=[VMEM, ANY],
        out_specs=(VMEM,) * 3,
        compiler_params=SMALL,
        cost_estimate=pl.CostEstimate(flops=GROUP * rows * HEAD * 8, bytes_accessed=GROUP * rows * HEAD * 8, transcendentals=0),
        name="sides",
    )(bounds, after)


def attend_kernel(
    chunk, total_rows, text_one, text_two, text_three, text_four, limit_ref, text_ref, keypos_ref,
    queries, keys, values, grads, key_one, key_two, key_three, query_one, query_two, query_three,
    edge_ref, query_own, query_to_one, query_to_two, query_to_three, main_ref, far_ref,
    key_all, value_all, query_all, grad_all, key_grad, value_grad, query_out,
):
    rows, width = queries.shape[0], edge_ref.shape[2]
    edge = (GROUP - 1) * rows
    span = STEPS * rows
    scale = HEAD ** (-0.5)
    place = lax.rem(lax.axis_index("ctx"), GROUP)
    counted = text_one[...] + text_two[...] + text_three[...] + text_four[...]
    factor = total_rows / jnp.sum(counted, axis=1, keepdims=True)
    lanes = columns(place, 0, chunk, width)
    key_all[:edge, :] = edge_ref[0]
    value_all[:edge, :] = edge_ref[1]
    sources = [(keys.at[:, lanes], values.at[:, lanes], queries.at[:, lanes], grads.at[:, lanes])]
    for pair, query_pair in ((key_one, query_one), (key_two, query_two), (key_three, query_three)):
        sources.append((pair.at[0], pair.at[1], query_pair.at[0], query_pair.at[1]))
    for away in range(GROUP):
        start = pl.multiple_of(lax.rem(place + GROUP - away, GROUP) * rows, rows)
        key, value, query, grad = sources[away]
        key_all[pl.ds(edge + start, rows), :] = key[...]
        value_all[pl.ds(edge + start, rows), :] = value[...]
        query_all[pl.ds(start, rows), :] = query[...]
        grad_all[pl.ds(start, rows), :] = grad[...]
    key_grad[...] = jnp.zeros_like(key_grad)
    value_grad[...] = jnp.zeros_like(value_grad)
    for block in range(GROUP):
        at = slice(block * rows, (block + 1) * rows)
        window = slice(block * rows, block * rows + span)
        limit = limit_ref[block]
        allowed = jnp.concatenate(
            [
                keypos_ref[block, 0:1, tile * HEAD : (tile + 1) * HEAD] <= limit
                for tile in range(span // HEAD)
            ],
            axis=1,
        )
        weight = text_ref[block] * factor
        for head in range(width // HEAD):
            lanes = slice(head * HEAD, (head + 1) * HEAD)
            query = query_all[at, lanes]
            grad = (grad_all[at, lanes].astype(jnp.float32) * weight).astype(jnp.bfloat16)
            key = key_all[window, lanes]
            value = value_all[window, lanes]
            scores = lax.dot_general(
                query, key, (((1,), (1,)), ((), ())), preferred_element_type=jnp.float32
            )
            scores = jnp.where(allowed, scores, MASKED)
            largest = jnp.max(scores, axis=1, keepdims=True)
            prob = jnp.exp2((scores - largest) * (scale * LOG2E))
            dprob = lax.dot_general(
                grad, value, (((1,), (1,)), ((), ())), preferred_element_type=jnp.float32
            )
            total = jnp.sum(prob, axis=1, keepdims=True)
            inverse = 1.0 / total
            delta = jnp.sum(prob * dprob, axis=1, keepdims=True) * inverse
            prob = prob * inverse
            dscore = (prob * (dprob - delta)).astype(jnp.bfloat16)
            prob_half = prob.astype(jnp.bfloat16)
            query_out[at, lanes] = (
                jnp.dot(dscore, key, preferred_element_type=jnp.float32) * scale
            ).astype(jnp.bfloat16)
            key_grad[window, lanes] += lax.dot_general(
                dscore, query, (((0,), (0,)), ((), ())), preferred_element_type=jnp.float32
            )
            value_grad[window, lanes] += lax.dot_general(
                prob_half, grad, (((0,), (0,)), ((), ())), preferred_element_type=jnp.float32
            )
    for away, block in enumerate((query_own, query_to_one, query_to_two, query_to_three)):
        index = lax.rem(place + away, GROUP)
        block[...] = query_out[pl.ds(pl.multiple_of(index * rows, rows), rows), :]
    far_ref[0] = (key_grad[:edge, :] * scale).astype(jnp.bfloat16)
    far_ref[1] = value_grad[:edge, :].astype(jnp.bfloat16)
    main_ref[0] = (key_grad[edge:, :] * scale).astype(jnp.bfloat16)
    main_ref[1] = value_grad[edge:, :].astype(jnp.bfloat16)


def attend(texts, marks, arrays, key_blocks, query_blocks, edge, chunk, total_rows):
    _, rows, width = key_blocks[0].shape
    heads = width // HEAD
    keys = (2 * GROUP - 1) * rows
    pairs = heads * GROUP * rows * STEPS * rows
    return pl.pallas_call(
        functools.partial(attend_kernel, chunk, total_rows),
        out_shape=(
            *[jax.ShapeDtypeStruct((rows, width), jnp.bfloat16)] * GROUP,
            jax.ShapeDtypeStruct((2, GROUP * rows, width), jnp.bfloat16),
            jax.ShapeDtypeStruct((2, (GROUP - 1) * rows, width), jnp.bfloat16),
        ),
        in_specs=[VMEM] * (len(texts) + 14),
        out_specs=(VMEM,) * (GROUP + 2),
        scratch_shapes=[
            pltpu.VMEM((keys, width), jnp.bfloat16),
            pltpu.VMEM((keys, width), jnp.bfloat16),
            pltpu.VMEM((GROUP * rows, width), jnp.bfloat16),
            pltpu.VMEM((GROUP * rows, width), jnp.bfloat16),
            pltpu.VMEM((keys, width), jnp.float32),
            pltpu.VMEM((keys, width), jnp.float32),
            pltpu.VMEM((GROUP * rows, width), jnp.bfloat16),
        ],
        compiler_params=pltpu.CompilerParams(vmem_limit_bytes=24 * 1024 * 1024),
        cost_estimate=pl.CostEstimate(
            flops=4500000000, bytes_accessed=0, transcendentals=0
        ),
        name="attend",
    )(*texts, *marks, *arrays, *key_blocks, *query_blocks, edge)


def settle_kernel(main_ref, far_ref, *refs):
    extra = refs[: len(refs) // GROUP * GROUP - GROUP]
    outs = refs[len(refs) - GROUP :]
    rows = outs[0].shape[1]
    first_kind = 1 if extra else 0
    place = lax.rem(lax.axis_index("ctx"), GROUP)
    for away, block in enumerate(outs):
        index = lax.rem(place + away, GROUP)
        start = pl.multiple_of(index * rows, rows)
        if extra:
            block[0] = extra[away][...]

        @pl.when(index == 0)
        def first():
            block[first_kind:] = main_ref[:, :rows, :]

        @pl.when(index > 0)
        def later():
            behind = pl.multiple_of(start - rows, rows)
            block[first_kind:] = (
                main_ref[:, pl.ds(start, rows), :].astype(jnp.float32)
                + far_ref[:, pl.ds(behind, rows), :].astype(jnp.float32)
            ).astype(jnp.bfloat16)


def settle(main, far, extra=(), after=()):
    _, total, width = main.shape
    rows = total // GROUP
    count = 2 + (1 if extra else 0)

    def kernel(main_ref, far_ref, *refs):
        refs = list(refs)
        settle_kernel(main_ref, far_ref, *refs[: len(extra)], *refs[-GROUP:])

    return pl.pallas_call(
        kernel,
        out_shape=(jax.ShapeDtypeStruct((count, rows, width), jnp.bfloat16),) * GROUP,
        in_specs=[VMEM, VMEM] + [VMEM] * len(extra) + [ANY] * len(after),
        out_specs=(VMEM,) * GROUP,
        compiler_params=SMALL,
        cost_estimate=pl.CostEstimate(
            flops=SETTLE_COST if extra else 0, bytes_accessed=main.size * 8, transcendentals=0
        ),
        name="settle",
    )(main, far, *extra, *after)


def place_copies(moves, sems):
    copies = []
    for source, target, chunk, away in moves:
        lanes = columns(lax.rem(lax.axis_index("ctx"), GROUP), -away, chunk, source.shape[1])
        copies.append(pltpu.make_async_copy(source, target.at[:, lanes], sems.at[len(copies)]))
    for copy in copies:
        copy.start()
    for copy in copies:
        copy.wait()


def early_kernel(*refs):
    queries, mixed = refs[:GROUP], refs[GROUP : 2 * GROUP]
    query_ref, key_ref, value_ref, sems = refs[2 * GROUP :]
    moves = []
    for away in range(GROUP):
        moves += [
            (queries[away], query_ref, 0, away),
            (mixed[away].at[0], query_ref, 1, away),
            (mixed[away].at[1], key_ref, 0, away),
            (mixed[away].at[2], value_ref, 0, away),
        ]
    place_copies(moves, sems)


def late_kernel(*refs):
    pairs = refs[:GROUP]
    key_ref, value_ref, sems = refs[GROUP + 2 :]
    moves = []
    for away in range(GROUP):
        moves += [
            (pairs[away].at[0], key_ref, 1, away),
            (pairs[away].at[1], value_ref, 1, away),
        ]
    place_copies(moves, sems)


def gathered(queries, mixed, pairs):
    rows, width = queries[0].shape
    out = jax.ShapeDtypeStruct((rows, width * CHUNKS * GROUP), jnp.bfloat16)
    grad_queries, grad_keys, grad_values = pl.pallas_call(
        early_kernel,
        out_shape=(out, out, out),
        in_specs=[VMEM] * (2 * GROUP),
        out_specs=(ANY,) * 3,
        scratch_shapes=[pltpu.SemaphoreType.DMA((4 * GROUP,))],
        compiler_params=SMALL,
        cost_estimate=pl.CostEstimate(flops=0, bytes_accessed=out.size * 6, transcendentals=0),
        name="early",
    )(*queries, *mixed)
    grad_keys, grad_values = pl.pallas_call(
        late_kernel,
        out_shape=(out, out),
        in_specs=[VMEM] * GROUP + [ANY, ANY],
        out_specs=(ANY, ANY),
        input_output_aliases={GROUP: 0, GROUP + 1: 1},
        scratch_shapes=[pltpu.SemaphoreType.DMA((2 * GROUP,))],
        compiler_params=SMALL,
        cost_estimate=pl.CostEstimate(flops=0, bytes_accessed=out.size * 6, transcendentals=0),
        name="late",
    )(*pairs, grad_keys, grad_values)
    return grad_queries, grad_keys, grad_values


def shards(queries, keys, values, grad_out, lengths, image_flags):
    query_rows, key_rows, value_rows, grad_rows = queries[0], keys[0], values[0], grad_out[0]
    row_count = query_rows.shape[0]
    cycle_size = lax.axis_size("ctx")
    samples = lax.axis_size("dp")

    def swap(value, away):
        pairs = [
            (source, source - source % GROUP + (source + away) % GROUP)
            for source in range(cycle_size)
        ]
        return lax.ppermute(value, "ctx", pairs)

    def next_row(value, rows):
        pairs = [(source, (source + rows * GROUP) % cycle_size) for source in range(cycle_size)]
        return lax.ppermute(value, "ctx", pairs)

    def swapped(messages):
        one = swap(messages[0], 1)
        three = swap(messages[2], 3)
        return [one, swap(messages[1], 2), three]

    first_messages, text = first_pack(key_rows, value_rows, lengths, image_flags)
    texts = [text] + [
        lax.ppermute(text, "dp", [(source, (source + away) % samples) for source in range(samples)])
        for away in range(1, samples)
    ]
    total_rows = float(row_count * cycle_size * samples)

    ending = jnp.cumsum(lengths[0])
    bounds = jnp.stack([ending - lengths[0], ending, image_flags[0]])
    bounds = jnp.pad(bounds, ((0, 5), (0, HEAD - bounds.shape[1])))
    key_packs, query_packs, edges = [None] * CHUNKS, [None] * CHUNKS, [None] * CHUNKS
    key_packs[0] = first_messages
    key_packs[1] = pack(key_rows, value_rows, text, 1)
    key_blocks = [swapped(messages) for messages in key_packs]
    edges[0] = make_edge(
        key_rows, value_rows, key_blocks[0], (*texts[1:], key_packs[1][0]), 0, EDGE_COST[0]
    )
    after = edges[0]
    for index in range(CHUNKS):
        query_packs[index] = pack(query_rows, grad_rows, after, index)
        after = query_packs[index][0]
    marks = sides(bounds, after, row_count // 2, cycle_size)
    edges[1] = make_edge(
        key_rows, value_rows, key_blocks[1], (marks[1],), 1, EDGE_COST[1]
    )
    query_blocks = [swapped(messages) for messages in query_packs]
    edges = [next_row(edge, 1) for edge in edges]
    arrays = (query_rows, key_rows, value_rows, grad_rows)
    halves = []
    for chunk in range(CHUNKS):
        *query_grads, main, far = attend(
            texts, marks, arrays,
            key_blocks[chunk], query_blocks[chunk], edges[chunk], chunk, total_rows,
        )
        halves.append((query_grads, main, next_row(far, -1)))
    (first_queries, main, far), (second_queries, last_main, last_far) = halves
    queries = [first_queries[0]] + swapped(first_queries[1:])
    mixed = settle(main, far, extra=second_queries, after=queries[1:])
    pairs = settle(last_main, last_far)
    mixed = [mixed[0]] + swapped(mixed[1:])
    pairs = [pairs[0]] + swapped(pairs[1:])
    grad_queries, grad_keys, grad_values = gathered(queries, mixed, pairs)
    return grad_queries[None], grad_keys[None], grad_values[None]


def solution(mesh):
    in_specs = (
        P("dp", "ctx", None),
        P("dp", "ctx", None),
        P("dp", "ctx", None),
        P("dp", "ctx", None),
        P("dp", None),
        P("dp", None),
    )
    out_specs = (P("dp", "ctx", None), P("dp", "ctx", None), P("dp", "ctx", None))
    return jax.shard_map(shards, mesh=mesh, in_specs=in_specs, out_specs=out_specs, check_vma=False)
```

time: 447 us -> 89.4 us (0.20)
  waiting for transfers between devices: 219 us -> 20.4 us
  blocking collectives: 90.9 us -> 0 us
  local copies, waits for them, and re-layouts: 49.9 us -> 0.03 us
  other arithmetic: 28.5 us -> 0.22 us
  matrix products: 27.7 us -> 0 us
  starting transfers between devices: 28.2 us -> 48.9 us
  Pallas kernels: 0 us -> 18.7 us
    ppermute x12 -> x28, waiting for transfers between devices: 219 us -> 20.4 us  [the longest x21 10.5 us: swap(): return lax.ppermute(value, 'ctx', pairs)]
    psum x1 -> x0, blocking collectives: 90.9 us -> none  [shards(): text_count = lax.psum(jnp.sum(text_rows), ('dp', 'ctx'))]
    dot_general x24 -> x0, matrix products: 27.7 us -> none  [the longest x4 8.36 us: shards(): jnp.einsum('hqk,qhd->khd', dscore, queries_grp, preferred_element_type=jn...]
    reshape x16 -> x0, local copies, waits for them, and re-layouts: 27.2 us -> none  [the longest x4 13.4 us: shards(): value_parts.append(grad_value.reshape(key_span, group_width))]
    ppermute x12 -> x28, starting transfers between devices: 28.2 us -> 48.9 us  [the longest x21 32.4 us: swap(): return lax.ppermute(value, 'ctx', pairs)]
    pallas_call x0 -> x13, Pallas kernels: none -> 18.7 us  [the longest x2 12.6 us: attend(): pl.pallas_call(functools.partial(attend_kernel, chunk, total_rows), out_s...]
    concatenate x10 -> x0, other arithmetic: 13.6 us -> none  [the longest x1 3.72 us: shards(): window_values = jnp.concatenate(value_blocks, axis=0)]
    ppermute x6 -> x0, local copies, waits for them, and re-layouts: 10.9 us -> none  [shifted(): return lax.ppermute(value, axis, pairs)]
  transfers between devices with their start and end apart: 12 -> 28, of which waited for: 10 -> 9; matrix products, arithmetic and copies ran while one was open for 9% -> 0% of each run, Pallas kernels for 0% -> 17%
where the time goes in v1:
time: 89.4 us; the launch traced here: 89.2 us
  starting transfers between devices  48.9 us (55%)
  waiting for transfers between devices  20.4 us (23%)
  Pallas kernels  18.7 us (21%)
  between operations  1.01 us (1%)
    ppermute x21, starting transfers between devices, swap(): return lax.ppermute(value, 'ctx', pairs)  32.4 us
    ppermute x4, starting transfers between devices, next_row(): return lax.ppermute(value, 'ctx', pairs)  13.7 us
    pallas_call x2, Pallas kernels, attend(): pl.pallas_call(functools.partial(attend_kernel, chunk, total_rows), out_s...  12.6 us
    ppermute x21, waiting for transfers between devices, swap(): return lax.ppermute(value, 'ctx', pairs)  10.5 us
    ppermute x4, waiting for transfers between devices, next_row(): return lax.ppermute(value, 'ctx', pairs)  8.6 us
    pallas_call x1, Pallas kernels, first_pack(): pl.pallas_call(first_pack_kernel, out_shape=(message,) * (GROUP - 1) + (j...  2.79 us
    ppermute x3, starting transfers between devices, shards(): lax.ppermute(text, 'dp', [(source, (source + away) % samples) for source...  2.73 us
  transfers between devices with their start and end apart: 28, of which 9 were waited for; matrix products, arithmetic and copies ran while one was open for 0% of the time, Pallas kernels for 17%

profile of v1, /device:TPU:0, one launch (start us, length us, event | category | flops | bytes accessed | tf_op | source)
XLA Modules:
  0.0 89.2 jit_solution(3630087550469478651)
XLA Ops:
  0.7 2.8 %first_pack.1 = (bf16[2,192,256]{2,1,0:T(8,128)(2,1)}, bf16[2,192,256]{2,1,0:T(8,128)(2,1)}, bf16[2,192,256]{2,1,0:T(8,128)(2,1)}, f32[1,32]{1,0:T(1,128)}) custom-call(bf16[192,2048]{1,0:T(8,128)(2,1)} %bitcast.7, bf16[192,2048]{1,0:T(8,128)(2,1)} %bitcast.13, s32[1,32]{1,0:T(1,128)} %lengths.1, s32[1,32]{1,0:T(1,128)} %flags.1), custom_call_target="tpu_custom_call" | custom-call | bytes 1179648 | tf_op jit(solution)/shard_map/first_pack/pallas_call | solution.py:73
  3.4 1.7 %collective-permute-start.3 = (bf16[2,192,256]{2,1,0:T(8,128)(2,1)}, bf16[2,192,256]{2,1,0:T(8,128)(2,1)S(1)}, u32[]{:S(2)}, u32[]{:S(2)}) collective-permute-start(bf16[2,192,256]{2,1,0:T(8,128)(2,1)} %get-tuple-element.45), channel_id=1, source_target_pairs={{0,1},{1,2},{2,3},{3,0},{4,5},{5,6},{6,7},{7,4},{8,9},{9,10},{10,1... | collective-permute-start | bytes 589832 | tf_op jit(solution)/shard_map/ppermute | solution.py:403
  5.2 2.9 %collective-permute-start.4 = (bf16[2,192,256]{2,1,0:T(8,128)(2,1)}, bf16[2,192,256]{2,1,0:T(8,128)(2,1)S(1)}, u32[]{:S(2)}, u32[]{:S(2)}) collective-permute-start(bf16[2,192,256]{2,1,0:T(8,128)(2,1)} %get-tuple-element.46), channel_id=1, source_target_pairs={{0,2},{1,3},{2,0},{3,1},{4,6},{5,7},{6,4},{7,5},{8,10},{9,11},{10,... | collective-permute-start | bytes 589832 | tf_op jit(solution)/shard_map/ppermute | solution.py:403
  8.1 1.3 %collective-permute-start.5 = (bf16[2,192,256]{2,1,0:T(8,128)(2,1)}, bf16[2,192,256]{2,1,0:T(8,128)(2,1)S(1)}, u32[]{:S(2)}, u32[]{:S(2)}) collective-permute-start(bf16[2,192,256]{2,1,0:T(8,128)(2,1)} %get-tuple-element.47), channel_id=1, source_target_pairs={{0,3},{1,0},{2,1},{3,2},{4,7},{5,4},{6,5},{7,6},{8,11},{9,8},{10,9... | collective-permute-start | bytes 589832 | tf_op jit(solution)/shard_map/ppermute | solution.py:403
  9.5 1.4 %collective-permute-start.1 = (f32[1,32]{1,0:T(1,128)S(1)}, f32[1,32]{1,0:T(1,128)S(1)}, u32[]{:S(2)}, u32[]{:S(2)}) collective-permute-start(f32[1,32]{1,0:T(1,128)S(1)} %copy-done.4), channel_id=1, source_target_pairs={{0,64},{32,96},{64,0},{96,32},{1,65},{33,97},{65,1},{97,33},{2,66}... | collective-permute-start | bytes 392 | tf_op jit(solution)/shard_map/ppermute | solution.py:416
  11.0 1.2 %collective-permute-start = (f32[1,32]{1,0:T(1,128)S(1)}, f32[1,32]{1,0:T(1,128)S(1)}, u32[]{:S(2)}, u32[]{:S(2)}) collective-permute-start(f32[1,32]{1,0:T(1,128)S(1)} %copy-done.4), channel_id=1, source_target_pairs={{0,32},{32,64},{64,96},{96,0},{1,33},{33,65},{65,97},{97,1},{2,34}... | collective-permute-start | bytes 392 | tf_op jit(solution)/shard_map/ppermute | solution.py:416
  12.3 0.8 collective-permute-done.1.refs_1_.text_three
  14.1 2.4 %collective-permute-start.16 = (bf16[2,192,256]{2,1,0:T(8,128)(2,1)S(1)}, bf16[2,192,256]{2,1,0:T(8,128)(2,1)S(1)}, u32[]{:S(2)}, u32[]{:S(2)}) collective-permute-start(bf16[2,192,256]{2,1,0:T(8,128)(2,1)S(1)} %get-tuple-element.63), channel_id=1, source_target_pairs={{0,3},{1,0},{2,1},{3,2},{4,7},{5,4},{6,5},{7,6},{8,11},{9,8},{10,9... | collective-permute-start | bytes 589832 | tf_op jit(solution)/shard_map/ppermute | solution.py:403
  16.7 1.1 %collective-permute-done.4.two.key_two = bf16[2,192,256]{2,1,0:T(8,128)(2,1)S(1)} collective-permute-done((bf16[2,192,256]{2,1,0:T(8,128)(2,1)}, bf16[2,192,256]{2,1,0:T(8,128)(2,1)S(1)}, u32[]{:S(2)}, u32[]{:S(2)}) %collective-permute-start.4) | collective-permute-done | bytes 196640 | tf_op jit(solution)/shard_map/ppermute | solution.py:403
  17.9 3.2 %collective-permute-start.9 = (bf16[2,576,256]{2,1,0:T(8,128)(2,1)S(1)}, bf16[2,576,256]{2,1,0:T(8,128)(2,1)S(1)}, u32[]{:S(2)}, u32[]{:S(2)}) collective-permute-start(bf16[2,576,256]{2,1,0:T(8,128)(2,1)S(1)} %edge.2.after), channel_id=1, source_target_pairs={{0,4},{1,5},{2,6},{3,7},{4,8},{5,9},{6,10},{7,11},{8,12},{9,13},{1... | collective-permute-start | bytes 1769480 | tf_op jit(solution)/shard_map/ppermute | solution.py:407
  21.2 4.2 %collective-permute-start.6 = (bf16[2,192,256]{2,1,0:T(8,128)(2,1)S(1)}, bf16[2,192,256]{2,1,0:T(8,128)(2,1)S(1)}, u32[]{:S(2)}, u32[]{:S(2)}) collective-permute-start(bf16[2,192,256]{2,1,0:T(8,128)(2,1)S(1)} %get-tuple-element.49.after), channel_id=1, source_target_pairs={{0,1},{1,2},{2,3},{3,0},{4,5},{5,6},{6,7},{7,4},{8,9},{9,10},{10,1... | collective-permute-start | bytes 589832 | tf_op jit(solution)/shard_map/ppermute | solution.py:403
  25.9 2.3 %collective-permute-start.7 = (bf16[2,192,256]{2,1,0:T(8,128)(2,1)S(1)}, bf16[2,192,256]{2,1,0:T(8,128)(2,1)S(1)}, u32[]{:S(2)}, u32[]{:S(2)}) collective-permute-start(bf16[2,192,256]{2,1,0:T(8,128)(2,1)S(1)} %get-tuple-element.54), channel_id=1, source_target_pairs={{0,2},{1,3},{2,0},{3,1},{4,6},{5,7},{6,4},{7,5},{8,10},{9,11},{10,... | collective-permute-start | bytes 589832 | tf_op jit(solution)/shard_map/ppermute | solution.py:403
  28.7 3.2 %collective-permute-start.20 = (bf16[2,576,256]{2,1,0:T(8,128)(2,1)S(1)}, bf16[2,576,256]{2,1,0:T(8,128)(2,1)S(1)}, u32[]{:S(2)}, u32[]{:S(2)}) collective-permute-start(bf16[2,576,256]{2,1,0:T(8,128)(2,1)S(1)} %edge.3), channel_id=1, source_target_pairs={{0,4},{1,5},{2,6},{3,7},{4,8},{5,9},{6,10},{7,11},{8,12},{9,13},{1... | collective-permute-start | bytes 1769480 | tf_op jit(solution)/shard_map/ppermute | solution.py:407
  31.9 2.9 %collective-permute-done.7.query_two = bf16[2,192,256]{2,1,0:T(8,128)(2,1)S(1)} collective-permute-done((bf16[2,192,256]{2,1,0:T(8,128)(2,1)S(1)}, bf16[2,192,256]{2,1,0:T(8,128)(2,1)S(1)}, u32[]{:S(2)}, u32[]{:S(2)}) %collective-permute-start.7) | collective-permute-done | bytes 196640 | tf_op jit(solution)/shard_map/ppermute | solution.py:403
  34.8 1.9 %collective-permute-start.18 = (bf16[2,192,256]{2,1,0:T(8,128)(2,1)S(1)}, bf16[2,192,256]{2,1,0:T(8,128)(2,1)S(1)}, u32[]{:S(2)}, u32[]{:S(2)}) collective-permute-start(bf16[2,192,256]{2,1,0:T(8,128)(2,1)S(1)} %get-tuple-element.64), channel_id=1, source_target_pairs={{0,2},{1,3},{2,0},{3,1},{4,6},{5,7},{6,4},{7,5},{8,10},{9,11},{10,... | collective-permute-start | bytes 589832 | tf_op jit(solution)/shard_map/ppermute | solution.py:403
  36.6 1.9 %collective-permute-start.19 = (bf16[2,192,256]{2,1,0:T(8,128)(2,1)S(1)}, bf16[2,192,256]{2,1,0:T(8,128)(2,1)S(1)}, u32[]{:S(2)}, u32[]{:S(2)}) collective-permute-start(bf16[2,192,256]{2,1,0:T(8,128)(2,1)S(1)} %get-tuple-element.65), channel_id=1, source_target_pairs={{0,3},{1,0},{2,1},{3,2},{4,7},{5,4},{6,5},{7,6},{8,11},{9,8},{10,9... | collective-permute-start | bytes 589832 | tf_op jit(solution)/shard_map/ppermute | solution.py:403
  38.5 6.3 %attend.2 = (bf16[192,256]{1,0:T(8,128)(2,1)S(1)}, bf16[192,256]{1,0:T(8,128)(2,1)S(1)}, bf16[192,256]{1,0:T(8,128)(2,1)S(1)}, bf16[192,256]{1,0:T(8,128)(2,1)S(...) custom-call(f32[1,32]{1,0:T(1,128)S(1)} %copy-done.4, ...), custom_call_target="tpu_custom_call" | custom-call | flops 4499999744 | tf_op jit(solution)/shard_map/attend/pallas_call | solution.py:255
  44.8 6.6 %collective-permute-start.13 = (bf16[2,576,256]{2,1,0:T(8,128)(2,1)S(1)}, bf16[2,576,256]{2,1,0:T(8,128)(2,1)S(1)}, u32[]{:S(2)}, u32[]{:S(2)}) collective-permute-start(bf16[2,576,256]{2,1,0:T(8,128)(2,1)S(1)} %get-tuple-element.61), channel_id=1, source_target_pairs={{0,28},{1,29},{2,30},{3,31},{4,0},{5,1},{6,2},{7,3},{8,4},{9,5},{1... | collective-permute-start | bytes 1769480 | tf_op jit(solution)/shard_map/ppermute | solution.py:407
  51.7 3.4 %collective-permute-start.11 = (bf16[192,256]{1,0:T(8,128)(2,1)S(1)}, bf16[192,256]{1,0:T(8,128)(2,1)S(1)}, u32[]{:S(2)}, u32[]{:S(2)}) collective-permute-start(bf16[192,256]{1,0:T(8,128)(2,1)S(1)} %get-tuple-element.58), channel_id=1, source_target_pairs={{0,2},{1,3},{2,0},{3,1},{4,6},{5,7},{6,4},{7,5},{8,10},{9,11},{10,... | collective-permute-start | bytes 294920 | tf_op jit(solution)/shard_map/ppermute | solution.py:403
  55.1 1.0 %collective-permute-start.12 = (bf16[192,256]{1,0:T(8,128)(2,1)S(1)}, bf16[192,256]{1,0:T(8,128)(2,1)S(1)}, u32[]{:S(2)}, u32[]{:S(2)}) collective-permute-start(bf16[192,256]{1,0:T(8,128)(2,1)S(1)} %get-tuple-element.59), channel_id=1, source_target_pairs={{0,3},{1,0},{2,1},{3,2},{4,7},{5,4},{6,5},{7,6},{8,11},{9,8},{10,9... | collective-permute-start | bytes 294920 | tf_op jit(solution)/shard_map/ppermute | solution.py:403
  56.1 6.3 %attend.3 = (bf16[192,256]{1,0:T(8,128)(2,1)S(1)}, bf16[192,256]{1,0:T(8,128)(2,1)S(1)}, bf16[192,256]{1,0:T(8,128)(2,1)S(1)}, bf16[192,256]{1,0:T(8,128)(2,1)S(...) custom-call(f32[1,32]{1,0:T(1,128)S(1)} %copy-done.4, ...), custom_call_target="tpu_custom_call" | custom-call | flops 4499999744 | tf_op jit(solution)/shard_map/attend/pallas_call | solution.py:255
  62.4 0.8 collective-permute-start.24
  63.5 1.8 %collective-permute-start.21 = (bf16[3,192,256]{2,1,0:T(8,128)(2,1)S(1)}, bf16[3,192,256]{2,1,0:T(8,128)(2,1)S(1)}, u32[]{:S(2)}, u32[]{:S(2)}) collective-permute-start(bf16[3,192,256]{2,1,0:T(8,128)(2,1)S(1)} %get-tuple-element.71), channel_id=1, source_target_pairs={{0,1},{1,2},{2,3},{3,0},{4,5},{5,6},{6,7},{7,4},{8,9},{9,10},{10,1... | collective-permute-start | bytes 884744 | tf_op jit(solution)/shard_map/ppermute | solution.py:403
  65.9 2.1 %collective-permute-start.23 = (bf16[3,192,256]{2,1,0:T(8,128)(2,1)S(1)}, bf16[3,192,256]{2,1,0:T(8,128)(2,1)S(1)}, u32[]{:S(2)}, u32[]{:S(2)}) collective-permute-start(bf16[3,192,256]{2,1,0:T(8,128)(2,1)S(1)} %get-tuple-element.73), channel_id=1, source_target_pairs={{0,3},{1,0},{2,1},{3,2},{4,7},{5,4},{6,5},{7,6},{8,11},{9,8},{10,9... | collective-permute-start | bytes 884744 | tf_op jit(solution)/shard_map/ppermute | solution.py:403
  68.0 8.6 %collective-permute-done.24.far_ref = bf16[2,576,256]{2,1,0:T(8,128)(2,1)S(1)} collective-permute-done((bf16[2,576,256]{2,1,0:T(8,128)(2,1)S(1)}, bf16[2,576,256]{2,1,0:T(8,128)(2,1)S(1)}, u32[]{:S(2)}, u32[]{:S(2)}) %collective-permute-start.24) | collective-permute-done | bytes 589856 | tf_op jit(solution)/shard_map/ppermute | solution.py:407
  76.9 1.8 %collective-permute-start.26 = (bf16[2,192,256]{2,1,0:T(8,128)(2,1)S(1)}, bf16[2,192,256]{2,1,0:T(8,128)(2,1)S(1)}, u32[]{:S(2)}, u32[]{:S(2)}) collective-permute-start(bf16[2,192,256]{2,1,0:T(8,128)(2,1)S(1)} %get-tuple-element.79), channel_id=1, source_target_pairs={{0,2},{1,3},{2,0},{3,1},{4,6},{5,7},{6,4},{7,5},{8,10},{9,11},{10,... | collective-permute-start | bytes 589832 | tf_op jit(solution)/shard_map/ppermute | solution.py:403
  78.7 0.8 collective-permute-done.21.refs_5_
  79.4 1.8 %collective-permute-start.27 = (bf16[2,192,256]{2,1,0:T(8,128)(2,1)S(1)}, bf16[2,192,256]{2,1,0:T(8,128)(2,1)S(1)}, u32[]{:S(2)}, u32[]{:S(2)}) collective-permute-start(bf16[2,192,256]{2,1,0:T(8,128)(2,1)S(1)} %get-tuple-element.80), channel_id=1, source_target_pairs={{0,3},{1,0},{2,1},{3,2},{4,7},{5,4},{6,5},{7,6},{8,11},{9,8},{10,9... | collective-permute-start | bytes 589832 | tf_op jit(solution)/shard_map/ppermute | solution.py:403
  81.2 1.3 %early.1 = (bf16[192,2048]{1,0:T(8,128)(2,1)}, bf16[192,2048]{1,0:T(8,128)(2,1)}, bf16[192,2048]{1,0:T(8,128)(2,1)}) custom-call(bf16[192,256]{1,0:T(8,128)(2,1)S(1)} %get-tuple-element.56.refs_0_, bf16[192,256]{1,0:T(8,128)(2,1)S(1)} %collective-permute-done.10.refs_4_.refs_1_, bf16[192,256]{1,0:T(8,128)(2,1)S(1)} %collective-permute-done.11.refs_5_.refs_2_, ...), custom_call_target="tpu_custom_call" | custom-call | bytes 2359296 | tf_op jit(solution)/shard_map/early/pallas_call | solution.py:368
  82.5 5.0 %collective-permute-done.25.refs_1_ = bf16[2,192,256]{2,1,0:T(8,128)(2,1)S(1)} collective-permute-done((bf16[2,192,256]{2,1,0:T(8,128)(2,1)S(1)}, bf16[2,192,256]{2,1,0:T(8,128)(2,1)S(1)}, u32[]{:S(2)}, u32[]{:S(2)}) %collective-permute-start.25) | collective-permute-done | bytes 196640 | tf_op jit(solution)/shard_map/ppermute | solution.py:403
  87.5 0.7 collective-permute-done.27.refs_3_
  88.1 0.9 %late.1 = (bf16[192,2048]{1,0:T(8,128)(2,1)}, bf16[192,2048]{1,0:T(8,128)(2,1)}) custom-call(bf16[2,192,256]{2,1,0:T(8,128)(2,1)S(1)} %get-tuple-element.77.refs_0_, bf16[2,192,256]{2,1,0:T(8,128)(2,1)S(1)} %collective-permute-done.25.refs_1_, ...), custom_call_target="tpu_custom_call", output_to_operand_aliasing={{0}: (4, {}), {1}: (5, {})} | custom-call | bytes 2359296 | tf_op jit(solution)/shard_map/late/pallas_call | solution.py:378
  (55 shorter events, 4.1 us)
Async XLA Ops:
  0.6 10.3 %copy-start = (bf16[1,192,2048]{2,1,0:T(8,128)(2,1)S(1)}, bf16[1,192,2048]{2,1,0:T(8,128)(2,1)}, u32[]{:S(2)}) copy-start(bf16[1,192,2048]{2,1,0:T(8,128)(2,1)} %param.7) | copy-start | bytes 2359300
  0.6 10.3 %copy-start.1 = (bf16[1,192,2048]{2,1,0:T(8,128)(2,1)S(1)}, bf16[1,192,2048]{2,1,0:T(8,128)(2,1)}, u32[]{:S(2)}) copy-start(bf16[1,192,2048]{2,1,0:T(8,128)(2,1)} %param.8) | copy-start | bytes 2359300
  3.4 13.0 %collective-permute-start.3 = (bf16[2,192,256]{2,1,0:T(8,128)(2,1)}, bf16[2,192,256]{2,1,0:T(8,128)(2,1)S(1)}, u32[]{:S(2)}, u32[]{:S(2)}) collective-permute-start(bf16[2,192,256]{2,1,0:T(8,128)(2,1)} %get-tuple-element.45), channel_id=1, source_target_pairs={{0,1},{1,2},{2,3},{3,0},{4,5},{5,6},{6,7},{7,4},{8,9},{9,10},{10,1... | collective-permute-start | bytes 589832 | tf_op jit(solution)/shard_map/ppermute | solution.py:403
  5.2 12.5 %collective-permute-start.4 = (bf16[2,192,256]{2,1,0:T(8,128)(2,1)}, bf16[2,192,256]{2,1,0:T(8,128)(2,1)S(1)}, u32[]{:S(2)}, u32[]{:S(2)}) collective-permute-start(bf16[2,192,256]{2,1,0:T(8,128)(2,1)} %get-tuple-element.46), channel_id=1, source_target_pairs={{0,2},{1,3},{2,0},{3,1},{4,6},{5,7},{6,4},{7,5},{8,10},{9,11},{10,... | collective-permute-start | bytes 589832 | tf_op jit(solution)/shard_map/ppermute | solution.py:403
  8.1 9.7 %collective-permute-start.5 = (bf16[2,192,256]{2,1,0:T(8,128)(2,1)}, bf16[2,192,256]{2,1,0:T(8,128)(2,1)S(1)}, u32[]{:S(2)}, u32[]{:S(2)}) collective-permute-start(bf16[2,192,256]{2,1,0:T(8,128)(2,1)} %get-tuple-element.47), channel_id=1, source_target_pairs={{0,3},{1,0},{2,1},{3,2},{4,7},{5,4},{6,5},{7,6},{8,11},{9,8},{10,9... | collective-permute-start | bytes 589832 | tf_op jit(solution)/shard_map/ppermute | solution.py:403
  9.4 1.6 %collective-permute-start.2 = (f32[1,32]{1,0:T(1,128)S(1)}, f32[1,32]{1,0:T(1,128)S(1)}, u32[]{:S(2)}, u32[]{:S(2)}) collective-permute-start(f32[1,32]{1,0:T(1,128)S(1)} %copy-done.4), channel_id=1, source_target_pairs={{0,96},{32,0},{64,32},{96,64},{1,97},{33,1},{65,33},{97,65},{2,98}... | collective-permute-start | bytes 392 | tf_op jit(solution)/shard_map/ppermute | solution.py:416
  9.5 3.5 %collective-permute-start.1 = (f32[1,32]{1,0:T(1,128)S(1)}, f32[1,32]{1,0:T(1,128)S(1)}, u32[]{:S(2)}, u32[]{:S(2)}) collective-permute-start(f32[1,32]{1,0:T(1,128)S(1)} %copy-done.4), channel_id=1, source_target_pairs={{0,64},{32,96},{64,0},{96,32},{1,65},{33,97},{65,1},{97,33},{2,66}... | collective-permute-start | bytes 392 | tf_op jit(solution)/shard_map/ppermute | solution.py:416
  11.0 3.0 %collective-permute-start = (f32[1,32]{1,0:T(1,128)S(1)}, f32[1,32]{1,0:T(1,128)S(1)}, u32[]{:S(2)}, u32[]{:S(2)}) collective-permute-start(f32[1,32]{1,0:T(1,128)S(1)} %copy-done.4), channel_id=1, source_target_pairs={{0,32},{32,64},{64,96},{96,0},{1,33},{33,65},{65,97},{97,1},{2,34}... | collective-permute-start | bytes 392 | tf_op jit(solution)/shard_map/ppermute | solution.py:416
  13.1 12.8 %collective-permute-start.15 = (bf16[2,192,256]{2,1,0:T(8,128)(2,1)S(1)}, bf16[2,192,256]{2,1,0:T(8,128)(2,1)S(1)}, u32[]{:S(2)}, u32[]{:S(2)}) collective-permute-start(bf16[2,192,256]{2,1,0:T(8,128)(2,1)S(1)} %get-tuple-element.62), channel_id=1, source_target_pairs={{0,2},{1,3},{2,0},{3,1},{4,6},{5,7},{6,4},{7,5},{8,10},{9,11},{10,... | collective-permute-start | bytes 589832 | tf_op jit(solution)/shard_map/ppermute | solution.py:403
  14.1 14.1 %collective-permute-start.16 = (bf16[2,192,256]{2,1,0:T(8,128)(2,1)S(1)}, bf16[2,192,256]{2,1,0:T(8,128)(2,1)S(1)}, u32[]{:S(2)}, u32[]{:S(2)}) collective-permute-start(bf16[2,192,256]{2,1,0:T(8,128)(2,1)S(1)} %get-tuple-element.63), channel_id=1, source_target_pairs={{0,3},{1,0},{2,1},{3,2},{4,7},{5,4},{6,5},{7,6},{8,11},{9,8},{10,9... | collective-permute-start | bytes 589832 | tf_op jit(solution)/shard_map/ppermute | solution.py:403
  16.4 12.2 %collective-permute-start.14 = (bf16[2,192,256]{2,1,0:T(8,128)(2,1)S(1)}, bf16[2,192,256]{2,1,0:T(8,128)(2,1)S(1)}, u32[]{:S(2)}, u32[]{:S(2)}) collective-permute-start(bf16[2,192,256]{2,1,0:T(8,128)(2,1)S(1)} %get-tuple-element.48.refs_3_), channel_id=1, source_target_pairs={{0,1},{1,2},{2,3},{3,0},{4,5},{5,6},{6,7},{7,4},{8,9},{9,10},{10,1... | collective-permute-start | bytes 589832 | tf_op jit(solution)/shard_map/ppermute | solution.py:403
  16.6 4.4 %copy-start.2 = (bf16[1,192,2048]{2,1,0:T(8,128)(2,1)S(1)}, bf16[1,192,2048]{2,1,0:T(8,128)(2,1)}, u32[]{:S(2)}) copy-start(bf16[1,192,2048]{2,1,0:T(8,128)(2,1)} %param.6) | copy-start | bytes 2359300
  16.7 4.4 %copy-start.3 = (bf16[1,192,2048]{2,1,0:T(8,128)(2,1)S(1)}, bf16[1,192,2048]{2,1,0:T(8,128)(2,1)}, u32[]{:S(2)}) copy-start(bf16[1,192,2048]{2,1,0:T(8,128)(2,1)} %param.9) | copy-start | bytes 2359300
  17.9 20.7 %collective-permute-start.9 = (bf16[2,576,256]{2,1,0:T(8,128)(2,1)S(1)}, bf16[2,576,256]{2,1,0:T(8,128)(2,1)S(1)}, u32[]{:S(2)}, u32[]{:S(2)}) collective-permute-start(bf16[2,576,256]{2,1,0:T(8,128)(2,1)S(1)} %edge.2.after), channel_id=1, source_target_pairs={{0,4},{1,5},{2,6},{3,7},{4,8},{5,9},{6,10},{7,11},{8,12},{9,13},{1... | collective-permute-start | bytes 1769480 | tf_op jit(solution)/shard_map/ppermute | solution.py:407
  21.2 15.4 %collective-permute-start.6 = (bf16[2,192,256]{2,1,0:T(8,128)(2,1)S(1)}, bf16[2,192,256]{2,1,0:T(8,128)(2,1)S(1)}, u32[]{:S(2)}, u32[]{:S(2)}) collective-permute-start(bf16[2,192,256]{2,1,0:T(8,128)(2,1)S(1)} %get-tuple-element.49.after), channel_id=1, source_target_pairs={{0,1},{1,2},{2,3},{3,0},{4,5},{5,6},{6,7},{7,4},{8,9},{9,10},{10,1... | collective-permute-start | bytes 589832 | tf_op jit(solution)/shard_map/ppermute | solution.py:403
  25.9 8.9 %collective-permute-start.7 = (bf16[2,192,256]{2,1,0:T(8,128)(2,1)S(1)}, bf16[2,192,256]{2,1,0:T(8,128)(2,1)S(1)}, u32[]{:S(2)}, u32[]{:S(2)}) collective-permute-start(bf16[2,192,256]{2,1,0:T(8,128)(2,1)S(1)} %get-tuple-element.54), channel_id=1, source_target_pairs={{0,2},{1,3},{2,0},{3,1},{4,6},{5,7},{6,4},{7,5},{8,10},{9,11},{10,... | collective-permute-start | bytes 589832 | tf_op jit(solution)/shard_map/ppermute | solution.py:403
  28.1 6.6 %collective-permute-start.8 = (bf16[2,192,256]{2,1,0:T(8,128)(2,1)S(1)}, bf16[2,192,256]{2,1,0:T(8,128)(2,1)S(1)}, u32[]{:S(2)}, u32[]{:S(2)}) collective-permute-start(bf16[2,192,256]{2,1,0:T(8,128)(2,1)S(1)} %get-tuple-element.55), channel_id=1, source_target_pairs={{0,3},{1,0},{2,1},{3,2},{4,7},{5,4},{6,5},{7,6},{8,11},{9,8},{10,9... | collective-permute-start | bytes 589832 | tf_op jit(solution)/shard_map/ppermute | solution.py:403
  28.7 27.3 %collective-permute-start.20 = (bf16[2,576,256]{2,1,0:T(8,128)(2,1)S(1)}, bf16[2,576,256]{2,1,0:T(8,128)(2,1)S(1)}, u32[]{:S(2)}, u32[]{:S(2)}) collective-permute-start(bf16[2,576,256]{2,1,0:T(8,128)(2,1)S(1)} %edge.3), channel_id=1, source_target_pairs={{0,4},{1,5},{2,6},{3,7},{4,8},{5,9},{6,10},{7,11},{8,12},{9,13},{1... | collective-permute-start | bytes 1769480 | tf_op jit(solution)/shard_map/ppermute | solution.py:407
  34.8 20.3 %collective-permute-start.17 = (bf16[2,192,256]{2,1,0:T(8,128)(2,1)S(1)}, bf16[2,192,256]{2,1,0:T(8,128)(2,1)S(1)}, u32[]{:S(2)}, u32[]{:S(2)}) collective-permute-start(bf16[2,192,256]{2,1,0:T(8,128)(2,1)S(1)} %get-tuple-element.50.after), channel_id=1, source_target_pairs={{0,1},{1,2},{2,3},{3,0},{4,5},{5,6},{6,7},{7,4},{8,9},{9,10},{10,1... | collective-permute-start | bytes 589832 | tf_op jit(solution)/shard_map/ppermute | solution.py:403
  34.8 16.7 %collective-permute-start.18 = (bf16[2,192,256]{2,1,0:T(8,128)(2,1)S(1)}, bf16[2,192,256]{2,1,0:T(8,128)(2,1)S(1)}, u32[]{:S(2)}, u32[]{:S(2)}) collective-permute-start(bf16[2,192,256]{2,1,0:T(8,128)(2,1)S(1)} %get-tuple-element.64), channel_id=1, source_target_pairs={{0,2},{1,3},{2,0},{3,1},{4,6},{5,7},{6,4},{7,5},{8,10},{9,11},{10,... | collective-permute-start | bytes 589832 | tf_op jit(solution)/shard_map/ppermute | solution.py:403
  36.6 15.1 %collective-permute-start.19 = (bf16[2,192,256]{2,1,0:T(8,128)(2,1)S(1)}, bf16[2,192,256]{2,1,0:T(8,128)(2,1)S(1)}, u32[]{:S(2)}, u32[]{:S(2)}) collective-permute-start(bf16[2,192,256]{2,1,0:T(8,128)(2,1)S(1)} %get-tuple-element.65), channel_id=1, source_target_pairs={{0,3},{1,0},{2,1},{3,2},{4,7},{5,4},{6,5},{7,6},{8,11},{9,8},{10,9... | collective-permute-start | bytes 589832 | tf_op jit(solution)/shard_map/ppermute | solution.py:403
  44.8 18.4 %collective-permute-start.13 = (bf16[2,576,256]{2,1,0:T(8,128)(2,1)S(1)}, bf16[2,576,256]{2,1,0:T(8,128)(2,1)S(1)}, u32[]{:S(2)}, u32[]{:S(2)}) collective-permute-start(bf16[2,576,256]{2,1,0:T(8,128)(2,1)S(1)} %get-tuple-element.61), channel_id=1, source_target_pairs={{0,28},{1,29},{2,30},{3,31},{4,0},{5,1},{6,2},{7,3},{8,4},{9,5},{1... | collective-permute-start | bytes 1769480 | tf_op jit(solution)/shard_map/ppermute | solution.py:407
  51.4 11.8 %collective-permute-start.10 = (bf16[192,256]{1,0:T(8,128)(2,1)S(1)}, bf16[192,256]{1,0:T(8,128)(2,1)S(1)}, u32[]{:S(2)}, u32[]{:S(2)}) collective-permute-start(bf16[192,256]{1,0:T(8,128)(2,1)S(1)} %get-tuple-element.57), channel_id=1, source_target_pairs={{0,1},{1,2},{2,3},{3,0},{4,5},{5,6},{6,7},{7,4},{8,9},{9,10},{10,1... | collective-permute-start | bytes 294920 | tf_op jit(solution)/shard_map/ppermute | solution.py:403
  51.7 11.5 %collective-permute-start.11 = (bf16[192,256]{1,0:T(8,128)(2,1)S(1)}, bf16[192,256]{1,0:T(8,128)(2,1)S(1)}, u32[]{:S(2)}, u32[]{:S(2)}) collective-permute-start(bf16[192,256]{1,0:T(8,128)(2,1)S(1)} %get-tuple-element.58), channel_id=1, source_target_pairs={{0,2},{1,3},{2,0},{3,1},{4,6},{5,7},{6,4},{7,5},{8,10},{9,11},{10,... | collective-permute-start | bytes 294920 | tf_op jit(solution)/shard_map/ppermute | solution.py:403
  55.1 8.1 %collective-permute-start.12 = (bf16[192,256]{1,0:T(8,128)(2,1)S(1)}, bf16[192,256]{1,0:T(8,128)(2,1)S(1)}, u32[]{:S(2)}, u32[]{:S(2)}) collective-permute-start(bf16[192,256]{1,0:T(8,128)(2,1)S(1)} %get-tuple-element.59), channel_id=1, source_target_pairs={{0,3},{1,0},{2,1},{3,2},{4,7},{5,4},{6,5},{7,6},{8,11},{9,8},{10,9... | collective-permute-start | bytes 294920 | tf_op jit(solution)/shard_map/ppermute | solution.py:403
  62.4 14.2 %collective-permute-start.24 = (bf16[2,576,256]{2,1,0:T(8,128)(2,1)S(1)}, bf16[2,576,256]{2,1,0:T(8,128)(2,1)S(1)}, u32[]{:S(2)}, u32[]{:S(2)}) collective-permute-start(bf16[2,576,256]{2,1,0:T(8,128)(2,1)S(1)} %get-tuple-element.76), channel_id=1, source_target_pairs={{0,28},{1,29},{2,30},{3,31},{4,0},{5,1},{6,2},{7,3},{8,4},{9,5},{1... | collective-permute-start | bytes 1769480 | tf_op jit(solution)/shard_map/ppermute | solution.py:407
  63.5 16.0 %collective-permute-start.21 = (bf16[3,192,256]{2,1,0:T(8,128)(2,1)S(1)}, bf16[3,192,256]{2,1,0:T(8,128)(2,1)S(1)}, u32[]{:S(2)}, u32[]{:S(2)}) collective-permute-start(bf16[3,192,256]{2,1,0:T(8,128)(2,1)S(1)} %get-tuple-element.71), channel_id=1, source_target_pairs={{0,1},{1,2},{2,3},{3,0},{4,5},{5,6},{6,7},{7,4},{8,9},{9,10},{10,1... | collective-permute-start | bytes 884744 | tf_op jit(solution)/shard_map/ppermute | solution.py:403
  65.2 16.0 %collective-permute-start.22 = (bf16[3,192,256]{2,1,0:T(8,128)(2,1)S(1)}, bf16[3,192,256]{2,1,0:T(8,128)(2,1)S(1)}, u32[]{:S(2)}, u32[]{:S(2)}) collective-permute-start(bf16[3,192,256]{2,1,0:T(8,128)(2,1)S(1)} %get-tuple-element.72), channel_id=1, source_target_pairs={{0,2},{1,3},{2,0},{3,1},{4,6},{5,7},{6,4},{7,5},{8,10},{9,11},{10,... | collective-permute-start | bytes 884744 | tf_op jit(solution)/shard_map/ppermute | solution.py:403
  65.9 15.3 %collective-permute-start.23 = (bf16[3,192,256]{2,1,0:T(8,128)(2,1)S(1)}, bf16[3,192,256]{2,1,0:T(8,128)(2,1)S(1)}, u32[]{:S(2)}, u32[]{:S(2)}) collective-permute-start(bf16[3,192,256]{2,1,0:T(8,128)(2,1)S(1)} %get-tuple-element.73), channel_id=1, source_target_pairs={{0,3},{1,0},{2,1},{3,2},{4,7},{5,4},{6,5},{7,6},{8,11},{9,8},{10,9... | collective-permute-start | bytes 884744 | tf_op jit(solution)/shard_map/ppermute | solution.py:403
  76.8 10.6 %collective-permute-start.25 = (bf16[2,192,256]{2,1,0:T(8,128)(2,1)S(1)}, bf16[2,192,256]{2,1,0:T(8,128)(2,1)S(1)}, u32[]{:S(2)}, u32[]{:S(2)}) collective-permute-start(bf16[2,192,256]{2,1,0:T(8,128)(2,1)S(1)} %get-tuple-element.78), channel_id=1, source_target_pairs={{0,1},{1,2},{2,3},{3,0},{4,5},{5,6},{6,7},{7,4},{8,9},{9,10},{10,1... | collective-permute-start | bytes 589832 | tf_op jit(solution)/shard_map/ppermute | solution.py:403
  76.9 10.6 %collective-permute-start.26 = (bf16[2,192,256]{2,1,0:T(8,128)(2,1)S(1)}, bf16[2,192,256]{2,1,0:T(8,128)(2,1)S(1)}, u32[]{:S(2)}, u32[]{:S(2)}) collective-permute-start(bf16[2,192,256]{2,1,0:T(8,128)(2,1)S(1)} %get-tuple-element.79), channel_id=1, source_target_pairs={{0,2},{1,3},{2,0},{3,1},{4,6},{5,7},{6,4},{7,5},{8,10},{9,11},{10,... | collective-permute-start | bytes 589832 | tf_op jit(solution)/shard_map/ppermute | solution.py:403
  79.4 8.7 %collective-permute-start.27 = (bf16[2,192,256]{2,1,0:T(8,128)(2,1)S(1)}, bf16[2,192,256]{2,1,0:T(8,128)(2,1)S(1)}, u32[]{:S(2)}, u32[]{:S(2)}) collective-permute-start(bf16[2,192,256]{2,1,0:T(8,128)(2,1)S(1)} %get-tuple-element.80), channel_id=1, source_target_pairs={{0,3},{1,0},{2,1},{3,2},{4,7},{5,4},{6,5},{7,6},{8,11},{9,8},{10,9... | collective-permute-start | bytes 589832 | tf_op jit(solution)/shard_map/ppermute | solution.py:403
  (3 other events, 8.1 us)

commit v2 on v1

--- a/solution.py
+++ b/solution.py
@@ -16,8 +16,8 @@
 VMEM = pl.BlockSpec(memory_space=pltpu.VMEM)
 ANY = pl.BlockSpec(memory_space=pl.ANY)
 LARGE = pltpu.CompilerParams(vmem_limit_bytes=60 * 1024 * 1024)
-EDGE_COST = (0, 6000000000)
-SETTLE_COST = 3000000000
+EDGE_COST = (0, 3000000000)
+SETTLE_COST = 0
 SMALL = pltpu.CompilerParams(vmem_limit_bytes=10 * 1024 * 1024)
 
 
@@ -34,7 +34,7 @@
         message[1] = second[:, lanes]
 
 
-def first_pack_kernel(first, second, lengths, flags, one, two, three, text, sems):
+def first_pack_kernel(first, second, lengths, flags, one, two, three, text, held, sems):
     width = one.shape[2]
     place = lax.rem(lax.axis_index("ctx"), GROUP)
     copies = []
@@ -44,11 +44,13 @@
             copies.append(
                 pltpu.make_async_copy(source.at[:, lanes], message.at[part], sems.at[len(copies)])
             )
+    for part, source in enumerate((lengths, flags)):
+        copies.append(pltpu.make_async_copy(source, held.at[part], sems.at[len(copies)]))
     for copy in copies:
         copy.start()
-    text[...] = (lengths[...] * (1 - flags[...])).astype(jnp.float32)
     for copy in copies:
         copy.wait()
+    text[...] = (held[0] * (1 - held[1])).astype(jnp.float32)
 
 
 def pack(first, second, after, chunk):
@@ -73,9 +75,12 @@
     *messages, text = pl.pallas_call(
         first_pack_kernel,
         out_shape=(message,) * (GROUP - 1) + (jax.ShapeDtypeStruct(lengths.shape, jnp.float32),),
-        in_specs=[ANY, ANY, VMEM, VMEM],
+        in_specs=[ANY, ANY, ANY, ANY],
         out_specs=(VMEM,) * GROUP,
-        scratch_shapes=[pltpu.SemaphoreType.DMA((2 * (GROUP - 1),))],
+        scratch_shapes=[
+            pltpu.VMEM((2, *lengths.shape), lengths.dtype),
+            pltpu.SemaphoreType.DMA((2 * GROUP,)),
+        ],
         compiler_params=LARGE,
         cost_estimate=pl.CostEstimate(flops=0, bytes_accessed=12 * rows * width * 2, transcendentals=0),
         name="first_pack",
@@ -171,9 +176,11 @@
 def attend_kernel(
     chunk, total_rows, text_one, text_two, text_three, text_four, limit_ref, text_ref, keypos_ref,
     queries, keys, values, grads, key_one, key_two, key_three, query_one, query_two, query_three,
-    edge_ref, query_own, query_to_one, query_to_two, query_to_three, main_ref, far_ref,
-    key_all, value_all, query_all, grad_all, key_grad, value_grad, query_out,
+    edge_ref, *refs,
 ):
+    earlier, refs = refs[: len(refs) - 13], refs[len(refs) - 13 :]
+    outs, main_ref, far_ref = refs[:GROUP], refs[GROUP], refs[GROUP + 1]
+    key_all, value_all, query_all, grad_all, key_grad, value_grad, query_out = refs[GROUP + 2 :]
     rows, width = queries.shape[0], edge_ref.shape[2]
     edge = (GROUP - 1) * rows
     span = STEPS * rows
@@ -238,16 +245,18 @@
             value_grad[window, lanes] += lax.dot_general(
                 prob_half, grad, (((0,), (0,)), ((), ())), preferred_element_type=jnp.float32
             )
-    for away, block in enumerate((query_own, query_to_one, query_to_two, query_to_three)):
+    for away, block in enumerate(outs):
         index = lax.rem(place + away, GROUP)
-        block[...] = query_out[pl.ds(pl.multiple_of(index * rows, rows), rows), :]
+        if earlier:
+            block[0] = earlier[away][0]
+        block[1 if earlier else 0] = query_out[pl.ds(pl.multiple_of(index * rows, rows), rows), :]
     far_ref[0] = (key_grad[:edge, :] * scale).astype(jnp.bfloat16)
     far_ref[1] = value_grad[:edge, :].astype(jnp.bfloat16)
     main_ref[0] = (key_grad[edge:, :] * scale).astype(jnp.bfloat16)
     main_ref[1] = value_grad[edge:, :].astype(jnp.bfloat16)
 
 
-def attend(texts, marks, arrays, key_blocks, query_blocks, edge, chunk, total_rows):
+def attend(texts, marks, arrays, key_blocks, query_blocks, edge, chunk, total_rows, earlier=()):
     _, rows, width = key_blocks[0].shape
     heads = width // HEAD
     keys = (2 * GROUP - 1) * rows
@@ -255,11 +264,11 @@
     return pl.pallas_call(
         functools.partial(attend_kernel, chunk, total_rows),
         out_shape=(
-            *[jax.ShapeDtypeStruct((rows, width), jnp.bfloat16)] * GROUP,
+            *[jax.ShapeDtypeStruct((2 if earlier else 1, rows, width), jnp.bfloat16)] * GROUP,
             jax.ShapeDtypeStruct((2, GROUP * rows, width), jnp.bfloat16),
             jax.ShapeDtypeStruct((2, (GROUP - 1) * rows, width), jnp.bfloat16),
         ),
-        in_specs=[VMEM] * (len(texts) + 14),
+        in_specs=[VMEM] * (len(texts) + 14 + len(earlier)),
         out_specs=(VMEM,) * (GROUP + 2),
         scratch_shapes=[
             pltpu.VMEM((keys, width), jnp.bfloat16),
@@ -275,54 +284,42 @@
             flops=4500000000, bytes_accessed=0, transcendentals=0
         ),
         name="attend",
-    )(*texts, *marks, *arrays, *key_blocks, *query_blocks, edge)
+    )(*texts, *marks, *arrays, *key_blocks, *query_blocks, edge, *earlier)
 
 
 def settle_kernel(main_ref, far_ref, *refs):
-    extra = refs[: len(refs) // GROUP * GROUP - GROUP]
     outs = refs[len(refs) - GROUP :]
     rows = outs[0].shape[1]
-    first_kind = 1 if extra else 0
     place = lax.rem(lax.axis_index("ctx"), GROUP)
     for away, block in enumerate(outs):
         index = lax.rem(place + away, GROUP)
         start = pl.multiple_of(index * rows, rows)
-        if extra:
-            block[0] = extra[away][...]
 
         @pl.when(index == 0)
         def first():
-            block[first_kind:] = main_ref[:, :rows, :]
+            block[...] = main_ref[:, :rows, :]
 
         @pl.when(index > 0)
         def later():
             behind = pl.multiple_of(start - rows, rows)
-            block[first_kind:] = (
+            block[...] = (
                 main_ref[:, pl.ds(start, rows), :].astype(jnp.float32)
                 + far_ref[:, pl.ds(behind, rows), :].astype(jnp.float32)
             ).astype(jnp.bfloat16)
 
 
-def settle(main, far, extra=(), after=()):
+def settle(main, far, after, cost):
     _, total, width = main.shape
     rows = total // GROUP
-    count = 2 + (1 if extra else 0)
-
-    def kernel(main_ref, far_ref, *refs):
-        refs = list(refs)
-        settle_kernel(main_ref, far_ref, *refs[: len(extra)], *refs[-GROUP:])
-
     return pl.pallas_call(
-        kernel,
-        out_shape=(jax.ShapeDtypeStruct((count, rows, width), jnp.bfloat16),) * GROUP,
-        in_specs=[VMEM, VMEM] + [VMEM] * len(extra) + [ANY] * len(after),
+        settle_kernel,
+        out_shape=(jax.ShapeDtypeStruct((2, rows, width), jnp.bfloat16),) * GROUP,
+        in_specs=[VMEM, VMEM] + [ANY] * len(after),
         out_specs=(VMEM,) * GROUP,
         compiler_params=SMALL,
-        cost_estimate=pl.CostEstimate(
-            flops=SETTLE_COST if extra else 0, bytes_accessed=main.size * 8, transcendentals=0
-        ),
+        cost_estimate=pl.CostEstimate(flops=cost, bytes_accessed=main.size * 8, transcendentals=0),
         name="settle",
-    )(main, far, *extra, *after)
+    )(main, far, *after)
 
 
 def place_copies(moves, sems):
@@ -337,15 +334,15 @@
 
 
 def early_kernel(*refs):
-    queries, mixed = refs[:GROUP], refs[GROUP : 2 * GROUP]
+    queries, pairs = refs[:GROUP], refs[GROUP : 2 * GROUP]
     query_ref, key_ref, value_ref, sems = refs[2 * GROUP :]
     moves = []
     for away in range(GROUP):
         moves += [
-            (queries[away], query_ref, 0, away),
-            (mixed[away].at[0], query_ref, 1, away),
-            (mixed[away].at[1], key_ref, 0, away),
-            (mixed[away].at[2], value_ref, 0, away),
+            (queries[away].at[0], query_ref, 0, away),
+            (queries[away].at[1], query_ref, 1, away),
+            (pairs[away].at[0], key_ref, 0, away),
+            (pairs[away].at[1], value_ref, 0, away),
         ]
     place_copies(moves, sems)
 
@@ -363,7 +360,7 @@
 
 
 def gathered(queries, mixed, pairs):
-    rows, width = queries[0].shape
+    _, rows, width = queries[0].shape
     out = jax.ShapeDtypeStruct((rows, width * CHUNKS * GROUP), jnp.bfloat16)
     grad_queries, grad_keys, grad_values = pl.pallas_call(
         early_kernel,
@@ -440,19 +437,19 @@
     edges = [next_row(edge, 1) for edge in edges]
     arrays = (query_rows, key_rows, value_rows, grad_rows)
     halves = []
+    query_grads = ()
     for chunk in range(CHUNKS):
         *query_grads, main, far = attend(
-            texts, marks, arrays,
-            key_blocks[chunk], query_blocks[chunk], edges[chunk], chunk, total_rows,
+            texts, marks, arrays, key_blocks[chunk], query_blocks[chunk], edges[chunk], chunk,
+            total_rows, query_grads,
         )
-        halves.append((query_grads, main, next_row(far, -1)))
-    (first_queries, main, far), (second_queries, last_main, last_far) = halves
-    queries = [first_queries[0]] + swapped(first_queries[1:])
-    mixed = settle(main, far, extra=second_queries, after=queries[1:])
-    pairs = settle(last_main, last_far)
-    mixed = [mixed[0]] + swapped(mixed[1:])
-    pairs = [pairs[0]] + swapped(pairs[1:])
-    grad_queries, grad_keys, grad_values = gathered(queries, mixed, pairs)
+        halves.append((main, next_row(far, -1)))
+    queries = [query_grads[0]] + swapped(query_grads[1:])
+    first_pairs = settle(*halves[0], queries[1:], SETTLE_COST)
+    last_pairs = settle(*halves[1], first_pairs[:1], 0)
+    first_pairs = [first_pairs[0]] + swapped(first_pairs[1:])
+    last_pairs = [last_pairs[0]] + swapped(last_pairs[1:])
+    grad_queries, grad_keys, grad_values = gathered(queries, first_pairs, last_pairs)
     return grad_queries[None], grad_keys[None], grad_values[None]
 
 

time: 89.4 us -> 92.4 us (1.034)
  Pallas kernels: 18.7 us -> 23 us
  starting transfers between devices: 48.9 us -> 46.6 us
  other arithmetic: 0.22 us -> 2.1 us
  waiting for transfers between devices: 20.4 us -> 19.4 us
    ppermute x4, waiting for transfers between devices: 8.6 us -> 0.01 us  [next_row(): return lax.ppermute(value, 'ctx', pairs)]
    ppermute x21, waiting for transfers between devices: 10.5 us -> 17.4 us  [swap(): return lax.ppermute(value, 'ctx', pairs)]
    pallas_call x2, Pallas kernels: 12.6 us -> 14.8 us  [attend(): pl.pallas_call(functools.partial(attend_kernel, chunk, total_rows), out_s...]
    pallas_call x2, Pallas kernels: 0.11 us -> 2.09 us  [make_edge(): pl.pallas_call(functools.partial(edge_kernel, chunk), out_shape=jax.Shape...]
    ppermute x4, starting transfers between devices: 13.7 us -> 12.4 us  [next_row(): return lax.ppermute(value, 'ctx', pairs)]
    another operation x1, other arithmetic: 0.21 us -> 1.36 us
  transfers between devices with their start and end apart: 28 -> 28, of which waited for: 9 -> 11; matrix products, arithmetic and copies ran while one was open for 0% -> 2% of each run, Pallas kernels for 17% -> 22%
where the time goes in v2:
time: 92.4 us; the launch traced here: 92.2 us
  starting transfers between devices  46.6 us (50%)
  Pallas kernels  23 us (25%)
  waiting for transfers between devices  19.4 us (21%)
  other arithmetic  2.1 us (2%)
  between operations  0.99 us (1%)
    ppermute x21, starting transfers between devices, swap(): return lax.ppermute(value, 'ctx', pairs)  32.3 us
    ppermute x21, waiting for transfers between devices, swap(): return lax.ppermute(value, 'ctx', pairs)  17.4 us
    pallas_call x2, Pallas kernels, attend(): pl.pallas_call(functools.partial(attend_kernel, chunk, total_rows), out_s...  14.8 us
    ppermute x4, starting transfers between devices, next_row(): return lax.ppermute(value, 'ctx', pairs)  12.4 us
    pallas_call x1, Pallas kernels, first_pack(): pl.pallas_call(first_pack_kernel, out_shape=(message,) * (GROUP - 1) + (j...  2.15 us
    pallas_call x2, Pallas kernels, make_edge(): pl.pallas_call(functools.partial(edge_kernel, chunk), out_shape=jax.Shape...  2.09 us
    ppermute x3, waiting for transfers between devices, shards(): lax.ppermute(text, 'dp', [(source, (source + away) % samples) for source...  2.05 us
    ppermute x3, starting transfers between devices, shards(): lax.ppermute(text, 'dp', [(source, (source + away) % samples) for source...  1.92 us
  transfers between devices with their start and end apart: 28, of which 11 were waited for; matrix products, arithmetic and copies ran while one was open for 2% of the time, Pallas kernels for 22%

profile of v2, /device:TPU:0, one launch (start us, length us, event | category | flops | bytes accessed | tf_op | source)
XLA Modules:
  0.0 92.2 jit_solution(16726409628511812563)
XLA Ops:
  0.7 2.1 %first_pack.1 = (bf16[2,192,256]{2,1,0:T(8,128)(2,1)}, bf16[2,192,256]{2,1,0:T(8,128)(2,1)}, bf16[2,192,256]{2,1,0:T(8,128)(2,1)}, f32[1,32]{1,0:T(1,128)}) custom-call(bf16[192,2048]{1,0:T(8,128)(2,1)} %bitcast.7, bf16[192,2048]{1,0:T(8,128)(2,1)} %bitcast.13, s32[1,32]{1,0:T(1,128)} %lengths.1, s32[1,32]{1,0:T(1,128)} %flags.1), custom_call_target="tpu_custom_call" | custom-call | bytes 1179648 | tf_op jit(solution)/shard_map/first_pack/pallas_call | solution.py:75
  2.8 1.7 %collective-permute-start.3 = (bf16[2,192,256]{2,1,0:T(8,128)(2,1)}, bf16[2,192,256]{2,1,0:T(8,128)(2,1)S(1)}, u32[]{:S(2)}, u32[]{:S(2)}) collective-permute-start(bf16[2,192,256]{2,1,0:T(8,128)(2,1)} %get-tuple-element.45), channel_id=1, source_target_pairs={{0,1},{1,2},{2,3},{3,0},{4,5},{5,6},{6,7},{7,4},{8,9},{9,10},{10,1... | collective-permute-start | bytes 589832 | tf_op jit(solution)/shard_map/ppermute | solution.py:400
  4.5 2.9 %collective-permute-start.4 = (bf16[2,192,256]{2,1,0:T(8,128)(2,1)}, bf16[2,192,256]{2,1,0:T(8,128)(2,1)S(1)}, u32[]{:S(2)}, u32[]{:S(2)}) collective-permute-start(bf16[2,192,256]{2,1,0:T(8,128)(2,1)} %get-tuple-element.46), channel_id=1, source_target_pairs={{0,2},{1,3},{2,0},{3,1},{4,6},{5,7},{6,4},{7,5},{8,10},{9,11},{10,... | collective-permute-start | bytes 589832 | tf_op jit(solution)/shard_map/ppermute | solution.py:400
  7.4 1.3 %collective-permute-start.5 = (bf16[2,192,256]{2,1,0:T(8,128)(2,1)}, bf16[2,192,256]{2,1,0:T(8,128)(2,1)S(1)}, u32[]{:S(2)}, u32[]{:S(2)}) collective-permute-start(bf16[2,192,256]{2,1,0:T(8,128)(2,1)} %get-tuple-element.47), channel_id=1, source_target_pairs={{0,3},{1,0},{2,1},{3,2},{4,7},{5,4},{6,5},{7,6},{8,11},{9,8},{10,9... | collective-permute-start | bytes 589832 | tf_op jit(solution)/shard_map/ppermute | solution.py:400
  8.9 1.4 %collective-permute-start.1 = (f32[1,32]{1,0:T(1,128)S(1)}, f32[1,32]{1,0:T(1,128)S(1)}, u32[]{:S(2)}, u32[]{:S(2)}) collective-permute-start(f32[1,32]{1,0:T(1,128)S(1)} %copy-done.6), channel_id=1, source_target_pairs={{0,64},{32,96},{64,0},{96,32},{1,65},{33,97},{65,1},{97,33},{2,66}... | collective-permute-start | bytes 392 | tf_op jit(solution)/shard_map/ppermute | solution.py:413
  10.3 0.9 pack.3
  12.9 1.3 %collective-permute-done.refs_0_.text_two = f32[1,32]{1,0:T(1,128)S(1)} collective-permute-done((f32[1,32]{1,0:T(1,128)S(1)}, f32[1,32]{1,0:T(1,128)S(1)}, u32[]{:S(2)}, u32[]{:S(2)}) %collective-permute-start) | collective-permute-done | bytes 160 | tf_op jit(solution)/shard_map/ppermute | solution.py:413
  14.2 1.6 %collective-permute-start.8 = (bf16[2,192,256]{2,1,0:T(8,128)(2,1)}, bf16[2,192,256]{2,1,0:T(8,128)(2,1)}, u32[]{:S(2)}, u32[]{:S(2)}) collective-permute-start(bf16[2,192,256]{2,1,0:T(8,128)(2,1)} %get-tuple-element.55), channel_id=1, source_target_pairs={{0,3},{1,0},{2,1},{3,2},{4,7},{5,4},{6,5},{7,6},{8,11},{9,8},{10,9... | collective-permute-start | bytes 589832 | tf_op jit(solution)/shard_map/ppermute | solution.py:400
  18.0 3.1 %collective-permute-start.16 = (bf16[2,576,256]{2,1,0:T(8,128)(2,1)}, bf16[2,576,256]{2,1,0:T(8,128)(2,1)}, u32[]{:S(2)}, u32[]{:S(2)}) collective-permute-start(bf16[2,576,256]{2,1,0:T(8,128)(2,1)} %edge.2.after), channel_id=1, source_target_pairs={{0,4},{1,5},{2,6},{3,7},{4,8},{5,9},{6,10},{7,11},{8,12},{9,13},{1... | collective-permute-start | bytes 1769480 | tf_op jit(solution)/shard_map/ppermute | solution.py:404
  21.2 1.4 %reduce-window_clone.1 = s32[1,32]{1,0:T(1,128)} reduce-window(s32[1,32]{1,0:T(1,128)} %lengths.1, s32[]{:T(128)} %constant.4.clone.1), window={size=1x32 pad=0_0x31_0}, to_apply=%region_0.0 | reduce-window | flops 992 | bytes 260 | tf_op jit(solution)/shard_map/reduce-window.clone
  23.4 4.2 %collective-permute-start.13 = (bf16[2,192,256]{2,1,0:T(8,128)(2,1)S(1)}, bf16[2,192,256]{2,1,0:T(8,128)(2,1)S(1)}, u32[]{:S(2)}, u32[]{:S(2)}) collective-permute-start(bf16[2,192,256]{2,1,0:T(8,128)(2,1)S(1)} %get-tuple-element.49.after), channel_id=1, source_target_pairs={{0,1},{1,2},{2,3},{3,0},{4,5},{5,6},{6,7},{7,4},{8,9},{9,10},{10,1... | collective-permute-start | bytes 589832 | tf_op jit(solution)/shard_map/ppermute | solution.py:400
  28.1 2.3 %collective-permute-start.14 = (bf16[2,192,256]{2,1,0:T(8,128)(2,1)S(1)}, bf16[2,192,256]{2,1,0:T(8,128)(2,1)S(1)}, u32[]{:S(2)}, u32[]{:S(2)}) collective-permute-start(bf16[2,192,256]{2,1,0:T(8,128)(2,1)S(1)} %get-tuple-element.58), channel_id=1, source_target_pairs={{0,2},{1,3},{2,0},{3,1},{4,6},{5,7},{6,4},{7,5},{8,10},{9,11},{10,... | collective-permute-start | bytes 589832 | tf_op jit(solution)/shard_map/ppermute | solution.py:400
  30.9 1.2 %edge.3 = bf16[2,576,256]{2,1,0:T(8,128)(2,1)S(1)} custom-call(bf16[192,2048]{1,0:T(8,128)(2,1)S(1)} %bitcast.10, bf16[192,2048]{1,0:T(8,128)(2,1)S(1)} %bitcast.16, bf16[2,192,256]{2,1,0:T(8,128)(2,1)} %collective-permute-done.6.one.key_one, bf16[2,192,256]{2,1,0:T(8,128)(2,1)} %collective-permute-done.7.two.key_two, ...), custom_call_target="tpu_custom_call" | custom-call | flops 3000000000 | tf_op jit(solution)/shard_map/edge/pallas_call | solution.py:112
  32.1 1.9 %collective-permute-start.12 = (bf16[2,576,256]{2,1,0:T(8,128)(2,1)S(1)}, bf16[2,576,256]{2,1,0:T(8,128)(2,1)S(1)}, u32[]{:S(2)}, u32[]{:S(2)}) collective-permute-start(bf16[2,576,256]{2,1,0:T(8,128)(2,1)S(1)} %edge.3), channel_id=1, source_target_pairs={{0,4},{1,5},{2,6},{3,7},{4,8},{5,9},{6,10},{7,11},{8,12},{9,13},{1... | collective-permute-start | bytes 1769480 | tf_op jit(solution)/shard_map/ppermute | solution.py:404
  34.0 2.8 %collective-permute-done.14.query_two = bf16[2,192,256]{2,1,0:T(8,128)(2,1)S(1)} collective-permute-done((bf16[2,192,256]{2,1,0:T(8,128)(2,1)S(1)}, bf16[2,192,256]{2,1,0:T(8,128)(2,1)S(1)}, u32[]{:S(2)}, u32[]{:S(2)}) %collective-permute-start.14) | collective-permute-done | bytes 196640 | tf_op jit(solution)/shard_map/ppermute | solution.py:400
  36.8 1.9 %collective-permute-start.10 = (bf16[2,192,256]{2,1,0:T(8,128)(2,1)S(1)}, bf16[2,192,256]{2,1,0:T(8,128)(2,1)S(1)}, u32[]{:S(2)}, u32[]{:S(2)}) collective-permute-start(bf16[2,192,256]{2,1,0:T(8,128)(2,1)S(1)} %get-tuple-element.56), channel_id=1, source_target_pairs={{0,2},{1,3},{2,0},{3,1},{4,6},{5,7},{6,4},{7,5},{8,10},{9,11},{10,... | collective-permute-start | bytes 589832 | tf_op jit(solution)/shard_map/ppermute | solution.py:400
  38.7 2.6 %collective-permute-start.11 = (bf16[2,192,256]{2,1,0:T(8,128)(2,1)S(1)}, bf16[2,192,256]{2,1,0:T(8,128)(2,1)S(1)}, u32[]{:S(2)}, u32[]{:S(2)}) collective-permute-start(bf16[2,192,256]{2,1,0:T(8,128)(2,1)S(1)} %get-tuple-element.57), channel_id=1, source_target_pairs={{0,3},{1,0},{2,1},{3,2},{4,7},{5,4},{6,5},{7,6},{8,11},{9,8},{10,9... | collective-permute-start | bytes 589832 | tf_op jit(solution)/shard_map/ppermute | solution.py:400
  41.3 7.4 %attend.2 = (bf16[1,192,256]{2,1,0:T(8,128)(2,1)S(1)}, bf16[1,192,256]{2,1,0:T(8,128)(2,1)S(1)}, bf16[1,192,256]{2,1,0:T(8,128)(2,1)S(1)}, bf16[1,192,256]{2,1,0...) custom-call(f32[1,32]{1,0:T(1,128)S(1)} %copy-done.6, ...), custom_call_target="tpu_custom_call" | custom-call | flops 4499999744 | tf_op jit(solution)/shard_map/attend/pallas_call | solution.py:264
  48.7 3.5 %collective-permute-start.20 = (bf16[2,576,256]{2,1,0:T(8,128)(2,1)S(1)}, bf16[2,576,256]{2,1,0:T(8,128)(2,1)S(1)}, u32[]{:S(2)}, u32[]{:S(2)}) collective-permute-start(bf16[2,576,256]{2,1,0:T(8,128)(2,1)S(1)} %get-tuple-element.69), channel_id=1, source_target_pairs={{0,28},{1,29},{2,30},{3,31},{4,0},{5,1},{6,2},{7,3},{8,4},{9,5},{1... | collective-permute-start | bytes 1769480 | tf_op jit(solution)/shard_map/ppermute | solution.py:404
  52.2 7.5 %attend.3 = (bf16[2,192,256]{2,1,0:T(8,128)(2,1)S(1)}, bf16[2,192,256]{2,1,0:T(8,128)(2,1)S(1)}, bf16[2,192,256]{2,1,0:T(8,128)(2,1)S(1)}, bf16[2,192,256]{2,1,0...) custom-call(f32[1,32]{1,0:T(1,128)S(1)} %copy-done.6, ...), custom_call_target="tpu_custom_call" | custom-call | flops 4499999744 | tf_op jit(solution)/shard_map/attend/pallas_call | solution.py:264
  59.6 3.9 %collective-permute-start.24 = (bf16[2,576,256]{2,1,0:T(8,128)(2,1)S(1)}, bf16[2,576,256]{2,1,0:T(8,128)(2,1)S(1)}, u32[]{:S(2)}, u32[]{:S(2)}) collective-permute-start(bf16[2,576,256]{2,1,0:T(8,128)(2,1)S(1)} %get-tuple-element.76), channel_id=1, source_target_pairs={{0,28},{1,29},{2,30},{3,31},{4,0},{5,1},{6,2},{7,3},{8,4},{9,5},{1... | collective-permute-start | bytes 1769480 | tf_op jit(solution)/shard_map/ppermute | solution.py:404
  63.5 4.9 %collective-permute-start.18 = (bf16[2,192,256]{2,1,0:T(8,128)(2,1)S(1)}, bf16[2,192,256]{2,1,0:T(8,128)(2,1)S(1)}, u32[]{:S(2)}, u32[]{:S(2)}) collective-permute-start(bf16[2,192,256]{2,1,0:T(8,128)(2,1)S(1)} %get-tuple-element.66), channel_id=1, source_target_pairs={{0,2},{1,3},{2,0},{3,1},{4,6},{5,7},{6,4},{7,5},{8,10},{9,11},{10,... | collective-permute-start | bytes 589832 | tf_op jit(solution)/shard_map/ppermute | solution.py:400
  68.5 2.2 %collective-permute-done.17.refs_0_.refs_1_ = bf16[2,192,256]{2,1,0:T(8,128)(2,1)S(1)} collective-permute-done((bf16[2,192,256]{2,1,0:T(8,128)(2,1)S(1)}, bf16[2,192,256]{2,1,0:T(8,128)(2,1)S(1)}, u32[]{:S(2)}, u32[]{:S(2)}) %collective-permute-start.17) | collective-permute-done | bytes 196640 | tf_op jit(solution)/shard_map/ppermute | solution.py:400
  70.7 4.6 %collective-permute-done.18.refs_1_.refs_2_ = bf16[2,192,256]{2,1,0:T(8,128)(2,1)S(1)} collective-permute-done((bf16[2,192,256]{2,1,0:T(8,128)(2,1)S(1)}, bf16[2,192,256]{2,1,0:T(8,128)(2,1)S(1)}, u32[]{:S(2)}, u32[]{:S(2)}) %collective-permute-start.18) | collective-permute-done | bytes 196640 | tf_op jit(solution)/shard_map/ppermute | solution.py:400
  75.6 2.6 %collective-permute-start.22 = (bf16[2,192,256]{2,1,0:T(8,128)(2,1)S(1)}, bf16[2,192,256]{2,1,0:T(8,128)(2,1)S(1)}, u32[]{:S(2)}, u32[]{:S(2)}) collective-permute-start(bf16[2,192,256]{2,1,0:T(8,128)(2,1)S(1)} %get-tuple-element.72), channel_id=1, source_target_pairs={{0,2},{1,3},{2,0},{3,1},{4,6},{5,7},{6,4},{7,5},{8,10},{9,11},{10,... | collective-permute-start | bytes 589832 | tf_op jit(solution)/shard_map/ppermute | solution.py:400
  78.3 2.5 %collective-permute-start.23 = (bf16[2,192,256]{2,1,0:T(8,128)(2,1)S(1)}, bf16[2,192,256]{2,1,0:T(8,128)(2,1)S(1)}, u32[]{:S(2)}, u32[]{:S(2)}) collective-permute-start(bf16[2,192,256]{2,1,0:T(8,128)(2,1)S(1)} %get-tuple-element.73), channel_id=1, source_target_pairs={{0,3},{1,0},{2,1},{3,2},{4,7},{5,4},{6,5},{7,6},{8,11},{9,8},{10,9... | collective-permute-start | bytes 589832 | tf_op jit(solution)/shard_map/ppermute | solution.py:400
  81.0 1.4 %collective-permute-start.26 = (bf16[2,192,256]{2,1,0:T(8,128)(2,1)S(1)}, bf16[2,192,256]{2,1,0:T(8,128)(2,1)S(1)}, u32[]{:S(2)}, u32[]{:S(2)}) collective-permute-start(bf16[2,192,256]{2,1,0:T(8,128)(2,1)S(1)} %get-tuple-element.79), channel_id=1, source_target_pairs={{0,2},{1,3},{2,0},{3,1},{4,6},{5,7},{6,4},{7,5},{8,10},{9,11},{10,... | collective-permute-start | bytes 589832 | tf_op jit(solution)/shard_map/ppermute | solution.py:400
  82.5 1.6 %collective-permute-done.21.refs_5_ = bf16[2,192,256]{2,1,0:T(8,128)(2,1)S(1)} collective-permute-done((bf16[2,192,256]{2,1,0:T(8,128)(2,1)S(1)}, bf16[2,192,256]{2,1,0:T(8,128)(2,1)S(1)}, u32[]{:S(2)}, u32[]{:S(2)}) %collective-permute-start.21) | collective-permute-done | bytes 196640 | tf_op jit(solution)/shard_map/ppermute | solution.py:400
  84.7 2.3 %collective-permute-done.22.refs_6_ = bf16[2,192,256]{2,1,0:T(8,128)(2,1)S(1)} collective-permute-done((bf16[2,192,256]{2,1,0:T(8,128)(2,1)S(1)}, bf16[2,192,256]{2,1,0:T(8,128)(2,1)S(1)}, u32[]{:S(2)}, u32[]{:S(2)}) %collective-permute-start.22) | collective-permute-done | bytes 196640 | tf_op jit(solution)/shard_map/ppermute | solution.py:400
  87.0 1.3 %early.1 = (bf16[192,2048]{1,0:T(8,128)(2,1)}, bf16[192,2048]{1,0:T(8,128)(2,1)}, bf16[192,2048]{1,0:T(8,128)(2,1)}) custom-call(bf16[2,192,256]{2,1,0:T(8,128)(2,1)S(1)} %get-tuple-element.64.refs_0_, bf16[2,192,256]{2,1,0:T(8,128)(2,1)S(1)} %collective-permute-done.17.refs_0_.refs_1_, bf16[2,192,256]{2,1,0:T(8,128)(2,1)S(1)} %collective-permute-done.18.refs_1_.refs_2_, ...), custom_call_target="tpu_custom_call" | custom-call | bytes 2359296 | tf_op jit(solution)/shard_map/early/pallas_call | solution.py:365
  89.0 2.1 %collective-permute-done.26.refs_2_ = bf16[2,192,256]{2,1,0:T(8,128)(2,1)S(1)} collective-permute-done((bf16[2,192,256]{2,1,0:T(8,128)(2,1)S(1)}, bf16[2,192,256]{2,1,0:T(8,128)(2,1)S(1)}, u32[]{:S(2)}, u32[]{:S(2)}) %collective-permute-start.26) | collective-permute-done | bytes 196640 | tf_op jit(solution)/shard_map/ppermute | solution.py:400
  91.1 0.9 %late.1 = (bf16[192,2048]{1,0:T(8,128)(2,1)}, bf16[192,2048]{1,0:T(8,128)(2,1)}) custom-call(bf16[2,192,256]{2,1,0:T(8,128)(2,1)S(1)} %get-tuple-element.77.refs_0_, bf16[2,192,256]{2,1,0:T(8,128)(2,1)S(1)} %collective-permute-done.25.refs_1_, ...), custom_call_target="tpu_custom_call", output_to_operand_aliasing={{0}: (4, {}), {1}: (5, {})} | custom-call | bytes 2359296 | tf_op jit(solution)/shard_map/late/pallas_call | solution.py:375
  (59 shorter events, 7.7 us)
Async XLA Ops:
  0.6 9.7 %copy-start = (bf16[1,192,2048]{2,1,0:T(8,128)(2,1)S(1)}, bf16[1,192,2048]{2,1,0:T(8,128)(2,1)}, u32[]{:S(2)}) copy-start(bf16[1,192,2048]{2,1,0:T(8,128)(2,1)} %param.7) | copy-start | bytes 2359300
  0.6 9.6 %copy-start.1 = (bf16[1,192,2048]{2,1,0:T(8,128)(2,1)S(1)}, bf16[1,192,2048]{2,1,0:T(8,128)(2,1)}, u32[]{:S(2)}) copy-start(bf16[1,192,2048]{2,1,0:T(8,128)(2,1)} %param.8) | copy-start | bytes 2359300
  2.8 13.0 %collective-permute-start.3 = (bf16[2,192,256]{2,1,0:T(8,128)(2,1)}, bf16[2,192,256]{2,1,0:T(8,128)(2,1)S(1)}, u32[]{:S(2)}, u32[]{:S(2)}) collective-permute-start(bf16[2,192,256]{2,1,0:T(8,128)(2,1)} %get-tuple-element.45), channel_id=1, source_target_pairs={{0,1},{1,2},{2,3},{3,0},{4,5},{5,6},{6,7},{7,4},{8,9},{9,10},{10,1... | collective-permute-start | bytes 589832 | tf_op jit(solution)/shard_map/ppermute | solution.py:400
  4.5 12.1 %collective-permute-start.4 = (bf16[2,192,256]{2,1,0:T(8,128)(2,1)}, bf16[2,192,256]{2,1,0:T(8,128)(2,1)S(1)}, u32[]{:S(2)}, u32[]{:S(2)}) collective-permute-start(bf16[2,192,256]{2,1,0:T(8,128)(2,1)} %get-tuple-element.46), channel_id=1, source_target_pairs={{0,2},{1,3},{2,0},{3,1},{4,6},{5,7},{6,4},{7,5},{8,10},{9,11},{10,... | collective-permute-start | bytes 589832 | tf_op jit(solution)/shard_map/ppermute | solution.py:400
  7.4 9.7 %collective-permute-start.5 = (bf16[2,192,256]{2,1,0:T(8,128)(2,1)}, bf16[2,192,256]{2,1,0:T(8,128)(2,1)S(1)}, u32[]{:S(2)}, u32[]{:S(2)}) collective-permute-start(bf16[2,192,256]{2,1,0:T(8,128)(2,1)} %get-tuple-element.47), channel_id=1, source_target_pairs={{0,3},{1,0},{2,1},{3,2},{4,7},{5,4},{6,5},{7,6},{8,11},{9,8},{10,9... | collective-permute-start | bytes 589832 | tf_op jit(solution)/shard_map/ppermute | solution.py:400
  8.8 2.4 %collective-permute-start.2 = (f32[1,32]{1,0:T(1,128)S(1)}, f32[1,32]{1,0:T(1,128)S(1)}, u32[]{:S(2)}, u32[]{:S(2)}) collective-permute-start(f32[1,32]{1,0:T(1,128)S(1)} %copy-done.6), channel_id=1, source_target_pairs={{0,96},{32,0},{64,32},{96,64},{1,97},{33,1},{65,33},{97,65},{2,98}... | collective-permute-start | bytes 392 | tf_op jit(solution)/shard_map/ppermute | solution.py:413
  8.9 3.5 %collective-permute-start.1 = (f32[1,32]{1,0:T(1,128)S(1)}, f32[1,32]{1,0:T(1,128)S(1)}, u32[]{:S(2)}, u32[]{:S(2)}) collective-permute-start(f32[1,32]{1,0:T(1,128)S(1)} %copy-done.6), channel_id=1, source_target_pairs={{0,64},{32,96},{64,0},{96,32},{1,65},{33,97},{65,1},{97,33},{2,66}... | collective-permute-start | bytes 392 | tf_op jit(solution)/shard_map/ppermute | solution.py:413
  11.2 3.0 %collective-permute-start = (f32[1,32]{1,0:T(1,128)S(1)}, f32[1,32]{1,0:T(1,128)S(1)}, u32[]{:S(2)}, u32[]{:S(2)}) collective-permute-start(f32[1,32]{1,0:T(1,128)S(1)} %copy-done.6), channel_id=1, source_target_pairs={{0,32},{32,64},{64,96},{96,0},{1,33},{33,65},{65,97},{97,1},{2,34}... | collective-permute-start | bytes 392 | tf_op jit(solution)/shard_map/ppermute | solution.py:413
  12.4 15.6 %collective-permute-start.7 = (bf16[2,192,256]{2,1,0:T(8,128)(2,1)}, bf16[2,192,256]{2,1,0:T(8,128)(2,1)}, u32[]{:S(2)}, u32[]{:S(2)}) collective-permute-start(bf16[2,192,256]{2,1,0:T(8,128)(2,1)} %get-tuple-element.54), channel_id=1, source_target_pairs={{0,2},{1,3},{2,0},{3,1},{4,6},{5,7},{6,4},{7,5},{8,10},{9,11},{10,... | collective-permute-start | bytes 589832 | tf_op jit(solution)/shard_map/ppermute | solution.py:400
  14.2 16.2 %collective-permute-start.8 = (bf16[2,192,256]{2,1,0:T(8,128)(2,1)}, bf16[2,192,256]{2,1,0:T(8,128)(2,1)}, u32[]{:S(2)}, u32[]{:S(2)}) collective-permute-start(bf16[2,192,256]{2,1,0:T(8,128)(2,1)} %get-tuple-element.55), channel_id=1, source_target_pairs={{0,3},{1,0},{2,1},{3,2},{4,7},{5,4},{6,5},{7,6},{8,11},{9,8},{10,9... | collective-permute-start | bytes 589832 | tf_op jit(solution)/shard_map/ppermute | solution.py:400
  15.8 7.5 %copy-start.3 = (bf16[1,192,2048]{2,1,0:T(8,128)(2,1)S(1)}, bf16[1,192,2048]{2,1,0:T(8,128)(2,1)}, u32[]{:S(2)}) copy-start(bf16[1,192,2048]{2,1,0:T(8,128)(2,1)} %param.9) | copy-start | bytes 2359300
  15.8 15.1 %collective-permute-start.6 = (bf16[2,192,256]{2,1,0:T(8,128)(2,1)}, bf16[2,192,256]{2,1,0:T(8,128)(2,1)}, u32[]{:S(2)}, u32[]{:S(2)}) collective-permute-start(bf16[2,192,256]{2,1,0:T(8,128)(2,1)} %get-tuple-element.48.refs_3_), channel_id=1, source_target_pairs={{0,1},{1,2},{2,3},{3,0},{4,5},{5,6},{6,7},{7,4},{8,9},{9,10},{10,1... | collective-permute-start | bytes 589832 | tf_op jit(solution)/shard_map/ppermute | solution.py:400
  18.0 23.3 %collective-permute-start.16 = (bf16[2,576,256]{2,1,0:T(8,128)(2,1)}, bf16[2,576,256]{2,1,0:T(8,128)(2,1)}, u32[]{:S(2)}, u32[]{:S(2)}) collective-permute-start(bf16[2,576,256]{2,1,0:T(8,128)(2,1)} %edge.2.after), channel_id=1, source_target_pairs={{0,4},{1,5},{2,6},{3,7},{4,8},{5,9},{6,10},{7,11},{8,12},{9,13},{1... | collective-permute-start | bytes 1769480 | tf_op jit(solution)/shard_map/ppermute | solution.py:404
  23.4 15.3 %collective-permute-start.13 = (bf16[2,192,256]{2,1,0:T(8,128)(2,1)S(1)}, bf16[2,192,256]{2,1,0:T(8,128)(2,1)S(1)}, u32[]{:S(2)}, u32[]{:S(2)}) collective-permute-start(bf16[2,192,256]{2,1,0:T(8,128)(2,1)S(1)} %get-tuple-element.49.after), channel_id=1, source_target_pairs={{0,1},{1,2},{2,3},{3,0},{4,5},{5,6},{6,7},{7,4},{8,9},{9,10},{10,1... | collective-permute-start | bytes 589832 | tf_op jit(solution)/shard_map/ppermute | solution.py:400
  28.1 8.7 %collective-permute-start.14 = (bf16[2,192,256]{2,1,0:T(8,128)(2,1)S(1)}, bf16[2,192,256]{2,1,0:T(8,128)(2,1)S(1)}, u32[]{:S(2)}, u32[]{:S(2)}) collective-permute-start(bf16[2,192,256]{2,1,0:T(8,128)(2,1)S(1)} %get-tuple-element.58), channel_id=1, source_target_pairs={{0,2},{1,3},{2,0},{3,1},{4,6},{5,7},{6,4},{7,5},{8,10},{9,11},{10,... | collective-permute-start | bytes 589832 | tf_op jit(solution)/shard_map/ppermute | solution.py:400
  30.3 6.5 %collective-permute-start.15 = (bf16[2,192,256]{2,1,0:T(8,128)(2,1)S(1)}, bf16[2,192,256]{2,1,0:T(8,128)(2,1)S(1)}, u32[]{:S(2)}, u32[]{:S(2)}) collective-permute-start(bf16[2,192,256]{2,1,0:T(8,128)(2,1)S(1)} %get-tuple-element.59), channel_id=1, source_target_pairs={{0,3},{1,0},{2,1},{3,2},{4,7},{5,4},{6,5},{7,6},{8,11},{9,8},{10,9... | collective-permute-start | bytes 589832 | tf_op jit(solution)/shard_map/ppermute | solution.py:400
  30.9 10.5 %copy-start.5 = (bf16[2,192,256]{2,1,0:T(8,128)(2,1)S(1)}, bf16[2,192,256]{2,1,0:T(8,128)(2,1)}, u32[]{:S(2)}) copy-start(bf16[2,192,256]{2,1,0:T(8,128)(2,1)} %copy-done.4) | copy-start | bytes 589828
  32.1 20.1 %collective-permute-start.12 = (bf16[2,576,256]{2,1,0:T(8,128)(2,1)S(1)}, bf16[2,576,256]{2,1,0:T(8,128)(2,1)S(1)}, u32[]{:S(2)}, u32[]{:S(2)}) collective-permute-start(bf16[2,576,256]{2,1,0:T(8,128)(2,1)S(1)} %edge.3), channel_id=1, source_target_pairs={{0,4},{1,5},{2,6},{3,7},{4,8},{5,9},{6,10},{7,11},{8,12},{9,13},{1... | collective-permute-start | bytes 1769480 | tf_op jit(solution)/shard_map/ppermute | solution.py:404
  36.8 15.4 %collective-permute-start.9 = (bf16[2,192,256]{2,1,0:T(8,128)(2,1)S(1)}, bf16[2,192,256]{2,1,0:T(8,128)(2,1)S(1)}, u32[]{:S(2)}, u32[]{:S(2)}) collective-permute-start(bf16[2,192,256]{2,1,0:T(8,128)(2,1)S(1)} %get-tuple-element.50.after), channel_id=1, source_target_pairs={{0,1},{1,2},{2,3},{3,0},{4,5},{5,6},{6,7},{7,4},{8,9},{9,10},{10,1... | collective-permute-start | bytes 589832 | tf_op jit(solution)/shard_map/ppermute | solution.py:400
  36.8 15.4 %collective-permute-start.10 = (bf16[2,192,256]{2,1,0:T(8,128)(2,1)S(1)}, bf16[2,192,256]{2,1,0:T(8,128)(2,1)S(1)}, u32[]{:S(2)}, u32[]{:S(2)}) collective-permute-start(bf16[2,192,256]{2,1,0:T(8,128)(2,1)S(1)} %get-tuple-element.56), channel_id=1, source_target_pairs={{0,2},{1,3},{2,0},{3,1},{4,6},{5,7},{6,4},{7,5},{8,10},{9,11},{10,... | collective-permute-start | bytes 589832 | tf_op jit(solution)/shard_map/ppermute | solution.py:400
  38.7 13.5 %collective-permute-start.11 = (bf16[2,192,256]{2,1,0:T(8,128)(2,1)S(1)}, bf16[2,192,256]{2,1,0:T(8,128)(2,1)S(1)}, u32[]{:S(2)}, u32[]{:S(2)}) collective-permute-start(bf16[2,192,256]{2,1,0:T(8,128)(2,1)S(1)} %get-tuple-element.57), channel_id=1, source_target_pairs={{0,3},{1,0},{2,1},{3,2},{4,7},{5,4},{6,5},{7,6},{8,11},{9,8},{10,9... | collective-permute-start | bytes 589832 | tf_op jit(solution)/shard_map/ppermute | solution.py:400
  48.7 26.6 %collective-permute-start.20 = (bf16[2,576,256]{2,1,0:T(8,128)(2,1)S(1)}, bf16[2,576,256]{2,1,0:T(8,128)(2,1)S(1)}, u32[]{:S(2)}, u32[]{:S(2)}) collective-permute-start(bf16[2,576,256]{2,1,0:T(8,128)(2,1)S(1)} %get-tuple-element.69), channel_id=1, source_target_pairs={{0,28},{1,29},{2,30},{3,31},{4,0},{5,1},{6,2},{7,3},{8,4},{9,5},{1... | collective-permute-start | bytes 1769480 | tf_op jit(solution)/shard_map/ppermute | solution.py:404
  59.6 21.1 %collective-permute-start.24 = (bf16[2,576,256]{2,1,0:T(8,128)(2,1)S(1)}, bf16[2,576,256]{2,1,0:T(8,128)(2,1)S(1)}, u32[]{:S(2)}, u32[]{:S(2)}) collective-permute-start(bf16[2,576,256]{2,1,0:T(8,128)(2,1)S(1)} %get-tuple-element.76), channel_id=1, source_target_pairs={{0,28},{1,29},{2,30},{3,31},{4,0},{5,1},{6,2},{7,3},{8,4},{9,5},{1... | collective-permute-start | bytes 1769480 | tf_op jit(solution)/shard_map/ppermute | solution.py:404
  63.5 7.1 %collective-permute-start.17 = (bf16[2,192,256]{2,1,0:T(8,128)(2,1)S(1)}, bf16[2,192,256]{2,1,0:T(8,128)(2,1)S(1)}, u32[]{:S(2)}, u32[]{:S(2)}) collective-permute-start(bf16[2,192,256]{2,1,0:T(8,128)(2,1)S(1)} %get-tuple-element.65), channel_id=1, source_target_pairs={{0,1},{1,2},{2,3},{3,0},{4,5},{5,6},{6,7},{7,4},{8,9},{9,10},{10,1... | collective-permute-start | bytes 589832 | tf_op jit(solution)/shard_map/ppermute | solution.py:400
  63.5 11.8 %collective-permute-start.18 = (bf16[2,192,256]{2,1,0:T(8,128)(2,1)S(1)}, bf16[2,192,256]{2,1,0:T(8,128)(2,1)S(1)}, u32[]{:S(2)}, u32[]{:S(2)}) collective-permute-start(bf16[2,192,256]{2,1,0:T(8,128)(2,1)S(1)} %get-tuple-element.66), channel_id=1, source_target_pairs={{0,2},{1,3},{2,0},{3,1},{4,6},{5,7},{6,4},{7,5},{8,10},{9,11},{10,... | collective-permute-start | bytes 589832 | tf_op jit(solution)/shard_map/ppermute | solution.py:400
  68.5 6.9 %collective-permute-start.19 = (bf16[2,192,256]{2,1,0:T(8,128)(2,1)S(1)}, bf16[2,192,256]{2,1,0:T(8,128)(2,1)S(1)}, u32[]{:S(2)}, u32[]{:S(2)}) collective-permute-start(bf16[2,192,256]{2,1,0:T(8,128)(2,1)S(1)} %get-tuple-element.67), channel_id=1, source_target_pairs={{0,3},{1,0},{2,1},{3,2},{4,7},{5,4},{6,5},{7,6},{8,11},{9,8},{10,9... | collective-permute-start | bytes 589832 | tf_op jit(solution)/shard_map/ppermute | solution.py:400
  75.5 8.5 %collective-permute-start.21 = (bf16[2,192,256]{2,1,0:T(8,128)(2,1)S(1)}, bf16[2,192,256]{2,1,0:T(8,128)(2,1)S(1)}, u32[]{:S(2)}, u32[]{:S(2)}) collective-permute-start(bf16[2,192,256]{2,1,0:T(8,128)(2,1)S(1)} %get-tuple-element.71), channel_id=1, source_target_pairs={{0,1},{1,2},{2,3},{3,0},{4,5},{5,6},{6,7},{7,4},{8,9},{9,10},{10,1... | collective-permute-start | bytes 589832 | tf_op jit(solution)/shard_map/ppermute | solution.py:400
  75.6 11.4 %collective-permute-start.22 = (bf16[2,192,256]{2,1,0:T(8,128)(2,1)S(1)}, bf16[2,192,256]{2,1,0:T(8,128)(2,1)S(1)}, u32[]{:S(2)}, u32[]{:S(2)}) collective-permute-start(bf16[2,192,256]{2,1,0:T(8,128)(2,1)S(1)} %get-tuple-element.72), channel_id=1, source_target_pairs={{0,2},{1,3},{2,0},{3,1},{4,6},{5,7},{6,4},{7,5},{8,10},{9,11},{10,... | collective-permute-start | bytes 589832 | tf_op jit(solution)/shard_map/ppermute | solution.py:400
  78.3 8.7 %collective-permute-start.23 = (bf16[2,192,256]{2,1,0:T(8,128)(2,1)S(1)}, bf16[2,192,256]{2,1,0:T(8,128)(2,1)S(1)}, u32[]{:S(2)}, u32[]{:S(2)}) collective-permute-start(bf16[2,192,256]{2,1,0:T(8,128)(2,1)S(1)} %get-tuple-element.73), channel_id=1, source_target_pairs={{0,3},{1,0},{2,1},{3,2},{4,7},{5,4},{6,5},{7,6},{8,11},{9,8},{10,9... | collective-permute-start | bytes 589832 | tf_op jit(solution)/shard_map/ppermute | solution.py:400
  80.9 8.0 %collective-permute-start.25 = (bf16[2,192,256]{2,1,0:T(8,128)(2,1)S(1)}, bf16[2,192,256]{2,1,0:T(8,128)(2,1)S(1)}, u32[]{:S(2)}, u32[]{:S(2)}) collective-permute-start(bf16[2,192,256]{2,1,0:T(8,128)(2,1)S(1)} %get-tuple-element.78), channel_id=1, source_target_pairs={{0,1},{1,2},{2,3},{3,0},{4,5},{5,6},{6,7},{7,4},{8,9},{9,10},{10,1... | collective-permute-start | bytes 589832 | tf_op jit(solution)/shard_map/ppermute | solution.py:400
  81.0 10.0 %collective-permute-start.26 = (bf16[2,192,256]{2,1,0:T(8,128)(2,1)S(1)}, bf16[2,192,256]{2,1,0:T(8,128)(2,1)S(1)}, u32[]{:S(2)}, u32[]{:S(2)}) collective-permute-start(bf16[2,192,256]{2,1,0:T(8,128)(2,1)S(1)} %get-tuple-element.79), channel_id=1, source_target_pairs={{0,2},{1,3},{2,0},{3,1},{4,6},{5,7},{6,4},{7,5},{8,10},{9,11},{10,... | collective-permute-start | bytes 589832 | tf_op jit(solution)/shard_map/ppermute | solution.py:400
  84.1 7.0 %collective-permute-start.27 = (bf16[2,192,256]{2,1,0:T(8,128)(2,1)S(1)}, bf16[2,192,256]{2,1,0:T(8,128)(2,1)S(1)}, u32[]{:S(2)}, u32[]{:S(2)}) collective-permute-start(bf16[2,192,256]{2,1,0:T(8,128)(2,1)S(1)} %get-tuple-element.80), channel_id=1, source_target_pairs={{0,3},{1,0},{2,1},{3,2},{4,7},{5,4},{6,5},{7,6},{8,11},{9,8},{10,9... | collective-permute-start | bytes 589832 | tf_op jit(solution)/shard_map/ppermute | solution.py:400
  (5 other events, 11.2 us)

commit v3 on v2

--- a/solution.py
+++ b/solution.py
@@ -120,14 +120,31 @@
     )(first, second, *blocks, *afters)
 
 
-def sides_kernel(stretch_rows, cycle_size, bounds_ref, after, limit_ref, text_ref, key_ref):
+def sides_kernel(stretch_rows, cycle_size, lengths_ref, flags_ref, after, limit_ref, text_ref, key_ref):
     rows = 2 * stretch_rows
     device_here = lax.axis_index("ctx")
     start = device_here - lax.rem(device_here, GROUP)
-    first = bounds_ref[0:1, :]
-    ending = bounds_ref[1:2, :]
-    flag = bounds_ref[2:3, :].astype(jnp.float32)
-    last = ending.astype(jnp.float32)
+    segments = lengths_ref.shape[1]
+    square = (segments, segments)
+    diagonal = lax.broadcasted_iota(jnp.int32, square, 0) == lax.broadcasted_iota(
+        jnp.int32, square, 1
+    )
+
+    def upright(ref):
+        row = jnp.broadcast_to(ref[...].astype(jnp.float32), square)
+        return jnp.sum(jnp.where(diagonal, row, 0.0), axis=1, keepdims=True)
+
+    lengths, flags = upright(lengths_ref), upright(flags_ref)
+    source = lax.broadcasted_iota(jnp.int32, (segments, HEAD), 0)
+    target = lax.broadcasted_iota(jnp.int32, (segments, HEAD), 1)
+
+    def gathered_sum(mask, column):
+        return jnp.sum(jnp.where(mask, column, 0.0), axis=0, keepdims=True)
+
+    last = gathered_sum(source <= target, lengths)
+    first = gathered_sum(source < target, lengths).astype(jnp.int32)
+    flag = gathered_sum(source == target, flags)
+    ending = last.astype(jnp.int32)
     shape = (rows, HEAD)
     offset = lax.broadcasted_iota(jnp.int32, shape, 0)
     for block in range(GROUP):
@@ -156,7 +173,7 @@
         )
 
 
-def sides(bounds, after, stretch_rows, cycle_size):
+def sides(lengths, flags, after, stretch_rows, cycle_size):
     rows = 2 * stretch_rows
     return pl.pallas_call(
         functools.partial(sides_kernel, stretch_rows, cycle_size),
@@ -165,12 +182,12 @@
             jax.ShapeDtypeStruct((GROUP, rows, HEAD), jnp.float32),
             jax.ShapeDtypeStruct((GROUP, 8, STEPS * rows), jnp.int32),
         ),
-        in_specs=[VMEM, ANY],
+        in_specs=[VMEM, VMEM, ANY],
         out_specs=(VMEM,) * 3,
         compiler_params=SMALL,
         cost_estimate=pl.CostEstimate(flops=GROUP * rows * HEAD * 8, bytes_accessed=GROUP * rows * HEAD * 8, transcendentals=0),
         name="sides",
-    )(bounds, after)
+    )(lengths, flags, after)
 
 
 def attend_kernel(
@@ -415,9 +432,6 @@
     ]
     total_rows = float(row_count * cycle_size * samples)
 
-    ending = jnp.cumsum(lengths[0])
-    bounds = jnp.stack([ending - lengths[0], ending, image_flags[0]])
-    bounds = jnp.pad(bounds, ((0, 5), (0, HEAD - bounds.shape[1])))
     key_packs, query_packs, edges = [None] * CHUNKS, [None] * CHUNKS, [None] * CHUNKS
     key_packs[0] = first_messages
     key_packs[1] = pack(key_rows, value_rows, text, 1)
@@ -429,7 +443,7 @@
     for index in range(CHUNKS):
         query_packs[index] = pack(query_rows, grad_rows, after, index)
         after = query_packs[index][0]
-    marks = sides(bounds, after, row_count // 2, cycle_size)
+    marks = sides(lengths, image_flags, after, row_count // 2, cycle_size)
     edges[1] = make_edge(
         key_rows, value_rows, key_blocks[1], (marks[1],), 1, EDGE_COST[1]
     )

time: 92.4 us -> 92.4 us (level)
  Pallas kernels: 23 us -> 18.1 us
  waiting for transfers between devices: 19.4 us -> 23.8 us
  other arithmetic: 2.1 us -> 0 us
  starting transfers between devices: 46.6 us -> 48.6 us
    ppermute x21, waiting for transfers between devices: 17.4 us -> 22.5 us  [swap(): return lax.ppermute(value, 'ctx', pairs)]
    pallas_call x2, Pallas kernels: 14.8 us -> 12.7 us  [attend(): pl.pallas_call(functools.partial(attend_kernel, chunk, total_rows), out_s...]
    pallas_call x2, Pallas kernels: 2.09 us -> 0.11 us  [make_edge(): pl.pallas_call(functools.partial(edge_kernel, chunk), out_shape=jax.Shape...]
    ppermute x21, starting transfers between devices: 32.3 us -> 33.8 us  [swap(): return lax.ppermute(value, 'ctx', pairs)]
    another operation x2 -> x0, other arithmetic: 1.37 us -> none
  transfers between devices with their start and end apart: 28 -> 28, of which waited for: 11 -> 13; matrix products, arithmetic and copies ran while one was open for 2% -> 0% of each run, Pallas kernels for 22% -> 16%
where the time goes in v3:
time: 92.4 us; the launch traced here: 92.2 us
  starting transfers between devices  48.6 us (53%)
  waiting for transfers between devices  23.8 us (26%)
  Pallas kernels  18.1 us (20%)
  between operations  0.99 us (1%)
    ppermute x21, starting transfers between devices, swap(): return lax.ppermute(value, 'ctx', pairs)  33.8 us
    ppermute x21, waiting for transfers between devices, swap(): return lax.ppermute(value, 'ctx', pairs)  22.5 us
    pallas_call x2, Pallas kernels, attend(): pl.pallas_call(functools.partial(attend_kernel, chunk, total_rows), out_s...  12.7 us
    ppermute x4, starting transfers between devices, next_row(): return lax.ppermute(value, 'ctx', pairs)  12.1 us
    ppermute x3, starting transfers between devices, shards(): lax.ppermute(text, 'dp', [(source, (source + away) % samples) for source...  2.73 us
    pallas_call x1, Pallas kernels, first_pack(): pl.pallas_call(first_pack_kernel, out_shape=(message,) * (GROUP - 1) + (j...  2.15 us
  transfers between devices with their start and end apart: 28, of which 13 were waited for; matrix products, arithmetic and copies ran while one was open for 0% of the time, Pallas kernels for 16%

profile of v3, /device:TPU:0, one launch (start us, length us, event | category | flops | bytes accessed | tf_op | source)
XLA Modules:
  0.0 92.2 jit_solution(18035514881405360260)
XLA Ops:
  0.7 2.1 %first_pack.1 = (bf16[2,192,256]{2,1,0:T(8,128)(2,1)}, bf16[2,192,256]{2,1,0:T(8,128)(2,1)}, bf16[2,192,256]{2,1,0:T(8,128)(2,1)}, f32[1,32]{1,0:T(1,128)}) custom-call(bf16[192,2048]{1,0:T(8,128)(2,1)} %bitcast.7, bf16[192,2048]{1,0:T(8,128)(2,1)} %bitcast.13, s32[1,32]{1,0:T(1,128)} %lengths_ref.1, s32[1,32]{1,0:T(1,128)} %flags_ref.1), custom_call_target="tpu_custom_call" | custom-call | bytes 1179648 | tf_op jit(solution)/shard_map/first_pack/pallas_call | solution.py:75
  2.8 1.7 %collective-permute-start.3 = (bf16[2,192,256]{2,1,0:T(8,128)(2,1)}, bf16[2,192,256]{2,1,0:T(8,128)(2,1)S(1)}, u32[]{:S(2)}, u32[]{:S(2)}) collective-permute-start(bf16[2,192,256]{2,1,0:T(8,128)(2,1)} %get-tuple-element.45), channel_id=1, source_target_pairs={{0,1},{1,2},{2,3},{3,0},{4,5},{5,6},{6,7},{7,4},{8,9},{9,10},{10,1... | collective-permute-start | bytes 589832 | tf_op jit(solution)/shard_map/ppermute | solution.py:417
  4.5 2.9 %collective-permute-start.4 = (bf16[2,192,256]{2,1,0:T(8,128)(2,1)}, bf16[2,192,256]{2,1,0:T(8,128)(2,1)S(1)}, u32[]{:S(2)}, u32[]{:S(2)}) collective-permute-start(bf16[2,192,256]{2,1,0:T(8,128)(2,1)} %get-tuple-element.46), channel_id=1, source_target_pairs={{0,2},{1,3},{2,0},{3,1},{4,6},{5,7},{6,4},{7,5},{8,10},{9,11},{10,... | collective-permute-start | bytes 589832 | tf_op jit(solution)/shard_map/ppermute | solution.py:417
  7.4 1.3 %collective-permute-start.5 = (bf16[2,192,256]{2,1,0:T(8,128)(2,1)}, bf16[2,192,256]{2,1,0:T(8,128)(2,1)S(1)}, u32[]{:S(2)}, u32[]{:S(2)}) collective-permute-start(bf16[2,192,256]{2,1,0:T(8,128)(2,1)} %get-tuple-element.47), channel_id=1, source_target_pairs={{0,3},{1,0},{2,1},{3,2},{4,7},{5,4},{6,5},{7,6},{8,11},{9,8},{10,9... | collective-permute-start | bytes 589832 | tf_op jit(solution)/shard_map/ppermute | solution.py:417
  8.9 1.4 %collective-permute-start.1 = (f32[1,32]{1,0:T(1,128)S(1)}, f32[1,32]{1,0:T(1,128)S(1)}, u32[]{:S(2)}, u32[]{:S(2)}) collective-permute-start(f32[1,32]{1,0:T(1,128)S(1)} %copy-done.6), channel_id=1, source_target_pairs={{0,64},{32,96},{64,0},{96,32},{1,65},{33,97},{65,1},{97,33},{2,66}... | collective-permute-start | bytes 392 | tf_op jit(solution)/shard_map/ppermute | solution.py:430
  10.4 1.2 %collective-permute-start = (f32[1,32]{1,0:T(1,128)S(1)}, f32[1,32]{1,0:T(1,128)S(1)}, u32[]{:S(2)}, u32[]{:S(2)}) collective-permute-start(f32[1,32]{1,0:T(1,128)S(1)} %copy-done.6), channel_id=1, source_target_pairs={{0,32},{32,64},{64,96},{96,0},{1,33},{33,65},{65,97},{97,1},{2,34}... | collective-permute-start | bytes 392 | tf_op jit(solution)/shard_map/ppermute | solution.py:430
  11.6 0.8 collective-permute-done.1.refs_1_.text_three
  13.4 2.4 %collective-permute-start.8 = (bf16[2,192,256]{2,1,0:T(8,128)(2,1)S(1)}, bf16[2,192,256]{2,1,0:T(8,128)(2,1)S(1)}, u32[]{:S(2)}, u32[]{:S(2)}) collective-permute-start(bf16[2,192,256]{2,1,0:T(8,128)(2,1)S(1)} %get-tuple-element.55), channel_id=1, source_target_pairs={{0,3},{1,0},{2,1},{3,2},{4,7},{5,4},{6,5},{7,6},{8,11},{9,8},{10,9... | collective-permute-start | bytes 589832 | tf_op jit(solution)/shard_map/ppermute | solution.py:417
  15.8 1.3 %collective-permute-done.4.two.key_two = bf16[2,192,256]{2,1,0:T(8,128)(2,1)S(1)} collective-permute-done((bf16[2,192,256]{2,1,0:T(8,128)(2,1)}, bf16[2,192,256]{2,1,0:T(8,128)(2,1)S(1)}, u32[]{:S(2)}, u32[]{:S(2)}) %collective-permute-start.4) | collective-permute-done | bytes 196640 | tf_op jit(solution)/shard_map/ppermute | solution.py:417
  17.2 3.2 %collective-permute-start.16 = (bf16[2,576,256]{2,1,0:T(8,128)(2,1)S(1)}, bf16[2,576,256]{2,1,0:T(8,128)(2,1)S(1)}, u32[]{:S(2)}, u32[]{:S(2)}) collective-permute-start(bf16[2,576,256]{2,1,0:T(8,128)(2,1)S(1)} %edge.2.after), channel_id=1, source_target_pairs={{0,4},{1,5},{2,6},{3,7},{4,8},{5,9},{6,10},{7,11},{8,12},{9,13},{1... | collective-permute-start | bytes 1769480 | tf_op jit(solution)/shard_map/ppermute | solution.py:421
  20.5 4.2 %collective-permute-start.13 = (bf16[2,192,256]{2,1,0:T(8,128)(2,1)S(1)}, bf16[2,192,256]{2,1,0:T(8,128)(2,1)S(1)}, u32[]{:S(2)}, u32[]{:S(2)}) collective-permute-start(bf16[2,192,256]{2,1,0:T(8,128)(2,1)S(1)} %get-tuple-element.49.after), channel_id=1, source_target_pairs={{0,1},{1,2},{2,3},{3,0},{4,5},{5,6},{6,7},{7,4},{8,9},{9,10},{10,1... | collective-permute-start | bytes 589832 | tf_op jit(solution)/shard_map/ppermute | solution.py:417
  25.9 2.3 %collective-permute-start.14 = (bf16[2,192,256]{2,1,0:T(8,128)(2,1)S(1)}, bf16[2,192,256]{2,1,0:T(8,128)(2,1)S(1)}, u32[]{:S(2)}, u32[]{:S(2)}) collective-permute-start(bf16[2,192,256]{2,1,0:T(8,128)(2,1)S(1)} %get-tuple-element.58), channel_id=1, source_target_pairs={{0,2},{1,3},{2,0},{3,1},{4,6},{5,7},{6,4},{7,5},{8,10},{9,11},{10,... | collective-permute-start | bytes 589832 | tf_op jit(solution)/shard_map/ppermute | solution.py:417
  28.8 1.9 %collective-permute-start.12 = (bf16[2,576,256]{2,1,0:T(8,128)(2,1)S(1)}, bf16[2,576,256]{2,1,0:T(8,128)(2,1)S(1)}, u32[]{:S(2)}, u32[]{:S(2)}) collective-permute-start(bf16[2,576,256]{2,1,0:T(8,128)(2,1)S(1)} %edge.3), channel_id=1, source_target_pairs={{0,4},{1,5},{2,6},{3,7},{4,8},{5,9},{6,10},{7,11},{8,12},{9,13},{1... | collective-permute-start | bytes 1769480 | tf_op jit(solution)/shard_map/ppermute | solution.py:421
  30.7 2.7 %collective-permute-done.14.query_two = bf16[2,192,256]{2,1,0:T(8,128)(2,1)S(1)} collective-permute-done((bf16[2,192,256]{2,1,0:T(8,128)(2,1)S(1)}, bf16[2,192,256]{2,1,0:T(8,128)(2,1)S(1)}, u32[]{:S(2)}, u32[]{:S(2)}) %collective-permute-start.14) | collective-permute-done | bytes 196640 | tf_op jit(solution)/shard_map/ppermute | solution.py:417
  33.8 2.7 %collective-permute-start.10 = (bf16[2,192,256]{2,1,0:T(8,128)(2,1)S(1)}, bf16[2,192,256]{2,1,0:T(8,128)(2,1)S(1)}, u32[]{:S(2)}, u32[]{:S(2)}) collective-permute-start(bf16[2,192,256]{2,1,0:T(8,128)(2,1)S(1)} %get-tuple-element.56), channel_id=1, source_target_pairs={{0,2},{1,3},{2,0},{3,1},{4,6},{5,7},{6,4},{7,5},{8,10},{9,11},{10,... | collective-permute-start | bytes 589832 | tf_op jit(solution)/shard_map/ppermute | solution.py:417
  36.5 2.6 %collective-permute-start.11 = (bf16[2,192,256]{2,1,0:T(8,128)(2,1)S(1)}, bf16[2,192,256]{2,1,0:T(8,128)(2,1)S(1)}, u32[]{:S(2)}, u32[]{:S(2)}) collective-permute-start(bf16[2,192,256]{2,1,0:T(8,128)(2,1)S(1)} %get-tuple-element.57), channel_id=1, source_target_pairs={{0,3},{1,0},{2,1},{3,2},{4,7},{5,4},{6,5},{7,6},{8,11},{9,8},{10,9... | collective-permute-start | bytes 589832 | tf_op jit(solution)/shard_map/ppermute | solution.py:417
  39.1 6.3 %attend.2 = (bf16[1,192,256]{2,1,0:T(8,128)(2,1)S(1)}, bf16[1,192,256]{2,1,0:T(8,128)(2,1)S(1)}, bf16[1,192,256]{2,1,0:T(8,128)(2,1)S(1)}, bf16[1,192,256]{2,1,0...) custom-call(f32[1,32]{1,0:T(1,128)S(1)} %copy-done.6, ...), custom_call_target="tpu_custom_call" | custom-call | flops 4499999744 | tf_op jit(solution)/shard_map/attend/pallas_call | solution.py:281
  45.4 5.5 %collective-permute-start.20 = (bf16[2,576,256]{2,1,0:T(8,128)(2,1)S(1)}, bf16[2,576,256]{2,1,0:T(8,128)(2,1)S(1)}, u32[]{:S(2)}, u32[]{:S(2)}) collective-permute-start(bf16[2,576,256]{2,1,0:T(8,128)(2,1)S(1)} %get-tuple-element.69), channel_id=1, source_target_pairs={{0,28},{1,29},{2,30},{3,31},{4,0},{5,1},{6,2},{7,3},{8,4},{9,5},{1... | collective-permute-start | bytes 1769480 | tf_op jit(solution)/shard_map/ppermute | solution.py:421
  51.0 6.3 %attend.3 = (bf16[2,192,256]{2,1,0:T(8,128)(2,1)S(1)}, bf16[2,192,256]{2,1,0:T(8,128)(2,1)S(1)}, bf16[2,192,256]{2,1,0:T(8,128)(2,1)S(1)}, bf16[2,192,256]{2,1,0...) custom-call(f32[1,32]{1,0:T(1,128)S(1)} %copy-done.6, ...), custom_call_target="tpu_custom_call" | custom-call | flops 4499999744 | tf_op jit(solution)/shard_map/attend/pallas_call | solution.py:281
  57.3 1.5 %collective-permute-start.24 = (bf16[2,576,256]{2,1,0:T(8,128)(2,1)S(1)}, bf16[2,576,256]{2,1,0:T(8,128)(2,1)S(1)}, u32[]{:S(2)}, u32[]{:S(2)}) collective-permute-start(bf16[2,576,256]{2,1,0:T(8,128)(2,1)S(1)} %get-tuple-element.76), channel_id=1, source_target_pairs={{0,28},{1,29},{2,30},{3,31},{4,0},{5,1},{6,2},{7,3},{8,4},{9,5},{1... | collective-permute-start | bytes 1769480 | tf_op jit(solution)/shard_map/ppermute | solution.py:421
  58.8 1.1 %collective-permute-start.17 = (bf16[2,192,256]{2,1,0:T(8,128)(2,1)S(1)}, bf16[2,192,256]{2,1,0:T(8,128)(2,1)S(1)}, u32[]{:S(2)}, u32[]{:S(2)}) collective-permute-start(bf16[2,192,256]{2,1,0:T(8,128)(2,1)S(1)} %get-tuple-element.65), channel_id=1, source_target_pairs={{0,1},{1,2},{2,3},{3,0},{4,5},{5,6},{6,7},{7,4},{8,9},{9,10},{10,1... | collective-permute-start | bytes 589832 | tf_op jit(solution)/shard_map/ppermute | solution.py:417
  59.9 5.2 %collective-permute-start.18 = (bf16[2,192,256]{2,1,0:T(8,128)(2,1)S(1)}, bf16[2,192,256]{2,1,0:T(8,128)(2,1)S(1)}, u32[]{:S(2)}, u32[]{:S(2)}) collective-permute-start(bf16[2,192,256]{2,1,0:T(8,128)(2,1)S(1)} %get-tuple-element.66), channel_id=1, source_target_pairs={{0,2},{1,3},{2,0},{3,1},{4,6},{5,7},{6,4},{7,5},{8,10},{9,11},{10,... | collective-permute-start | bytes 589832 | tf_op jit(solution)/shard_map/ppermute | solution.py:417
  65.1 4.3 %collective-permute-done.17.refs_0_.refs_1_ = bf16[2,192,256]{2,1,0:T(8,128)(2,1)S(1)} collective-permute-done((bf16[2,192,256]{2,1,0:T(8,128)(2,1)S(1)}, bf16[2,192,256]{2,1,0:T(8,128)(2,1)S(1)}, u32[]{:S(2)}, u32[]{:S(2)}) %collective-permute-start.17) | collective-permute-done | bytes 196640 | tf_op jit(solution)/shard_map/ppermute | solution.py:417
  69.4 2.4 %collective-permute-done.18.refs_1_.refs_2_ = bf16[2,192,256]{2,1,0:T(8,128)(2,1)S(1)} collective-permute-done((bf16[2,192,256]{2,1,0:T(8,128)(2,1)S(1)}, bf16[2,192,256]{2,1,0:T(8,128)(2,1)S(1)}, u32[]{:S(2)}, u32[]{:S(2)}) %collective-permute-start.18) | collective-permute-done | bytes 196640 | tf_op jit(solution)/shard_map/ppermute | solution.py:417
  72.4 3.1 %collective-permute-start.22 = (bf16[2,192,256]{2,1,0:T(8,128)(2,1)S(1)}, bf16[2,192,256]{2,1,0:T(8,128)(2,1)S(1)}, u32[]{:S(2)}, u32[]{:S(2)}) collective-permute-start(bf16[2,192,256]{2,1,0:T(8,128)(2,1)S(1)} %get-tuple-element.72), channel_id=1, source_target_pairs={{0,2},{1,3},{2,0},{3,1},{4,6},{5,7},{6,4},{7,5},{8,10},{9,11},{10,... | collective-permute-start | bytes 589832 | tf_op jit(solution)/shard_map/ppermute | solution.py:417
  75.8 1.9 %collective-permute-start.25 = (bf16[2,192,256]{2,1,0:T(8,128)(2,1)S(1)}, bf16[2,192,256]{2,1,0:T(8,128)(2,1)S(1)}, u32[]{:S(2)}, u32[]{:S(2)}) collective-permute-start(bf16[2,192,256]{2,1,0:T(8,128)(2,1)S(1)} %get-tuple-element.78), channel_id=1, source_target_pairs={{0,1},{1,2},{2,3},{3,0},{4,5},{5,6},{6,7},{7,4},{8,9},{9,10},{10,1... | collective-permute-start | bytes 589832 | tf_op jit(solution)/shard_map/ppermute | solution.py:417
  78.5 5.0 %collective-permute-done.21.refs_5_ = bf16[2,192,256]{2,1,0:T(8,128)(2,1)S(1)} collective-permute-done((bf16[2,192,256]{2,1,0:T(8,128)(2,1)S(1)}, bf16[2,192,256]{2,1,0:T(8,128)(2,1)S(1)}, u32[]{:S(2)}, u32[]{:S(2)}) %collective-permute-start.21) | collective-permute-done | bytes 196640 | tf_op jit(solution)/shard_map/ppermute | solution.py:417
  83.6 2.0 %collective-permute-done.22.refs_6_ = bf16[2,192,256]{2,1,0:T(8,128)(2,1)S(1)} collective-permute-done((bf16[2,192,256]{2,1,0:T(8,128)(2,1)S(1)}, bf16[2,192,256]{2,1,0:T(8,128)(2,1)S(1)}, u32[]{:S(2)}, u32[]{:S(2)}) %collective-permute-start.22) | collective-permute-done | bytes 196640 | tf_op jit(solution)/shard_map/ppermute | solution.py:417
  86.2 1.3 %early.1 = (bf16[192,2048]{1,0:T(8,128)(2,1)}, bf16[192,2048]{1,0:T(8,128)(2,1)}, bf16[192,2048]{1,0:T(8,128)(2,1)}) custom-call(bf16[2,192,256]{2,1,0:T(8,128)(2,1)S(1)} %get-tuple-element.64.refs_0_, bf16[2,192,256]{2,1,0:T(8,128)(2,1)S(1)} %collective-permute-done.17.refs_0_.refs_1_, bf16[2,192,256]{2,1,0:T(8,128)(2,1)S(1)} %collective-permute-done.18.refs_1_.refs_2_, ...), custom_call_target="tpu_custom_call" | custom-call | bytes 2359296 | tf_op jit(solution)/shard_map/early/pallas_call | solution.py:382
  87.4 1.5 %collective-permute-done.25.refs_1_ = bf16[2,192,256]{2,1,0:T(8,128)(2,1)S(1)} collective-permute-done((bf16[2,192,256]{2,1,0:T(8,128)(2,1)S(1)}, bf16[2,192,256]{2,1,0:T(8,128)(2,1)S(1)}, u32[]{:S(2)}, u32[]{:S(2)}) %collective-permute-start.25) | collective-permute-done | bytes 196640 | tf_op jit(solution)/shard_map/ppermute | solution.py:417
  89.0 2.1 %collective-permute-done.26.refs_2_ = bf16[2,192,256]{2,1,0:T(8,128)(2,1)S(1)} collective-permute-done((bf16[2,192,256]{2,1,0:T(8,128)(2,1)S(1)}, bf16[2,192,256]{2,1,0:T(8,128)(2,1)S(1)}, u32[]{:S(2)}, u32[]{:S(2)}) %collective-permute-start.26) | collective-permute-done | bytes 196640 | tf_op jit(solution)/shard_map/ppermute | solution.py:417
  91.1 0.9 %late.1 = (bf16[192,2048]{1,0:T(8,128)(2,1)}, bf16[192,2048]{1,0:T(8,128)(2,1)}) custom-call(bf16[2,192,256]{2,1,0:T(8,128)(2,1)S(1)} %get-tuple-element.77.refs_0_, bf16[2,192,256]{2,1,0:T(8,128)(2,1)S(1)} %collective-permute-done.25.refs_1_, ...), custom_call_target="tpu_custom_call", output_to_operand_aliasing={{0}: (4, {}), {1}: (5, {})} | custom-call | bytes 2359296 | tf_op jit(solution)/shard_map/late/pallas_call | solution.py:392
  (51 shorter events, 6.0 us)
Async XLA Ops:
  0.6 9.7 %copy-start = (bf16[1,192,2048]{2,1,0:T(8,128)(2,1)S(1)}, bf16[1,192,2048]{2,1,0:T(8,128)(2,1)}, u32[]{:S(2)}) copy-start(bf16[1,192,2048]{2,1,0:T(8,128)(2,1)} %param.7) | copy-start | bytes 2359300
  0.6 9.6 %copy-start.1 = (bf16[1,192,2048]{2,1,0:T(8,128)(2,1)S(1)}, bf16[1,192,2048]{2,1,0:T(8,128)(2,1)}, u32[]{:S(2)}) copy-start(bf16[1,192,2048]{2,1,0:T(8,128)(2,1)} %param.8) | copy-start | bytes 2359300
  2.8 13.0 %collective-permute-start.3 = (bf16[2,192,256]{2,1,0:T(8,128)(2,1)}, bf16[2,192,256]{2,1,0:T(8,128)(2,1)S(1)}, u32[]{:S(2)}, u32[]{:S(2)}) collective-permute-start(bf16[2,192,256]{2,1,0:T(8,128)(2,1)} %get-tuple-element.45), channel_id=1, source_target_pairs={{0,1},{1,2},{2,3},{3,0},{4,5},{5,6},{6,7},{7,4},{8,9},{9,10},{10,1... | collective-permute-start | bytes 589832 | tf_op jit(solution)/shard_map/ppermute | solution.py:417
  4.5 12.5 %collective-permute-start.4 = (bf16[2,192,256]{2,1,0:T(8,128)(2,1)}, bf16[2,192,256]{2,1,0:T(8,128)(2,1)S(1)}, u32[]{:S(2)}, u32[]{:S(2)}) collective-permute-start(bf16[2,192,256]{2,1,0:T(8,128)(2,1)} %get-tuple-element.46), channel_id=1, source_target_pairs={{0,2},{1,3},{2,0},{3,1},{4,6},{5,7},{6,4},{7,5},{8,10},{9,11},{10,... | collective-permute-start | bytes 589832 | tf_op jit(solution)/shard_map/ppermute | solution.py:417
  7.4 9.7 %collective-permute-start.5 = (bf16[2,192,256]{2,1,0:T(8,128)(2,1)}, bf16[2,192,256]{2,1,0:T(8,128)(2,1)S(1)}, u32[]{:S(2)}, u32[]{:S(2)}) collective-permute-start(bf16[2,192,256]{2,1,0:T(8,128)(2,1)} %get-tuple-element.47), channel_id=1, source_target_pairs={{0,3},{1,0},{2,1},{3,2},{4,7},{5,4},{6,5},{7,6},{8,11},{9,8},{10,9... | collective-permute-start | bytes 589832 | tf_op jit(solution)/shard_map/ppermute | solution.py:417
  8.8 1.6 %collective-permute-start.2 = (f32[1,32]{1,0:T(1,128)S(1)}, f32[1,32]{1,0:T(1,128)S(1)}, u32[]{:S(2)}, u32[]{:S(2)}) collective-permute-start(f32[1,32]{1,0:T(1,128)S(1)} %copy-done.6), channel_id=1, source_target_pairs={{0,96},{32,0},{64,32},{96,64},{1,97},{33,1},{65,33},{97,65},{2,98}... | collective-permute-start | bytes 392 | tf_op jit(solution)/shard_map/ppermute | solution.py:430
  8.9 3.5 %collective-permute-start.1 = (f32[1,32]{1,0:T(1,128)S(1)}, f32[1,32]{1,0:T(1,128)S(1)}, u32[]{:S(2)}, u32[]{:S(2)}) collective-permute-start(f32[1,32]{1,0:T(1,128)S(1)} %copy-done.6), channel_id=1, source_target_pairs={{0,64},{32,96},{64,0},{96,32},{1,65},{33,97},{65,1},{97,33},{2,66}... | collective-permute-start | bytes 392 | tf_op jit(solution)/shard_map/ppermute | solution.py:430
  10.4 3.0 %collective-permute-start = (f32[1,32]{1,0:T(1,128)S(1)}, f32[1,32]{1,0:T(1,128)S(1)}, u32[]{:S(2)}, u32[]{:S(2)}) collective-permute-start(f32[1,32]{1,0:T(1,128)S(1)} %copy-done.6), channel_id=1, source_target_pairs={{0,32},{32,64},{64,96},{96,0},{1,33},{33,65},{65,97},{97,1},{2,34}... | collective-permute-start | bytes 392 | tf_op jit(solution)/shard_map/ppermute | solution.py:430
  12.4 13.5 %collective-permute-start.7 = (bf16[2,192,256]{2,1,0:T(8,128)(2,1)S(1)}, bf16[2,192,256]{2,1,0:T(8,128)(2,1)S(1)}, u32[]{:S(2)}, u32[]{:S(2)}) collective-permute-start(bf16[2,192,256]{2,1,0:T(8,128)(2,1)S(1)} %get-tuple-element.54), channel_id=1, source_target_pairs={{0,2},{1,3},{2,0},{3,1},{4,6},{5,7},{6,4},{7,5},{8,10},{9,11},{10,... | collective-permute-start | bytes 589832 | tf_op jit(solution)/shard_map/ppermute | solution.py:417
  13.4 14.7 %collective-permute-start.8 = (bf16[2,192,256]{2,1,0:T(8,128)(2,1)S(1)}, bf16[2,192,256]{2,1,0:T(8,128)(2,1)S(1)}, u32[]{:S(2)}, u32[]{:S(2)}) collective-permute-start(bf16[2,192,256]{2,1,0:T(8,128)(2,1)S(1)} %get-tuple-element.55), channel_id=1, source_target_pairs={{0,3},{1,0},{2,1},{3,2},{4,7},{5,4},{6,5},{7,6},{8,11},{9,8},{10,9... | collective-permute-start | bytes 589832 | tf_op jit(solution)/shard_map/ppermute | solution.py:417
  15.8 4.6 %copy-start.2 = (bf16[1,192,2048]{2,1,0:T(8,128)(2,1)S(1)}, bf16[1,192,2048]{2,1,0:T(8,128)(2,1)}, u32[]{:S(2)}) copy-start(bf16[1,192,2048]{2,1,0:T(8,128)(2,1)} %param.6) | copy-start | bytes 2359300
  15.8 4.6 %copy-start.3 = (bf16[1,192,2048]{2,1,0:T(8,128)(2,1)S(1)}, bf16[1,192,2048]{2,1,0:T(8,128)(2,1)}, u32[]{:S(2)}) copy-start(bf16[1,192,2048]{2,1,0:T(8,128)(2,1)} %param.9) | copy-start | bytes 2359300
  15.8 12.9 %collective-permute-start.6 = (bf16[2,192,256]{2,1,0:T(8,128)(2,1)S(1)}, bf16[2,192,256]{2,1,0:T(8,128)(2,1)S(1)}, u32[]{:S(2)}, u32[]{:S(2)}) collective-permute-start(bf16[2,192,256]{2,1,0:T(8,128)(2,1)S(1)} %get-tuple-element.48.refs_3_), channel_id=1, source_target_pairs={{0,1},{1,2},{2,3},{3,0},{4,5},{5,6},{6,7},{7,4},{8,9},{9,10},{10,1... | collective-permute-start | bytes 589832 | tf_op jit(solution)/shard_map/ppermute | solution.py:417
  17.2 21.9 %collective-permute-start.16 = (bf16[2,576,256]{2,1,0:T(8,128)(2,1)S(1)}, bf16[2,576,256]{2,1,0:T(8,128)(2,1)S(1)}, u32[]{:S(2)}, u32[]{:S(2)}) collective-permute-start(bf16[2,576,256]{2,1,0:T(8,128)(2,1)S(1)} %edge.2.after), channel_id=1, source_target_pairs={{0,4},{1,5},{2,6},{3,7},{4,8},{5,9},{6,10},{7,11},{8,12},{9,13},{1... | collective-permute-start | bytes 1769480 | tf_op jit(solution)/shard_map/ppermute | solution.py:421
  20.5 16.0 %collective-permute-start.13 = (bf16[2,192,256]{2,1,0:T(8,128)(2,1)S(1)}, bf16[2,192,256]{2,1,0:T(8,128)(2,1)S(1)}, u32[]{:S(2)}, u32[]{:S(2)}) collective-permute-start(bf16[2,192,256]{2,1,0:T(8,128)(2,1)S(1)} %get-tuple-element.49.after), channel_id=1, source_target_pairs={{0,1},{1,2},{2,3},{3,0},{4,5},{5,6},{6,7},{7,4},{8,9},{9,10},{10,1... | collective-permute-start | bytes 589832 | tf_op jit(solution)/shard_map/ppermute | solution.py:417
  25.9 7.4 %collective-permute-start.14 = (bf16[2,192,256]{2,1,0:T(8,128)(2,1)S(1)}, bf16[2,192,256]{2,1,0:T(8,128)(2,1)S(1)}, u32[]{:S(2)}, u32[]{:S(2)}) collective-permute-start(bf16[2,192,256]{2,1,0:T(8,128)(2,1)S(1)} %get-tuple-element.58), channel_id=1, source_target_pairs={{0,2},{1,3},{2,0},{3,1},{4,6},{5,7},{6,4},{7,5},{8,10},{9,11},{10,... | collective-permute-start | bytes 589832 | tf_op jit(solution)/shard_map/ppermute | solution.py:417
  28.2 5.7 %collective-permute-start.15 = (bf16[2,192,256]{2,1,0:T(8,128)(2,1)S(1)}, bf16[2,192,256]{2,1,0:T(8,128)(2,1)S(1)}, u32[]{:S(2)}, u32[]{:S(2)}) collective-permute-start(bf16[2,192,256]{2,1,0:T(8,128)(2,1)S(1)} %get-tuple-element.59), channel_id=1, source_target_pairs={{0,3},{1,0},{2,1},{3,2},{4,7},{5,4},{6,5},{7,6},{8,11},{9,8},{10,9... | collective-permute-start | bytes 589832 | tf_op jit(solution)/shard_map/ppermute | solution.py:417
  28.8 22.2 %collective-permute-start.12 = (bf16[2,576,256]{2,1,0:T(8,128)(2,1)S(1)}, bf16[2,576,256]{2,1,0:T(8,128)(2,1)S(1)}, u32[]{:S(2)}, u32[]{:S(2)}) collective-permute-start(bf16[2,576,256]{2,1,0:T(8,128)(2,1)S(1)} %edge.3), channel_id=1, source_target_pairs={{0,4},{1,5},{2,6},{3,7},{4,8},{5,9},{6,10},{7,11},{8,12},{9,13},{1... | collective-permute-start | bytes 1769480 | tf_op jit(solution)/shard_map/ppermute | solution.py:421
  33.3 17.7 %collective-permute-start.9 = (bf16[2,192,256]{2,1,0:T(8,128)(2,1)S(1)}, bf16[2,192,256]{2,1,0:T(8,128)(2,1)S(1)}, u32[]{:S(2)}, u32[]{:S(2)}) collective-permute-start(bf16[2,192,256]{2,1,0:T(8,128)(2,1)S(1)} %get-tuple-element.50.after), channel_id=1, source_target_pairs={{0,1},{1,2},{2,3},{3,0},{4,5},{5,6},{6,7},{7,4},{8,9},{9,10},{10,1... | collective-permute-start | bytes 589832 | tf_op jit(solution)/shard_map/ppermute | solution.py:417
  33.8 17.2 %collective-permute-start.10 = (bf16[2,192,256]{2,1,0:T(8,128)(2,1)S(1)}, bf16[2,192,256]{2,1,0:T(8,128)(2,1)S(1)}, u32[]{:S(2)}, u32[]{:S(2)}) collective-permute-start(bf16[2,192,256]{2,1,0:T(8,128)(2,1)S(1)} %get-tuple-element.56), channel_id=1, source_target_pairs={{0,2},{1,3},{2,0},{3,1},{4,6},{5,7},{6,4},{7,5},{8,10},{9,11},{10,... | collective-permute-start | bytes 589832 | tf_op jit(solution)/shard_map/ppermute | solution.py:417
  36.5 14.5 %collective-permute-start.11 = (bf16[2,192,256]{2,1,0:T(8,128)(2,1)S(1)}, bf16[2,192,256]{2,1,0:T(8,128)(2,1)S(1)}, u32[]{:S(2)}, u32[]{:S(2)}) collective-permute-start(bf16[2,192,256]{2,1,0:T(8,128)(2,1)S(1)} %get-tuple-element.57), channel_id=1, source_target_pairs={{0,3},{1,0},{2,1},{3,2},{4,7},{5,4},{6,5},{7,6},{8,11},{9,8},{10,9... | collective-permute-start | bytes 589832 | tf_op jit(solution)/shard_map/ppermute | solution.py:417
  45.4 26.3 %collective-permute-start.20 = (bf16[2,576,256]{2,1,0:T(8,128)(2,1)S(1)}, bf16[2,576,256]{2,1,0:T(8,128)(2,1)S(1)}, u32[]{:S(2)}, u32[]{:S(2)}) collective-permute-start(bf16[2,576,256]{2,1,0:T(8,128)(2,1)S(1)} %get-tuple-element.69), channel_id=1, source_target_pairs={{0,28},{1,29},{2,30},{3,31},{4,0},{5,1},{6,2},{7,3},{8,4},{9,5},{1... | collective-permute-start | bytes 1769480 | tf_op jit(solution)/shard_map/ppermute | solution.py:421
  57.3 18.3 %collective-permute-start.24 = (bf16[2,576,256]{2,1,0:T(8,128)(2,1)S(1)}, bf16[2,576,256]{2,1,0:T(8,128)(2,1)S(1)}, u32[]{:S(2)}, u32[]{:S(2)}) collective-permute-start(bf16[2,576,256]{2,1,0:T(8,128)(2,1)S(1)} %get-tuple-element.76), channel_id=1, source_target_pairs={{0,28},{1,29},{2,30},{3,31},{4,0},{5,1},{6,2},{7,3},{8,4},{9,5},{1... | collective-permute-start | bytes 1769480 | tf_op jit(solution)/shard_map/ppermute | solution.py:421
  58.8 10.5 %collective-permute-start.17 = (bf16[2,192,256]{2,1,0:T(8,128)(2,1)S(1)}, bf16[2,192,256]{2,1,0:T(8,128)(2,1)S(1)}, u32[]{:S(2)}, u32[]{:S(2)}) collective-permute-start(bf16[2,192,256]{2,1,0:T(8,128)(2,1)S(1)} %get-tuple-element.65), channel_id=1, source_target_pairs={{0,1},{1,2},{2,3},{3,0},{4,5},{5,6},{6,7},{7,4},{8,9},{9,10},{10,1... | collective-permute-start | bytes 589832 | tf_op jit(solution)/shard_map/ppermute | solution.py:417
  59.9 11.8 %collective-permute-start.18 = (bf16[2,192,256]{2,1,0:T(8,128)(2,1)S(1)}, bf16[2,192,256]{2,1,0:T(8,128)(2,1)S(1)}, u32[]{:S(2)}, u32[]{:S(2)}) collective-permute-start(bf16[2,192,256]{2,1,0:T(8,128)(2,1)S(1)} %get-tuple-element.66), channel_id=1, source_target_pairs={{0,2},{1,3},{2,0},{3,1},{4,6},{5,7},{6,4},{7,5},{8,10},{9,11},{10,... | collective-permute-start | bytes 589832 | tf_op jit(solution)/shard_map/ppermute | solution.py:417
  65.1 6.7 %collective-permute-start.19 = (bf16[2,192,256]{2,1,0:T(8,128)(2,1)S(1)}, bf16[2,192,256]{2,1,0:T(8,128)(2,1)S(1)}, u32[]{:S(2)}, u32[]{:S(2)}) collective-permute-start(bf16[2,192,256]{2,1,0:T(8,128)(2,1)S(1)} %get-tuple-element.67), channel_id=1, source_target_pairs={{0,3},{1,0},{2,1},{3,2},{4,7},{5,4},{6,5},{7,6},{8,11},{9,8},{10,9... | collective-permute-start | bytes 589832 | tf_op jit(solution)/shard_map/ppermute | solution.py:417
  71.9 11.6 %collective-permute-start.21 = (bf16[2,192,256]{2,1,0:T(8,128)(2,1)S(1)}, bf16[2,192,256]{2,1,0:T(8,128)(2,1)S(1)}, u32[]{:S(2)}, u32[]{:S(2)}) collective-permute-start(bf16[2,192,256]{2,1,0:T(8,128)(2,1)S(1)} %get-tuple-element.71), channel_id=1, source_target_pairs={{0,1},{1,2},{2,3},{3,0},{4,5},{5,6},{6,7},{7,4},{8,9},{9,10},{10,1... | collective-permute-start | bytes 589832 | tf_op jit(solution)/shard_map/ppermute | solution.py:417
  72.4 13.2 %collective-permute-start.22 = (bf16[2,192,256]{2,1,0:T(8,128)(2,1)S(1)}, bf16[2,192,256]{2,1,0:T(8,128)(2,1)S(1)}, u32[]{:S(2)}, u32[]{:S(2)}) collective-permute-start(bf16[2,192,256]{2,1,0:T(8,128)(2,1)S(1)} %get-tuple-element.72), channel_id=1, source_target_pairs={{0,2},{1,3},{2,0},{3,1},{4,6},{5,7},{6,4},{7,5},{8,10},{9,11},{10,... | collective-permute-start | bytes 589832 | tf_op jit(solution)/shard_map/ppermute | solution.py:417
  75.5 10.7 %collective-permute-start.23 = (bf16[2,192,256]{2,1,0:T(8,128)(2,1)S(1)}, bf16[2,192,256]{2,1,0:T(8,128)(2,1)S(1)}, u32[]{:S(2)}, u32[]{:S(2)}) collective-permute-start(bf16[2,192,256]{2,1,0:T(8,128)(2,1)S(1)} %get-tuple-element.73), channel_id=1, source_target_pairs={{0,3},{1,0},{2,1},{3,2},{4,7},{5,4},{6,5},{7,6},{8,11},{9,8},{10,9... | collective-permute-start | bytes 589832 | tf_op jit(solution)/shard_map/ppermute | solution.py:417
  75.8 13.1 %collective-permute-start.25 = (bf16[2,192,256]{2,1,0:T(8,128)(2,1)S(1)}, bf16[2,192,256]{2,1,0:T(8,128)(2,1)S(1)}, u32[]{:S(2)}, u32[]{:S(2)}) collective-permute-start(bf16[2,192,256]{2,1,0:T(8,128)(2,1)S(1)} %get-tuple-element.78), channel_id=1, source_target_pairs={{0,1},{1,2},{2,3},{3,0},{4,5},{5,6},{6,7},{7,4},{8,9},{9,10},{10,1... | collective-permute-start | bytes 589832 | tf_op jit(solution)/shard_map/ppermute | solution.py:417
  77.8 13.4 %collective-permute-start.26 = (bf16[2,192,256]{2,1,0:T(8,128)(2,1)S(1)}, bf16[2,192,256]{2,1,0:T(8,128)(2,1)S(1)}, u32[]{:S(2)}, u32[]{:S(2)}) collective-permute-start(bf16[2,192,256]{2,1,0:T(8,128)(2,1)S(1)} %get-tuple-element.79), channel_id=1, source_target_pairs={{0,2},{1,3},{2,0},{3,1},{4,6},{5,7},{6,4},{7,5},{8,10},{9,11},{10,... | collective-permute-start | bytes 589832 | tf_op jit(solution)/shard_map/ppermute | solution.py:417
  83.5 7.6 %collective-permute-start.27 = (bf16[2,192,256]{2,1,0:T(8,128)(2,1)S(1)}, bf16[2,192,256]{2,1,0:T(8,128)(2,1)S(1)}, u32[]{:S(2)}, u32[]{:S(2)}) collective-permute-start(bf16[2,192,256]{2,1,0:T(8,128)(2,1)S(1)} %get-tuple-element.80), channel_id=1, source_target_pairs={{0,3},{1,0},{2,1},{3,2},{4,7},{5,4},{6,5},{7,6},{8,11},{9,8},{10,9... | collective-permute-start | bytes 589832 | tf_op jit(solution)/shard_map/ppermute | solution.py:417
  (3 other events, 2.7 us)

commit v4 on v1

--- a/solution.py
+++ b/solution.py
@@ -21,6 +21,11 @@
 SMALL = pltpu.CompilerParams(vmem_limit_bytes=10 * 1024 * 1024)
 
 
+def aways():
+    core = lax.rem(lax.axis_index("dp"), 2)
+    return 0, 1 + 2 * core, 3 - 2 * core, 2
+
+
 def columns(place, away, chunk, width):
     index = lax.rem(place + GROUP + away, GROUP)
     return pl.ds(pl.multiple_of((index * CHUNKS + chunk) * width, width), width)
@@ -28,27 +33,29 @@
 
 def pack_kernel(chunk, first, second, after, one, two, three):
     width = one.shape[2]
-    for away, message in ((1, one), (2, two), (3, three)):
+    for away, message in zip(aways()[1:], (one, two, three)):
         lanes = columns(lax.rem(lax.axis_index("ctx"), GROUP), away, chunk, width)
         message[0] = first[:, lanes]
         message[1] = second[:, lanes]
 
 
-def first_pack_kernel(first, second, lengths, flags, one, two, three, text, sems):
+def first_pack_kernel(first, second, lengths, flags, one, two, three, text, held, sems):
     width = one.shape[2]
     place = lax.rem(lax.axis_index("ctx"), GROUP)
     copies = []
-    for away, message in ((1, one), (2, two), (3, three)):
+    for away, message in zip(aways()[1:], (one, two, three)):
         lanes = columns(place, away, 0, width)
         for part, source in enumerate((first, second)):
             copies.append(
                 pltpu.make_async_copy(source.at[:, lanes], message.at[part], sems.at[len(copies)])
             )
+    for part, source in enumerate((lengths, flags)):
+        copies.append(pltpu.make_async_copy(source, held.at[part], sems.at[len(copies)]))
     for copy in copies:
         copy.start()
-    text[...] = (lengths[...] * (1 - flags[...])).astype(jnp.float32)
     for copy in copies:
         copy.wait()
+    text[...] = (held[0] * (1 - held[1])).astype(jnp.float32)
 
 
 def pack(first, second, after, chunk):
@@ -73,9 +80,12 @@
     *messages, text = pl.pallas_call(
         first_pack_kernel,
         out_shape=(message,) * (GROUP - 1) + (jax.ShapeDtypeStruct(lengths.shape, jnp.float32),),
-        in_specs=[ANY, ANY, VMEM, VMEM],
+        in_specs=[ANY, ANY, ANY, ANY],
         out_specs=(VMEM,) * GROUP,
-        scratch_shapes=[pltpu.SemaphoreType.DMA((2 * (GROUP - 1),))],
+        scratch_shapes=[
+            pltpu.VMEM((2, *lengths.shape), lengths.dtype),
+            pltpu.SemaphoreType.DMA((2 * GROUP,)),
+        ],
         compiler_params=LARGE,
         cost_estimate=pl.CostEstimate(flops=0, bytes_accessed=12 * rows * width * 2, transcendentals=0),
         name="first_pack",
@@ -88,7 +98,7 @@
     rows = edge.shape[1] // (GROUP - 1)
     width = edge.shape[2]
     place = lax.rem(lax.axis_index("ctx"), GROUP)
-    for away, message in enumerate((None, one, two, three)):
+    for away, message in zip(aways(), (None, one, two, three)):
         index = lax.rem(place + GROUP - away, GROUP)
 
         @pl.when(index > 0)
@@ -115,14 +125,31 @@
     )(first, second, *blocks, *afters)
 
 
-def sides_kernel(stretch_rows, cycle_size, bounds_ref, after, limit_ref, text_ref, key_ref):
+def sides_kernel(stretch_rows, cycle_size, lengths_ref, flags_ref, after, limit_ref, text_ref, key_ref):
     rows = 2 * stretch_rows
     device_here = lax.axis_index("ctx")
     start = device_here - lax.rem(device_here, GROUP)
-    first = bounds_ref[0:1, :]
-    ending = bounds_ref[1:2, :]
-    flag = bounds_ref[2:3, :].astype(jnp.float32)
-    last = ending.astype(jnp.float32)
+    segments = lengths_ref.shape[1]
+    square = (segments, segments)
+    diagonal = lax.broadcasted_iota(jnp.int32, square, 0) == lax.broadcasted_iota(
+        jnp.int32, square, 1
+    )
+
+    def upright(ref):
+        row = jnp.broadcast_to(ref[...].astype(jnp.float32), square)
+        return jnp.sum(jnp.where(diagonal, row, 0.0), axis=1, keepdims=True)
+
+    lengths, flags = upright(lengths_ref), upright(flags_ref)
+    source = lax.broadcasted_iota(jnp.int32, (segments, HEAD), 0)
+    target = lax.broadcasted_iota(jnp.int32, (segments, HEAD), 1)
+
+    def gathered_sum(mask, column):
+        return jnp.sum(jnp.where(mask, column, 0.0), axis=0, keepdims=True)
+
+    last = gathered_sum(source <= target, lengths)
+    first = gathered_sum(source < target, lengths).astype(jnp.int32)
+    flag = gathered_sum(source == target, flags)
+    ending = last.astype(jnp.int32)
     shape = (rows, HEAD)
     offset = lax.broadcasted_iota(jnp.int32, shape, 0)
     for block in range(GROUP):
@@ -151,7 +178,7 @@
         )
 
 
-def sides(bounds, after, stretch_rows, cycle_size):
+def sides(lengths, flags, after, stretch_rows, cycle_size):
     rows = 2 * stretch_rows
     return pl.pallas_call(
         functools.partial(sides_kernel, stretch_rows, cycle_size),
@@ -160,12 +187,12 @@
             jax.ShapeDtypeStruct((GROUP, rows, HEAD), jnp.float32),
             jax.ShapeDtypeStruct((GROUP, 8, STEPS * rows), jnp.int32),
         ),
-        in_specs=[VMEM, ANY],
+        in_specs=[VMEM, VMEM, ANY],
         out_specs=(VMEM,) * 3,
         compiler_params=SMALL,
         cost_estimate=pl.CostEstimate(flops=GROUP * rows * HEAD * 8, bytes_accessed=GROUP * rows * HEAD * 8, transcendentals=0),
         name="sides",
-    )(bounds, after)
+    )(lengths, flags, after)
 
 
 def attend_kernel(
@@ -187,9 +214,9 @@
     sources = [(keys.at[:, lanes], values.at[:, lanes], queries.at[:, lanes], grads.at[:, lanes])]
     for pair, query_pair in ((key_one, query_one), (key_two, query_two), (key_three, query_three)):
         sources.append((pair.at[0], pair.at[1], query_pair.at[0], query_pair.at[1]))
-    for away in range(GROUP):
+    for slot, away in enumerate(aways()):
         start = pl.multiple_of(lax.rem(place + GROUP - away, GROUP) * rows, rows)
-        key, value, query, grad = sources[away]
+        key, value, query, grad = sources[slot]
         key_all[pl.ds(edge + start, rows), :] = key[...]
         value_all[pl.ds(edge + start, rows), :] = value[...]
         query_all[pl.ds(start, rows), :] = query[...]
@@ -238,7 +265,7 @@
             value_grad[window, lanes] += lax.dot_general(
                 prob_half, grad, (((0,), (0,)), ((), ())), preferred_element_type=jnp.float32
             )
-    for away, block in enumerate((query_own, query_to_one, query_to_two, query_to_three)):
+    for away, block in zip(aways(), (query_own, query_to_one, query_to_two, query_to_three)):
         index = lax.rem(place + away, GROUP)
         block[...] = query_out[pl.ds(pl.multiple_of(index * rows, rows), rows), :]
     far_ref[0] = (key_grad[:edge, :] * scale).astype(jnp.bfloat16)
@@ -284,11 +311,11 @@
     rows = outs[0].shape[1]
     first_kind = 1 if extra else 0
     place = lax.rem(lax.axis_index("ctx"), GROUP)
-    for away, block in enumerate(outs):
+    for slot, (away, block) in enumerate(zip(aways(), outs)):
         index = lax.rem(place + away, GROUP)
         start = pl.multiple_of(index * rows, rows)
         if extra:
-            block[0] = extra[away][...]
+            block[0] = extra[slot][...]
 
         @pl.when(index == 0)
         def first():
@@ -327,8 +354,8 @@
 
 def place_copies(moves, sems):
     copies = []
-    for source, target, chunk, away in moves:
-        lanes = columns(lax.rem(lax.axis_index("ctx"), GROUP), -away, chunk, source.shape[1])
+    for source, target, chunk, slot in moves:
+        lanes = columns(lax.rem(lax.axis_index("ctx"), GROUP), -aways()[slot], chunk, source.shape[1])
         copies.append(pltpu.make_async_copy(source, target.at[:, lanes], sems.at[len(copies)]))
     for copy in copies:
         copy.start()
@@ -395,21 +422,22 @@
     cycle_size = lax.axis_size("ctx")
     samples = lax.axis_size("dp")
 
-    def swap(value, away):
-        pairs = [
-            (source, source - source % GROUP + (source + away) % GROUP)
-            for source in range(cycle_size)
-        ]
-        return lax.ppermute(value, "ctx", pairs)
+    def swap(value, slot):
+        pairs = []
+        for sample in range(samples):
+            core = sample % 2
+            away = (1 + 2 * core, 3 - 2 * core, 2)[slot]
+            for source in range(cycle_size):
+                target = source - source % GROUP + (source + away) % GROUP
+                pairs.append((sample * cycle_size + source, sample * cycle_size + target))
+        return lax.ppermute(value, ("dp", "ctx"), pairs)
 
     def next_row(value, rows):
         pairs = [(source, (source + rows * GROUP) % cycle_size) for source in range(cycle_size)]
         return lax.ppermute(value, "ctx", pairs)
 
     def swapped(messages):
-        one = swap(messages[0], 1)
-        three = swap(messages[2], 3)
-        return [one, swap(messages[1], 2), three]
+        return [swap(message, slot) for slot, message in enumerate(messages)]
 
     first_messages, text = first_pack(key_rows, value_rows, lengths, image_flags)
     texts = [text] + [
@@ -418,9 +446,6 @@
     ]
     total_rows = float(row_count * cycle_size * samples)
 
-    ending = jnp.cumsum(lengths[0])
-    bounds = jnp.stack([ending - lengths[0], ending, image_flags[0]])
-    bounds = jnp.pad(bounds, ((0, 5), (0, HEAD - bounds.shape[1])))
     key_packs, query_packs, edges = [None] * CHUNKS, [None] * CHUNKS, [None] * CHUNKS
     key_packs[0] = first_messages
     key_packs[1] = pack(key_rows, value_rows, text, 1)
@@ -432,7 +457,7 @@
     for index in range(CHUNKS):
         query_packs[index] = pack(query_rows, grad_rows, after, index)
         after = query_packs[index][0]
-    marks = sides(bounds, after, row_count // 2, cycle_size)
+    marks = sides(lengths, image_flags, after, row_count // 2, cycle_size)
     edges[1] = make_edge(
         key_rows, value_rows, key_blocks[1], (marks[1],), 1, EDGE_COST[1]
     )

time: 89.4 us -> 87.4 us (0.978)
  starting transfers between devices: 48.9 us -> 47.1 us
    ppermute x4, starting transfers between devices: 13.7 us -> 11.8 us  [next_row(): return lax.ppermute(value, 'ctx', pairs)]
    ppermute x21, waiting for transfers between devices: 10.5 us -> 11.9 us  [swap(): return lax.ppermute(value, ('dp', 'ctx'), pairs)]
    ppermute x4, waiting for transfers between devices: 8.6 us -> 7.69 us  [next_row(): return lax.ppermute(value, 'ctx', pairs)]
  transfers between devices with their start and end apart: 28 -> 28, of which waited for: 9 -> 8; matrix products, arithmetic and copies ran while one was open for 0% -> 0% of each run, Pallas kernels for 17% -> 17%
where the time goes in v4:
time: 87.4 us; the launch traced here: 87.3 us
  starting transfers between devices  47.1 us (54%)
  waiting for transfers between devices  20.4 us (23%)
  Pallas kernels  18.1 us (21%)
  between operations  1.01 us (1%)
    ppermute x21, starting transfers between devices, swap(): return lax.ppermute(value, ('dp', 'ctx'), pairs)  32.5 us
    pallas_call x2, Pallas kernels, attend(): pl.pallas_call(functools.partial(attend_kernel, chunk, total_rows), out_s...  12.7 us
    ppermute x21, waiting for transfers between devices, swap(): return lax.ppermute(value, ('dp', 'ctx'), pairs)  11.9 us
    ppermute x4, starting transfers between devices, next_row(): return lax.ppermute(value, 'ctx', pairs)  11.8 us
    ppermute x4, waiting for transfers between devices, next_row(): return lax.ppermute(value, 'ctx', pairs)  7.69 us
    ppermute x3, starting transfers between devices, shards(): lax.ppermute(text, 'dp', [(source, (source + away) % samples) for source...  2.73 us
    pallas_call x1, Pallas kernels, first_pack(): pl.pallas_call(first_pack_kernel, out_shape=(message,) * (GROUP - 1) + (j...  2.15 us
  transfers between devices with their start and end apart: 28, of which 8 were waited for; matrix products, arithmetic and copies ran while one was open for 0% of the time, Pallas kernels for 17%

profile of v4, /device:TPU:0, one launch (start us, length us, event | category | flops | bytes accessed | tf_op | source)
XLA Modules:
  0.0 87.3 jit_solution(11639712680317975107)
XLA Ops:
  0.7 2.1 %first_pack.1 = (bf16[2,192,256]{2,1,0:T(8,128)(2,1)}, bf16[2,192,256]{2,1,0:T(8,128)(2,1)}, bf16[2,192,256]{2,1,0:T(8,128)(2,1)}, f32[1,32]{1,0:T(1,128)}) custom-call(bf16[192,2048]{1,0:T(8,128)(2,1)} %bitcast.7, bf16[192,2048]{1,0:T(8,128)(2,1)} %bitcast.13, s32[1,32]{1,0:T(1,128)} %lengths_ref.1, s32[1,32]{1,0:T(1,128)} %flags_ref.1), custom_call_target="tpu_custom_call" | custom-call | bytes 1179648 | tf_op jit(solution)/shard_map/first_pack/pallas_call | solution.py:80
  2.8 1.7 %collective-permute-start.3 = (bf16[2,192,256]{2,1,0:T(8,128)(2,1)}, bf16[2,192,256]{2,1,0:T(8,128)(2,1)S(1)}, u32[]{:S(2)}, u32[]{:S(2)}) collective-permute-start(bf16[2,192,256]{2,1,0:T(8,128)(2,1)} %get-tuple-element.45), channel_id=1, source_target_pairs={{0,1},{1,2},{2,3},{3,0},{4,5},{5,6},{6,7},{7,4},{8,9},{9,10},{10,1... | collective-permute-start | bytes 589832 | tf_op jit(solution)/shard_map/ppermute | solution.py:433
  4.5 1.6 %collective-permute-start.4 = (bf16[2,192,256]{2,1,0:T(8,128)(2,1)}, bf16[2,192,256]{2,1,0:T(8,128)(2,1)S(1)}, u32[]{:S(2)}, u32[]{:S(2)}) collective-permute-start(bf16[2,192,256]{2,1,0:T(8,128)(2,1)} %get-tuple-element.46), channel_id=1, source_target_pairs={{0,3},{1,0},{2,1},{3,2},{4,7},{5,4},{6,5},{7,6},{8,11},{9,8},{10,9... | collective-permute-start | bytes 589832 | tf_op jit(solution)/shard_map/ppermute | solution.py:433
  6.1 2.1 %collective-permute-start.5 = (bf16[2,192,256]{2,1,0:T(8,128)(2,1)}, bf16[2,192,256]{2,1,0:T(8,128)(2,1)S(1)}, u32[]{:S(2)}, u32[]{:S(2)}) collective-permute-start(bf16[2,192,256]{2,1,0:T(8,128)(2,1)} %get-tuple-element.47), channel_id=1, source_target_pairs={{0,2},{1,3},{2,0},{3,1},{4,6},{5,7},{6,4},{7,5},{8,10},{9,11},{10,... | collective-permute-start | bytes 589832 | tf_op jit(solution)/shard_map/ppermute | solution.py:433
  8.3 1.4 %collective-permute-start.1 = (f32[1,32]{1,0:T(1,128)S(1)}, f32[1,32]{1,0:T(1,128)S(1)}, u32[]{:S(2)}, u32[]{:S(2)}) collective-permute-start(f32[1,32]{1,0:T(1,128)S(1)} %copy-done.6), channel_id=1, source_target_pairs={{0,64},{32,96},{64,0},{96,32},{1,65},{33,97},{65,1},{97,33},{2,66}... | collective-permute-start | bytes 392 | tf_op jit(solution)/shard_map/ppermute | solution.py:444
  9.8 1.2 %collective-permute-start = (f32[1,32]{1,0:T(1,128)S(1)}, f32[1,32]{1,0:T(1,128)S(1)}, u32[]{:S(2)}, u32[]{:S(2)}) collective-permute-start(f32[1,32]{1,0:T(1,128)S(1)} %copy-done.6), channel_id=1, source_target_pairs={{0,32},{32,64},{64,96},{96,0},{1,33},{33,65},{65,97},{97,1},{2,34}... | collective-permute-start | bytes 392 | tf_op jit(solution)/shard_map/ppermute | solution.py:444
  11.8 2.0 %collective-permute-start.15 = (bf16[2,192,256]{2,1,0:T(8,128)(2,1)S(1)}, bf16[2,192,256]{2,1,0:T(8,128)(2,1)S(1)}, u32[]{:S(2)}, u32[]{:S(2)}) collective-permute-start(bf16[2,192,256]{2,1,0:T(8,128)(2,1)S(1)} %get-tuple-element.62), channel_id=1, source_target_pairs={{0,3},{1,0},{2,1},{3,2},{4,7},{5,4},{6,5},{7,6},{8,11},{9,8},{10,9... | collective-permute-start | bytes 589832 | tf_op jit(solution)/shard_map/ppermute | solution.py:433
  13.8 2.0 %collective-permute-start.16 = (bf16[2,192,256]{2,1,0:T(8,128)(2,1)S(1)}, bf16[2,192,256]{2,1,0:T(8,128)(2,1)S(1)}, u32[]{:S(2)}, u32[]{:S(2)}) collective-permute-start(bf16[2,192,256]{2,1,0:T(8,128)(2,1)S(1)} %get-tuple-element.63), channel_id=1, source_target_pairs={{0,2},{1,3},{2,0},{3,1},{4,6},{5,7},{6,4},{7,5},{8,10},{9,11},{10,... | collective-permute-start | bytes 589832 | tf_op jit(solution)/shard_map/ppermute | solution.py:433
  15.8 1.8 %collective-permute-done.5.three.key_three = bf16[2,192,256]{2,1,0:T(8,128)(2,1)S(1)} collective-permute-done((bf16[2,192,256]{2,1,0:T(8,128)(2,1)}, bf16[2,192,256]{2,1,0:T(8,128)(2,1)S(1)}, u32[]{:S(2)}, u32[]{:S(2)}) %collective-permute-start.5) | collective-permute-done | bytes 196640 | tf_op jit(solution)/shard_map/ppermute | solution.py:433
  17.6 3.1 %collective-permute-start.9 = (bf16[2,576,256]{2,1,0:T(8,128)(2,1)S(1)}, bf16[2,576,256]{2,1,0:T(8,128)(2,1)S(1)}, u32[]{:S(2)}, u32[]{:S(2)}) collective-permute-start(bf16[2,576,256]{2,1,0:T(8,128)(2,1)S(1)} %edge.2.after), channel_id=1, source_target_pairs={{0,4},{1,5},{2,6},{3,7},{4,8},{5,9},{6,10},{7,11},{8,12},{9,13},{1... | collective-permute-start | bytes 1769480 | tf_op jit(solution)/shard_map/ppermute | solution.py:437
  22.1 4.0 %collective-permute-start.7 = (bf16[2,192,256]{2,1,0:T(8,128)(2,1)S(1)}, bf16[2,192,256]{2,1,0:T(8,128)(2,1)S(1)}, u32[]{:S(2)}, u32[]{:S(2)}) collective-permute-start(bf16[2,192,256]{2,1,0:T(8,128)(2,1)S(1)} %get-tuple-element.54), channel_id=1, source_target_pairs={{0,3},{1,0},{2,1},{3,2},{4,7},{5,4},{6,5},{7,6},{8,11},{9,8},{10,9... | collective-permute-start | bytes 589832 | tf_op jit(solution)/shard_map/ppermute | solution.py:433
  26.1 1.7 %collective-permute-start.8 = (bf16[2,192,256]{2,1,0:T(8,128)(2,1)S(1)}, bf16[2,192,256]{2,1,0:T(8,128)(2,1)S(1)}, u32[]{:S(2)}, u32[]{:S(2)}) collective-permute-start(bf16[2,192,256]{2,1,0:T(8,128)(2,1)S(1)} %get-tuple-element.55), channel_id=1, source_target_pairs={{0,2},{1,3},{2,0},{3,1},{4,6},{5,7},{6,4},{7,5},{8,10},{9,11},{10,... | collective-permute-start | bytes 589832 | tf_op jit(solution)/shard_map/ppermute | solution.py:433
  27.8 2.6 %collective-permute-start.20 = (bf16[2,576,256]{2,1,0:T(8,128)(2,1)S(1)}, bf16[2,576,256]{2,1,0:T(8,128)(2,1)S(1)}, u32[]{:S(2)}, u32[]{:S(2)}) collective-permute-start(bf16[2,576,256]{2,1,0:T(8,128)(2,1)S(1)} %edge.3), channel_id=1, source_target_pairs={{0,4},{1,5},{2,6},{3,7},{4,8},{5,9},{6,10},{7,11},{8,12},{9,13},{1... | collective-permute-start | bytes 1769480 | tf_op jit(solution)/shard_map/ppermute | solution.py:437
  30.4 1.5 %collective-permute-done.7.query_two = bf16[2,192,256]{2,1,0:T(8,128)(2,1)S(1)} collective-permute-done((bf16[2,192,256]{2,1,0:T(8,128)(2,1)S(1)}, bf16[2,192,256]{2,1,0:T(8,128)(2,1)S(1)}, u32[]{:S(2)}, u32[]{:S(2)}) %collective-permute-start.7) | collective-permute-done | bytes 196640 | tf_op jit(solution)/shard_map/ppermute | solution.py:433
  31.8 1.3 %collective-permute-start.17 = (bf16[2,192,256]{2,1,0:T(8,128)(2,1)S(1)}, bf16[2,192,256]{2,1,0:T(8,128)(2,1)S(1)}, u32[]{:S(2)}, u32[]{:S(2)}) collective-permute-start(bf16[2,192,256]{2,1,0:T(8,128)(2,1)S(1)} %get-tuple-element.50.after), channel_id=1, source_target_pairs={{0,1},{1,2},{2,3},{3,0},{4,5},{5,6},{6,7},{7,4},{8,9},{9,10},{10,1... | collective-permute-start | bytes 589832 | tf_op jit(solution)/shard_map/ppermute | solution.py:433
  33.8 1.8 %collective-permute-start.18 = (bf16[2,192,256]{2,1,0:T(8,128)(2,1)S(1)}, bf16[2,192,256]{2,1,0:T(8,128)(2,1)S(1)}, u32[]{:S(2)}, u32[]{:S(2)}) collective-permute-start(bf16[2,192,256]{2,1,0:T(8,128)(2,1)S(1)} %get-tuple-element.64), channel_id=1, source_target_pairs={{0,3},{1,0},{2,1},{3,2},{4,7},{5,4},{6,5},{7,6},{8,11},{9,8},{10,9... | collective-permute-start | bytes 589832 | tf_op jit(solution)/shard_map/ppermute | solution.py:433
  35.7 1.9 %collective-permute-start.19 = (bf16[2,192,256]{2,1,0:T(8,128)(2,1)S(1)}, bf16[2,192,256]{2,1,0:T(8,128)(2,1)S(1)}, u32[]{:S(2)}, u32[]{:S(2)}) collective-permute-start(bf16[2,192,256]{2,1,0:T(8,128)(2,1)S(1)} %get-tuple-element.65), channel_id=1, source_target_pairs={{0,2},{1,3},{2,0},{3,1},{4,6},{5,7},{6,4},{7,5},{8,10},{9,11},{10,... | collective-permute-start | bytes 589832 | tf_op jit(solution)/shard_map/ppermute | solution.py:433
  37.6 0.8 collective-permute-done.9.edge_ref
  38.4 6.3 %attend.2 = (bf16[192,256]{1,0:T(8,128)(2,1)S(1)}, bf16[192,256]{1,0:T(8,128)(2,1)S(1)}, bf16[192,256]{1,0:T(8,128)(2,1)S(1)}, bf16[192,256]{1,0:T(8,128)(2,1)S(...) custom-call(f32[1,32]{1,0:T(1,128)S(1)} %copy-done.6, ...), custom_call_target="tpu_custom_call" | custom-call | flops 4499999744 | tf_op jit(solution)/shard_map/attend/pallas_call | solution.py:282
  44.8 6.0 %collective-permute-start.13 = (bf16[2,576,256]{2,1,0:T(8,128)(2,1)S(1)}, bf16[2,576,256]{2,1,0:T(8,128)(2,1)S(1)}, u32[]{:S(2)}, u32[]{:S(2)}) collective-permute-start(bf16[2,576,256]{2,1,0:T(8,128)(2,1)S(1)} %get-tuple-element.61), channel_id=1, source_target_pairs={{0,28},{1,29},{2,30},{3,31},{4,0},{5,1},{6,2},{7,3},{8,4},{9,5},{1... | collective-permute-start | bytes 1769480 | tf_op jit(solution)/shard_map/ppermute | solution.py:437
  51.6 2.5 %collective-permute-start.11 = (bf16[192,256]{1,0:T(8,128)(2,1)S(1)}, bf16[192,256]{1,0:T(8,128)(2,1)S(1)}, u32[]{:S(2)}, u32[]{:S(2)}) collective-permute-start(bf16[192,256]{1,0:T(8,128)(2,1)S(1)} %get-tuple-element.58), channel_id=1, source_target_pairs={{0,3},{1,0},{2,1},{3,2},{4,7},{5,4},{6,5},{7,6},{8,11},{9,8},{10,9... | collective-permute-start | bytes 294920 | tf_op jit(solution)/shard_map/ppermute | solution.py:433
  54.1 0.9 collective-permute-start.12
  54.9 6.3 %attend.3 = (bf16[192,256]{1,0:T(8,128)(2,1)S(1)}, bf16[192,256]{1,0:T(8,128)(2,1)S(1)}, bf16[192,256]{1,0:T(8,128)(2,1)S(1)}, bf16[192,256]{1,0:T(8,128)(2,1)S(...) custom-call(f32[1,32]{1,0:T(1,128)S(1)} %copy-done.6, ...), custom_call_target="tpu_custom_call" | custom-call | flops 4499999744 | tf_op jit(solution)/shard_map/attend/pallas_call | solution.py:282
  62.4 2.5 %collective-permute-start.22 = (bf16[3,192,256]{2,1,0:T(8,128)(2,1)S(1)}, bf16[3,192,256]{2,1,0:T(8,128)(2,1)S(1)}, u32[]{:S(2)}, u32[]{:S(2)}) collective-permute-start(bf16[3,192,256]{2,1,0:T(8,128)(2,1)S(1)} %get-tuple-element.72), channel_id=1, source_target_pairs={{0,3},{1,0},{2,1},{3,2},{4,7},{5,4},{6,5},{7,6},{8,11},{9,8},{10,9... | collective-permute-start | bytes 884744 | tf_op jit(solution)/shard_map/ppermute | solution.py:433
  65.0 1.6 %collective-permute-start.23 = (bf16[3,192,256]{2,1,0:T(8,128)(2,1)S(1)}, bf16[3,192,256]{2,1,0:T(8,128)(2,1)S(1)}, u32[]{:S(2)}, u32[]{:S(2)}) collective-permute-start(bf16[3,192,256]{2,1,0:T(8,128)(2,1)S(1)} %get-tuple-element.73), channel_id=1, source_target_pairs={{0,2},{1,3},{2,0},{3,1},{4,6},{5,7},{6,4},{7,5},{8,10},{9,11},{10,... | collective-permute-start | bytes 884744 | tf_op jit(solution)/shard_map/ppermute | solution.py:433
  66.5 6.9 %collective-permute-done.24.far_ref = bf16[2,576,256]{2,1,0:T(8,128)(2,1)S(1)} collective-permute-done((bf16[2,576,256]{2,1,0:T(8,128)(2,1)S(1)}, bf16[2,576,256]{2,1,0:T(8,128)(2,1)S(1)}, u32[]{:S(2)}, u32[]{:S(2)}) %collective-permute-start.24) | collective-permute-done | bytes 589856 | tf_op jit(solution)/shard_map/ppermute | solution.py:437
  73.6 0.9 %collective-permute-start.25 = (bf16[2,192,256]{2,1,0:T(8,128)(2,1)S(1)}, bf16[2,192,256]{2,1,0:T(8,128)(2,1)S(1)}, u32[]{:S(2)}, u32[]{:S(2)}) collective-permute-start(bf16[2,192,256]{2,1,0:T(8,128)(2,1)S(1)} %get-tuple-element.78), channel_id=1, source_target_pairs={{0,1},{1,2},{2,3},{3,0},{4,5},{5,6},{6,7},{7,4},{8,9},{9,10},{10,1... | collective-permute-start | bytes 589832 | tf_op jit(solution)/shard_map/ppermute | solution.py:433
  74.5 2.4 %collective-permute-start.26 = (bf16[2,192,256]{2,1,0:T(8,128)(2,1)S(1)}, bf16[2,192,256]{2,1,0:T(8,128)(2,1)S(1)}, u32[]{:S(2)}, u32[]{:S(2)}) collective-permute-start(bf16[2,192,256]{2,1,0:T(8,128)(2,1)S(1)} %get-tuple-element.79), channel_id=1, source_target_pairs={{0,3},{1,0},{2,1},{3,2},{4,7},{5,4},{6,5},{7,6},{8,11},{9,8},{10,9... | collective-permute-start | bytes 589832 | tf_op jit(solution)/shard_map/ppermute | solution.py:433
  76.9 1.6 %collective-permute-done.21.refs_5_ = bf16[3,192,256]{2,1,0:T(8,128)(2,1)S(1)} collective-permute-done((bf16[3,192,256]{2,1,0:T(8,128)(2,1)S(1)}, bf16[3,192,256]{2,1,0:T(8,128)(2,1)S(1)}, u32[]{:S(2)}, u32[]{:S(2)}) %collective-permute-start.21) | collective-permute-done | bytes 294944 | tf_op jit(solution)/shard_map/ppermute | solution.py:433
  78.5 1.3 %early.1 = (bf16[192,2048]{1,0:T(8,128)(2,1)}, bf16[192,2048]{1,0:T(8,128)(2,1)}, bf16[192,2048]{1,0:T(8,128)(2,1)}) custom-call(bf16[192,256]{1,0:T(8,128)(2,1)S(1)} %get-tuple-element.56.refs_0_, bf16[192,256]{1,0:T(8,128)(2,1)S(1)} %collective-permute-done.10.refs_4_.refs_1_, bf16[192,256]{1,0:T(8,128)(2,1)S(1)} %collective-permute-done.11.refs_5_.refs_2_, ...), custom_call_target="tpu_custom_call" | custom-call | bytes 2359296 | tf_op jit(solution)/shard_map/early/pallas_call | solution.py:395
  79.8 6.4 %collective-permute-done.25.refs_1_ = bf16[2,192,256]{2,1,0:T(8,128)(2,1)S(1)} collective-permute-done((bf16[2,192,256]{2,1,0:T(8,128)(2,1)S(1)}, bf16[2,192,256]{2,1,0:T(8,128)(2,1)S(1)}, u32[]{:S(2)}, u32[]{:S(2)}) %collective-permute-start.25) | collective-permute-done | bytes 196640 | tf_op jit(solution)/shard_map/ppermute | solution.py:433
  86.2 0.9 %late.1 = (bf16[192,2048]{1,0:T(8,128)(2,1)}, bf16[192,2048]{1,0:T(8,128)(2,1)}) custom-call(bf16[2,192,256]{2,1,0:T(8,128)(2,1)S(1)} %get-tuple-element.77.refs_0_, bf16[2,192,256]{2,1,0:T(8,128)(2,1)S(1)} %collective-permute-done.25.refs_1_, ...), custom_call_target="tpu_custom_call", output_to_operand_aliasing={{0}: (4, {}), {1}: (5, {})} | custom-call | bytes 2359296 | tf_op jit(solution)/shard_map/late/pallas_call | solution.py:405
  (51 shorter events, 5.2 us)
Async XLA Ops:
  0.6 9.1 %copy-start = (bf16[1,192,2048]{2,1,0:T(8,128)(2,1)S(1)}, bf16[1,192,2048]{2,1,0:T(8,128)(2,1)}, u32[]{:S(2)}) copy-start(bf16[1,192,2048]{2,1,0:T(8,128)(2,1)} %param.7) | copy-start | bytes 2359300
  0.6 9.0 %copy-start.1 = (bf16[1,192,2048]{2,1,0:T(8,128)(2,1)S(1)}, bf16[1,192,2048]{2,1,0:T(8,128)(2,1)}, u32[]{:S(2)}) copy-start(bf16[1,192,2048]{2,1,0:T(8,128)(2,1)} %param.8) | copy-start | bytes 2359300
  2.8 13.0 %collective-permute-start.3 = (bf16[2,192,256]{2,1,0:T(8,128)(2,1)}, bf16[2,192,256]{2,1,0:T(8,128)(2,1)S(1)}, u32[]{:S(2)}, u32[]{:S(2)}) collective-permute-start(bf16[2,192,256]{2,1,0:T(8,128)(2,1)} %get-tuple-element.45), channel_id=1, source_target_pairs={{0,1},{1,2},{2,3},{3,0},{4,5},{5,6},{6,7},{7,4},{8,9},{9,10},{10,1... | collective-permute-start | bytes 589832 | tf_op jit(solution)/shard_map/ppermute | solution.py:433
  4.5 11.3 %collective-permute-start.4 = (bf16[2,192,256]{2,1,0:T(8,128)(2,1)}, bf16[2,192,256]{2,1,0:T(8,128)(2,1)S(1)}, u32[]{:S(2)}, u32[]{:S(2)}) collective-permute-start(bf16[2,192,256]{2,1,0:T(8,128)(2,1)} %get-tuple-element.46), channel_id=1, source_target_pairs={{0,3},{1,0},{2,1},{3,2},{4,7},{5,4},{6,5},{7,6},{8,11},{9,8},{10,9... | collective-permute-start | bytes 589832 | tf_op jit(solution)/shard_map/ppermute | solution.py:433
  6.1 11.4 %collective-permute-start.5 = (bf16[2,192,256]{2,1,0:T(8,128)(2,1)}, bf16[2,192,256]{2,1,0:T(8,128)(2,1)S(1)}, u32[]{:S(2)}, u32[]{:S(2)}) collective-permute-start(bf16[2,192,256]{2,1,0:T(8,128)(2,1)} %get-tuple-element.47), channel_id=1, source_target_pairs={{0,2},{1,3},{2,0},{3,1},{4,6},{5,7},{6,4},{7,5},{8,10},{9,11},{10,... | collective-permute-start | bytes 589832 | tf_op jit(solution)/shard_map/ppermute | solution.py:433
  8.2 1.6 %collective-permute-start.2 = (f32[1,32]{1,0:T(1,128)S(1)}, f32[1,32]{1,0:T(1,128)S(1)}, u32[]{:S(2)}, u32[]{:S(2)}) collective-permute-start(f32[1,32]{1,0:T(1,128)S(1)} %copy-done.6), channel_id=1, source_target_pairs={{0,96},{32,0},{64,32},{96,64},{1,97},{33,1},{65,33},{97,65},{2,98}... | collective-permute-start | bytes 392 | tf_op jit(solution)/shard_map/ppermute | solution.py:444
  8.3 3.5 %collective-permute-start.1 = (f32[1,32]{1,0:T(1,128)S(1)}, f32[1,32]{1,0:T(1,128)S(1)}, u32[]{:S(2)}, u32[]{:S(2)}) collective-permute-start(f32[1,32]{1,0:T(1,128)S(1)} %copy-done.6), channel_id=1, source_target_pairs={{0,64},{32,96},{64,0},{96,32},{1,65},{33,97},{65,1},{97,33},{2,66}... | collective-permute-start | bytes 392 | tf_op jit(solution)/shard_map/ppermute | solution.py:444
  9.8 4.0 %collective-permute-start = (f32[1,32]{1,0:T(1,128)S(1)}, f32[1,32]{1,0:T(1,128)S(1)}, u32[]{:S(2)}, u32[]{:S(2)}) collective-permute-start(f32[1,32]{1,0:T(1,128)S(1)} %copy-done.6), channel_id=1, source_target_pairs={{0,32},{32,64},{64,96},{96,0},{1,33},{33,65},{65,97},{97,1},{2,34}... | collective-permute-start | bytes 392 | tf_op jit(solution)/shard_map/ppermute | solution.py:444
  11.8 10.2 %collective-permute-start.15 = (bf16[2,192,256]{2,1,0:T(8,128)(2,1)S(1)}, bf16[2,192,256]{2,1,0:T(8,128)(2,1)S(1)}, u32[]{:S(2)}, u32[]{:S(2)}) collective-permute-start(bf16[2,192,256]{2,1,0:T(8,128)(2,1)S(1)} %get-tuple-element.62), channel_id=1, source_target_pairs={{0,3},{1,0},{2,1},{3,2},{4,7},{5,4},{6,5},{7,6},{8,11},{9,8},{10,9... | collective-permute-start | bytes 589832 | tf_op jit(solution)/shard_map/ppermute | solution.py:433
  13.8 12.3 %collective-permute-start.16 = (bf16[2,192,256]{2,1,0:T(8,128)(2,1)S(1)}, bf16[2,192,256]{2,1,0:T(8,128)(2,1)S(1)}, u32[]{:S(2)}, u32[]{:S(2)}) collective-permute-start(bf16[2,192,256]{2,1,0:T(8,128)(2,1)S(1)} %get-tuple-element.63), channel_id=1, source_target_pairs={{0,2},{1,3},{2,0},{3,1},{4,6},{5,7},{6,4},{7,5},{8,10},{9,11},{10,... | collective-permute-start | bytes 589832 | tf_op jit(solution)/shard_map/ppermute | solution.py:433
  15.8 4.9 %copy-start.2 = (bf16[1,192,2048]{2,1,0:T(8,128)(2,1)S(1)}, bf16[1,192,2048]{2,1,0:T(8,128)(2,1)}, u32[]{:S(2)}) copy-start(bf16[1,192,2048]{2,1,0:T(8,128)(2,1)} %param.6) | copy-start | bytes 2359300
  15.8 4.9 %copy-start.3 = (bf16[1,192,2048]{2,1,0:T(8,128)(2,1)S(1)}, bf16[1,192,2048]{2,1,0:T(8,128)(2,1)}, u32[]{:S(2)}) copy-start(bf16[1,192,2048]{2,1,0:T(8,128)(2,1)} %param.9) | copy-start | bytes 2359300
  15.8 12.0 %collective-permute-start.14 = (bf16[2,192,256]{2,1,0:T(8,128)(2,1)S(1)}, bf16[2,192,256]{2,1,0:T(8,128)(2,1)S(1)}, u32[]{:S(2)}, u32[]{:S(2)}) collective-permute-start(bf16[2,192,256]{2,1,0:T(8,128)(2,1)S(1)} %get-tuple-element.48.refs_3_), channel_id=1, source_target_pairs={{0,1},{1,2},{2,3},{3,0},{4,5},{5,6},{6,7},{7,4},{8,9},{9,10},{10,1... | collective-permute-start | bytes 589832 | tf_op jit(solution)/shard_map/ppermute | solution.py:433
  17.6 20.8 %collective-permute-start.9 = (bf16[2,576,256]{2,1,0:T(8,128)(2,1)S(1)}, bf16[2,576,256]{2,1,0:T(8,128)(2,1)S(1)}, u32[]{:S(2)}, u32[]{:S(2)}) collective-permute-start(bf16[2,576,256]{2,1,0:T(8,128)(2,1)S(1)} %edge.2.after), channel_id=1, source_target_pairs={{0,4},{1,5},{2,6},{3,7},{4,8},{5,9},{6,10},{7,11},{8,12},{9,13},{1... | collective-permute-start | bytes 1769480 | tf_op jit(solution)/shard_map/ppermute | solution.py:437
  20.8 14.9 %collective-permute-start.6 = (bf16[2,192,256]{2,1,0:T(8,128)(2,1)S(1)}, bf16[2,192,256]{2,1,0:T(8,128)(2,1)S(1)}, u32[]{:S(2)}, u32[]{:S(2)}) collective-permute-start(bf16[2,192,256]{2,1,0:T(8,128)(2,1)S(1)} %get-tuple-element.49.after), channel_id=1, source_target_pairs={{0,1},{1,2},{2,3},{3,0},{4,5},{5,6},{6,7},{7,4},{8,9},{9,10},{10,1... | collective-permute-start | bytes 589832 | tf_op jit(solution)/shard_map/ppermute | solution.py:433
  22.1 9.8 %collective-permute-start.7 = (bf16[2,192,256]{2,1,0:T(8,128)(2,1)S(1)}, bf16[2,192,256]{2,1,0:T(8,128)(2,1)S(1)}, u32[]{:S(2)}, u32[]{:S(2)}) collective-permute-start(bf16[2,192,256]{2,1,0:T(8,128)(2,1)S(1)} %get-tuple-element.54), channel_id=1, source_target_pairs={{0,3},{1,0},{2,1},{3,2},{4,7},{5,4},{6,5},{7,6},{8,11},{9,8},{10,9... | collective-permute-start | bytes 589832 | tf_op jit(solution)/shard_map/ppermute | solution.py:433
  26.1 7.8 %collective-permute-start.8 = (bf16[2,192,256]{2,1,0:T(8,128)(2,1)S(1)}, bf16[2,192,256]{2,1,0:T(8,128)(2,1)S(1)}, u32[]{:S(2)}, u32[]{:S(2)}) collective-permute-start(bf16[2,192,256]{2,1,0:T(8,128)(2,1)S(1)} %get-tuple-element.55), channel_id=1, source_target_pairs={{0,2},{1,3},{2,0},{3,1},{4,6},{5,7},{6,4},{7,5},{8,10},{9,11},{10,... | collective-permute-start | bytes 589832 | tf_op jit(solution)/shard_map/ppermute | solution.py:433
  27.8 27.1 %collective-permute-start.20 = (bf16[2,576,256]{2,1,0:T(8,128)(2,1)S(1)}, bf16[2,576,256]{2,1,0:T(8,128)(2,1)S(1)}, u32[]{:S(2)}, u32[]{:S(2)}) collective-permute-start(bf16[2,576,256]{2,1,0:T(8,128)(2,1)S(1)} %edge.3), channel_id=1, source_target_pairs={{0,4},{1,5},{2,6},{3,7},{4,8},{5,9},{6,10},{7,11},{8,12},{9,13},{1... | collective-permute-start | bytes 1769480 | tf_op jit(solution)/shard_map/ppermute | solution.py:437
  31.8 22.2 %collective-permute-start.17 = (bf16[2,192,256]{2,1,0:T(8,128)(2,1)S(1)}, bf16[2,192,256]{2,1,0:T(8,128)(2,1)S(1)}, u32[]{:S(2)}, u32[]{:S(2)}) collective-permute-start(bf16[2,192,256]{2,1,0:T(8,128)(2,1)S(1)} %get-tuple-element.50.after), channel_id=1, source_target_pairs={{0,1},{1,2},{2,3},{3,0},{4,5},{5,6},{6,7},{7,4},{8,9},{9,10},{10,1... | collective-permute-start | bytes 589832 | tf_op jit(solution)/shard_map/ppermute | solution.py:433
  33.8 17.0 %collective-permute-start.18 = (bf16[2,192,256]{2,1,0:T(8,128)(2,1)S(1)}, bf16[2,192,256]{2,1,0:T(8,128)(2,1)S(1)}, u32[]{:S(2)}, u32[]{:S(2)}) collective-permute-start(bf16[2,192,256]{2,1,0:T(8,128)(2,1)S(1)} %get-tuple-element.64), channel_id=1, source_target_pairs={{0,3},{1,0},{2,1},{3,2},{4,7},{5,4},{6,5},{7,6},{8,11},{9,8},{10,9... | collective-permute-start | bytes 589832 | tf_op jit(solution)/shard_map/ppermute | solution.py:433
  35.7 15.9 %collective-permute-start.19 = (bf16[2,192,256]{2,1,0:T(8,128)(2,1)S(1)}, bf16[2,192,256]{2,1,0:T(8,128)(2,1)S(1)}, u32[]{:S(2)}, u32[]{:S(2)}) collective-permute-start(bf16[2,192,256]{2,1,0:T(8,128)(2,1)S(1)} %get-tuple-element.65), channel_id=1, source_target_pairs={{0,2},{1,3},{2,0},{3,1},{4,6},{5,7},{6,4},{7,5},{8,10},{9,11},{10,... | collective-permute-start | bytes 589832 | tf_op jit(solution)/shard_map/ppermute | solution.py:433
  44.8 16.7 %collective-permute-start.13 = (bf16[2,576,256]{2,1,0:T(8,128)(2,1)S(1)}, bf16[2,576,256]{2,1,0:T(8,128)(2,1)S(1)}, u32[]{:S(2)}, u32[]{:S(2)}) collective-permute-start(bf16[2,576,256]{2,1,0:T(8,128)(2,1)S(1)} %get-tuple-element.61), channel_id=1, source_target_pairs={{0,28},{1,29},{2,30},{3,31},{4,0},{5,1},{6,2},{7,3},{8,4},{9,5},{1... | collective-permute-start | bytes 1769480 | tf_op jit(solution)/shard_map/ppermute | solution.py:437
  50.8 10.6 %collective-permute-start.10 = (bf16[192,256]{1,0:T(8,128)(2,1)S(1)}, bf16[192,256]{1,0:T(8,128)(2,1)S(1)}, u32[]{:S(2)}, u32[]{:S(2)}) collective-permute-start(bf16[192,256]{1,0:T(8,128)(2,1)S(1)} %get-tuple-element.57), channel_id=1, source_target_pairs={{0,1},{1,2},{2,3},{3,0},{4,5},{5,6},{6,7},{7,4},{8,9},{9,10},{10,1... | collective-permute-start | bytes 294920 | tf_op jit(solution)/shard_map/ppermute | solution.py:433
  51.6 9.9 %collective-permute-start.11 = (bf16[192,256]{1,0:T(8,128)(2,1)S(1)}, bf16[192,256]{1,0:T(8,128)(2,1)S(1)}, u32[]{:S(2)}, u32[]{:S(2)}) collective-permute-start(bf16[192,256]{1,0:T(8,128)(2,1)S(1)} %get-tuple-element.58), channel_id=1, source_target_pairs={{0,3},{1,0},{2,1},{3,2},{4,7},{5,4},{6,5},{7,6},{8,11},{9,8},{10,9... | collective-permute-start | bytes 294920 | tf_op jit(solution)/shard_map/ppermute | solution.py:433
  54.1 7.4 %collective-permute-start.12 = (bf16[192,256]{1,0:T(8,128)(2,1)S(1)}, bf16[192,256]{1,0:T(8,128)(2,1)S(1)}, u32[]{:S(2)}, u32[]{:S(2)}) collective-permute-start(bf16[192,256]{1,0:T(8,128)(2,1)S(1)} %get-tuple-element.59), channel_id=1, source_target_pairs={{0,2},{1,3},{2,0},{3,1},{4,6},{5,7},{6,4},{7,5},{8,10},{9,11},{10,... | collective-permute-start | bytes 294920 | tf_op jit(solution)/shard_map/ppermute | solution.py:433
  61.3 12.1 %collective-permute-start.24 = (bf16[2,576,256]{2,1,0:T(8,128)(2,1)S(1)}, bf16[2,576,256]{2,1,0:T(8,128)(2,1)S(1)}, u32[]{:S(2)}, u32[]{:S(2)}) collective-permute-start(bf16[2,576,256]{2,1,0:T(8,128)(2,1)S(1)} %get-tuple-element.76), channel_id=1, source_target_pairs={{0,28},{1,29},{2,30},{3,31},{4,0},{5,1},{6,2},{7,3},{8,4},{9,5},{1... | collective-permute-start | bytes 1769480 | tf_op jit(solution)/shard_map/ppermute | solution.py:437
  61.7 16.8 %collective-permute-start.21 = (bf16[3,192,256]{2,1,0:T(8,128)(2,1)S(1)}, bf16[3,192,256]{2,1,0:T(8,128)(2,1)S(1)}, u32[]{:S(2)}, u32[]{:S(2)}) collective-permute-start(bf16[3,192,256]{2,1,0:T(8,128)(2,1)S(1)} %get-tuple-element.71), channel_id=1, source_target_pairs={{0,1},{1,2},{2,3},{3,0},{4,5},{5,6},{6,7},{7,4},{8,9},{9,10},{10,1... | collective-permute-start | bytes 884744 | tf_op jit(solution)/shard_map/ppermute | solution.py:433
  62.4 16.1 %collective-permute-start.22 = (bf16[3,192,256]{2,1,0:T(8,128)(2,1)S(1)}, bf16[3,192,256]{2,1,0:T(8,128)(2,1)S(1)}, u32[]{:S(2)}, u32[]{:S(2)}) collective-permute-start(bf16[3,192,256]{2,1,0:T(8,128)(2,1)S(1)} %get-tuple-element.72), channel_id=1, source_target_pairs={{0,3},{1,0},{2,1},{3,2},{4,7},{5,4},{6,5},{7,6},{8,11},{9,8},{10,9... | collective-permute-start | bytes 884744 | tf_op jit(solution)/shard_map/ppermute | solution.py:433
  65.0 13.5 %collective-permute-start.23 = (bf16[3,192,256]{2,1,0:T(8,128)(2,1)S(1)}, bf16[3,192,256]{2,1,0:T(8,128)(2,1)S(1)}, u32[]{:S(2)}, u32[]{:S(2)}) collective-permute-start(bf16[3,192,256]{2,1,0:T(8,128)(2,1)S(1)} %get-tuple-element.73), channel_id=1, source_target_pairs={{0,2},{1,3},{2,0},{3,1},{4,6},{5,7},{6,4},{7,5},{8,10},{9,11},{10,... | collective-permute-start | bytes 884744 | tf_op jit(solution)/shard_map/ppermute | solution.py:433
  73.6 12.6 %collective-permute-start.25 = (bf16[2,192,256]{2,1,0:T(8,128)(2,1)S(1)}, bf16[2,192,256]{2,1,0:T(8,128)(2,1)S(1)}, u32[]{:S(2)}, u32[]{:S(2)}) collective-permute-start(bf16[2,192,256]{2,1,0:T(8,128)(2,1)S(1)} %get-tuple-element.78), channel_id=1, source_target_pairs={{0,1},{1,2},{2,3},{3,0},{4,5},{5,6},{6,7},{7,4},{8,9},{9,10},{10,1... | collective-permute-start | bytes 589832 | tf_op jit(solution)/shard_map/ppermute | solution.py:433
  74.5 11.6 %collective-permute-start.26 = (bf16[2,192,256]{2,1,0:T(8,128)(2,1)S(1)}, bf16[2,192,256]{2,1,0:T(8,128)(2,1)S(1)}, u32[]{:S(2)}, u32[]{:S(2)}) collective-permute-start(bf16[2,192,256]{2,1,0:T(8,128)(2,1)S(1)} %get-tuple-element.79), channel_id=1, source_target_pairs={{0,3},{1,0},{2,1},{3,2},{4,7},{5,4},{6,5},{7,6},{8,11},{9,8},{10,9... | collective-permute-start | bytes 589832 | tf_op jit(solution)/shard_map/ppermute | solution.py:433
  78.5 7.7 %collective-permute-start.27 = (bf16[2,192,256]{2,1,0:T(8,128)(2,1)S(1)}, bf16[2,192,256]{2,1,0:T(8,128)(2,1)S(1)}, u32[]{:S(2)}, u32[]{:S(2)}) collective-permute-start(bf16[2,192,256]{2,1,0:T(8,128)(2,1)S(1)} %get-tuple-element.80), channel_id=1, source_target_pairs={{0,2},{1,3},{2,0},{3,1},{4,6},{5,7},{6,4},{7,5},{8,10},{9,11},{10,... | collective-permute-start | bytes 589832 | tf_op jit(solution)/shard_map/ppermute | solution.py:433
  (3 other events, 3.4 us)

commit v5 on v4

--- a/solution.py
+++ b/solution.py
@@ -23,7 +23,7 @@
 
 def aways():
     core = lax.rem(lax.axis_index("dp"), 2)
-    return 0, 1 + 2 * core, 3 - 2 * core, 2
+    return 0, 1 + core, 3 - 2 * core, 2 + core
 
 
 def columns(place, away, chunk, width):
@@ -426,7 +426,7 @@
         pairs = []
         for sample in range(samples):
             core = sample % 2
-            away = (1 + 2 * core, 3 - 2 * core, 2)[slot]
+            away = (1 + core, 3 - 2 * core, 2 + core)[slot]
             for source in range(cycle_size):
                 target = source - source % GROUP + (source + away) % GROUP
                 pairs.append((sample * cycle_size + source, sample * cycle_size + target))

time: 87.4 us -> 90.6 us (1.037)
  starting transfers between devices: 47.1 us -> 49.2 us
  waiting for transfers between devices: 20.4 us -> 21.5 us
    ppermute x21, starting transfers between devices: 32.5 us -> 34 us  [swap(): return lax.ppermute(value, ('dp', 'ctx'), pairs)]
    ppermute x4, waiting for transfers between devices: 7.69 us -> 6.43 us  [next_row(): return lax.ppermute(value, 'ctx', pairs)]
    ppermute x3, waiting for transfers between devices: 0.81 us -> 2.05 us  [shards(): lax.ppermute(text, 'dp', [(source, (source + away) % samples) for source...]
    ppermute x21, waiting for transfers between devices: 11.9 us -> 13 us  [swap(): return lax.ppermute(value, ('dp', 'ctx'), pairs)]
  transfers between devices with their start and end apart: 28 -> 28, of which waited for: 8 -> 10; matrix products, arithmetic and copies ran while one was open for 0% -> 0% of each run, Pallas kernels for 17% -> 17%
where the time goes in v5:
time: 90.6 us; the launch traced here: 90.4 us
  starting transfers between devices  49.2 us (54%)
  waiting for transfers between devices  21.5 us (24%)
  Pallas kernels  18.1 us (20%)
  between operations  0.99 us (1%)
    ppermute x21, starting transfers between devices, swap(): return lax.ppermute(value, ('dp', 'ctx'), pairs)  34 us
    ppermute x21, waiting for transfers between devices, swap(): return lax.ppermute(value, ('dp', 'ctx'), pairs)  13 us
    pallas_call x2, Pallas kernels, attend(): pl.pallas_call(functools.partial(attend_kernel, chunk, total_rows), out_s...  12.6 us
    ppermute x4, starting transfers between devices, next_row(): return lax.ppermute(value, 'ctx', pairs)  12.4 us
    ppermute x4, waiting for transfers between devices, next_row(): return lax.ppermute(value, 'ctx', pairs)  6.43 us
    ppermute x3, starting transfers between devices, shards(): lax.ppermute(text, 'dp', [(source, (source + away) % samples) for source...  2.7 us
    pallas_call x1, Pallas kernels, first_pack(): pl.pallas_call(first_pack_kernel, out_shape=(message,) * (GROUP - 1) + (j...  2.15 us
    ppermute x3, waiting for transfers between devices, shards(): lax.ppermute(text, 'dp', [(source, (source + away) % samples) for source...  2.05 us
  transfers between devices with their start and end apart: 28, of which 10 were waited for; matrix products, arithmetic and copies ran while one was open for 0% of the time, Pallas kernels for 17%

profile of v5, /device:TPU:0, one launch (start us, length us, event | category | flops | bytes accessed | tf_op | source)
XLA Modules:
  0.0 90.4 jit_solution(5464267692725395968)
XLA Ops:
  0.7 2.2 %first_pack.1 = (bf16[2,192,256]{2,1,0:T(8,128)(2,1)}, bf16[2,192,256]{2,1,0:T(8,128)(2,1)}, bf16[2,192,256]{2,1,0:T(8,128)(2,1)}, f32[1,32]{1,0:T(1,128)}) custom-call(bf16[192,2048]{1,0:T(8,128)(2,1)} %bitcast.7, bf16[192,2048]{1,0:T(8,128)(2,1)} %bitcast.13, s32[1,32]{1,0:T(1,128)} %lengths_ref.1, s32[1,32]{1,0:T(1,128)} %flags_ref.1), custom_call_target="tpu_custom_call" | custom-call | bytes 1179648 | tf_op jit(solution)/shard_map/first_pack/pallas_call | solution.py:80
  2.8 1.7 %collective-permute-start.3 = (bf16[2,192,256]{2,1,0:T(8,128)(2,1)}, bf16[2,192,256]{2,1,0:T(8,128)(2,1)S(1)}, u32[]{:S(2)}, u32[]{:S(2)}) collective-permute-start(bf16[2,192,256]{2,1,0:T(8,128)(2,1)} %get-tuple-element.45), channel_id=1, source_target_pairs={{0,1},{1,2},{2,3},{3,0},{4,5},{5,6},{6,7},{7,4},{8,9},{9,10},{10,1... | collective-permute-start | bytes 589832 | tf_op jit(solution)/shard_map/ppermute | solution.py:433
  4.5 1.6 %collective-permute-start.4 = (bf16[2,192,256]{2,1,0:T(8,128)(2,1)}, bf16[2,192,256]{2,1,0:T(8,128)(2,1)S(1)}, u32[]{:S(2)}, u32[]{:S(2)}) collective-permute-start(bf16[2,192,256]{2,1,0:T(8,128)(2,1)} %get-tuple-element.46), channel_id=1, source_target_pairs={{0,3},{1,0},{2,1},{3,2},{4,7},{5,4},{6,5},{7,6},{8,11},{9,8},{10,9... | collective-permute-start | bytes 589832 | tf_op jit(solution)/shard_map/ppermute | solution.py:433
  6.1 2.1 %collective-permute-start.5 = (bf16[2,192,256]{2,1,0:T(8,128)(2,1)}, bf16[2,192,256]{2,1,0:T(8,128)(2,1)S(1)}, u32[]{:S(2)}, u32[]{:S(2)}) collective-permute-start(bf16[2,192,256]{2,1,0:T(8,128)(2,1)} %get-tuple-element.47), channel_id=1, source_target_pairs={{0,2},{1,3},{2,0},{3,1},{4,6},{5,7},{6,4},{7,5},{8,10},{9,11},{10,... | collective-permute-start | bytes 589832 | tf_op jit(solution)/shard_map/ppermute | solution.py:433
  8.2 1.3 %collective-permute-start.2 = (f32[1,32]{1,0:T(1,128)S(1)}, f32[1,32]{1,0:T(1,128)S(1)}, u32[]{:S(2)}, u32[]{:S(2)}) collective-permute-start(f32[1,32]{1,0:T(1,128)S(1)} %copy-done.6), channel_id=1, source_target_pairs={{0,96},{32,0},{64,32},{96,64},{1,97},{33,1},{65,33},{97,65},{2,98}... | collective-permute-start | bytes 392 | tf_op jit(solution)/shard_map/ppermute | solution.py:444
  10.1 0.7 collective-permute-done.2.refs_2_.text_four
  10.8 0.9 collective-permute-start
  11.7 1.4 %collective-permute-done.1.refs_1_.text_three = f32[1,32]{1,0:T(1,128)S(1)} collective-permute-done((f32[1,32]{1,0:T(1,128)S(1)}, f32[1,32]{1,0:T(1,128)S(1)}, u32[]{:S(2)}, u32[]{:S(2)}) %collective-permute-start.1) | collective-permute-done | bytes 160 | tf_op jit(solution)/shard_map/ppermute | solution.py:444
  13.0 0.9 %collective-permute-start.15 = (bf16[2,192,256]{2,1,0:T(8,128)(2,1)S(1)}, bf16[2,192,256]{2,1,0:T(8,128)(2,1)S(1)}, u32[]{:S(2)}, u32[]{:S(2)}) collective-permute-start(bf16[2,192,256]{2,1,0:T(8,128)(2,1)S(1)} %get-tuple-element.62), channel_id=1, source_target_pairs={{0,3},{1,0},{2,1},{3,2},{4,7},{5,4},{6,5},{7,6},{8,11},{9,8},{10,9... | collective-permute-start | bytes 589832 | tf_op jit(solution)/shard_map/ppermute | solution.py:433
  14.6 1.2 %collective-permute-start.14 = (bf16[2,192,256]{2,1,0:T(8,128)(2,1)S(1)}, bf16[2,192,256]{2,1,0:T(8,128)(2,1)S(1)}, u32[]{:S(2)}, u32[]{:S(2)}) collective-permute-start(bf16[2,192,256]{2,1,0:T(8,128)(2,1)S(1)} %get-tuple-element.48.refs_3_), channel_id=1, source_target_pairs={{0,1},{1,2},{2,3},{3,0},{4,5},{5,6},{6,7},{7,4},{8,9},{9,10},{10,1... | collective-permute-start | bytes 589832 | tf_op jit(solution)/shard_map/ppermute | solution.py:433
  16.2 3.3 %collective-permute-start.9 = (bf16[2,576,256]{2,1,0:T(8,128)(2,1)S(1)}, bf16[2,576,256]{2,1,0:T(8,128)(2,1)S(1)}, u32[]{:S(2)}, u32[]{:S(2)}) collective-permute-start(bf16[2,576,256]{2,1,0:T(8,128)(2,1)S(1)} %edge.2.after), channel_id=1, source_target_pairs={{0,4},{1,5},{2,6},{3,7},{4,8},{5,9},{6,10},{7,11},{8,12},{9,13},{1... | collective-permute-start | bytes 1769480 | tf_op jit(solution)/shard_map/ppermute | solution.py:437
  19.6 2.0 %collective-permute-start.6 = (bf16[2,192,256]{2,1,0:T(8,128)(2,1)S(1)}, bf16[2,192,256]{2,1,0:T(8,128)(2,1)S(1)}, u32[]{:S(2)}, u32[]{:S(2)}) collective-permute-start(bf16[2,192,256]{2,1,0:T(8,128)(2,1)S(1)} %get-tuple-element.49.after), channel_id=1, source_target_pairs={{0,1},{1,2},{2,3},{3,0},{4,5},{5,6},{6,7},{7,4},{8,9},{9,10},{10,1... | collective-permute-start | bytes 589832 | tf_op jit(solution)/shard_map/ppermute | solution.py:433
  21.7 0.6 copy-done.4
  22.7 6.6 %collective-permute-start.7 = (bf16[2,192,256]{2,1,0:T(8,128)(2,1)S(1)}, bf16[2,192,256]{2,1,0:T(8,128)(2,1)S(1)}, u32[]{:S(2)}, u32[]{:S(2)}) collective-permute-start(bf16[2,192,256]{2,1,0:T(8,128)(2,1)S(1)} %get-tuple-element.54), channel_id=1, source_target_pairs={{0,3},{1,0},{2,1},{3,2},{4,7},{5,4},{6,5},{7,6},{8,11},{9,8},{10,9... | collective-permute-start | bytes 589832 | tf_op jit(solution)/shard_map/ppermute | solution.py:433
  29.4 1.9 %collective-permute-start.20 = (bf16[2,576,256]{2,1,0:T(8,128)(2,1)S(1)}, bf16[2,576,256]{2,1,0:T(8,128)(2,1)S(1)}, u32[]{:S(2)}, u32[]{:S(2)}) collective-permute-start(bf16[2,576,256]{2,1,0:T(8,128)(2,1)S(1)} %edge.3), channel_id=1, source_target_pairs={{0,4},{1,5},{2,6},{3,7},{4,8},{5,9},{6,10},{7,11},{8,12},{9,13},{1... | collective-permute-start | bytes 1769480 | tf_op jit(solution)/shard_map/ppermute | solution.py:437
  31.4 6.5 %collective-permute-done.7.query_two = bf16[2,192,256]{2,1,0:T(8,128)(2,1)S(1)} collective-permute-done((bf16[2,192,256]{2,1,0:T(8,128)(2,1)S(1)}, bf16[2,192,256]{2,1,0:T(8,128)(2,1)S(1)}, u32[]{:S(2)}, u32[]{:S(2)}) %collective-permute-start.7) | collective-permute-done | bytes 196640 | tf_op jit(solution)/shard_map/ppermute | solution.py:433
  38.1 3.5 %collective-permute-start.18 = (bf16[2,192,256]{2,1,0:T(8,128)(2,1)S(1)}, bf16[2,192,256]{2,1,0:T(8,128)(2,1)S(1)}, u32[]{:S(2)}, u32[]{:S(2)}) collective-permute-start(bf16[2,192,256]{2,1,0:T(8,128)(2,1)S(1)} %get-tuple-element.64), channel_id=1, source_target_pairs={{0,3},{1,0},{2,1},{3,2},{4,7},{5,4},{6,5},{7,6},{8,11},{9,8},{10,9... | collective-permute-start | bytes 589832 | tf_op jit(solution)/shard_map/ppermute | solution.py:433
  41.6 1.7 %collective-permute-start.19 = (bf16[2,192,256]{2,1,0:T(8,128)(2,1)S(1)}, bf16[2,192,256]{2,1,0:T(8,128)(2,1)S(1)}, u32[]{:S(2)}, u32[]{:S(2)}) collective-permute-start(bf16[2,192,256]{2,1,0:T(8,128)(2,1)S(1)} %get-tuple-element.65), channel_id=1, source_target_pairs={{0,2},{1,3},{2,0},{3,1},{4,6},{5,7},{6,4},{7,5},{8,10},{9,11},{10,... | collective-permute-start | bytes 589832 | tf_op jit(solution)/shard_map/ppermute | solution.py:433
  43.3 6.3 %attend.2 = (bf16[192,256]{1,0:T(8,128)(2,1)S(1)}, bf16[192,256]{1,0:T(8,128)(2,1)S(1)}, bf16[192,256]{1,0:T(8,128)(2,1)S(1)}, bf16[192,256]{1,0:T(8,128)(2,1)S(...) custom-call(f32[1,32]{1,0:T(1,128)S(1)} %copy-done.6, ...), custom_call_target="tpu_custom_call" | custom-call | flops 4499999744 | tf_op jit(solution)/shard_map/attend/pallas_call | solution.py:282
  49.6 5.0 %collective-permute-start.13 = (bf16[2,576,256]{2,1,0:T(8,128)(2,1)S(1)}, bf16[2,576,256]{2,1,0:T(8,128)(2,1)S(1)}, u32[]{:S(2)}, u32[]{:S(2)}) collective-permute-start(bf16[2,576,256]{2,1,0:T(8,128)(2,1)S(1)} %get-tuple-element.61), channel_id=1, source_target_pairs={{0,28},{1,29},{2,30},{3,31},{4,0},{5,1},{6,2},{7,3},{8,4},{9,5},{1... | collective-permute-start | bytes 1769480 | tf_op jit(solution)/shard_map/ppermute | solution.py:437
  54.6 1.2 %collective-permute-start.10 = (bf16[192,256]{1,0:T(8,128)(2,1)S(1)}, bf16[192,256]{1,0:T(8,128)(2,1)S(1)}, u32[]{:S(2)}, u32[]{:S(2)}) collective-permute-start(bf16[192,256]{1,0:T(8,128)(2,1)S(1)} %get-tuple-element.57), channel_id=1, source_target_pairs={{0,1},{1,2},{2,3},{3,0},{4,5},{5,6},{6,7},{7,4},{8,9},{9,10},{10,1... | collective-permute-start | bytes 294920 | tf_op jit(solution)/shard_map/ppermute | solution.py:433
  55.8 2.0 %collective-permute-start.11 = (bf16[192,256]{1,0:T(8,128)(2,1)S(1)}, bf16[192,256]{1,0:T(8,128)(2,1)S(1)}, u32[]{:S(2)}, u32[]{:S(2)}) collective-permute-start(bf16[192,256]{1,0:T(8,128)(2,1)S(1)} %get-tuple-element.58), channel_id=1, source_target_pairs={{0,3},{1,0},{2,1},{3,2},{4,7},{5,4},{6,5},{7,6},{8,11},{9,8},{10,9... | collective-permute-start | bytes 294920 | tf_op jit(solution)/shard_map/ppermute | solution.py:433
  58.5 6.3 %attend.3 = (bf16[192,256]{1,0:T(8,128)(2,1)S(1)}, bf16[192,256]{1,0:T(8,128)(2,1)S(1)}, bf16[192,256]{1,0:T(8,128)(2,1)S(1)}, bf16[192,256]{1,0:T(8,128)(2,1)S(...) custom-call(f32[1,32]{1,0:T(1,128)S(1)} %copy-done.6, ...), custom_call_target="tpu_custom_call" | custom-call | flops 4499999744 | tf_op jit(solution)/shard_map/attend/pallas_call | solution.py:282
  64.8 2.1 %collective-permute-start.24 = (bf16[2,576,256]{2,1,0:T(8,128)(2,1)S(1)}, bf16[2,576,256]{2,1,0:T(8,128)(2,1)S(1)}, u32[]{:S(2)}, u32[]{:S(2)}) collective-permute-start(bf16[2,576,256]{2,1,0:T(8,128)(2,1)S(1)} %get-tuple-element.76), channel_id=1, source_target_pairs={{0,28},{1,29},{2,30},{3,31},{4,0},{5,1},{6,2},{7,3},{8,4},{9,5},{1... | collective-permute-start | bytes 1769480 | tf_op jit(solution)/shard_map/ppermute | solution.py:437
  67.8 2.7 %collective-permute-start.22 = (bf16[3,192,256]{2,1,0:T(8,128)(2,1)S(1)}, bf16[3,192,256]{2,1,0:T(8,128)(2,1)S(1)}, u32[]{:S(2)}, u32[]{:S(2)}) collective-permute-start(bf16[3,192,256]{2,1,0:T(8,128)(2,1)S(1)} %get-tuple-element.72), channel_id=1, source_target_pairs={{0,3},{1,0},{2,1},{3,2},{4,7},{5,4},{6,5},{7,6},{8,11},{9,8},{10,9... | collective-permute-start | bytes 884744 | tf_op jit(solution)/shard_map/ppermute | solution.py:433
  70.5 1.7 %collective-permute-start.23 = (bf16[3,192,256]{2,1,0:T(8,128)(2,1)S(1)}, bf16[3,192,256]{2,1,0:T(8,128)(2,1)S(1)}, u32[]{:S(2)}, u32[]{:S(2)}) collective-permute-start(bf16[3,192,256]{2,1,0:T(8,128)(2,1)S(1)} %get-tuple-element.73), channel_id=1, source_target_pairs={{0,2},{1,3},{2,0},{3,1},{4,6},{5,7},{6,4},{7,5},{8,10},{9,11},{10,... | collective-permute-start | bytes 884744 | tf_op jit(solution)/shard_map/ppermute | solution.py:433
  72.2 6.4 %collective-permute-done.24.far_ref = bf16[2,576,256]{2,1,0:T(8,128)(2,1)S(1)} collective-permute-done((bf16[2,576,256]{2,1,0:T(8,128)(2,1)S(1)}, bf16[2,576,256]{2,1,0:T(8,128)(2,1)S(1)}, u32[]{:S(2)}, u32[]{:S(2)}) %collective-permute-start.24) | collective-permute-done | bytes 589856 | tf_op jit(solution)/shard_map/ppermute | solution.py:437
  78.9 3.2 %collective-permute-start.26 = (bf16[2,192,256]{2,1,0:T(8,128)(2,1)S(1)}, bf16[2,192,256]{2,1,0:T(8,128)(2,1)S(1)}, u32[]{:S(2)}, u32[]{:S(2)}) collective-permute-start(bf16[2,192,256]{2,1,0:T(8,128)(2,1)S(1)} %get-tuple-element.79), channel_id=1, source_target_pairs={{0,3},{1,0},{2,1},{3,2},{4,7},{5,4},{6,5},{7,6},{8,11},{9,8},{10,9... | collective-permute-start | bytes 589832 | tf_op jit(solution)/shard_map/ppermute | solution.py:433
  82.4 1.3 %early.1 = (bf16[192,2048]{1,0:T(8,128)(2,1)}, bf16[192,2048]{1,0:T(8,128)(2,1)}, bf16[192,2048]{1,0:T(8,128)(2,1)}) custom-call(bf16[192,256]{1,0:T(8,128)(2,1)S(1)} %get-tuple-element.56.refs_0_, bf16[192,256]{1,0:T(8,128)(2,1)S(1)} %collective-permute-done.10.refs_4_.refs_1_, bf16[192,256]{1,0:T(8,128)(2,1)S(1)} %collective-permute-done.11.refs_5_.refs_2_, ...), custom_call_target="tpu_custom_call" | custom-call | bytes 2359296 | tf_op jit(solution)/shard_map/early/pallas_call | solution.py:395
  83.6 3.4 %collective-permute-done.25.refs_1_ = bf16[2,192,256]{2,1,0:T(8,128)(2,1)S(1)} collective-permute-done((bf16[2,192,256]{2,1,0:T(8,128)(2,1)S(1)}, bf16[2,192,256]{2,1,0:T(8,128)(2,1)S(1)}, u32[]{:S(2)}, u32[]{:S(2)}) %collective-permute-start.25) | collective-permute-done | bytes 196640 | tf_op jit(solution)/shard_map/ppermute | solution.py:433
  87.4 1.9 %collective-permute-done.27.refs_3_ = bf16[2,192,256]{2,1,0:T(8,128)(2,1)S(1)} collective-permute-done((bf16[2,192,256]{2,1,0:T(8,128)(2,1)S(1)}, bf16[2,192,256]{2,1,0:T(8,128)(2,1)S(1)}, u32[]{:S(2)}, u32[]{:S(2)}) %collective-permute-start.27) | collective-permute-done | bytes 196640 | tf_op jit(solution)/shard_map/ppermute | solution.py:433
  89.3 0.9 %late.1 = (bf16[192,2048]{1,0:T(8,128)(2,1)}, bf16[192,2048]{1,0:T(8,128)(2,1)}) custom-call(bf16[2,192,256]{2,1,0:T(8,128)(2,1)S(1)} %get-tuple-element.77.refs_0_, bf16[2,192,256]{2,1,0:T(8,128)(2,1)S(1)} %collective-permute-done.25.refs_1_, ...), custom_call_target="tpu_custom_call", output_to_operand_aliasing={{0}: (4, {}), {1}: (5, {})} | custom-call | bytes 2359296 | tf_op jit(solution)/shard_map/late/pallas_call | solution.py:405
  (51 shorter events, 4.8 us)
Async XLA Ops:
  0.6 9.4 %copy-start = (bf16[1,192,2048]{2,1,0:T(8,128)(2,1)S(1)}, bf16[1,192,2048]{2,1,0:T(8,128)(2,1)}, u32[]{:S(2)}) copy-start(bf16[1,192,2048]{2,1,0:T(8,128)(2,1)} %param.7) | copy-start | bytes 2359300
  0.6 9.4 %copy-start.1 = (bf16[1,192,2048]{2,1,0:T(8,128)(2,1)S(1)}, bf16[1,192,2048]{2,1,0:T(8,128)(2,1)}, u32[]{:S(2)}) copy-start(bf16[1,192,2048]{2,1,0:T(8,128)(2,1)} %param.8) | copy-start | bytes 2359300
  2.8 11.8 %collective-permute-start.3 = (bf16[2,192,256]{2,1,0:T(8,128)(2,1)}, bf16[2,192,256]{2,1,0:T(8,128)(2,1)S(1)}, u32[]{:S(2)}, u32[]{:S(2)}) collective-permute-start(bf16[2,192,256]{2,1,0:T(8,128)(2,1)} %get-tuple-element.45), channel_id=1, source_target_pairs={{0,1},{1,2},{2,3},{3,0},{4,5},{5,6},{6,7},{7,4},{8,9},{9,10},{10,1... | collective-permute-start | bytes 589832 | tf_op jit(solution)/shard_map/ppermute | solution.py:433
  4.5 11.2 %collective-permute-start.4 = (bf16[2,192,256]{2,1,0:T(8,128)(2,1)}, bf16[2,192,256]{2,1,0:T(8,128)(2,1)S(1)}, u32[]{:S(2)}, u32[]{:S(2)}) collective-permute-start(bf16[2,192,256]{2,1,0:T(8,128)(2,1)} %get-tuple-element.46), channel_id=1, source_target_pairs={{0,3},{1,0},{2,1},{3,2},{4,7},{5,4},{6,5},{7,6},{8,11},{9,8},{10,9... | collective-permute-start | bytes 589832 | tf_op jit(solution)/shard_map/ppermute | solution.py:433
  6.1 10.0 %collective-permute-start.5 = (bf16[2,192,256]{2,1,0:T(8,128)(2,1)}, bf16[2,192,256]{2,1,0:T(8,128)(2,1)S(1)}, u32[]{:S(2)}, u32[]{:S(2)}) collective-permute-start(bf16[2,192,256]{2,1,0:T(8,128)(2,1)} %get-tuple-element.47), channel_id=1, source_target_pairs={{0,2},{1,3},{2,0},{3,1},{4,6},{5,7},{6,4},{7,5},{8,10},{9,11},{10,... | collective-permute-start | bytes 589832 | tf_op jit(solution)/shard_map/ppermute | solution.py:433
  8.2 2.6 %collective-permute-start.2 = (f32[1,32]{1,0:T(1,128)S(1)}, f32[1,32]{1,0:T(1,128)S(1)}, u32[]{:S(2)}, u32[]{:S(2)}) collective-permute-start(f32[1,32]{1,0:T(1,128)S(1)} %copy-done.6), channel_id=1, source_target_pairs={{0,96},{32,0},{64,32},{96,64},{1,97},{33,1},{65,33},{97,65},{2,98}... | collective-permute-start | bytes 392 | tf_op jit(solution)/shard_map/ppermute | solution.py:444
  9.5 3.5 %collective-permute-start.1 = (f32[1,32]{1,0:T(1,128)S(1)}, f32[1,32]{1,0:T(1,128)S(1)}, u32[]{:S(2)}, u32[]{:S(2)}) collective-permute-start(f32[1,32]{1,0:T(1,128)S(1)} %copy-done.6), channel_id=1, source_target_pairs={{0,64},{32,96},{64,0},{96,32},{1,65},{33,97},{65,1},{97,33},{2,66}... | collective-permute-start | bytes 392 | tf_op jit(solution)/shard_map/ppermute | solution.py:444
  10.8 3.2 %collective-permute-start = (f32[1,32]{1,0:T(1,128)S(1)}, f32[1,32]{1,0:T(1,128)S(1)}, u32[]{:S(2)}, u32[]{:S(2)}) collective-permute-start(f32[1,32]{1,0:T(1,128)S(1)} %copy-done.6), channel_id=1, source_target_pairs={{0,32},{32,64},{64,96},{96,0},{1,33},{33,65},{65,97},{97,1},{2,34}... | collective-permute-start | bytes 392 | tf_op jit(solution)/shard_map/ppermute | solution.py:444
  13.0 9.7 %collective-permute-start.15 = (bf16[2,192,256]{2,1,0:T(8,128)(2,1)S(1)}, bf16[2,192,256]{2,1,0:T(8,128)(2,1)S(1)}, u32[]{:S(2)}, u32[]{:S(2)}) collective-permute-start(bf16[2,192,256]{2,1,0:T(8,128)(2,1)S(1)} %get-tuple-element.62), channel_id=1, source_target_pairs={{0,3},{1,0},{2,1},{3,2},{4,7},{5,4},{6,5},{7,6},{8,11},{9,8},{10,9... | collective-permute-start | bytes 589832 | tf_op jit(solution)/shard_map/ppermute | solution.py:433
  14.0 15.3 %collective-permute-start.16 = (bf16[2,192,256]{2,1,0:T(8,128)(2,1)S(1)}, bf16[2,192,256]{2,1,0:T(8,128)(2,1)S(1)}, u32[]{:S(2)}, u32[]{:S(2)}) collective-permute-start(bf16[2,192,256]{2,1,0:T(8,128)(2,1)S(1)} %get-tuple-element.63), channel_id=1, source_target_pairs={{0,2},{1,3},{2,0},{3,1},{4,6},{5,7},{6,4},{7,5},{8,10},{9,11},{10,... | collective-permute-start | bytes 589832 | tf_op jit(solution)/shard_map/ppermute | solution.py:433
  14.6 5.0 %copy-start.2 = (bf16[1,192,2048]{2,1,0:T(8,128)(2,1)S(1)}, bf16[1,192,2048]{2,1,0:T(8,128)(2,1)}, u32[]{:S(2)}) copy-start(bf16[1,192,2048]{2,1,0:T(8,128)(2,1)} %param.6) | copy-start | bytes 2359300
  14.6 5.0 %copy-start.3 = (bf16[1,192,2048]{2,1,0:T(8,128)(2,1)S(1)}, bf16[1,192,2048]{2,1,0:T(8,128)(2,1)}, u32[]{:S(2)}) copy-start(bf16[1,192,2048]{2,1,0:T(8,128)(2,1)} %param.9) | copy-start | bytes 2359300
  14.6 14.7 %collective-permute-start.14 = (bf16[2,192,256]{2,1,0:T(8,128)(2,1)S(1)}, bf16[2,192,256]{2,1,0:T(8,128)(2,1)S(1)}, u32[]{:S(2)}, u32[]{:S(2)}) collective-permute-start(bf16[2,192,256]{2,1,0:T(8,128)(2,1)S(1)} %get-tuple-element.48.refs_3_), channel_id=1, source_target_pairs={{0,1},{1,2},{2,3},{3,0},{4,5},{5,6},{6,7},{7,4},{8,9},{9,10},{10,1... | collective-permute-start | bytes 589832 | tf_op jit(solution)/shard_map/ppermute | solution.py:433
  16.2 27.1 %collective-permute-start.9 = (bf16[2,576,256]{2,1,0:T(8,128)(2,1)S(1)}, bf16[2,576,256]{2,1,0:T(8,128)(2,1)S(1)}, u32[]{:S(2)}, u32[]{:S(2)}) collective-permute-start(bf16[2,576,256]{2,1,0:T(8,128)(2,1)S(1)} %edge.2.after), channel_id=1, source_target_pairs={{0,4},{1,5},{2,6},{3,7},{4,8},{5,9},{6,10},{7,11},{8,12},{9,13},{1... | collective-permute-start | bytes 1769480 | tf_op jit(solution)/shard_map/ppermute | solution.py:437
  19.6 22.0 %collective-permute-start.6 = (bf16[2,192,256]{2,1,0:T(8,128)(2,1)S(1)}, bf16[2,192,256]{2,1,0:T(8,128)(2,1)S(1)}, u32[]{:S(2)}, u32[]{:S(2)}) collective-permute-start(bf16[2,192,256]{2,1,0:T(8,128)(2,1)S(1)} %get-tuple-element.49.after), channel_id=1, source_target_pairs={{0,1},{1,2},{2,3},{3,0},{4,5},{5,6},{6,7},{7,4},{8,9},{9,10},{10,1... | collective-permute-start | bytes 589832 | tf_op jit(solution)/shard_map/ppermute | solution.py:433
  22.7 15.1 %collective-permute-start.7 = (bf16[2,192,256]{2,1,0:T(8,128)(2,1)S(1)}, bf16[2,192,256]{2,1,0:T(8,128)(2,1)S(1)}, u32[]{:S(2)}, u32[]{:S(2)}) collective-permute-start(bf16[2,192,256]{2,1,0:T(8,128)(2,1)S(1)} %get-tuple-element.54), channel_id=1, source_target_pairs={{0,3},{1,0},{2,1},{3,2},{4,7},{5,4},{6,5},{7,6},{8,11},{9,8},{10,9... | collective-permute-start | bytes 589832 | tf_op jit(solution)/shard_map/ppermute | solution.py:433
  29.3 8.8 %collective-permute-start.8 = (bf16[2,192,256]{2,1,0:T(8,128)(2,1)S(1)}, bf16[2,192,256]{2,1,0:T(8,128)(2,1)S(1)}, u32[]{:S(2)}, u32[]{:S(2)}) collective-permute-start(bf16[2,192,256]{2,1,0:T(8,128)(2,1)S(1)} %get-tuple-element.55), channel_id=1, source_target_pairs={{0,2},{1,3},{2,0},{3,1},{4,6},{5,7},{6,4},{7,5},{8,10},{9,11},{10,... | collective-permute-start | bytes 589832 | tf_op jit(solution)/shard_map/ppermute | solution.py:433
  29.4 29.1 %collective-permute-start.20 = (bf16[2,576,256]{2,1,0:T(8,128)(2,1)S(1)}, bf16[2,576,256]{2,1,0:T(8,128)(2,1)S(1)}, u32[]{:S(2)}, u32[]{:S(2)}) collective-permute-start(bf16[2,576,256]{2,1,0:T(8,128)(2,1)S(1)} %edge.3), channel_id=1, source_target_pairs={{0,4},{1,5},{2,6},{3,7},{4,8},{5,9},{6,10},{7,11},{8,12},{9,13},{1... | collective-permute-start | bytes 1769480 | tf_op jit(solution)/shard_map/ppermute | solution.py:437
  37.9 20.0 %collective-permute-start.17 = (bf16[2,192,256]{2,1,0:T(8,128)(2,1)S(1)}, bf16[2,192,256]{2,1,0:T(8,128)(2,1)S(1)}, u32[]{:S(2)}, u32[]{:S(2)}) collective-permute-start(bf16[2,192,256]{2,1,0:T(8,128)(2,1)S(1)} %get-tuple-element.50.after), channel_id=1, source_target_pairs={{0,1},{1,2},{2,3},{3,0},{4,5},{5,6},{6,7},{7,4},{8,9},{9,10},{10,1... | collective-permute-start | bytes 589832 | tf_op jit(solution)/shard_map/ppermute | solution.py:433
  38.1 16.5 %collective-permute-start.18 = (bf16[2,192,256]{2,1,0:T(8,128)(2,1)S(1)}, bf16[2,192,256]{2,1,0:T(8,128)(2,1)S(1)}, u32[]{:S(2)}, u32[]{:S(2)}) collective-permute-start(bf16[2,192,256]{2,1,0:T(8,128)(2,1)S(1)} %get-tuple-element.64), channel_id=1, source_target_pairs={{0,3},{1,0},{2,1},{3,2},{4,7},{5,4},{6,5},{7,6},{8,11},{9,8},{10,9... | collective-permute-start | bytes 589832 | tf_op jit(solution)/shard_map/ppermute | solution.py:433
  41.6 14.2 %collective-permute-start.19 = (bf16[2,192,256]{2,1,0:T(8,128)(2,1)S(1)}, bf16[2,192,256]{2,1,0:T(8,128)(2,1)S(1)}, u32[]{:S(2)}, u32[]{:S(2)}) collective-permute-start(bf16[2,192,256]{2,1,0:T(8,128)(2,1)S(1)} %get-tuple-element.65), channel_id=1, source_target_pairs={{0,2},{1,3},{2,0},{3,1},{4,6},{5,7},{6,4},{7,5},{8,10},{9,11},{10,... | collective-permute-start | bytes 589832 | tf_op jit(solution)/shard_map/ppermute | solution.py:433
  49.6 17.4 %collective-permute-start.13 = (bf16[2,576,256]{2,1,0:T(8,128)(2,1)S(1)}, bf16[2,576,256]{2,1,0:T(8,128)(2,1)S(1)}, u32[]{:S(2)}, u32[]{:S(2)}) collective-permute-start(bf16[2,576,256]{2,1,0:T(8,128)(2,1)S(1)} %get-tuple-element.61), channel_id=1, source_target_pairs={{0,28},{1,29},{2,30},{3,31},{4,0},{5,1},{6,2},{7,3},{8,4},{9,5},{1... | collective-permute-start | bytes 1769480 | tf_op jit(solution)/shard_map/ppermute | solution.py:437
  54.6 12.4 %collective-permute-start.10 = (bf16[192,256]{1,0:T(8,128)(2,1)S(1)}, bf16[192,256]{1,0:T(8,128)(2,1)S(1)}, u32[]{:S(2)}, u32[]{:S(2)}) collective-permute-start(bf16[192,256]{1,0:T(8,128)(2,1)S(1)} %get-tuple-element.57), channel_id=1, source_target_pairs={{0,1},{1,2},{2,3},{3,0},{4,5},{5,6},{6,7},{7,4},{8,9},{9,10},{10,1... | collective-permute-start | bytes 294920 | tf_op jit(solution)/shard_map/ppermute | solution.py:433
  55.8 11.2 %collective-permute-start.11 = (bf16[192,256]{1,0:T(8,128)(2,1)S(1)}, bf16[192,256]{1,0:T(8,128)(2,1)S(1)}, u32[]{:S(2)}, u32[]{:S(2)}) collective-permute-start(bf16[192,256]{1,0:T(8,128)(2,1)S(1)} %get-tuple-element.58), channel_id=1, source_target_pairs={{0,3},{1,0},{2,1},{3,2},{4,7},{5,4},{6,5},{7,6},{8,11},{9,8},{10,9... | collective-permute-start | bytes 294920 | tf_op jit(solution)/shard_map/ppermute | solution.py:433
  57.9 9.1 %collective-permute-start.12 = (bf16[192,256]{1,0:T(8,128)(2,1)S(1)}, bf16[192,256]{1,0:T(8,128)(2,1)S(1)}, u32[]{:S(2)}, u32[]{:S(2)}) collective-permute-start(bf16[192,256]{1,0:T(8,128)(2,1)S(1)} %get-tuple-element.59), channel_id=1, source_target_pairs={{0,2},{1,3},{2,0},{3,1},{4,6},{5,7},{6,4},{7,5},{8,10},{9,11},{10,... | collective-permute-start | bytes 294920 | tf_op jit(solution)/shard_map/ppermute | solution.py:433
  64.8 13.8 %collective-permute-start.24 = (bf16[2,576,256]{2,1,0:T(8,128)(2,1)S(1)}, bf16[2,576,256]{2,1,0:T(8,128)(2,1)S(1)}, u32[]{:S(2)}, u32[]{:S(2)}) collective-permute-start(bf16[2,576,256]{2,1,0:T(8,128)(2,1)S(1)} %get-tuple-element.76), channel_id=1, source_target_pairs={{0,28},{1,29},{2,30},{3,31},{4,0},{5,1},{6,2},{7,3},{8,4},{9,5},{1... | collective-permute-start | bytes 1769480 | tf_op jit(solution)/shard_map/ppermute | solution.py:437
  67.2 14.9 %collective-permute-start.21 = (bf16[3,192,256]{2,1,0:T(8,128)(2,1)S(1)}, bf16[3,192,256]{2,1,0:T(8,128)(2,1)S(1)}, u32[]{:S(2)}, u32[]{:S(2)}) collective-permute-start(bf16[3,192,256]{2,1,0:T(8,128)(2,1)S(1)} %get-tuple-element.71), channel_id=1, source_target_pairs={{0,1},{1,2},{2,3},{3,0},{4,5},{5,6},{6,7},{7,4},{8,9},{9,10},{10,1... | collective-permute-start | bytes 884744 | tf_op jit(solution)/shard_map/ppermute | solution.py:433
  67.8 14.3 %collective-permute-start.22 = (bf16[3,192,256]{2,1,0:T(8,128)(2,1)S(1)}, bf16[3,192,256]{2,1,0:T(8,128)(2,1)S(1)}, u32[]{:S(2)}, u32[]{:S(2)}) collective-permute-start(bf16[3,192,256]{2,1,0:T(8,128)(2,1)S(1)} %get-tuple-element.72), channel_id=1, source_target_pairs={{0,3},{1,0},{2,1},{3,2},{4,7},{5,4},{6,5},{7,6},{8,11},{9,8},{10,9... | collective-permute-start | bytes 884744 | tf_op jit(solution)/shard_map/ppermute | solution.py:433
  70.5 11.9 %collective-permute-start.23 = (bf16[3,192,256]{2,1,0:T(8,128)(2,1)S(1)}, bf16[3,192,256]{2,1,0:T(8,128)(2,1)S(1)}, u32[]{:S(2)}, u32[]{:S(2)}) collective-permute-start(bf16[3,192,256]{2,1,0:T(8,128)(2,1)S(1)} %get-tuple-element.73), channel_id=1, source_target_pairs={{0,2},{1,3},{2,0},{3,1},{4,6},{5,7},{6,4},{7,5},{8,10},{9,11},{10,... | collective-permute-start | bytes 884744 | tf_op jit(solution)/shard_map/ppermute | solution.py:433
  78.8 8.2 %collective-permute-start.25 = (bf16[2,192,256]{2,1,0:T(8,128)(2,1)S(1)}, bf16[2,192,256]{2,1,0:T(8,128)(2,1)S(1)}, u32[]{:S(2)}, u32[]{:S(2)}) collective-permute-start(bf16[2,192,256]{2,1,0:T(8,128)(2,1)S(1)} %get-tuple-element.78), channel_id=1, source_target_pairs={{0,1},{1,2},{2,3},{3,0},{4,5},{5,6},{6,7},{7,4},{8,9},{9,10},{10,1... | collective-permute-start | bytes 589832 | tf_op jit(solution)/shard_map/ppermute | solution.py:433
  78.9 8.5 %collective-permute-start.26 = (bf16[2,192,256]{2,1,0:T(8,128)(2,1)S(1)}, bf16[2,192,256]{2,1,0:T(8,128)(2,1)S(1)}, u32[]{:S(2)}, u32[]{:S(2)}) collective-permute-start(bf16[2,192,256]{2,1,0:T(8,128)(2,1)S(1)} %get-tuple-element.79), channel_id=1, source_target_pairs={{0,3},{1,0},{2,1},{3,2},{4,7},{5,4},{6,5},{7,6},{8,11},{9,8},{10,9... | collective-permute-start | bytes 589832 | tf_op jit(solution)/shard_map/ppermute | solution.py:433
  82.1 7.2 %collective-permute-start.27 = (bf16[2,192,256]{2,1,0:T(8,128)(2,1)S(1)}, bf16[2,192,256]{2,1,0:T(8,128)(2,1)S(1)}, u32[]{:S(2)}, u32[]{:S(2)}) collective-permute-start(bf16[2,192,256]{2,1,0:T(8,128)(2,1)S(1)} %get-tuple-element.80), channel_id=1, source_target_pairs={{0,2},{1,3},{2,0},{3,1},{4,6},{5,7},{6,4},{7,5},{8,10},{9,11},{10,... | collective-permute-start | bytes 589832 | tf_op jit(solution)/shard_map/ppermute | solution.py:433
  (3 other events, 3.4 us)

commit v6 on v4

--- a/solution.py
+++ b/solution.py
@@ -221,8 +221,6 @@
         value_all[pl.ds(edge + start, rows), :] = value[...]
         query_all[pl.ds(start, rows), :] = query[...]
         grad_all[pl.ds(start, rows), :] = grad[...]
-    key_grad[...] = jnp.zeros_like(key_grad)
-    value_grad[...] = jnp.zeros_like(value_grad)
     for block in range(GROUP):
         at = slice(block * rows, (block + 1) * rows)
         window = slice(block * rows, block * rows + span)
@@ -259,19 +257,28 @@
             query_out[at, lanes] = (
                 jnp.dot(dscore, key, preferred_element_type=jnp.float32) * scale
             ).astype(jnp.bfloat16)
-            key_grad[window, lanes] += lax.dot_general(
-                dscore, query, (((0,), (0,)), ((), ())), preferred_element_type=jnp.float32
-            )
-            value_grad[window, lanes] += lax.dot_general(
-                prob_half, grad, (((0,), (0,)), ((), ())), preferred_element_type=jnp.float32
-            )
+            for kind, (left, right, held, scaling) in enumerate(
+                ((dscore, query, key_grad, scale), (prob_half, grad, value_grad, 1.0))
+            ):
+                term = lax.dot_general(
+                    left, right, (((0,), (0,)), ((), ())), preferred_element_type=jnp.float32
+                )
+                for step in range(STEPS):
+                    index = block + step
+                    here = slice(index * rows, (index + 1) * rows)
+                    part = term[step * rows : (step + 1) * rows]
+                    if block > 0 and step < STEPS - 1:
+                        part = part + held[here, lanes]
+                    if step > 0 and block < GROUP - 1:
+                        held[here, lanes] = part
+                    elif index < GROUP - 1:
+                        far_ref[kind, here, lanes] = (part * scaling).astype(jnp.bfloat16)
+                    else:
+                        there = slice((index - GROUP + 1) * rows, (index - GROUP + 2) * rows)
+                        main_ref[kind, there, lanes] = (part * scaling).astype(jnp.bfloat16)
     for away, block in zip(aways(), (query_own, query_to_one, query_to_two, query_to_three)):
         index = lax.rem(place + away, GROUP)
         block[...] = query_out[pl.ds(pl.multiple_of(index * rows, rows), rows), :]
-    far_ref[0] = (key_grad[:edge, :] * scale).astype(jnp.bfloat16)
-    far_ref[1] = value_grad[:edge, :].astype(jnp.bfloat16)
-    main_ref[0] = (key_grad[edge:, :] * scale).astype(jnp.bfloat16)
-    main_ref[1] = value_grad[edge:, :].astype(jnp.bfloat16)
 
 
 def attend(texts, marks, arrays, key_blocks, query_blocks, edge, chunk, total_rows):

time: 87.4 us -> 87.4 us (level)
  no operation moved by 1% of the time
where the time goes in v6:
time: 87.4 us; the launch traced here: 87.3 us
  starting transfers between devices  47.1 us (54%)
  waiting for transfers between devices  20.4 us (23%)
  Pallas kernels  18.1 us (21%)
  between operations  1.01 us (1%)
    ppermute x21, starting transfers between devices, swap(): return lax.ppermute(value, ('dp', 'ctx'), pairs)  32.5 us
    pallas_call x2, Pallas kernels, attend(): pl.pallas_call(functools.partial(attend_kernel, chunk, total_rows), out_s...  12.7 us
    ppermute x21, waiting for transfers between devices, swap(): return lax.ppermute(value, ('dp', 'ctx'), pairs)  11.9 us
    ppermute x4, starting transfers between devices, next_row(): return lax.ppermute(value, 'ctx', pairs)  11.9 us
    ppermute x4, waiting for transfers between devices, next_row(): return lax.ppermute(value, 'ctx', pairs)  7.7 us
    ppermute x3, starting transfers between devices, shards(): lax.ppermute(text, 'dp', [(source, (source + away) % samples) for source...  2.73 us
    pallas_call x1, Pallas kernels, first_pack(): pl.pallas_call(first_pack_kernel, out_shape=(message,) * (GROUP - 1) + (j...  2.15 us
  transfers between devices with their start and end apart: 28, of which 8 were waited for; matrix products, arithmetic and copies ran while one was open for 0% of the time, Pallas kernels for 17%

profile of v6, /device:TPU:0, one launch (start us, length us, event | category | flops | bytes accessed | tf_op | source)
XLA Modules:
  0.0 87.3 jit_solution(8709142384562223708)
XLA Ops:
  0.7 2.1 %first_pack.1 = (bf16[2,192,256]{2,1,0:T(8,128)(2,1)}, bf16[2,192,256]{2,1,0:T(8,128)(2,1)}, bf16[2,192,256]{2,1,0:T(8,128)(2,1)}, f32[1,32]{1,0:T(1,128)}) custom-call(bf16[192,2048]{1,0:T(8,128)(2,1)} %bitcast.7, bf16[192,2048]{1,0:T(8,128)(2,1)} %bitcast.13, s32[1,32]{1,0:T(1,128)} %lengths_ref.1, s32[1,32]{1,0:T(1,128)} %flags_ref.1), custom_call_target="tpu_custom_call" | custom-call | bytes 1179648 | tf_op jit(solution)/shard_map/first_pack/pallas_call | solution.py:80
  2.8 1.7 %collective-permute-start.3 = (bf16[2,192,256]{2,1,0:T(8,128)(2,1)}, bf16[2,192,256]{2,1,0:T(8,128)(2,1)S(1)}, u32[]{:S(2)}, u32[]{:S(2)}) collective-permute-start(bf16[2,192,256]{2,1,0:T(8,128)(2,1)} %get-tuple-element.45), channel_id=1, source_target_pairs={{0,1},{1,2},{2,3},{3,0},{4,5},{5,6},{6,7},{7,4},{8,9},{9,10},{10,1... | collective-permute-start | bytes 589832 | tf_op jit(solution)/shard_map/ppermute | solution.py:440
  4.5 1.6 %collective-permute-start.4 = (bf16[2,192,256]{2,1,0:T(8,128)(2,1)}, bf16[2,192,256]{2,1,0:T(8,128)(2,1)S(1)}, u32[]{:S(2)}, u32[]{:S(2)}) collective-permute-start(bf16[2,192,256]{2,1,0:T(8,128)(2,1)} %get-tuple-element.46), channel_id=1, source_target_pairs={{0,3},{1,0},{2,1},{3,2},{4,7},{5,4},{6,5},{7,6},{8,11},{9,8},{10,9... | collective-permute-start | bytes 589832 | tf_op jit(solution)/shard_map/ppermute | solution.py:440
  6.1 2.1 %collective-permute-start.5 = (bf16[2,192,256]{2,1,0:T(8,128)(2,1)}, bf16[2,192,256]{2,1,0:T(8,128)(2,1)S(1)}, u32[]{:S(2)}, u32[]{:S(2)}) collective-permute-start(bf16[2,192,256]{2,1,0:T(8,128)(2,1)} %get-tuple-element.47), channel_id=1, source_target_pairs={{0,2},{1,3},{2,0},{3,1},{4,6},{5,7},{6,4},{7,5},{8,10},{9,11},{10,... | collective-permute-start | bytes 589832 | tf_op jit(solution)/shard_map/ppermute | solution.py:440
  8.3 1.4 %collective-permute-start.1 = (f32[1,32]{1,0:T(1,128)S(1)}, f32[1,32]{1,0:T(1,128)S(1)}, u32[]{:S(2)}, u32[]{:S(2)}) collective-permute-start(f32[1,32]{1,0:T(1,128)S(1)} %copy-done.6), channel_id=1, source_target_pairs={{0,64},{32,96},{64,0},{96,32},{1,65},{33,97},{65,1},{97,33},{2,66}... | collective-permute-start | bytes 392 | tf_op jit(solution)/shard_map/ppermute | solution.py:451
  9.8 1.2 %collective-permute-start = (f32[1,32]{1,0:T(1,128)S(1)}, f32[1,32]{1,0:T(1,128)S(1)}, u32[]{:S(2)}, u32[]{:S(2)}) collective-permute-start(f32[1,32]{1,0:T(1,128)S(1)} %copy-done.6), channel_id=1, source_target_pairs={{0,32},{32,64},{64,96},{96,0},{1,33},{33,65},{65,97},{97,1},{2,34}... | collective-permute-start | bytes 392 | tf_op jit(solution)/shard_map/ppermute | solution.py:451
  11.8 2.0 %collective-permute-start.15 = (bf16[2,192,256]{2,1,0:T(8,128)(2,1)S(1)}, bf16[2,192,256]{2,1,0:T(8,128)(2,1)S(1)}, u32[]{:S(2)}, u32[]{:S(2)}) collective-permute-start(bf16[2,192,256]{2,1,0:T(8,128)(2,1)S(1)} %get-tuple-element.62), channel_id=1, source_target_pairs={{0,3},{1,0},{2,1},{3,2},{4,7},{5,4},{6,5},{7,6},{8,11},{9,8},{10,9... | collective-permute-start | bytes 589832 | tf_op jit(solution)/shard_map/ppermute | solution.py:440
  13.8 2.0 %collective-permute-start.16 = (bf16[2,192,256]{2,1,0:T(8,128)(2,1)S(1)}, bf16[2,192,256]{2,1,0:T(8,128)(2,1)S(1)}, u32[]{:S(2)}, u32[]{:S(2)}) collective-permute-start(bf16[2,192,256]{2,1,0:T(8,128)(2,1)S(1)} %get-tuple-element.63), channel_id=1, source_target_pairs={{0,2},{1,3},{2,0},{3,1},{4,6},{5,7},{6,4},{7,5},{8,10},{9,11},{10,... | collective-permute-start | bytes 589832 | tf_op jit(solution)/shard_map/ppermute | solution.py:440
  15.8 1.8 %collective-permute-done.5.three.key_three = bf16[2,192,256]{2,1,0:T(8,128)(2,1)S(1)} collective-permute-done((bf16[2,192,256]{2,1,0:T(8,128)(2,1)}, bf16[2,192,256]{2,1,0:T(8,128)(2,1)S(1)}, u32[]{:S(2)}, u32[]{:S(2)}) %collective-permute-start.5) | collective-permute-done | bytes 196640 | tf_op jit(solution)/shard_map/ppermute | solution.py:440
  17.6 3.1 %collective-permute-start.9 = (bf16[2,576,256]{2,1,0:T(8,128)(2,1)S(1)}, bf16[2,576,256]{2,1,0:T(8,128)(2,1)S(1)}, u32[]{:S(2)}, u32[]{:S(2)}) collective-permute-start(bf16[2,576,256]{2,1,0:T(8,128)(2,1)S(1)} %edge.2.after), channel_id=1, source_target_pairs={{0,4},{1,5},{2,6},{3,7},{4,8},{5,9},{6,10},{7,11},{8,12},{9,13},{1... | collective-permute-start | bytes 1769480 | tf_op jit(solution)/shard_map/ppermute | solution.py:444
  22.1 4.0 %collective-permute-start.7 = (bf16[2,192,256]{2,1,0:T(8,128)(2,1)S(1)}, bf16[2,192,256]{2,1,0:T(8,128)(2,1)S(1)}, u32[]{:S(2)}, u32[]{:S(2)}) collective-permute-start(bf16[2,192,256]{2,1,0:T(8,128)(2,1)S(1)} %get-tuple-element.54), channel_id=1, source_target_pairs={{0,3},{1,0},{2,1},{3,2},{4,7},{5,4},{6,5},{7,6},{8,11},{9,8},{10,9... | collective-permute-start | bytes 589832 | tf_op jit(solution)/shard_map/ppermute | solution.py:440
  26.1 1.7 %collective-permute-start.8 = (bf16[2,192,256]{2,1,0:T(8,128)(2,1)S(1)}, bf16[2,192,256]{2,1,0:T(8,128)(2,1)S(1)}, u32[]{:S(2)}, u32[]{:S(2)}) collective-permute-start(bf16[2,192,256]{2,1,0:T(8,128)(2,1)S(1)} %get-tuple-element.55), channel_id=1, source_target_pairs={{0,2},{1,3},{2,0},{3,1},{4,6},{5,7},{6,4},{7,5},{8,10},{9,11},{10,... | collective-permute-start | bytes 589832 | tf_op jit(solution)/shard_map/ppermute | solution.py:440
  27.8 2.6 %collective-permute-start.20 = (bf16[2,576,256]{2,1,0:T(8,128)(2,1)S(1)}, bf16[2,576,256]{2,1,0:T(8,128)(2,1)S(1)}, u32[]{:S(2)}, u32[]{:S(2)}) collective-permute-start(bf16[2,576,256]{2,1,0:T(8,128)(2,1)S(1)} %edge.3), channel_id=1, source_target_pairs={{0,4},{1,5},{2,6},{3,7},{4,8},{5,9},{6,10},{7,11},{8,12},{9,13},{1... | collective-permute-start | bytes 1769480 | tf_op jit(solution)/shard_map/ppermute | solution.py:444
  30.4 1.5 %collective-permute-done.7.query_two = bf16[2,192,256]{2,1,0:T(8,128)(2,1)S(1)} collective-permute-done((bf16[2,192,256]{2,1,0:T(8,128)(2,1)S(1)}, bf16[2,192,256]{2,1,0:T(8,128)(2,1)S(1)}, u32[]{:S(2)}, u32[]{:S(2)}) %collective-permute-start.7) | collective-permute-done | bytes 196640 | tf_op jit(solution)/shard_map/ppermute | solution.py:440
  31.8 1.3 %collective-permute-start.17 = (bf16[2,192,256]{2,1,0:T(8,128)(2,1)S(1)}, bf16[2,192,256]{2,1,0:T(8,128)(2,1)S(1)}, u32[]{:S(2)}, u32[]{:S(2)}) collective-permute-start(bf16[2,192,256]{2,1,0:T(8,128)(2,1)S(1)} %get-tuple-element.50.after), channel_id=1, source_target_pairs={{0,1},{1,2},{2,3},{3,0},{4,5},{5,6},{6,7},{7,4},{8,9},{9,10},{10,1... | collective-permute-start | bytes 589832 | tf_op jit(solution)/shard_map/ppermute | solution.py:440
  33.8 1.8 %collective-permute-start.18 = (bf16[2,192,256]{2,1,0:T(8,128)(2,1)S(1)}, bf16[2,192,256]{2,1,0:T(8,128)(2,1)S(1)}, u32[]{:S(2)}, u32[]{:S(2)}) collective-permute-start(bf16[2,192,256]{2,1,0:T(8,128)(2,1)S(1)} %get-tuple-element.64), channel_id=1, source_target_pairs={{0,3},{1,0},{2,1},{3,2},{4,7},{5,4},{6,5},{7,6},{8,11},{9,8},{10,9... | collective-permute-start | bytes 589832 | tf_op jit(solution)/shard_map/ppermute | solution.py:440
  35.7 1.9 %collective-permute-start.19 = (bf16[2,192,256]{2,1,0:T(8,128)(2,1)S(1)}, bf16[2,192,256]{2,1,0:T(8,128)(2,1)S(1)}, u32[]{:S(2)}, u32[]{:S(2)}) collective-permute-start(bf16[2,192,256]{2,1,0:T(8,128)(2,1)S(1)} %get-tuple-element.65), channel_id=1, source_target_pairs={{0,2},{1,3},{2,0},{3,1},{4,6},{5,7},{6,4},{7,5},{8,10},{9,11},{10,... | collective-permute-start | bytes 589832 | tf_op jit(solution)/shard_map/ppermute | solution.py:440
  37.6 0.8 collective-permute-done.9.edge_ref
  38.4 6.3 %attend.2 = (bf16[192,256]{1,0:T(8,128)(2,1)S(1)}, bf16[192,256]{1,0:T(8,128)(2,1)S(1)}, bf16[192,256]{1,0:T(8,128)(2,1)S(1)}, bf16[192,256]{1,0:T(8,128)(2,1)S(...) custom-call(f32[1,32]{1,0:T(1,128)S(1)} %copy-done.6, ...), custom_call_target="tpu_custom_call" | custom-call | flops 4499999744 | tf_op jit(solution)/shard_map/attend/pallas_call | solution.py:289
  44.8 6.1 %collective-permute-start.13 = (bf16[2,576,256]{2,1,0:T(8,128)(2,1)S(1)}, bf16[2,576,256]{2,1,0:T(8,128)(2,1)S(1)}, u32[]{:S(2)}, u32[]{:S(2)}) collective-permute-start(bf16[2,576,256]{2,1,0:T(8,128)(2,1)S(1)} %get-tuple-element.61), channel_id=1, source_target_pairs={{0,28},{1,29},{2,30},{3,31},{4,0},{5,1},{6,2},{7,3},{8,4},{9,5},{1... | collective-permute-start | bytes 1769480 | tf_op jit(solution)/shard_map/ppermute | solution.py:444
  51.6 2.5 %collective-permute-start.11 = (bf16[192,256]{1,0:T(8,128)(2,1)S(1)}, bf16[192,256]{1,0:T(8,128)(2,1)S(1)}, u32[]{:S(2)}, u32[]{:S(2)}) collective-permute-start(bf16[192,256]{1,0:T(8,128)(2,1)S(1)} %get-tuple-element.58), channel_id=1, source_target_pairs={{0,3},{1,0},{2,1},{3,2},{4,7},{5,4},{6,5},{7,6},{8,11},{9,8},{10,9... | collective-permute-start | bytes 294920 | tf_op jit(solution)/shard_map/ppermute | solution.py:440
  54.1 0.9 collective-permute-start.12
  54.9 6.3 %attend.3 = (bf16[192,256]{1,0:T(8,128)(2,1)S(1)}, bf16[192,256]{1,0:T(8,128)(2,1)S(1)}, bf16[192,256]{1,0:T(8,128)(2,1)S(1)}, bf16[192,256]{1,0:T(8,128)(2,1)S(...) custom-call(f32[1,32]{1,0:T(1,128)S(1)} %copy-done.6, ...), custom_call_target="tpu_custom_call" | custom-call | flops 4499999744 | tf_op jit(solution)/shard_map/attend/pallas_call | solution.py:289
  62.4 2.6 %collective-permute-start.22 = (bf16[3,192,256]{2,1,0:T(8,128)(2,1)S(1)}, bf16[3,192,256]{2,1,0:T(8,128)(2,1)S(1)}, u32[]{:S(2)}, u32[]{:S(2)}) collective-permute-start(bf16[3,192,256]{2,1,0:T(8,128)(2,1)S(1)} %get-tuple-element.72), channel_id=1, source_target_pairs={{0,3},{1,0},{2,1},{3,2},{4,7},{5,4},{6,5},{7,6},{8,11},{9,8},{10,9... | collective-permute-start | bytes 884744 | tf_op jit(solution)/shard_map/ppermute | solution.py:440
  65.0 1.6 %collective-permute-start.23 = (bf16[3,192,256]{2,1,0:T(8,128)(2,1)S(1)}, bf16[3,192,256]{2,1,0:T(8,128)(2,1)S(1)}, u32[]{:S(2)}, u32[]{:S(2)}) collective-permute-start(bf16[3,192,256]{2,1,0:T(8,128)(2,1)S(1)} %get-tuple-element.73), channel_id=1, source_target_pairs={{0,2},{1,3},{2,0},{3,1},{4,6},{5,7},{6,4},{7,5},{8,10},{9,11},{10,... | collective-permute-start | bytes 884744 | tf_op jit(solution)/shard_map/ppermute | solution.py:440
  66.5 6.9 %collective-permute-done.24.far_ref = bf16[2,576,256]{2,1,0:T(8,128)(2,1)S(1)} collective-permute-done((bf16[2,576,256]{2,1,0:T(8,128)(2,1)S(1)}, bf16[2,576,256]{2,1,0:T(8,128)(2,1)S(1)}, u32[]{:S(2)}, u32[]{:S(2)}) %collective-permute-start.24) | collective-permute-done | bytes 589856 | tf_op jit(solution)/shard_map/ppermute | solution.py:444
  73.6 0.9 %collective-permute-start.25 = (bf16[2,192,256]{2,1,0:T(8,128)(2,1)S(1)}, bf16[2,192,256]{2,1,0:T(8,128)(2,1)S(1)}, u32[]{:S(2)}, u32[]{:S(2)}) collective-permute-start(bf16[2,192,256]{2,1,0:T(8,128)(2,1)S(1)} %get-tuple-element.78), channel_id=1, source_target_pairs={{0,1},{1,2},{2,3},{3,0},{4,5},{5,6},{6,7},{7,4},{8,9},{9,10},{10,1... | collective-permute-start | bytes 589832 | tf_op jit(solution)/shard_map/ppermute | solution.py:440
  74.5 2.4 %collective-permute-start.26 = (bf16[2,192,256]{2,1,0:T(8,128)(2,1)S(1)}, bf16[2,192,256]{2,1,0:T(8,128)(2,1)S(1)}, u32[]{:S(2)}, u32[]{:S(2)}) collective-permute-start(bf16[2,192,256]{2,1,0:T(8,128)(2,1)S(1)} %get-tuple-element.79), channel_id=1, source_target_pairs={{0,3},{1,0},{2,1},{3,2},{4,7},{5,4},{6,5},{7,6},{8,11},{9,8},{10,9... | collective-permute-start | bytes 589832 | tf_op jit(solution)/shard_map/ppermute | solution.py:440
  76.9 1.6 %collective-permute-done.21.refs_5_ = bf16[3,192,256]{2,1,0:T(8,128)(2,1)S(1)} collective-permute-done((bf16[3,192,256]{2,1,0:T(8,128)(2,1)S(1)}, bf16[3,192,256]{2,1,0:T(8,128)(2,1)S(1)}, u32[]{:S(2)}, u32[]{:S(2)}) %collective-permute-start.21) | collective-permute-done | bytes 294944 | tf_op jit(solution)/shard_map/ppermute | solution.py:440
  78.5 1.3 %early.1 = (bf16[192,2048]{1,0:T(8,128)(2,1)}, bf16[192,2048]{1,0:T(8,128)(2,1)}, bf16[192,2048]{1,0:T(8,128)(2,1)}) custom-call(bf16[192,256]{1,0:T(8,128)(2,1)S(1)} %get-tuple-element.56.refs_0_, bf16[192,256]{1,0:T(8,128)(2,1)S(1)} %collective-permute-done.10.refs_4_.refs_1_, bf16[192,256]{1,0:T(8,128)(2,1)S(1)} %collective-permute-done.11.refs_5_.refs_2_, ...), custom_call_target="tpu_custom_call" | custom-call | bytes 2359296 | tf_op jit(solution)/shard_map/early/pallas_call | solution.py:402
  79.8 6.3 %collective-permute-done.25.refs_1_ = bf16[2,192,256]{2,1,0:T(8,128)(2,1)S(1)} collective-permute-done((bf16[2,192,256]{2,1,0:T(8,128)(2,1)S(1)}, bf16[2,192,256]{2,1,0:T(8,128)(2,1)S(1)}, u32[]{:S(2)}, u32[]{:S(2)}) %collective-permute-start.25) | collective-permute-done | bytes 196640 | tf_op jit(solution)/shard_map/ppermute | solution.py:440
  86.2 0.9 %late.1 = (bf16[192,2048]{1,0:T(8,128)(2,1)}, bf16[192,2048]{1,0:T(8,128)(2,1)}) custom-call(bf16[2,192,256]{2,1,0:T(8,128)(2,1)S(1)} %get-tuple-element.77.refs_0_, bf16[2,192,256]{2,1,0:T(8,128)(2,1)S(1)} %collective-permute-done.25.refs_1_, ...), custom_call_target="tpu_custom_call", output_to_operand_aliasing={{0}: (4, {}), {1}: (5, {})} | custom-call | bytes 2359296 | tf_op jit(solution)/shard_map/late/pallas_call | solution.py:412
  (51 shorter events, 5.1 us)
Async XLA Ops:
  0.6 9.1 %copy-start = (bf16[1,192,2048]{2,1,0:T(8,128)(2,1)S(1)}, bf16[1,192,2048]{2,1,0:T(8,128)(2,1)}, u32[]{:S(2)}) copy-start(bf16[1,192,2048]{2,1,0:T(8,128)(2,1)} %param.7) | copy-start | bytes 2359300
  0.6 9.0 %copy-start.1 = (bf16[1,192,2048]{2,1,0:T(8,128)(2,1)S(1)}, bf16[1,192,2048]{2,1,0:T(8,128)(2,1)}, u32[]{:S(2)}) copy-start(bf16[1,192,2048]{2,1,0:T(8,128)(2,1)} %param.8) | copy-start | bytes 2359300
  2.8 13.0 %collective-permute-start.3 = (bf16[2,192,256]{2,1,0:T(8,128)(2,1)}, bf16[2,192,256]{2,1,0:T(8,128)(2,1)S(1)}, u32[]{:S(2)}, u32[]{:S(2)}) collective-permute-start(bf16[2,192,256]{2,1,0:T(8,128)(2,1)} %get-tuple-element.45), channel_id=1, source_target_pairs={{0,1},{1,2},{2,3},{3,0},{4,5},{5,6},{6,7},{7,4},{8,9},{9,10},{10,1... | collective-permute-start | bytes 589832 | tf_op jit(solution)/shard_map/ppermute | solution.py:440
  4.5 11.3 %collective-permute-start.4 = (bf16[2,192,256]{2,1,0:T(8,128)(2,1)}, bf16[2,192,256]{2,1,0:T(8,128)(2,1)S(1)}, u32[]{:S(2)}, u32[]{:S(2)}) collective-permute-start(bf16[2,192,256]{2,1,0:T(8,128)(2,1)} %get-tuple-element.46), channel_id=1, source_target_pairs={{0,3},{1,0},{2,1},{3,2},{4,7},{5,4},{6,5},{7,6},{8,11},{9,8},{10,9... | collective-permute-start | bytes 589832 | tf_op jit(solution)/shard_map/ppermute | solution.py:440
  6.1 11.4 %collective-permute-start.5 = (bf16[2,192,256]{2,1,0:T(8,128)(2,1)}, bf16[2,192,256]{2,1,0:T(8,128)(2,1)S(1)}, u32[]{:S(2)}, u32[]{:S(2)}) collective-permute-start(bf16[2,192,256]{2,1,0:T(8,128)(2,1)} %get-tuple-element.47), channel_id=1, source_target_pairs={{0,2},{1,3},{2,0},{3,1},{4,6},{5,7},{6,4},{7,5},{8,10},{9,11},{10,... | collective-permute-start | bytes 589832 | tf_op jit(solution)/shard_map/ppermute | solution.py:440
  8.2 1.6 %collective-permute-start.2 = (f32[1,32]{1,0:T(1,128)S(1)}, f32[1,32]{1,0:T(1,128)S(1)}, u32[]{:S(2)}, u32[]{:S(2)}) collective-permute-start(f32[1,32]{1,0:T(1,128)S(1)} %copy-done.6), channel_id=1, source_target_pairs={{0,96},{32,0},{64,32},{96,64},{1,97},{33,1},{65,33},{97,65},{2,98}... | collective-permute-start | bytes 392 | tf_op jit(solution)/shard_map/ppermute | solution.py:451
  8.3 3.5 %collective-permute-start.1 = (f32[1,32]{1,0:T(1,128)S(1)}, f32[1,32]{1,0:T(1,128)S(1)}, u32[]{:S(2)}, u32[]{:S(2)}) collective-permute-start(f32[1,32]{1,0:T(1,128)S(1)} %copy-done.6), channel_id=1, source_target_pairs={{0,64},{32,96},{64,0},{96,32},{1,65},{33,97},{65,1},{97,33},{2,66}... | collective-permute-start | bytes 392 | tf_op jit(solution)/shard_map/ppermute | solution.py:451
  9.8 4.0 %collective-permute-start = (f32[1,32]{1,0:T(1,128)S(1)}, f32[1,32]{1,0:T(1,128)S(1)}, u32[]{:S(2)}, u32[]{:S(2)}) collective-permute-start(f32[1,32]{1,0:T(1,128)S(1)} %copy-done.6), channel_id=1, source_target_pairs={{0,32},{32,64},{64,96},{96,0},{1,33},{33,65},{65,97},{97,1},{2,34}... | collective-permute-start | bytes 392 | tf_op jit(solution)/shard_map/ppermute | solution.py:451
  11.8 10.2 %collective-permute-start.15 = (bf16[2,192,256]{2,1,0:T(8,128)(2,1)S(1)}, bf16[2,192,256]{2,1,0:T(8,128)(2,1)S(1)}, u32[]{:S(2)}, u32[]{:S(2)}) collective-permute-start(bf16[2,192,256]{2,1,0:T(8,128)(2,1)S(1)} %get-tuple-element.62), channel_id=1, source_target_pairs={{0,3},{1,0},{2,1},{3,2},{4,7},{5,4},{6,5},{7,6},{8,11},{9,8},{10,9... | collective-permute-start | bytes 589832 | tf_op jit(solution)/shard_map/ppermute | solution.py:440
  13.8 12.3 %collective-permute-start.16 = (bf16[2,192,256]{2,1,0:T(8,128)(2,1)S(1)}, bf16[2,192,256]{2,1,0:T(8,128)(2,1)S(1)}, u32[]{:S(2)}, u32[]{:S(2)}) collective-permute-start(bf16[2,192,256]{2,1,0:T(8,128)(2,1)S(1)} %get-tuple-element.63), channel_id=1, source_target_pairs={{0,2},{1,3},{2,0},{3,1},{4,6},{5,7},{6,4},{7,5},{8,10},{9,11},{10,... | collective-permute-start | bytes 589832 | tf_op jit(solution)/shard_map/ppermute | solution.py:440
  15.8 4.9 %copy-start.2 = (bf16[1,192,2048]{2,1,0:T(8,128)(2,1)S(1)}, bf16[1,192,2048]{2,1,0:T(8,128)(2,1)}, u32[]{:S(2)}) copy-start(bf16[1,192,2048]{2,1,0:T(8,128)(2,1)} %param.6) | copy-start | bytes 2359300
  15.8 4.9 %copy-start.3 = (bf16[1,192,2048]{2,1,0:T(8,128)(2,1)S(1)}, bf16[1,192,2048]{2,1,0:T(8,128)(2,1)}, u32[]{:S(2)}) copy-start(bf16[1,192,2048]{2,1,0:T(8,128)(2,1)} %param.9) | copy-start | bytes 2359300
  15.8 12.0 %collective-permute-start.14 = (bf16[2,192,256]{2,1,0:T(8,128)(2,1)S(1)}, bf16[2,192,256]{2,1,0:T(8,128)(2,1)S(1)}, u32[]{:S(2)}, u32[]{:S(2)}) collective-permute-start(bf16[2,192,256]{2,1,0:T(8,128)(2,1)S(1)} %get-tuple-element.48.refs_3_), channel_id=1, source_target_pairs={{0,1},{1,2},{2,3},{3,0},{4,5},{5,6},{6,7},{7,4},{8,9},{9,10},{10,1... | collective-permute-start | bytes 589832 | tf_op jit(solution)/shard_map/ppermute | solution.py:440
  17.6 20.8 %collective-permute-start.9 = (bf16[2,576,256]{2,1,0:T(8,128)(2,1)S(1)}, bf16[2,576,256]{2,1,0:T(8,128)(2,1)S(1)}, u32[]{:S(2)}, u32[]{:S(2)}) collective-permute-start(bf16[2,576,256]{2,1,0:T(8,128)(2,1)S(1)} %edge.2.after), channel_id=1, source_target_pairs={{0,4},{1,5},{2,6},{3,7},{4,8},{5,9},{6,10},{7,11},{8,12},{9,13},{1... | collective-permute-start | bytes 1769480 | tf_op jit(solution)/shard_map/ppermute | solution.py:444
  20.8 14.9 %collective-permute-start.6 = (bf16[2,192,256]{2,1,0:T(8,128)(2,1)S(1)}, bf16[2,192,256]{2,1,0:T(8,128)(2,1)S(1)}, u32[]{:S(2)}, u32[]{:S(2)}) collective-permute-start(bf16[2,192,256]{2,1,0:T(8,128)(2,1)S(1)} %get-tuple-element.49.after), channel_id=1, source_target_pairs={{0,1},{1,2},{2,3},{3,0},{4,5},{5,6},{6,7},{7,4},{8,9},{9,10},{10,1... | collective-permute-start | bytes 589832 | tf_op jit(solution)/shard_map/ppermute | solution.py:440
  22.1 9.8 %collective-permute-start.7 = (bf16[2,192,256]{2,1,0:T(8,128)(2,1)S(1)}, bf16[2,192,256]{2,1,0:T(8,128)(2,1)S(1)}, u32[]{:S(2)}, u32[]{:S(2)}) collective-permute-start(bf16[2,192,256]{2,1,0:T(8,128)(2,1)S(1)} %get-tuple-element.54), channel_id=1, source_target_pairs={{0,3},{1,0},{2,1},{3,2},{4,7},{5,4},{6,5},{7,6},{8,11},{9,8},{10,9... | collective-permute-start | bytes 589832 | tf_op jit(solution)/shard_map/ppermute | solution.py:440
  26.1 7.8 %collective-permute-start.8 = (bf16[2,192,256]{2,1,0:T(8,128)(2,1)S(1)}, bf16[2,192,256]{2,1,0:T(8,128)(2,1)S(1)}, u32[]{:S(2)}, u32[]{:S(2)}) collective-permute-start(bf16[2,192,256]{2,1,0:T(8,128)(2,1)S(1)} %get-tuple-element.55), channel_id=1, source_target_pairs={{0,2},{1,3},{2,0},{3,1},{4,6},{5,7},{6,4},{7,5},{8,10},{9,11},{10,... | collective-permute-start | bytes 589832 | tf_op jit(solution)/shard_map/ppermute | solution.py:440
  27.8 27.1 %collective-permute-start.20 = (bf16[2,576,256]{2,1,0:T(8,128)(2,1)S(1)}, bf16[2,576,256]{2,1,0:T(8,128)(2,1)S(1)}, u32[]{:S(2)}, u32[]{:S(2)}) collective-permute-start(bf16[2,576,256]{2,1,0:T(8,128)(2,1)S(1)} %edge.3), channel_id=1, source_target_pairs={{0,4},{1,5},{2,6},{3,7},{4,8},{5,9},{6,10},{7,11},{8,12},{9,13},{1... | collective-permute-start | bytes 1769480 | tf_op jit(solution)/shard_map/ppermute | solution.py:444
  31.8 22.2 %collective-permute-start.17 = (bf16[2,192,256]{2,1,0:T(8,128)(2,1)S(1)}, bf16[2,192,256]{2,1,0:T(8,128)(2,1)S(1)}, u32[]{:S(2)}, u32[]{:S(2)}) collective-permute-start(bf16[2,192,256]{2,1,0:T(8,128)(2,1)S(1)} %get-tuple-element.50.after), channel_id=1, source_target_pairs={{0,1},{1,2},{2,3},{3,0},{4,5},{5,6},{6,7},{7,4},{8,9},{9,10},{10,1... | collective-permute-start | bytes 589832 | tf_op jit(solution)/shard_map/ppermute | solution.py:440
  33.8 17.0 %collective-permute-start.18 = (bf16[2,192,256]{2,1,0:T(8,128)(2,1)S(1)}, bf16[2,192,256]{2,1,0:T(8,128)(2,1)S(1)}, u32[]{:S(2)}, u32[]{:S(2)}) collective-permute-start(bf16[2,192,256]{2,1,0:T(8,128)(2,1)S(1)} %get-tuple-element.64), channel_id=1, source_target_pairs={{0,3},{1,0},{2,1},{3,2},{4,7},{5,4},{6,5},{7,6},{8,11},{9,8},{10,9... | collective-permute-start | bytes 589832 | tf_op jit(solution)/shard_map/ppermute | solution.py:440
  35.7 15.9 %collective-permute-start.19 = (bf16[2,192,256]{2,1,0:T(8,128)(2,1)S(1)}, bf16[2,192,256]{2,1,0:T(8,128)(2,1)S(1)}, u32[]{:S(2)}, u32[]{:S(2)}) collective-permute-start(bf16[2,192,256]{2,1,0:T(8,128)(2,1)S(1)} %get-tuple-element.65), channel_id=1, source_target_pairs={{0,2},{1,3},{2,0},{3,1},{4,6},{5,7},{6,4},{7,5},{8,10},{9,11},{10,... | collective-permute-start | bytes 589832 | tf_op jit(solution)/shard_map/ppermute | solution.py:440
  44.8 16.7 %collective-permute-start.13 = (bf16[2,576,256]{2,1,0:T(8,128)(2,1)S(1)}, bf16[2,576,256]{2,1,0:T(8,128)(2,1)S(1)}, u32[]{:S(2)}, u32[]{:S(2)}) collective-permute-start(bf16[2,576,256]{2,1,0:T(8,128)(2,1)S(1)} %get-tuple-element.61), channel_id=1, source_target_pairs={{0,28},{1,29},{2,30},{3,31},{4,0},{5,1},{6,2},{7,3},{8,4},{9,5},{1... | collective-permute-start | bytes 1769480 | tf_op jit(solution)/shard_map/ppermute | solution.py:444
  50.8 10.6 %collective-permute-start.10 = (bf16[192,256]{1,0:T(8,128)(2,1)S(1)}, bf16[192,256]{1,0:T(8,128)(2,1)S(1)}, u32[]{:S(2)}, u32[]{:S(2)}) collective-permute-start(bf16[192,256]{1,0:T(8,128)(2,1)S(1)} %get-tuple-element.57), channel_id=1, source_target_pairs={{0,1},{1,2},{2,3},{3,0},{4,5},{5,6},{6,7},{7,4},{8,9},{9,10},{10,1... | collective-permute-start | bytes 294920 | tf_op jit(solution)/shard_map/ppermute | solution.py:440
  51.6 9.9 %collective-permute-start.11 = (bf16[192,256]{1,0:T(8,128)(2,1)S(1)}, bf16[192,256]{1,0:T(8,128)(2,1)S(1)}, u32[]{:S(2)}, u32[]{:S(2)}) collective-permute-start(bf16[192,256]{1,0:T(8,128)(2,1)S(1)} %get-tuple-element.58), channel_id=1, source_target_pairs={{0,3},{1,0},{2,1},{3,2},{4,7},{5,4},{6,5},{7,6},{8,11},{9,8},{10,9... | collective-permute-start | bytes 294920 | tf_op jit(solution)/shard_map/ppermute | solution.py:440
  54.1 7.4 %collective-permute-start.12 = (bf16[192,256]{1,0:T(8,128)(2,1)S(1)}, bf16[192,256]{1,0:T(8,128)(2,1)S(1)}, u32[]{:S(2)}, u32[]{:S(2)}) collective-permute-start(bf16[192,256]{1,0:T(8,128)(2,1)S(1)} %get-tuple-element.59), channel_id=1, source_target_pairs={{0,2},{1,3},{2,0},{3,1},{4,6},{5,7},{6,4},{7,5},{8,10},{9,11},{10,... | collective-permute-start | bytes 294920 | tf_op jit(solution)/shard_map/ppermute | solution.py:440
  61.3 12.1 %collective-permute-start.24 = (bf16[2,576,256]{2,1,0:T(8,128)(2,1)S(1)}, bf16[2,576,256]{2,1,0:T(8,128)(2,1)S(1)}, u32[]{:S(2)}, u32[]{:S(2)}) collective-permute-start(bf16[2,576,256]{2,1,0:T(8,128)(2,1)S(1)} %get-tuple-element.76), channel_id=1, source_target_pairs={{0,28},{1,29},{2,30},{3,31},{4,0},{5,1},{6,2},{7,3},{8,4},{9,5},{1... | collective-permute-start | bytes 1769480 | tf_op jit(solution)/shard_map/ppermute | solution.py:444
  61.7 16.8 %collective-permute-start.21 = (bf16[3,192,256]{2,1,0:T(8,128)(2,1)S(1)}, bf16[3,192,256]{2,1,0:T(8,128)(2,1)S(1)}, u32[]{:S(2)}, u32[]{:S(2)}) collective-permute-start(bf16[3,192,256]{2,1,0:T(8,128)(2,1)S(1)} %get-tuple-element.71), channel_id=1, source_target_pairs={{0,1},{1,2},{2,3},{3,0},{4,5},{5,6},{6,7},{7,4},{8,9},{9,10},{10,1... | collective-permute-start | bytes 884744 | tf_op jit(solution)/shard_map/ppermute | solution.py:440
  62.4 16.1 %collective-permute-start.22 = (bf16[3,192,256]{2,1,0:T(8,128)(2,1)S(1)}, bf16[3,192,256]{2,1,0:T(8,128)(2,1)S(1)}, u32[]{:S(2)}, u32[]{:S(2)}) collective-permute-start(bf16[3,192,256]{2,1,0:T(8,128)(2,1)S(1)} %get-tuple-element.72), channel_id=1, source_target_pairs={{0,3},{1,0},{2,1},{3,2},{4,7},{5,4},{6,5},{7,6},{8,11},{9,8},{10,9... | collective-permute-start | bytes 884744 | tf_op jit(solution)/shard_map/ppermute | solution.py:440
  65.0 13.6 %collective-permute-start.23 = (bf16[3,192,256]{2,1,0:T(8,128)(2,1)S(1)}, bf16[3,192,256]{2,1,0:T(8,128)(2,1)S(1)}, u32[]{:S(2)}, u32[]{:S(2)}) collective-permute-start(bf16[3,192,256]{2,1,0:T(8,128)(2,1)S(1)} %get-tuple-element.73), channel_id=1, source_target_pairs={{0,2},{1,3},{2,0},{3,1},{4,6},{5,7},{6,4},{7,5},{8,10},{9,11},{10,... | collective-permute-start | bytes 884744 | tf_op jit(solution)/shard_map/ppermute | solution.py:440
  73.6 12.6 %collective-permute-start.25 = (bf16[2,192,256]{2,1,0:T(8,128)(2,1)S(1)}, bf16[2,192,256]{2,1,0:T(8,128)(2,1)S(1)}, u32[]{:S(2)}, u32[]{:S(2)}) collective-permute-start(bf16[2,192,256]{2,1,0:T(8,128)(2,1)S(1)} %get-tuple-element.78), channel_id=1, source_target_pairs={{0,1},{1,2},{2,3},{3,0},{4,5},{5,6},{6,7},{7,4},{8,9},{9,10},{10,1... | collective-permute-start | bytes 589832 | tf_op jit(solution)/shard_map/ppermute | solution.py:440
  74.5 11.6 %collective-permute-start.26 = (bf16[2,192,256]{2,1,0:T(8,128)(2,1)S(1)}, bf16[2,192,256]{2,1,0:T(8,128)(2,1)S(1)}, u32[]{:S(2)}, u32[]{:S(2)}) collective-permute-start(bf16[2,192,256]{2,1,0:T(8,128)(2,1)S(1)} %get-tuple-element.79), channel_id=1, source_target_pairs={{0,3},{1,0},{2,1},{3,2},{4,7},{5,4},{6,5},{7,6},{8,11},{9,8},{10,9... | collective-permute-start | bytes 589832 | tf_op jit(solution)/shard_map/ppermute | solution.py:440
  78.5 7.6 %collective-permute-start.27 = (bf16[2,192,256]{2,1,0:T(8,128)(2,1)S(1)}, bf16[2,192,256]{2,1,0:T(8,128)(2,1)S(1)}, u32[]{:S(2)}, u32[]{:S(2)}) collective-permute-start(bf16[2,192,256]{2,1,0:T(8,128)(2,1)S(1)} %get-tuple-element.80), channel_id=1, source_target_pairs={{0,2},{1,3},{2,0},{3,1},{4,6},{5,7},{6,4},{7,5},{8,10},{9,11},{10,... | collective-permute-start | bytes 589832 | tf_op jit(solution)/shard_map/ppermute | solution.py:440
  (3 other events, 3.4 us)

commit v7 on v6

--- a/solution.py
+++ b/solution.py
@@ -261,8 +261,8 @@
                 ((dscore, query, key_grad, scale), (prob_half, grad, value_grad, 1.0))
             ):
                 term = lax.dot_general(
-                    left, right, (((0,), (0,)), ((), ())), preferred_element_type=jnp.float32
-                )
+                    right, left, (((0,), (0,)), ((), ())), preferred_element_type=jnp.float32
+                ).T
                 for step in range(STEPS):
                     index = block + step
                     here = slice(index * rows, (index + 1) * rows)

time: 87.4 us -> 86.4 us (0.989)
  Pallas kernels: 18.1 us -> 16 us
    pallas_call x2, Pallas kernels: 12.7 us -> 10.6 us  [attend(): pl.pallas_call(functools.partial(attend_kernel, chunk, total_rows), out_s...]
    ppermute x4, waiting for transfers between devices: 7.7 us -> 8.87 us  [next_row(): return lax.ppermute(value, 'ctx', pairs)]
  transfers between devices with their start and end apart: 28 -> 28, of which waited for: 8 -> 10; matrix products, arithmetic and copies ran while one was open for 0% -> 0% of each run, Pallas kernels for 17% -> 15%
where the time goes in v7:
time: 86.4 us; the launch traced here: 86.2 us
  starting transfers between devices  47.3 us (55%)
  waiting for transfers between devices  21.2 us (25%)
  Pallas kernels  16 us (19%)
  between operations  1.01 us (1%)
    ppermute x21, starting transfers between devices, swap(): return lax.ppermute(value, ('dp', 'ctx'), pairs)  31.9 us
    ppermute x4, starting transfers between devices, next_row(): return lax.ppermute(value, 'ctx', pairs)  12.7 us
    ppermute x21, waiting for transfers between devices, swap(): return lax.ppermute(value, ('dp', 'ctx'), pairs)  11.6 us
    pallas_call x2, Pallas kernels, attend(): pl.pallas_call(functools.partial(attend_kernel, chunk, total_rows), out_s...  10.6 us
    ppermute x4, waiting for transfers between devices, next_row(): return lax.ppermute(value, 'ctx', pairs)  8.87 us
    ppermute x3, starting transfers between devices, shards(): lax.ppermute(text, 'dp', [(source, (source + away) % samples) for source...  2.73 us
    pallas_call x1, Pallas kernels, first_pack(): pl.pallas_call(first_pack_kernel, out_shape=(message,) * (GROUP - 1) + (j...  2.15 us
  transfers between devices with their start and end apart: 28, of which 10 were waited for; matrix products, arithmetic and copies ran while one was open for 0% of the time, Pallas kernels for 15%

profile of v7, /device:TPU:0, one launch (start us, length us, event | category | flops | bytes accessed | tf_op | source)
XLA Modules:
  0.0 86.2 jit_solution(15618769039482358426)
XLA Ops:
  0.7 2.1 %first_pack.1 = (bf16[2,192,256]{2,1,0:T(8,128)(2,1)}, bf16[2,192,256]{2,1,0:T(8,128)(2,1)}, bf16[2,192,256]{2,1,0:T(8,128)(2,1)}, f32[1,32]{1,0:T(1,128)}) custom-call(bf16[192,2048]{1,0:T(8,128)(2,1)} %bitcast.7, bf16[192,2048]{1,0:T(8,128)(2,1)} %bitcast.13, s32[1,32]{1,0:T(1,128)} %lengths_ref.1, s32[1,32]{1,0:T(1,128)} %flags_ref.1), custom_call_target="tpu_custom_call" | custom-call | bytes 1179648 | tf_op jit(solution)/shard_map/first_pack/pallas_call | solution.py:80
  2.8 1.7 %collective-permute-start.3 = (bf16[2,192,256]{2,1,0:T(8,128)(2,1)}, bf16[2,192,256]{2,1,0:T(8,128)(2,1)S(1)}, u32[]{:S(2)}, u32[]{:S(2)}) collective-permute-start(bf16[2,192,256]{2,1,0:T(8,128)(2,1)} %get-tuple-element.45), channel_id=1, source_target_pairs={{0,1},{1,2},{2,3},{3,0},{4,5},{5,6},{6,7},{7,4},{8,9},{9,10},{10,1... | collective-permute-start | bytes 589832 | tf_op jit(solution)/shard_map/ppermute | solution.py:440
  4.5 1.6 %collective-permute-start.4 = (bf16[2,192,256]{2,1,0:T(8,128)(2,1)}, bf16[2,192,256]{2,1,0:T(8,128)(2,1)S(1)}, u32[]{:S(2)}, u32[]{:S(2)}) collective-permute-start(bf16[2,192,256]{2,1,0:T(8,128)(2,1)} %get-tuple-element.46), channel_id=1, source_target_pairs={{0,3},{1,0},{2,1},{3,2},{4,7},{5,4},{6,5},{7,6},{8,11},{9,8},{10,9... | collective-permute-start | bytes 589832 | tf_op jit(solution)/shard_map/ppermute | solution.py:440
  6.1 2.1 %collective-permute-start.5 = (bf16[2,192,256]{2,1,0:T(8,128)(2,1)}, bf16[2,192,256]{2,1,0:T(8,128)(2,1)S(1)}, u32[]{:S(2)}, u32[]{:S(2)}) collective-permute-start(bf16[2,192,256]{2,1,0:T(8,128)(2,1)} %get-tuple-element.47), channel_id=1, source_target_pairs={{0,2},{1,3},{2,0},{3,1},{4,6},{5,7},{6,4},{7,5},{8,10},{9,11},{10,... | collective-permute-start | bytes 589832 | tf_op jit(solution)/shard_map/ppermute | solution.py:440
  8.3 1.4 %collective-permute-start.1 = (f32[1,32]{1,0:T(1,128)S(1)}, f32[1,32]{1,0:T(1,128)S(1)}, u32[]{:S(2)}, u32[]{:S(2)}) collective-permute-start(f32[1,32]{1,0:T(1,128)S(1)} %copy-done.6), channel_id=1, source_target_pairs={{0,64},{32,96},{64,0},{96,32},{1,65},{33,97},{65,1},{97,33},{2,66}... | collective-permute-start | bytes 392 | tf_op jit(solution)/shard_map/ppermute | solution.py:451
  9.8 1.2 %collective-permute-start = (f32[1,32]{1,0:T(1,128)S(1)}, f32[1,32]{1,0:T(1,128)S(1)}, u32[]{:S(2)}, u32[]{:S(2)}) collective-permute-start(f32[1,32]{1,0:T(1,128)S(1)} %copy-done.6), channel_id=1, source_target_pairs={{0,32},{32,64},{64,96},{96,0},{1,33},{33,65},{65,97},{97,1},{2,34}... | collective-permute-start | bytes 392 | tf_op jit(solution)/shard_map/ppermute | solution.py:451
  11.8 2.0 %collective-permute-start.15 = (bf16[2,192,256]{2,1,0:T(8,128)(2,1)S(1)}, bf16[2,192,256]{2,1,0:T(8,128)(2,1)S(1)}, u32[]{:S(2)}, u32[]{:S(2)}) collective-permute-start(bf16[2,192,256]{2,1,0:T(8,128)(2,1)S(1)} %get-tuple-element.62), channel_id=1, source_target_pairs={{0,3},{1,0},{2,1},{3,2},{4,7},{5,4},{6,5},{7,6},{8,11},{9,8},{10,9... | collective-permute-start | bytes 589832 | tf_op jit(solution)/shard_map/ppermute | solution.py:440
  13.8 2.0 %collective-permute-start.16 = (bf16[2,192,256]{2,1,0:T(8,128)(2,1)S(1)}, bf16[2,192,256]{2,1,0:T(8,128)(2,1)S(1)}, u32[]{:S(2)}, u32[]{:S(2)}) collective-permute-start(bf16[2,192,256]{2,1,0:T(8,128)(2,1)S(1)} %get-tuple-element.63), channel_id=1, source_target_pairs={{0,2},{1,3},{2,0},{3,1},{4,6},{5,7},{6,4},{7,5},{8,10},{9,11},{10,... | collective-permute-start | bytes 589832 | tf_op jit(solution)/shard_map/ppermute | solution.py:440
  15.8 1.8 %collective-permute-done.5.three.key_three = bf16[2,192,256]{2,1,0:T(8,128)(2,1)S(1)} collective-permute-done((bf16[2,192,256]{2,1,0:T(8,128)(2,1)}, bf16[2,192,256]{2,1,0:T(8,128)(2,1)S(1)}, u32[]{:S(2)}, u32[]{:S(2)}) %collective-permute-start.5) | collective-permute-done | bytes 196640 | tf_op jit(solution)/shard_map/ppermute | solution.py:440
  17.6 3.1 %collective-permute-start.9 = (bf16[2,576,256]{2,1,0:T(8,128)(2,1)S(1)}, bf16[2,576,256]{2,1,0:T(8,128)(2,1)S(1)}, u32[]{:S(2)}, u32[]{:S(2)}) collective-permute-start(bf16[2,576,256]{2,1,0:T(8,128)(2,1)S(1)} %edge.2.after), channel_id=1, source_target_pairs={{0,4},{1,5},{2,6},{3,7},{4,8},{5,9},{6,10},{7,11},{8,12},{9,13},{1... | collective-permute-start | bytes 1769480 | tf_op jit(solution)/shard_map/ppermute | solution.py:444
  22.1 4.0 %collective-permute-start.7 = (bf16[2,192,256]{2,1,0:T(8,128)(2,1)S(1)}, bf16[2,192,256]{2,1,0:T(8,128)(2,1)S(1)}, u32[]{:S(2)}, u32[]{:S(2)}) collective-permute-start(bf16[2,192,256]{2,1,0:T(8,128)(2,1)S(1)} %get-tuple-element.54), channel_id=1, source_target_pairs={{0,3},{1,0},{2,1},{3,2},{4,7},{5,4},{6,5},{7,6},{8,11},{9,8},{10,9... | collective-permute-start | bytes 589832 | tf_op jit(solution)/shard_map/ppermute | solution.py:440
  26.1 1.7 %collective-permute-start.8 = (bf16[2,192,256]{2,1,0:T(8,128)(2,1)S(1)}, bf16[2,192,256]{2,1,0:T(8,128)(2,1)S(1)}, u32[]{:S(2)}, u32[]{:S(2)}) collective-permute-start(bf16[2,192,256]{2,1,0:T(8,128)(2,1)S(1)} %get-tuple-element.55), channel_id=1, source_target_pairs={{0,2},{1,3},{2,0},{3,1},{4,6},{5,7},{6,4},{7,5},{8,10},{9,11},{10,... | collective-permute-start | bytes 589832 | tf_op jit(solution)/shard_map/ppermute | solution.py:440
  27.8 2.6 %collective-permute-start.20 = (bf16[2,576,256]{2,1,0:T(8,128)(2,1)S(1)}, bf16[2,576,256]{2,1,0:T(8,128)(2,1)S(1)}, u32[]{:S(2)}, u32[]{:S(2)}) collective-permute-start(bf16[2,576,256]{2,1,0:T(8,128)(2,1)S(1)} %edge.3), channel_id=1, source_target_pairs={{0,4},{1,5},{2,6},{3,7},{4,8},{5,9},{6,10},{7,11},{8,12},{9,13},{1... | collective-permute-start | bytes 1769480 | tf_op jit(solution)/shard_map/ppermute | solution.py:444
  30.4 1.5 %collective-permute-done.7.query_two = bf16[2,192,256]{2,1,0:T(8,128)(2,1)S(1)} collective-permute-done((bf16[2,192,256]{2,1,0:T(8,128)(2,1)S(1)}, bf16[2,192,256]{2,1,0:T(8,128)(2,1)S(1)}, u32[]{:S(2)}, u32[]{:S(2)}) %collective-permute-start.7) | collective-permute-done | bytes 196640 | tf_op jit(solution)/shard_map/ppermute | solution.py:440
  31.8 1.3 %collective-permute-start.17 = (bf16[2,192,256]{2,1,0:T(8,128)(2,1)S(1)}, bf16[2,192,256]{2,1,0:T(8,128)(2,1)S(1)}, u32[]{:S(2)}, u32[]{:S(2)}) collective-permute-start(bf16[2,192,256]{2,1,0:T(8,128)(2,1)S(1)} %get-tuple-element.50.after), channel_id=1, source_target_pairs={{0,1},{1,2},{2,3},{3,0},{4,5},{5,6},{6,7},{7,4},{8,9},{9,10},{10,1... | collective-permute-start | bytes 589832 | tf_op jit(solution)/shard_map/ppermute | solution.py:440
  33.8 1.8 %collective-permute-start.18 = (bf16[2,192,256]{2,1,0:T(8,128)(2,1)S(1)}, bf16[2,192,256]{2,1,0:T(8,128)(2,1)S(1)}, u32[]{:S(2)}, u32[]{:S(2)}) collective-permute-start(bf16[2,192,256]{2,1,0:T(8,128)(2,1)S(1)} %get-tuple-element.64), channel_id=1, source_target_pairs={{0,3},{1,0},{2,1},{3,2},{4,7},{5,4},{6,5},{7,6},{8,11},{9,8},{10,9... | collective-permute-start | bytes 589832 | tf_op jit(solution)/shard_map/ppermute | solution.py:440
  35.7 1.9 %collective-permute-start.19 = (bf16[2,192,256]{2,1,0:T(8,128)(2,1)S(1)}, bf16[2,192,256]{2,1,0:T(8,128)(2,1)S(1)}, u32[]{:S(2)}, u32[]{:S(2)}) collective-permute-start(bf16[2,192,256]{2,1,0:T(8,128)(2,1)S(1)} %get-tuple-element.65), channel_id=1, source_target_pairs={{0,2},{1,3},{2,0},{3,1},{4,6},{5,7},{6,4},{7,5},{8,10},{9,11},{10,... | collective-permute-start | bytes 589832 | tf_op jit(solution)/shard_map/ppermute | solution.py:440
  37.6 0.8 collective-permute-done.9.edge_ref
  38.4 5.3 %attend.2 = (bf16[192,256]{1,0:T(8,128)(2,1)S(1)}, bf16[192,256]{1,0:T(8,128)(2,1)S(1)}, bf16[192,256]{1,0:T(8,128)(2,1)S(1)}, bf16[192,256]{1,0:T(8,128)(2,1)S(...) custom-call(f32[1,32]{1,0:T(1,128)S(1)} %copy-done.6, ...), custom_call_target="tpu_custom_call" | custom-call | flops 4499999744 | tf_op jit(solution)/shard_map/attend/pallas_call | solution.py:289
  43.7 6.0 %collective-permute-start.13 = (bf16[2,576,256]{2,1,0:T(8,128)(2,1)S(1)}, bf16[2,576,256]{2,1,0:T(8,128)(2,1)S(1)}, u32[]{:S(2)}, u32[]{:S(2)}) collective-permute-start(bf16[2,576,256]{2,1,0:T(8,128)(2,1)S(1)} %get-tuple-element.61), channel_id=1, source_target_pairs={{0,28},{1,29},{2,30},{3,31},{4,0},{5,1},{6,2},{7,3},{8,4},{9,5},{1... | collective-permute-start | bytes 1769480 | tf_op jit(solution)/shard_map/ppermute | solution.py:444
  50.5 2.5 %collective-permute-start.11 = (bf16[192,256]{1,0:T(8,128)(2,1)S(1)}, bf16[192,256]{1,0:T(8,128)(2,1)S(1)}, u32[]{:S(2)}, u32[]{:S(2)}) collective-permute-start(bf16[192,256]{1,0:T(8,128)(2,1)S(1)} %get-tuple-element.58), channel_id=1, source_target_pairs={{0,3},{1,0},{2,1},{3,2},{4,7},{5,4},{6,5},{7,6},{8,11},{9,8},{10,9... | collective-permute-start | bytes 294920 | tf_op jit(solution)/shard_map/ppermute | solution.py:440
  53.0 0.9 collective-permute-start.12
  53.9 5.3 %attend.3 = (bf16[192,256]{1,0:T(8,128)(2,1)S(1)}, bf16[192,256]{1,0:T(8,128)(2,1)S(1)}, bf16[192,256]{1,0:T(8,128)(2,1)S(1)}, bf16[192,256]{1,0:T(8,128)(2,1)S(...) custom-call(f32[1,32]{1,0:T(1,128)S(1)} %copy-done.6, ...), custom_call_target="tpu_custom_call" | custom-call | flops 4499999744 | tf_op jit(solution)/shard_map/attend/pallas_call | solution.py:289
  59.2 1.0 %collective-permute-start.24 = (bf16[2,576,256]{2,1,0:T(8,128)(2,1)S(1)}, bf16[2,576,256]{2,1,0:T(8,128)(2,1)S(1)}, u32[]{:S(2)}, u32[]{:S(2)}) collective-permute-start(bf16[2,576,256]{2,1,0:T(8,128)(2,1)S(1)} %get-tuple-element.76), channel_id=1, source_target_pairs={{0,28},{1,29},{2,30},{3,31},{4,0},{5,1},{6,2},{7,3},{8,4},{9,5},{1... | collective-permute-start | bytes 1769480 | tf_op jit(solution)/shard_map/ppermute | solution.py:444
  60.2 0.9 %collective-permute-done.13.far_ref = bf16[2,576,256]{2,1,0:T(8,128)(2,1)S(1)} collective-permute-done((bf16[2,576,256]{2,1,0:T(8,128)(2,1)S(1)}, bf16[2,576,256]{2,1,0:T(8,128)(2,1)S(1)}, u32[]{:S(2)}, u32[]{:S(2)}) %collective-permute-start.13) | collective-permute-done | bytes 589856 | tf_op jit(solution)/shard_map/ppermute | solution.py:444
  61.4 3.2 %collective-permute-start.22 = (bf16[3,192,256]{2,1,0:T(8,128)(2,1)S(1)}, bf16[3,192,256]{2,1,0:T(8,128)(2,1)S(1)}, u32[]{:S(2)}, u32[]{:S(2)}) collective-permute-start(bf16[3,192,256]{2,1,0:T(8,128)(2,1)S(1)} %get-tuple-element.72), channel_id=1, source_target_pairs={{0,3},{1,0},{2,1},{3,2},{4,7},{5,4},{6,5},{7,6},{8,11},{9,8},{10,9... | collective-permute-start | bytes 884744 | tf_op jit(solution)/shard_map/ppermute | solution.py:440
  64.6 0.8 collective-permute-start.23
  65.5 7.1 %collective-permute-done.24.far_ref = bf16[2,576,256]{2,1,0:T(8,128)(2,1)S(1)} collective-permute-done((bf16[2,576,256]{2,1,0:T(8,128)(2,1)S(1)}, bf16[2,576,256]{2,1,0:T(8,128)(2,1)S(1)}, u32[]{:S(2)}, u32[]{:S(2)}) %collective-permute-start.24) | collective-permute-done | bytes 589856 | tf_op jit(solution)/shard_map/ppermute | solution.py:444
  73.3 2.8 %collective-permute-start.26 = (bf16[2,192,256]{2,1,0:T(8,128)(2,1)S(1)}, bf16[2,192,256]{2,1,0:T(8,128)(2,1)S(1)}, u32[]{:S(2)}, u32[]{:S(2)}) collective-permute-start(bf16[2,192,256]{2,1,0:T(8,128)(2,1)S(1)} %get-tuple-element.79), channel_id=1, source_target_pairs={{0,3},{1,0},{2,1},{3,2},{4,7},{5,4},{6,5},{7,6},{8,11},{9,8},{10,9... | collective-permute-start | bytes 589832 | tf_op jit(solution)/shard_map/ppermute | solution.py:440
  77.4 1.3 %early.1 = (bf16[192,2048]{1,0:T(8,128)(2,1)}, bf16[192,2048]{1,0:T(8,128)(2,1)}, bf16[192,2048]{1,0:T(8,128)(2,1)}) custom-call(bf16[192,256]{1,0:T(8,128)(2,1)S(1)} %get-tuple-element.56.refs_0_, bf16[192,256]{1,0:T(8,128)(2,1)S(1)} %collective-permute-done.10.refs_4_.refs_1_, bf16[192,256]{1,0:T(8,128)(2,1)S(1)} %collective-permute-done.11.refs_5_.refs_2_, ...), custom_call_target="tpu_custom_call" | custom-call | bytes 2359296 | tf_op jit(solution)/shard_map/early/pallas_call | solution.py:402
  78.7 6.5 %collective-permute-done.25.refs_1_ = bf16[2,192,256]{2,1,0:T(8,128)(2,1)S(1)} collective-permute-done((bf16[2,192,256]{2,1,0:T(8,128)(2,1)S(1)}, bf16[2,192,256]{2,1,0:T(8,128)(2,1)S(1)}, u32[]{:S(2)}, u32[]{:S(2)}) %collective-permute-start.25) | collective-permute-done | bytes 196640 | tf_op jit(solution)/shard_map/ppermute | solution.py:440
  85.1 0.9 %late.1 = (bf16[192,2048]{1,0:T(8,128)(2,1)}, bf16[192,2048]{1,0:T(8,128)(2,1)}) custom-call(bf16[2,192,256]{2,1,0:T(8,128)(2,1)S(1)} %get-tuple-element.77.refs_0_, bf16[2,192,256]{2,1,0:T(8,128)(2,1)S(1)} %collective-permute-done.25.refs_1_, ...), custom_call_target="tpu_custom_call", output_to_operand_aliasing={{0}: (4, {}), {1}: (5, {})} | custom-call | bytes 2359296 | tf_op jit(solution)/shard_map/late/pallas_call | solution.py:412
  (51 shorter events, 6.2 us)
Async XLA Ops:
  0.6 9.1 %copy-start = (bf16[1,192,2048]{2,1,0:T(8,128)(2,1)S(1)}, bf16[1,192,2048]{2,1,0:T(8,128)(2,1)}, u32[]{:S(2)}) copy-start(bf16[1,192,2048]{2,1,0:T(8,128)(2,1)} %param.7) | copy-start | bytes 2359300
  0.6 9.0 %copy-start.1 = (bf16[1,192,2048]{2,1,0:T(8,128)(2,1)S(1)}, bf16[1,192,2048]{2,1,0:T(8,128)(2,1)}, u32[]{:S(2)}) copy-start(bf16[1,192,2048]{2,1,0:T(8,128)(2,1)} %param.8) | copy-start | bytes 2359300
  2.8 13.0 %collective-permute-start.3 = (bf16[2,192,256]{2,1,0:T(8,128)(2,1)}, bf16[2,192,256]{2,1,0:T(8,128)(2,1)S(1)}, u32[]{:S(2)}, u32[]{:S(2)}) collective-permute-start(bf16[2,192,256]{2,1,0:T(8,128)(2,1)} %get-tuple-element.45), channel_id=1, source_target_pairs={{0,1},{1,2},{2,3},{3,0},{4,5},{5,6},{6,7},{7,4},{8,9},{9,10},{10,1... | collective-permute-start | bytes 589832 | tf_op jit(solution)/shard_map/ppermute | solution.py:440
  4.5 11.3 %collective-permute-start.4 = (bf16[2,192,256]{2,1,0:T(8,128)(2,1)}, bf16[2,192,256]{2,1,0:T(8,128)(2,1)S(1)}, u32[]{:S(2)}, u32[]{:S(2)}) collective-permute-start(bf16[2,192,256]{2,1,0:T(8,128)(2,1)} %get-tuple-element.46), channel_id=1, source_target_pairs={{0,3},{1,0},{2,1},{3,2},{4,7},{5,4},{6,5},{7,6},{8,11},{9,8},{10,9... | collective-permute-start | bytes 589832 | tf_op jit(solution)/shard_map/ppermute | solution.py:440
  6.1 11.4 %collective-permute-start.5 = (bf16[2,192,256]{2,1,0:T(8,128)(2,1)}, bf16[2,192,256]{2,1,0:T(8,128)(2,1)S(1)}, u32[]{:S(2)}, u32[]{:S(2)}) collective-permute-start(bf16[2,192,256]{2,1,0:T(8,128)(2,1)} %get-tuple-element.47), channel_id=1, source_target_pairs={{0,2},{1,3},{2,0},{3,1},{4,6},{5,7},{6,4},{7,5},{8,10},{9,11},{10,... | collective-permute-start | bytes 589832 | tf_op jit(solution)/shard_map/ppermute | solution.py:440
  8.2 1.6 %collective-permute-start.2 = (f32[1,32]{1,0:T(1,128)S(1)}, f32[1,32]{1,0:T(1,128)S(1)}, u32[]{:S(2)}, u32[]{:S(2)}) collective-permute-start(f32[1,32]{1,0:T(1,128)S(1)} %copy-done.6), channel_id=1, source_target_pairs={{0,96},{32,0},{64,32},{96,64},{1,97},{33,1},{65,33},{97,65},{2,98}... | collective-permute-start | bytes 392 | tf_op jit(solution)/shard_map/ppermute | solution.py:451
  8.3 3.5 %collective-permute-start.1 = (f32[1,32]{1,0:T(1,128)S(1)}, f32[1,32]{1,0:T(1,128)S(1)}, u32[]{:S(2)}, u32[]{:S(2)}) collective-permute-start(f32[1,32]{1,0:T(1,128)S(1)} %copy-done.6), channel_id=1, source_target_pairs={{0,64},{32,96},{64,0},{96,32},{1,65},{33,97},{65,1},{97,33},{2,66}... | collective-permute-start | bytes 392 | tf_op jit(solution)/shard_map/ppermute | solution.py:451
  9.8 4.0 %collective-permute-start = (f32[1,32]{1,0:T(1,128)S(1)}, f32[1,32]{1,0:T(1,128)S(1)}, u32[]{:S(2)}, u32[]{:S(2)}) collective-permute-start(f32[1,32]{1,0:T(1,128)S(1)} %copy-done.6), channel_id=1, source_target_pairs={{0,32},{32,64},{64,96},{96,0},{1,33},{33,65},{65,97},{97,1},{2,34}... | collective-permute-start | bytes 392 | tf_op jit(solution)/shard_map/ppermute | solution.py:451
  11.8 10.2 %collective-permute-start.15 = (bf16[2,192,256]{2,1,0:T(8,128)(2,1)S(1)}, bf16[2,192,256]{2,1,0:T(8,128)(2,1)S(1)}, u32[]{:S(2)}, u32[]{:S(2)}) collective-permute-start(bf16[2,192,256]{2,1,0:T(8,128)(2,1)S(1)} %get-tuple-element.62), channel_id=1, source_target_pairs={{0,3},{1,0},{2,1},{3,2},{4,7},{5,4},{6,5},{7,6},{8,11},{9,8},{10,9... | collective-permute-start | bytes 589832 | tf_op jit(solution)/shard_map/ppermute | solution.py:440
  13.8 12.3 %collective-permute-start.16 = (bf16[2,192,256]{2,1,0:T(8,128)(2,1)S(1)}, bf16[2,192,256]{2,1,0:T(8,128)(2,1)S(1)}, u32[]{:S(2)}, u32[]{:S(2)}) collective-permute-start(bf16[2,192,256]{2,1,0:T(8,128)(2,1)S(1)} %get-tuple-element.63), channel_id=1, source_target_pairs={{0,2},{1,3},{2,0},{3,1},{4,6},{5,7},{6,4},{7,5},{8,10},{9,11},{10,... | collective-permute-start | bytes 589832 | tf_op jit(solution)/shard_map/ppermute | solution.py:440
  15.8 4.9 %copy-start.2 = (bf16[1,192,2048]{2,1,0:T(8,128)(2,1)S(1)}, bf16[1,192,2048]{2,1,0:T(8,128)(2,1)}, u32[]{:S(2)}) copy-start(bf16[1,192,2048]{2,1,0:T(8,128)(2,1)} %param.6) | copy-start | bytes 2359300
  15.8 4.9 %copy-start.3 = (bf16[1,192,2048]{2,1,0:T(8,128)(2,1)S(1)}, bf16[1,192,2048]{2,1,0:T(8,128)(2,1)}, u32[]{:S(2)}) copy-start(bf16[1,192,2048]{2,1,0:T(8,128)(2,1)} %param.9) | copy-start | bytes 2359300
  15.8 12.0 %collective-permute-start.14 = (bf16[2,192,256]{2,1,0:T(8,128)(2,1)S(1)}, bf16[2,192,256]{2,1,0:T(8,128)(2,1)S(1)}, u32[]{:S(2)}, u32[]{:S(2)}) collective-permute-start(bf16[2,192,256]{2,1,0:T(8,128)(2,1)S(1)} %get-tuple-element.48.refs_3_), channel_id=1, source_target_pairs={{0,1},{1,2},{2,3},{3,0},{4,5},{5,6},{6,7},{7,4},{8,9},{9,10},{10,1... | collective-permute-start | bytes 589832 | tf_op jit(solution)/shard_map/ppermute | solution.py:440
  17.6 20.8 %collective-permute-start.9 = (bf16[2,576,256]{2,1,0:T(8,128)(2,1)S(1)}, bf16[2,576,256]{2,1,0:T(8,128)(2,1)S(1)}, u32[]{:S(2)}, u32[]{:S(2)}) collective-permute-start(bf16[2,576,256]{2,1,0:T(8,128)(2,1)S(1)} %edge.2.after), channel_id=1, source_target_pairs={{0,4},{1,5},{2,6},{3,7},{4,8},{5,9},{6,10},{7,11},{8,12},{9,13},{1... | collective-permute-start | bytes 1769480 | tf_op jit(solution)/shard_map/ppermute | solution.py:444
  20.8 14.9 %collective-permute-start.6 = (bf16[2,192,256]{2,1,0:T(8,128)(2,1)S(1)}, bf16[2,192,256]{2,1,0:T(8,128)(2,1)S(1)}, u32[]{:S(2)}, u32[]{:S(2)}) collective-permute-start(bf16[2,192,256]{2,1,0:T(8,128)(2,1)S(1)} %get-tuple-element.49.after), channel_id=1, source_target_pairs={{0,1},{1,2},{2,3},{3,0},{4,5},{5,6},{6,7},{7,4},{8,9},{9,10},{10,1... | collective-permute-start | bytes 589832 | tf_op jit(solution)/shard_map/ppermute | solution.py:440
  22.1 9.8 %collective-permute-start.7 = (bf16[2,192,256]{2,1,0:T(8,128)(2,1)S(1)}, bf16[2,192,256]{2,1,0:T(8,128)(2,1)S(1)}, u32[]{:S(2)}, u32[]{:S(2)}) collective-permute-start(bf16[2,192,256]{2,1,0:T(8,128)(2,1)S(1)} %get-tuple-element.54), channel_id=1, source_target_pairs={{0,3},{1,0},{2,1},{3,2},{4,7},{5,4},{6,5},{7,6},{8,11},{9,8},{10,9... | collective-permute-start | bytes 589832 | tf_op jit(solution)/shard_map/ppermute | solution.py:440
  26.1 7.8 %collective-permute-start.8 = (bf16[2,192,256]{2,1,0:T(8,128)(2,1)S(1)}, bf16[2,192,256]{2,1,0:T(8,128)(2,1)S(1)}, u32[]{:S(2)}, u32[]{:S(2)}) collective-permute-start(bf16[2,192,256]{2,1,0:T(8,128)(2,1)S(1)} %get-tuple-element.55), channel_id=1, source_target_pairs={{0,2},{1,3},{2,0},{3,1},{4,6},{5,7},{6,4},{7,5},{8,10},{9,11},{10,... | collective-permute-start | bytes 589832 | tf_op jit(solution)/shard_map/ppermute | solution.py:440
  27.8 26.1 %collective-permute-start.20 = (bf16[2,576,256]{2,1,0:T(8,128)(2,1)S(1)}, bf16[2,576,256]{2,1,0:T(8,128)(2,1)S(1)}, u32[]{:S(2)}, u32[]{:S(2)}) collective-permute-start(bf16[2,576,256]{2,1,0:T(8,128)(2,1)S(1)} %edge.3), channel_id=1, source_target_pairs={{0,4},{1,5},{2,6},{3,7},{4,8},{5,9},{6,10},{7,11},{8,12},{9,13},{1... | collective-permute-start | bytes 1769480 | tf_op jit(solution)/shard_map/ppermute | solution.py:444
  31.8 21.2 %collective-permute-start.17 = (bf16[2,192,256]{2,1,0:T(8,128)(2,1)S(1)}, bf16[2,192,256]{2,1,0:T(8,128)(2,1)S(1)}, u32[]{:S(2)}, u32[]{:S(2)}) collective-permute-start(bf16[2,192,256]{2,1,0:T(8,128)(2,1)S(1)} %get-tuple-element.50.after), channel_id=1, source_target_pairs={{0,1},{1,2},{2,3},{3,0},{4,5},{5,6},{6,7},{7,4},{8,9},{9,10},{10,1... | collective-permute-start | bytes 589832 | tf_op jit(solution)/shard_map/ppermute | solution.py:440
  33.8 15.9 %collective-permute-start.18 = (bf16[2,192,256]{2,1,0:T(8,128)(2,1)S(1)}, bf16[2,192,256]{2,1,0:T(8,128)(2,1)S(1)}, u32[]{:S(2)}, u32[]{:S(2)}) collective-permute-start(bf16[2,192,256]{2,1,0:T(8,128)(2,1)S(1)} %get-tuple-element.64), channel_id=1, source_target_pairs={{0,3},{1,0},{2,1},{3,2},{4,7},{5,4},{6,5},{7,6},{8,11},{9,8},{10,9... | collective-permute-start | bytes 589832 | tf_op jit(solution)/shard_map/ppermute | solution.py:440
  35.7 14.8 %collective-permute-start.19 = (bf16[2,192,256]{2,1,0:T(8,128)(2,1)S(1)}, bf16[2,192,256]{2,1,0:T(8,128)(2,1)S(1)}, u32[]{:S(2)}, u32[]{:S(2)}) collective-permute-start(bf16[2,192,256]{2,1,0:T(8,128)(2,1)S(1)} %get-tuple-element.65), channel_id=1, source_target_pairs={{0,2},{1,3},{2,0},{3,1},{4,6},{5,7},{6,4},{7,5},{8,10},{9,11},{10,... | collective-permute-start | bytes 589832 | tf_op jit(solution)/shard_map/ppermute | solution.py:440
  43.7 17.4 %collective-permute-start.13 = (bf16[2,576,256]{2,1,0:T(8,128)(2,1)S(1)}, bf16[2,576,256]{2,1,0:T(8,128)(2,1)S(1)}, u32[]{:S(2)}, u32[]{:S(2)}) collective-permute-start(bf16[2,576,256]{2,1,0:T(8,128)(2,1)S(1)} %get-tuple-element.61), channel_id=1, source_target_pairs={{0,28},{1,29},{2,30},{3,31},{4,0},{5,1},{6,2},{7,3},{8,4},{9,5},{1... | collective-permute-start | bytes 1769480 | tf_op jit(solution)/shard_map/ppermute | solution.py:444
  49.8 10.4 %collective-permute-start.10 = (bf16[192,256]{1,0:T(8,128)(2,1)S(1)}, bf16[192,256]{1,0:T(8,128)(2,1)S(1)}, u32[]{:S(2)}, u32[]{:S(2)}) collective-permute-start(bf16[192,256]{1,0:T(8,128)(2,1)S(1)} %get-tuple-element.57), channel_id=1, source_target_pairs={{0,1},{1,2},{2,3},{3,0},{4,5},{5,6},{6,7},{7,4},{8,9},{9,10},{10,1... | collective-permute-start | bytes 294920 | tf_op jit(solution)/shard_map/ppermute | solution.py:440
  50.5 9.7 %collective-permute-start.11 = (bf16[192,256]{1,0:T(8,128)(2,1)S(1)}, bf16[192,256]{1,0:T(8,128)(2,1)S(1)}, u32[]{:S(2)}, u32[]{:S(2)}) collective-permute-start(bf16[192,256]{1,0:T(8,128)(2,1)S(1)} %get-tuple-element.58), channel_id=1, source_target_pairs={{0,3},{1,0},{2,1},{3,2},{4,7},{5,4},{6,5},{7,6},{8,11},{9,8},{10,9... | collective-permute-start | bytes 294920 | tf_op jit(solution)/shard_map/ppermute | solution.py:440
  53.0 7.2 %collective-permute-start.12 = (bf16[192,256]{1,0:T(8,128)(2,1)S(1)}, bf16[192,256]{1,0:T(8,128)(2,1)S(1)}, u32[]{:S(2)}, u32[]{:S(2)}) collective-permute-start(bf16[192,256]{1,0:T(8,128)(2,1)S(1)} %get-tuple-element.59), channel_id=1, source_target_pairs={{0,2},{1,3},{2,0},{3,1},{4,6},{5,7},{6,4},{7,5},{8,10},{9,11},{10,... | collective-permute-start | bytes 294920 | tf_op jit(solution)/shard_map/ppermute | solution.py:440
  59.2 13.4 %collective-permute-start.24 = (bf16[2,576,256]{2,1,0:T(8,128)(2,1)S(1)}, bf16[2,576,256]{2,1,0:T(8,128)(2,1)S(1)}, u32[]{:S(2)}, u32[]{:S(2)}) collective-permute-start(bf16[2,576,256]{2,1,0:T(8,128)(2,1)S(1)} %get-tuple-element.76), channel_id=1, source_target_pairs={{0,28},{1,29},{2,30},{3,31},{4,0},{5,1},{6,2},{7,3},{8,4},{9,5},{1... | collective-permute-start | bytes 1769480 | tf_op jit(solution)/shard_map/ppermute | solution.py:444
  61.3 15.2 %collective-permute-start.21 = (bf16[3,192,256]{2,1,0:T(8,128)(2,1)S(1)}, bf16[3,192,256]{2,1,0:T(8,128)(2,1)S(1)}, u32[]{:S(2)}, u32[]{:S(2)}) collective-permute-start(bf16[3,192,256]{2,1,0:T(8,128)(2,1)S(1)} %get-tuple-element.71), channel_id=1, source_target_pairs={{0,1},{1,2},{2,3},{3,0},{4,5},{5,6},{6,7},{7,4},{8,9},{9,10},{10,1... | collective-permute-start | bytes 884744 | tf_op jit(solution)/shard_map/ppermute | solution.py:440
  61.4 15.2 %collective-permute-start.22 = (bf16[3,192,256]{2,1,0:T(8,128)(2,1)S(1)}, bf16[3,192,256]{2,1,0:T(8,128)(2,1)S(1)}, u32[]{:S(2)}, u32[]{:S(2)}) collective-permute-start(bf16[3,192,256]{2,1,0:T(8,128)(2,1)S(1)} %get-tuple-element.72), channel_id=1, source_target_pairs={{0,3},{1,0},{2,1},{3,2},{4,7},{5,4},{6,5},{7,6},{8,11},{9,8},{10,9... | collective-permute-start | bytes 884744 | tf_op jit(solution)/shard_map/ppermute | solution.py:440
  64.6 12.8 %collective-permute-start.23 = (bf16[3,192,256]{2,1,0:T(8,128)(2,1)S(1)}, bf16[3,192,256]{2,1,0:T(8,128)(2,1)S(1)}, u32[]{:S(2)}, u32[]{:S(2)}) collective-permute-start(bf16[3,192,256]{2,1,0:T(8,128)(2,1)S(1)} %get-tuple-element.73), channel_id=1, source_target_pairs={{0,2},{1,3},{2,0},{3,1},{4,6},{5,7},{6,4},{7,5},{8,10},{9,11},{10,... | collective-permute-start | bytes 884744 | tf_op jit(solution)/shard_map/ppermute | solution.py:440
  72.8 12.4 %collective-permute-start.25 = (bf16[2,192,256]{2,1,0:T(8,128)(2,1)S(1)}, bf16[2,192,256]{2,1,0:T(8,128)(2,1)S(1)}, u32[]{:S(2)}, u32[]{:S(2)}) collective-permute-start(bf16[2,192,256]{2,1,0:T(8,128)(2,1)S(1)} %get-tuple-element.78), channel_id=1, source_target_pairs={{0,1},{1,2},{2,3},{3,0},{4,5},{5,6},{6,7},{7,4},{8,9},{9,10},{10,1... | collective-permute-start | bytes 589832 | tf_op jit(solution)/shard_map/ppermute | solution.py:440
  73.3 11.8 %collective-permute-start.26 = (bf16[2,192,256]{2,1,0:T(8,128)(2,1)S(1)}, bf16[2,192,256]{2,1,0:T(8,128)(2,1)S(1)}, u32[]{:S(2)}, u32[]{:S(2)}) collective-permute-start(bf16[2,192,256]{2,1,0:T(8,128)(2,1)S(1)} %get-tuple-element.79), channel_id=1, source_target_pairs={{0,3},{1,0},{2,1},{3,2},{4,7},{5,4},{6,5},{7,6},{8,11},{9,8},{10,9... | collective-permute-start | bytes 589832 | tf_op jit(solution)/shard_map/ppermute | solution.py:440
  76.5 8.6 %collective-permute-start.27 = (bf16[2,192,256]{2,1,0:T(8,128)(2,1)S(1)}, bf16[2,192,256]{2,1,0:T(8,128)(2,1)S(1)}, u32[]{:S(2)}, u32[]{:S(2)}) collective-permute-start(bf16[2,192,256]{2,1,0:T(8,128)(2,1)S(1)} %get-tuple-element.80), channel_id=1, source_target_pairs={{0,2},{1,3},{2,0},{3,1},{4,6},{5,7},{6,4},{7,5},{8,10},{9,11},{10,... | collective-permute-start | bytes 589832 | tf_op jit(solution)/shard_map/ppermute | solution.py:440
  (3 other events, 3.4 us)

commit v8 on v7

--- a/solution.py
+++ b/solution.py
@@ -23,7 +23,7 @@
 
 def aways():
     core = lax.rem(lax.axis_index("dp"), 2)
-    return 0, 1 + 2 * core, 3 - 2 * core, 2
+    return 0, 2, 1 + 2 * core, 3 - 2 * core
 
 
 def columns(place, away, chunk, width):
@@ -433,7 +433,7 @@
         pairs = []
         for sample in range(samples):
             core = sample % 2
-            away = (1 + 2 * core, 3 - 2 * core, 2)[slot]
+            away = (2, 1 + 2 * core, 3 - 2 * core)[slot]
             for source in range(cycle_size):
                 target = source - source % GROUP + (source + away) % GROUP
                 pairs.append((sample * cycle_size + source, sample * cycle_size + target))

time: 86.4 us -> 89.5 us (1.036)
  waiting for transfers between devices: 21.2 us -> 23.5 us
    ppermute x21, waiting for transfers between devices: 11.6 us -> 15.2 us  [swap(): return lax.ppermute(value, ('dp', 'ctx'), pairs)]
    ppermute x4, waiting for transfers between devices: 8.87 us -> 6.81 us  [next_row(): return lax.ppermute(value, 'ctx', pairs)]
where the time goes in v8:
time: 89.5 us; the launch traced here: 89.2 us
  starting transfers between devices  48 us (54%)
  waiting for transfers between devices  23.5 us (26%)
  Pallas kernels  16 us (18%)
  between operations  1 us (1%)
    ppermute x21, starting transfers between devices, swap(): return lax.ppermute(value, ('dp', 'ctx'), pairs)  31.9 us
    ppermute x21, waiting for transfers between devices, swap(): return lax.ppermute(value, ('dp', 'ctx'), pairs)  15.2 us
    ppermute x4, starting transfers between devices, next_row(): return lax.ppermute(value, 'ctx', pairs)  13.1 us
    pallas_call x2, Pallas kernels, attend(): pl.pallas_call(functools.partial(attend_kernel, chunk, total_rows), out_s...  10.6 us
    ppermute x4, waiting for transfers between devices, next_row(): return lax.ppermute(value, 'ctx', pairs)  6.81 us
    ppermute x3, starting transfers between devices, shards(): lax.ppermute(text, 'dp', [(source, (source + away) % samples) for source...  3.02 us
    pallas_call x1, Pallas kernels, first_pack(): pl.pallas_call(first_pack_kernel, out_shape=(message,) * (GROUP - 1) + (j...  2.15 us
  transfers between devices with their start and end apart: 28, of which 10 were waited for; matrix products, arithmetic and copies ran while one was open for 0% of the time, Pallas kernels for 15%

profile of v8, /device:TPU:0, one launch (start us, length us, event | category | flops | bytes accessed | tf_op | source)
XLA Modules:
  0.0 89.2 jit_solution(4981138476721790545)
XLA Ops:
  0.7 2.1 %first_pack.1 = (bf16[2,192,256]{2,1,0:T(8,128)(2,1)}, bf16[2,192,256]{2,1,0:T(8,128)(2,1)}, bf16[2,192,256]{2,1,0:T(8,128)(2,1)}, f32[1,32]{1,0:T(1,128)}) custom-call(bf16[192,2048]{1,0:T(8,128)(2,1)} %bitcast.7, bf16[192,2048]{1,0:T(8,128)(2,1)} %bitcast.13, s32[1,32]{1,0:T(1,128)} %lengths_ref.1, s32[1,32]{1,0:T(1,128)} %flags_ref.1), custom_call_target="tpu_custom_call" | custom-call | bytes 1179648 | tf_op jit(solution)/shard_map/first_pack/pallas_call | solution.py:80
  2.8 3.4 %collective-permute-start.3 = (bf16[2,192,256]{2,1,0:T(8,128)(2,1)}, bf16[2,192,256]{2,1,0:T(8,128)(2,1)S(1)}, u32[]{:S(2)}, u32[]{:S(2)}) collective-permute-start(bf16[2,192,256]{2,1,0:T(8,128)(2,1)} %get-tuple-element.45), channel_id=1, source_target_pairs={{0,2},{1,3},{2,0},{3,1},{4,6},{5,7},{6,4},{7,5},{8,10},{9,11},{10,... | collective-permute-start | bytes 589832 | tf_op jit(solution)/shard_map/ppermute | solution.py:440
  6.2 0.7 collective-permute-start.4
  6.8 2.6 %collective-permute-start.5 = (bf16[2,192,256]{2,1,0:T(8,128)(2,1)}, bf16[2,192,256]{2,1,0:T(8,128)(2,1)S(1)}, u32[]{:S(2)}, u32[]{:S(2)}) collective-permute-start(bf16[2,192,256]{2,1,0:T(8,128)(2,1)} %get-tuple-element.47), channel_id=1, source_target_pairs={{0,3},{1,0},{2,1},{3,2},{4,7},{5,4},{6,5},{7,6},{8,11},{9,8},{10,9... | collective-permute-start | bytes 589832 | tf_op jit(solution)/shard_map/ppermute | solution.py:440
  9.4 1.5 %collective-permute-start.1 = (f32[1,32]{1,0:T(1,128)S(1)}, f32[1,32]{1,0:T(1,128)S(1)}, u32[]{:S(2)}, u32[]{:S(2)}) collective-permute-start(f32[1,32]{1,0:T(1,128)S(1)} %copy-done.6), channel_id=1, source_target_pairs={{0,64},{32,96},{64,0},{96,32},{1,65},{33,97},{65,1},{97,33},{2,66}... | collective-permute-start | bytes 392 | tf_op jit(solution)/shard_map/ppermute | solution.py:451
  11.0 1.5 %collective-permute-start = (f32[1,32]{1,0:T(1,128)S(1)}, f32[1,32]{1,0:T(1,128)S(1)}, u32[]{:S(2)}, u32[]{:S(2)}) collective-permute-start(f32[1,32]{1,0:T(1,128)S(1)} %copy-done.6), channel_id=1, source_target_pairs={{0,32},{32,64},{64,96},{96,0},{1,33},{33,65},{65,97},{97,1},{2,34}... | collective-permute-start | bytes 392 | tf_op jit(solution)/shard_map/ppermute | solution.py:451
  13.0 1.1 %collective-permute-done.refs_0_.text_two = f32[1,32]{1,0:T(1,128)S(1)} collective-permute-done((f32[1,32]{1,0:T(1,128)S(1)}, f32[1,32]{1,0:T(1,128)S(1)}, u32[]{:S(2)}, u32[]{:S(2)}) %collective-permute-start) | collective-permute-done | bytes 160 | tf_op jit(solution)/shard_map/ppermute | solution.py:451
  14.0 2.2 %collective-permute-start.16 = (bf16[2,192,256]{2,1,0:T(8,128)(2,1)S(1)}, bf16[2,192,256]{2,1,0:T(8,128)(2,1)S(1)}, u32[]{:S(2)}, u32[]{:S(2)}) collective-permute-start(bf16[2,192,256]{2,1,0:T(8,128)(2,1)S(1)} %get-tuple-element.63), channel_id=1, source_target_pairs={{0,3},{1,0},{2,1},{3,2},{4,7},{5,4},{6,5},{7,6},{8,11},{9,8},{10,9... | collective-permute-start | bytes 589832 | tf_op jit(solution)/shard_map/ppermute | solution.py:440
  16.6 3.1 %collective-permute-start.9 = (bf16[2,576,256]{2,1,0:T(8,128)(2,1)S(1)}, bf16[2,576,256]{2,1,0:T(8,128)(2,1)S(1)}, u32[]{:S(2)}, u32[]{:S(2)}) collective-permute-start(bf16[2,576,256]{2,1,0:T(8,128)(2,1)S(1)} %edge.2.after), channel_id=1, source_target_pairs={{0,4},{1,5},{2,6},{3,7},{4,8},{5,9},{6,10},{7,11},{8,12},{9,13},{1... | collective-permute-start | bytes 1769480 | tf_op jit(solution)/shard_map/ppermute | solution.py:444
  19.8 3.3 %collective-permute-start.6 = (bf16[2,192,256]{2,1,0:T(8,128)(2,1)S(1)}, bf16[2,192,256]{2,1,0:T(8,128)(2,1)S(1)}, u32[]{:S(2)}, u32[]{:S(2)}) collective-permute-start(bf16[2,192,256]{2,1,0:T(8,128)(2,1)S(1)} %get-tuple-element.49.after), channel_id=1, source_target_pairs={{0,2},{1,3},{2,0},{3,1},{4,6},{5,7},{6,4},{7,5},{8,10},{9,11},{10,... | collective-permute-start | bytes 589832 | tf_op jit(solution)/shard_map/ppermute | solution.py:440
  24.2 5.9 %collective-permute-done.15.two.key_two = bf16[2,192,256]{2,1,0:T(8,128)(2,1)S(1)} collective-permute-done((bf16[2,192,256]{2,1,0:T(8,128)(2,1)S(1)}, bf16[2,192,256]{2,1,0:T(8,128)(2,1)S(1)}, u32[]{:S(2)}, u32[]{:S(2)}) %collective-permute-start.15) | collective-permute-done | bytes 196640 | tf_op jit(solution)/shard_map/ppermute | solution.py:440
  30.1 3.2 %collective-permute-start.8 = (bf16[2,192,256]{2,1,0:T(8,128)(2,1)S(1)}, bf16[2,192,256]{2,1,0:T(8,128)(2,1)S(1)}, u32[]{:S(2)}, u32[]{:S(2)}) collective-permute-start(bf16[2,192,256]{2,1,0:T(8,128)(2,1)S(1)} %get-tuple-element.55), channel_id=1, source_target_pairs={{0,3},{1,0},{2,1},{3,2},{4,7},{5,4},{6,5},{7,6},{8,11},{9,8},{10,9... | collective-permute-start | bytes 589832 | tf_op jit(solution)/shard_map/ppermute | solution.py:440
  33.4 2.8 %collective-permute-start.20 = (bf16[2,576,256]{2,1,0:T(8,128)(2,1)S(1)}, bf16[2,576,256]{2,1,0:T(8,128)(2,1)S(1)}, u32[]{:S(2)}, u32[]{:S(2)}) collective-permute-start(bf16[2,576,256]{2,1,0:T(8,128)(2,1)S(1)} %edge.3), channel_id=1, source_target_pairs={{0,4},{1,5},{2,6},{3,7},{4,8},{5,9},{6,10},{7,11},{8,12},{9,13},{1... | collective-permute-start | bytes 1769480 | tf_op jit(solution)/shard_map/ppermute | solution.py:444
  36.2 3.8 %collective-permute-done.7.query_two = bf16[2,192,256]{2,1,0:T(8,128)(2,1)S(1)} collective-permute-done((bf16[2,192,256]{2,1,0:T(8,128)(2,1)S(1)}, bf16[2,192,256]{2,1,0:T(8,128)(2,1)S(1)}, u32[]{:S(2)}, u32[]{:S(2)}) %collective-permute-start.7) | collective-permute-done | bytes 196640 | tf_op jit(solution)/shard_map/ppermute | solution.py:440
  40.5 2.8 %collective-permute-start.19 = (bf16[2,192,256]{2,1,0:T(8,128)(2,1)S(1)}, bf16[2,192,256]{2,1,0:T(8,128)(2,1)S(1)}, u32[]{:S(2)}, u32[]{:S(2)}) collective-permute-start(bf16[2,192,256]{2,1,0:T(8,128)(2,1)S(1)} %get-tuple-element.65), channel_id=1, source_target_pairs={{0,3},{1,0},{2,1},{3,2},{4,7},{5,4},{6,5},{7,6},{8,11},{9,8},{10,9... | collective-permute-start | bytes 589832 | tf_op jit(solution)/shard_map/ppermute | solution.py:440
  43.3 5.3 %attend.2 = (bf16[192,256]{1,0:T(8,128)(2,1)S(1)}, bf16[192,256]{1,0:T(8,128)(2,1)S(1)}, bf16[192,256]{1,0:T(8,128)(2,1)S(1)}, bf16[192,256]{1,0:T(8,128)(2,1)S(...) custom-call(f32[1,32]{1,0:T(1,128)S(1)} %copy-done.6, ...), custom_call_target="tpu_custom_call" | custom-call | flops 4499999744 | tf_op jit(solution)/shard_map/attend/pallas_call | solution.py:289
  48.6 6.1 %collective-permute-start.13 = (bf16[2,576,256]{2,1,0:T(8,128)(2,1)S(1)}, bf16[2,576,256]{2,1,0:T(8,128)(2,1)S(1)}, u32[]{:S(2)}, u32[]{:S(2)}) collective-permute-start(bf16[2,576,256]{2,1,0:T(8,128)(2,1)S(1)} %get-tuple-element.61), channel_id=1, source_target_pairs={{0,28},{1,29},{2,30},{3,31},{4,0},{5,1},{6,2},{7,3},{8,4},{9,5},{1... | collective-permute-start | bytes 1769480 | tf_op jit(solution)/shard_map/ppermute | solution.py:444
  54.7 2.3 %collective-permute-start.10 = (bf16[192,256]{1,0:T(8,128)(2,1)S(1)}, bf16[192,256]{1,0:T(8,128)(2,1)S(1)}, u32[]{:S(2)}, u32[]{:S(2)}) collective-permute-start(bf16[192,256]{1,0:T(8,128)(2,1)S(1)} %get-tuple-element.57), channel_id=1, source_target_pairs={{0,2},{1,3},{2,0},{3,1},{4,6},{5,7},{6,4},{7,5},{8,10},{9,11},{10,... | collective-permute-start | bytes 294920 | tf_op jit(solution)/shard_map/ppermute | solution.py:440
  57.0 3.2 %collective-permute-start.12 = (bf16[192,256]{1,0:T(8,128)(2,1)S(1)}, bf16[192,256]{1,0:T(8,128)(2,1)S(1)}, u32[]{:S(2)}, u32[]{:S(2)}) collective-permute-start(bf16[192,256]{1,0:T(8,128)(2,1)S(1)} %get-tuple-element.59), channel_id=1, source_target_pairs={{0,3},{1,0},{2,1},{3,2},{4,7},{5,4},{6,5},{7,6},{8,11},{9,8},{10,9... | collective-permute-start | bytes 294920 | tf_op jit(solution)/shard_map/ppermute | solution.py:440
  60.3 5.3 %attend.3 = (bf16[192,256]{1,0:T(8,128)(2,1)S(1)}, bf16[192,256]{1,0:T(8,128)(2,1)S(1)}, bf16[192,256]{1,0:T(8,128)(2,1)S(1)}, bf16[192,256]{1,0:T(8,128)(2,1)S(...) custom-call(f32[1,32]{1,0:T(1,128)S(1)} %copy-done.6, ...), custom_call_target="tpu_custom_call" | custom-call | flops 4499999744 | tf_op jit(solution)/shard_map/attend/pallas_call | solution.py:289
  65.6 1.1 %collective-permute-start.24 = (bf16[2,576,256]{2,1,0:T(8,128)(2,1)S(1)}, bf16[2,576,256]{2,1,0:T(8,128)(2,1)S(1)}, u32[]{:S(2)}, u32[]{:S(2)}) collective-permute-start(bf16[2,576,256]{2,1,0:T(8,128)(2,1)S(1)} %get-tuple-element.76), channel_id=1, source_target_pairs={{0,28},{1,29},{2,30},{3,31},{4,0},{5,1},{6,2},{7,3},{8,4},{9,5},{1... | collective-permute-start | bytes 1769480 | tf_op jit(solution)/shard_map/ppermute | solution.py:444
  66.6 1.6 %collective-permute-done.13.far_ref = bf16[2,576,256]{2,1,0:T(8,128)(2,1)S(1)} collective-permute-done((bf16[2,576,256]{2,1,0:T(8,128)(2,1)S(1)}, bf16[2,576,256]{2,1,0:T(8,128)(2,1)S(1)}, u32[]{:S(2)}, u32[]{:S(2)}) %collective-permute-start.13) | collective-permute-done | bytes 589856 | tf_op jit(solution)/shard_map/ppermute | solution.py:444
  68.5 0.9 %collective-permute-start.22 = (bf16[3,192,256]{2,1,0:T(8,128)(2,1)S(1)}, bf16[3,192,256]{2,1,0:T(8,128)(2,1)S(1)}, u32[]{:S(2)}, u32[]{:S(2)}) collective-permute-start(bf16[3,192,256]{2,1,0:T(8,128)(2,1)S(1)} %get-tuple-element.72), channel_id=1, source_target_pairs={{0,1},{1,2},{2,3},{3,0},{4,5},{5,6},{6,7},{7,4},{8,9},{9,10},{10,1... | collective-permute-start | bytes 884744 | tf_op jit(solution)/shard_map/ppermute | solution.py:440
  69.4 2.4 %collective-permute-start.23 = (bf16[3,192,256]{2,1,0:T(8,128)(2,1)S(1)}, bf16[3,192,256]{2,1,0:T(8,128)(2,1)S(1)}, u32[]{:S(2)}, u32[]{:S(2)}) collective-permute-start(bf16[3,192,256]{2,1,0:T(8,128)(2,1)S(1)} %get-tuple-element.73), channel_id=1, source_target_pairs={{0,3},{1,0},{2,1},{3,2},{4,7},{5,4},{6,5},{7,6},{8,11},{9,8},{10,9... | collective-permute-start | bytes 884744 | tf_op jit(solution)/shard_map/ppermute | solution.py:440
  71.8 5.2 %collective-permute-done.24.far_ref = bf16[2,576,256]{2,1,0:T(8,128)(2,1)S(1)} collective-permute-done((bf16[2,576,256]{2,1,0:T(8,128)(2,1)S(1)}, bf16[2,576,256]{2,1,0:T(8,128)(2,1)S(1)}, u32[]{:S(2)}, u32[]{:S(2)}) %collective-permute-start.24) | collective-permute-done | bytes 589856 | tf_op jit(solution)/shard_map/ppermute | solution.py:444
  77.2 1.2 %collective-permute-start.25 = (bf16[2,192,256]{2,1,0:T(8,128)(2,1)S(1)}, bf16[2,192,256]{2,1,0:T(8,128)(2,1)S(1)}, u32[]{:S(2)}, u32[]{:S(2)}) collective-permute-start(bf16[2,192,256]{2,1,0:T(8,128)(2,1)S(1)} %get-tuple-element.78), channel_id=1, source_target_pairs={{0,2},{1,3},{2,0},{3,1},{4,6},{5,7},{6,4},{7,5},{8,10},{9,11},{10,... | collective-permute-start | bytes 589832 | tf_op jit(solution)/shard_map/ppermute | solution.py:440
  78.5 1.5 %collective-permute-start.26 = (bf16[2,192,256]{2,1,0:T(8,128)(2,1)S(1)}, bf16[2,192,256]{2,1,0:T(8,128)(2,1)S(1)}, u32[]{:S(2)}, u32[]{:S(2)}) collective-permute-start(bf16[2,192,256]{2,1,0:T(8,128)(2,1)S(1)} %get-tuple-element.79), channel_id=1, source_target_pairs={{0,1},{1,2},{2,3},{3,0},{4,5},{5,6},{6,7},{7,4},{8,9},{9,10},{10,1... | collective-permute-start | bytes 589832 | tf_op jit(solution)/shard_map/ppermute | solution.py:440
  80.0 1.7 %collective-permute-start.27 = (bf16[2,192,256]{2,1,0:T(8,128)(2,1)S(1)}, bf16[2,192,256]{2,1,0:T(8,128)(2,1)S(1)}, u32[]{:S(2)}, u32[]{:S(2)}) collective-permute-start(bf16[2,192,256]{2,1,0:T(8,128)(2,1)S(1)} %get-tuple-element.80), channel_id=1, source_target_pairs={{0,3},{1,0},{2,1},{3,2},{4,7},{5,4},{6,5},{7,6},{8,11},{9,8},{10,9... | collective-permute-start | bytes 589832 | tf_op jit(solution)/shard_map/ppermute | solution.py:440
  82.2 1.3 %early.1 = (bf16[192,2048]{1,0:T(8,128)(2,1)}, bf16[192,2048]{1,0:T(8,128)(2,1)}, bf16[192,2048]{1,0:T(8,128)(2,1)}) custom-call(bf16[192,256]{1,0:T(8,128)(2,1)S(1)} %get-tuple-element.56.refs_0_, bf16[192,256]{1,0:T(8,128)(2,1)S(1)} %collective-permute-done.10.refs_4_.refs_1_, bf16[192,256]{1,0:T(8,128)(2,1)S(1)} %collective-permute-done.11.refs_5_.refs_2_, ...), custom_call_target="tpu_custom_call" | custom-call | bytes 2359296 | tf_op jit(solution)/shard_map/early/pallas_call | solution.py:402
  83.4 2.9 %collective-permute-done.25.refs_1_ = bf16[2,192,256]{2,1,0:T(8,128)(2,1)S(1)} collective-permute-done((bf16[2,192,256]{2,1,0:T(8,128)(2,1)S(1)}, bf16[2,192,256]{2,1,0:T(8,128)(2,1)S(1)}, u32[]{:S(2)}, u32[]{:S(2)}) %collective-permute-start.25) | collective-permute-done | bytes 196640 | tf_op jit(solution)/shard_map/ppermute | solution.py:440
  86.3 1.8 %collective-permute-done.26.refs_2_ = bf16[2,192,256]{2,1,0:T(8,128)(2,1)S(1)} collective-permute-done((bf16[2,192,256]{2,1,0:T(8,128)(2,1)S(1)}, bf16[2,192,256]{2,1,0:T(8,128)(2,1)S(1)}, u32[]{:S(2)}, u32[]{:S(2)}) %collective-permute-start.26) | collective-permute-done | bytes 196640 | tf_op jit(solution)/shard_map/ppermute | solution.py:440
  88.1 0.9 %late.1 = (bf16[192,2048]{1,0:T(8,128)(2,1)}, bf16[192,2048]{1,0:T(8,128)(2,1)}) custom-call(bf16[2,192,256]{2,1,0:T(8,128)(2,1)S(1)} %get-tuple-element.77.refs_0_, bf16[2,192,256]{2,1,0:T(8,128)(2,1)S(1)} %collective-permute-done.25.refs_1_, ...), custom_call_target="tpu_custom_call", output_to_operand_aliasing={{0}: (4, {}), {1}: (5, {})} | custom-call | bytes 2359296 | tf_op jit(solution)/shard_map/late/pallas_call | solution.py:412
  (51 shorter events, 3.5 us)
Async XLA Ops:
  0.6 10.3 %copy-start = (bf16[1,192,2048]{2,1,0:T(8,128)(2,1)S(1)}, bf16[1,192,2048]{2,1,0:T(8,128)(2,1)}, u32[]{:S(2)}) copy-start(bf16[1,192,2048]{2,1,0:T(8,128)(2,1)} %param.7) | copy-start | bytes 2359300
  0.6 10.3 %copy-start.1 = (bf16[1,192,2048]{2,1,0:T(8,128)(2,1)S(1)}, bf16[1,192,2048]{2,1,0:T(8,128)(2,1)}, u32[]{:S(2)}) copy-start(bf16[1,192,2048]{2,1,0:T(8,128)(2,1)} %param.8) | copy-start | bytes 2359300
  2.8 13.4 %collective-permute-start.3 = (bf16[2,192,256]{2,1,0:T(8,128)(2,1)}, bf16[2,192,256]{2,1,0:T(8,128)(2,1)S(1)}, u32[]{:S(2)}, u32[]{:S(2)}) collective-permute-start(bf16[2,192,256]{2,1,0:T(8,128)(2,1)} %get-tuple-element.45), channel_id=1, source_target_pairs={{0,2},{1,3},{2,0},{3,1},{4,6},{5,7},{6,4},{7,5},{8,10},{9,11},{10,... | collective-permute-start | bytes 589832 | tf_op jit(solution)/shard_map/ppermute | solution.py:440
  6.2 10.0 %collective-permute-start.4 = (bf16[2,192,256]{2,1,0:T(8,128)(2,1)}, bf16[2,192,256]{2,1,0:T(8,128)(2,1)S(1)}, u32[]{:S(2)}, u32[]{:S(2)}) collective-permute-start(bf16[2,192,256]{2,1,0:T(8,128)(2,1)} %get-tuple-element.46), channel_id=1, source_target_pairs={{0,1},{1,2},{2,3},{3,0},{4,5},{5,6},{6,7},{7,4},{8,9},{9,10},{10,1... | collective-permute-start | bytes 589832 | tf_op jit(solution)/shard_map/ppermute | solution.py:440
  6.8 9.7 %collective-permute-start.5 = (bf16[2,192,256]{2,1,0:T(8,128)(2,1)}, bf16[2,192,256]{2,1,0:T(8,128)(2,1)S(1)}, u32[]{:S(2)}, u32[]{:S(2)}) collective-permute-start(bf16[2,192,256]{2,1,0:T(8,128)(2,1)} %get-tuple-element.47), channel_id=1, source_target_pairs={{0,3},{1,0},{2,1},{3,2},{4,7},{5,4},{6,5},{7,6},{8,11},{9,8},{10,9... | collective-permute-start | bytes 589832 | tf_op jit(solution)/shard_map/ppermute | solution.py:440
  9.4 1.6 %collective-permute-start.2 = (f32[1,32]{1,0:T(1,128)S(1)}, f32[1,32]{1,0:T(1,128)S(1)}, u32[]{:S(2)}, u32[]{:S(2)}) collective-permute-start(f32[1,32]{1,0:T(1,128)S(1)} %copy-done.6), channel_id=1, source_target_pairs={{0,96},{32,0},{64,32},{96,64},{1,97},{33,1},{65,33},{97,65},{2,98}... | collective-permute-start | bytes 392 | tf_op jit(solution)/shard_map/ppermute | solution.py:451
  9.4 3.5 %collective-permute-start.1 = (f32[1,32]{1,0:T(1,128)S(1)}, f32[1,32]{1,0:T(1,128)S(1)}, u32[]{:S(2)}, u32[]{:S(2)}) collective-permute-start(f32[1,32]{1,0:T(1,128)S(1)} %copy-done.6), channel_id=1, source_target_pairs={{0,64},{32,96},{64,0},{96,32},{1,65},{33,97},{65,1},{97,33},{2,66}... | collective-permute-start | bytes 392 | tf_op jit(solution)/shard_map/ppermute | solution.py:451
  11.0 3.0 %collective-permute-start = (f32[1,32]{1,0:T(1,128)S(1)}, f32[1,32]{1,0:T(1,128)S(1)}, u32[]{:S(2)}, u32[]{:S(2)}) collective-permute-start(f32[1,32]{1,0:T(1,128)S(1)} %copy-done.6), channel_id=1, source_target_pairs={{0,32},{32,64},{64,96},{96,0},{1,33},{33,65},{65,97},{97,1},{2,34}... | collective-permute-start | bytes 392 | tf_op jit(solution)/shard_map/ppermute | solution.py:451
  12.9 17.1 %collective-permute-start.15 = (bf16[2,192,256]{2,1,0:T(8,128)(2,1)S(1)}, bf16[2,192,256]{2,1,0:T(8,128)(2,1)S(1)}, u32[]{:S(2)}, u32[]{:S(2)}) collective-permute-start(bf16[2,192,256]{2,1,0:T(8,128)(2,1)S(1)} %get-tuple-element.62), channel_id=1, source_target_pairs={{0,1},{1,2},{2,3},{3,0},{4,5},{5,6},{6,7},{7,4},{8,9},{9,10},{10,1... | collective-permute-start | bytes 589832 | tf_op jit(solution)/shard_map/ppermute | solution.py:440
  14.0 16.1 %collective-permute-start.16 = (bf16[2,192,256]{2,1,0:T(8,128)(2,1)S(1)}, bf16[2,192,256]{2,1,0:T(8,128)(2,1)S(1)}, u32[]{:S(2)}, u32[]{:S(2)}) collective-permute-start(bf16[2,192,256]{2,1,0:T(8,128)(2,1)S(1)} %get-tuple-element.63), channel_id=1, source_target_pairs={{0,3},{1,0},{2,1},{3,2},{4,7},{5,4},{6,5},{7,6},{8,11},{9,8},{10,9... | collective-permute-start | bytes 589832 | tf_op jit(solution)/shard_map/ppermute | solution.py:440
  16.2 3.5 %copy-start.2 = (bf16[1,192,2048]{2,1,0:T(8,128)(2,1)S(1)}, bf16[1,192,2048]{2,1,0:T(8,128)(2,1)}, u32[]{:S(2)}) copy-start(bf16[1,192,2048]{2,1,0:T(8,128)(2,1)} %param.6) | copy-start | bytes 2359300
  16.2 3.5 %copy-start.3 = (bf16[1,192,2048]{2,1,0:T(8,128)(2,1)S(1)}, bf16[1,192,2048]{2,1,0:T(8,128)(2,1)}, u32[]{:S(2)}) copy-start(bf16[1,192,2048]{2,1,0:T(8,128)(2,1)} %param.9) | copy-start | bytes 2359300
  16.2 17.1 %collective-permute-start.14 = (bf16[2,192,256]{2,1,0:T(8,128)(2,1)S(1)}, bf16[2,192,256]{2,1,0:T(8,128)(2,1)S(1)}, u32[]{:S(2)}, u32[]{:S(2)}) collective-permute-start(bf16[2,192,256]{2,1,0:T(8,128)(2,1)S(1)} %get-tuple-element.48.refs_3_), channel_id=1, source_target_pairs={{0,2},{1,3},{2,0},{3,1},{4,6},{5,7},{6,4},{7,5},{8,10},{9,11},{10,... | collective-permute-start | bytes 589832 | tf_op jit(solution)/shard_map/ppermute | solution.py:440
  16.6 26.7 %collective-permute-start.9 = (bf16[2,576,256]{2,1,0:T(8,128)(2,1)S(1)}, bf16[2,576,256]{2,1,0:T(8,128)(2,1)S(1)}, u32[]{:S(2)}, u32[]{:S(2)}) collective-permute-start(bf16[2,576,256]{2,1,0:T(8,128)(2,1)S(1)} %edge.2.after), channel_id=1, source_target_pairs={{0,4},{1,5},{2,6},{3,7},{4,8},{5,9},{6,10},{7,11},{8,12},{9,13},{1... | collective-permute-start | bytes 1769480 | tf_op jit(solution)/shard_map/ppermute | solution.py:444
  19.8 20.6 %collective-permute-start.6 = (bf16[2,192,256]{2,1,0:T(8,128)(2,1)S(1)}, bf16[2,192,256]{2,1,0:T(8,128)(2,1)S(1)}, u32[]{:S(2)}, u32[]{:S(2)}) collective-permute-start(bf16[2,192,256]{2,1,0:T(8,128)(2,1)S(1)} %get-tuple-element.49.after), channel_id=1, source_target_pairs={{0,2},{1,3},{2,0},{3,1},{4,6},{5,7},{6,4},{7,5},{8,10},{9,11},{10,... | collective-permute-start | bytes 589832 | tf_op jit(solution)/shard_map/ppermute | solution.py:440
  30.1 10.0 %collective-permute-start.7 = (bf16[2,192,256]{2,1,0:T(8,128)(2,1)S(1)}, bf16[2,192,256]{2,1,0:T(8,128)(2,1)S(1)}, u32[]{:S(2)}, u32[]{:S(2)}) collective-permute-start(bf16[2,192,256]{2,1,0:T(8,128)(2,1)S(1)} %get-tuple-element.54), channel_id=1, source_target_pairs={{0,1},{1,2},{2,3},{3,0},{4,5},{5,6},{6,7},{7,4},{8,9},{9,10},{10,1... | collective-permute-start | bytes 589832 | tf_op jit(solution)/shard_map/ppermute | solution.py:440
  30.1 10.0 %collective-permute-start.8 = (bf16[2,192,256]{2,1,0:T(8,128)(2,1)S(1)}, bf16[2,192,256]{2,1,0:T(8,128)(2,1)S(1)}, u32[]{:S(2)}, u32[]{:S(2)}) collective-permute-start(bf16[2,192,256]{2,1,0:T(8,128)(2,1)S(1)} %get-tuple-element.55), channel_id=1, source_target_pairs={{0,3},{1,0},{2,1},{3,2},{4,7},{5,4},{6,5},{7,6},{8,11},{9,8},{10,9... | collective-permute-start | bytes 589832 | tf_op jit(solution)/shard_map/ppermute | solution.py:440
  33.4 26.9 %collective-permute-start.20 = (bf16[2,576,256]{2,1,0:T(8,128)(2,1)S(1)}, bf16[2,576,256]{2,1,0:T(8,128)(2,1)S(1)}, u32[]{:S(2)}, u32[]{:S(2)}) collective-permute-start(bf16[2,576,256]{2,1,0:T(8,128)(2,1)S(1)} %edge.3), channel_id=1, source_target_pairs={{0,4},{1,5},{2,6},{3,7},{4,8},{5,9},{6,10},{7,11},{8,12},{9,13},{1... | collective-permute-start | bytes 1769480 | tf_op jit(solution)/shard_map/ppermute | solution.py:444
  40.1 17.0 %collective-permute-start.17 = (bf16[2,192,256]{2,1,0:T(8,128)(2,1)S(1)}, bf16[2,192,256]{2,1,0:T(8,128)(2,1)S(1)}, u32[]{:S(2)}, u32[]{:S(2)}) collective-permute-start(bf16[2,192,256]{2,1,0:T(8,128)(2,1)S(1)} %get-tuple-element.50.after), channel_id=1, source_target_pairs={{0,2},{1,3},{2,0},{3,1},{4,6},{5,7},{6,4},{7,5},{8,10},{9,11},{10,... | collective-permute-start | bytes 589832 | tf_op jit(solution)/shard_map/ppermute | solution.py:440
  40.1 14.6 %collective-permute-start.18 = (bf16[2,192,256]{2,1,0:T(8,128)(2,1)S(1)}, bf16[2,192,256]{2,1,0:T(8,128)(2,1)S(1)}, u32[]{:S(2)}, u32[]{:S(2)}) collective-permute-start(bf16[2,192,256]{2,1,0:T(8,128)(2,1)S(1)} %get-tuple-element.64), channel_id=1, source_target_pairs={{0,1},{1,2},{2,3},{3,0},{4,5},{5,6},{6,7},{7,4},{8,9},{9,10},{10,1... | collective-permute-start | bytes 589832 | tf_op jit(solution)/shard_map/ppermute | solution.py:440
  40.5 16.5 %collective-permute-start.19 = (bf16[2,192,256]{2,1,0:T(8,128)(2,1)S(1)}, bf16[2,192,256]{2,1,0:T(8,128)(2,1)S(1)}, u32[]{:S(2)}, u32[]{:S(2)}) collective-permute-start(bf16[2,192,256]{2,1,0:T(8,128)(2,1)S(1)} %get-tuple-element.65), channel_id=1, source_target_pairs={{0,3},{1,0},{2,1},{3,2},{4,7},{5,4},{6,5},{7,6},{8,11},{9,8},{10,9... | collective-permute-start | bytes 589832 | tf_op jit(solution)/shard_map/ppermute | solution.py:440
  48.6 19.6 %collective-permute-start.13 = (bf16[2,576,256]{2,1,0:T(8,128)(2,1)S(1)}, bf16[2,576,256]{2,1,0:T(8,128)(2,1)S(1)}, u32[]{:S(2)}, u32[]{:S(2)}) collective-permute-start(bf16[2,576,256]{2,1,0:T(8,128)(2,1)S(1)} %get-tuple-element.61), channel_id=1, source_target_pairs={{0,28},{1,29},{2,30},{3,31},{4,0},{5,1},{6,2},{7,3},{8,4},{9,5},{1... | collective-permute-start | bytes 1769480 | tf_op jit(solution)/shard_map/ppermute | solution.py:444
  54.7 11.9 %collective-permute-start.10 = (bf16[192,256]{1,0:T(8,128)(2,1)S(1)}, bf16[192,256]{1,0:T(8,128)(2,1)S(1)}, u32[]{:S(2)}, u32[]{:S(2)}) collective-permute-start(bf16[192,256]{1,0:T(8,128)(2,1)S(1)} %get-tuple-element.57), channel_id=1, source_target_pairs={{0,2},{1,3},{2,0},{3,1},{4,6},{5,7},{6,4},{7,5},{8,10},{9,11},{10,... | collective-permute-start | bytes 294920 | tf_op jit(solution)/shard_map/ppermute | solution.py:440
  57.0 9.6 %collective-permute-start.11 = (bf16[192,256]{1,0:T(8,128)(2,1)S(1)}, bf16[192,256]{1,0:T(8,128)(2,1)S(1)}, u32[]{:S(2)}, u32[]{:S(2)}) collective-permute-start(bf16[192,256]{1,0:T(8,128)(2,1)S(1)} %get-tuple-element.58), channel_id=1, source_target_pairs={{0,1},{1,2},{2,3},{3,0},{4,5},{5,6},{6,7},{7,4},{8,9},{9,10},{10,1... | collective-permute-start | bytes 294920 | tf_op jit(solution)/shard_map/ppermute | solution.py:440
  57.0 9.6 %collective-permute-start.12 = (bf16[192,256]{1,0:T(8,128)(2,1)S(1)}, bf16[192,256]{1,0:T(8,128)(2,1)S(1)}, u32[]{:S(2)}, u32[]{:S(2)}) collective-permute-start(bf16[192,256]{1,0:T(8,128)(2,1)S(1)} %get-tuple-element.59), channel_id=1, source_target_pairs={{0,3},{1,0},{2,1},{3,2},{4,7},{5,4},{6,5},{7,6},{8,11},{9,8},{10,9... | collective-permute-start | bytes 294920 | tf_op jit(solution)/shard_map/ppermute | solution.py:440
  65.6 11.5 %collective-permute-start.24 = (bf16[2,576,256]{2,1,0:T(8,128)(2,1)S(1)}, bf16[2,576,256]{2,1,0:T(8,128)(2,1)S(1)}, u32[]{:S(2)}, u32[]{:S(2)}) collective-permute-start(bf16[2,576,256]{2,1,0:T(8,128)(2,1)S(1)} %get-tuple-element.76), channel_id=1, source_target_pairs={{0,28},{1,29},{2,30},{3,31},{4,0},{5,1},{6,2},{7,3},{8,4},{9,5},{1... | collective-permute-start | bytes 1769480 | tf_op jit(solution)/shard_map/ppermute | solution.py:444
  68.4 11.6 %collective-permute-start.21 = (bf16[3,192,256]{2,1,0:T(8,128)(2,1)S(1)}, bf16[3,192,256]{2,1,0:T(8,128)(2,1)S(1)}, u32[]{:S(2)}, u32[]{:S(2)}) collective-permute-start(bf16[3,192,256]{2,1,0:T(8,128)(2,1)S(1)} %get-tuple-element.71), channel_id=1, source_target_pairs={{0,2},{1,3},{2,0},{3,1},{4,6},{5,7},{6,4},{7,5},{8,10},{9,11},{10,... | collective-permute-start | bytes 884744 | tf_op jit(solution)/shard_map/ppermute | solution.py:440
  68.5 13.6 %collective-permute-start.22 = (bf16[3,192,256]{2,1,0:T(8,128)(2,1)S(1)}, bf16[3,192,256]{2,1,0:T(8,128)(2,1)S(1)}, u32[]{:S(2)}, u32[]{:S(2)}) collective-permute-start(bf16[3,192,256]{2,1,0:T(8,128)(2,1)S(1)} %get-tuple-element.72), channel_id=1, source_target_pairs={{0,1},{1,2},{2,3},{3,0},{4,5},{5,6},{6,7},{7,4},{8,9},{9,10},{10,1... | collective-permute-start | bytes 884744 | tf_op jit(solution)/shard_map/ppermute | solution.py:440
  69.4 12.7 %collective-permute-start.23 = (bf16[3,192,256]{2,1,0:T(8,128)(2,1)S(1)}, bf16[3,192,256]{2,1,0:T(8,128)(2,1)S(1)}, u32[]{:S(2)}, u32[]{:S(2)}) collective-permute-start(bf16[3,192,256]{2,1,0:T(8,128)(2,1)S(1)} %get-tuple-element.73), channel_id=1, source_target_pairs={{0,3},{1,0},{2,1},{3,2},{4,7},{5,4},{6,5},{7,6},{8,11},{9,8},{10,9... | collective-permute-start | bytes 884744 | tf_op jit(solution)/shard_map/ppermute | solution.py:440
  77.2 9.1 %collective-permute-start.25 = (bf16[2,192,256]{2,1,0:T(8,128)(2,1)S(1)}, bf16[2,192,256]{2,1,0:T(8,128)(2,1)S(1)}, u32[]{:S(2)}, u32[]{:S(2)}) collective-permute-start(bf16[2,192,256]{2,1,0:T(8,128)(2,1)S(1)} %get-tuple-element.78), channel_id=1, source_target_pairs={{0,2},{1,3},{2,0},{3,1},{4,6},{5,7},{6,4},{7,5},{8,10},{9,11},{10,... | collective-permute-start | bytes 589832 | tf_op jit(solution)/shard_map/ppermute | solution.py:440
  78.5 9.6 %collective-permute-start.26 = (bf16[2,192,256]{2,1,0:T(8,128)(2,1)S(1)}, bf16[2,192,256]{2,1,0:T(8,128)(2,1)S(1)}, u32[]{:S(2)}, u32[]{:S(2)}) collective-permute-start(bf16[2,192,256]{2,1,0:T(8,128)(2,1)S(1)} %get-tuple-element.79), channel_id=1, source_target_pairs={{0,1},{1,2},{2,3},{3,0},{4,5},{5,6},{6,7},{7,4},{8,9},{9,10},{10,1... | collective-permute-start | bytes 589832 | tf_op jit(solution)/shard_map/ppermute | solution.py:440
  80.0 8.1 %collective-permute-start.27 = (bf16[2,192,256]{2,1,0:T(8,128)(2,1)S(1)}, bf16[2,192,256]{2,1,0:T(8,128)(2,1)S(1)}, u32[]{:S(2)}, u32[]{:S(2)}) collective-permute-start(bf16[2,192,256]{2,1,0:T(8,128)(2,1)S(1)} %get-tuple-element.80), channel_id=1, source_target_pairs={{0,3},{1,0},{2,1},{3,2},{4,7},{5,4},{6,5},{7,6},{8,11},{9,8},{10,9... | collective-permute-start | bytes 589832 | tf_op jit(solution)/shard_map/ppermute | solution.py:440
  (3 other events, 3.9 us)

commit v9 on v7

--- a/solution.py
+++ b/solution.py
@@ -21,8 +21,10 @@
 SMALL = pltpu.CompilerParams(vmem_limit_bytes=10 * 1024 * 1024)
 
 
-def aways():
+def aways(turned=False):
     core = lax.rem(lax.axis_index("dp"), 2)
+    if turned:
+        return 0, 2, 1 + 2 * core, 3 - 2 * core
     return 0, 1 + 2 * core, 3 - 2 * core, 2
 
 
@@ -31,9 +33,9 @@
     return pl.ds(pl.multiple_of((index * CHUNKS + chunk) * width, width), width)
 
 
-def pack_kernel(chunk, first, second, after, one, two, three):
+def pack_kernel(chunk, turned, first, second, after, one, two, three):
     width = one.shape[2]
-    for away, message in zip(aways()[1:], (one, two, three)):
+    for away, message in zip(aways(turned)[1:], (one, two, three)):
         lanes = columns(lax.rem(lax.axis_index("ctx"), GROUP), away, chunk, width)
         message[0] = first[:, lanes]
         message[1] = second[:, lanes]
@@ -58,12 +60,12 @@
     text[...] = (held[0] * (1 - held[1])).astype(jnp.float32)
 
 
-def pack(first, second, after, chunk):
+def pack(first, second, after, chunk, turned=False):
     rows, total = first.shape
     width = total // (GROUP * CHUNKS)
     message = jax.ShapeDtypeStruct((2, rows, width), first.dtype)
     return pl.pallas_call(
-        functools.partial(pack_kernel, chunk),
+        functools.partial(pack_kernel, chunk, turned),
         out_shape=(message,) * (GROUP - 1),
         in_specs=[VMEM, VMEM, ANY],
         out_specs=(VMEM,) * (GROUP - 1),
@@ -93,12 +95,12 @@
     return messages, text
 
 
-def edge_kernel(chunk, first, second, one, two, three, *refs):
+def edge_kernel(chunk, turned, first, second, one, two, three, *refs):
     edge = refs[-1]
     rows = edge.shape[1] // (GROUP - 1)
     width = edge.shape[2]
     place = lax.rem(lax.axis_index("ctx"), GROUP)
-    for away, message in zip(aways(), (None, one, two, three)):
+    for away, message in zip(aways(turned), (None, one, two, three)):
         index = lax.rem(place + GROUP - away, GROUP)
 
         @pl.when(index > 0)
@@ -112,10 +114,10 @@
                 edge[:, at, :] = message[...]
 
 
-def make_edge(first, second, blocks, afters, chunk, cost):
+def make_edge(first, second, blocks, afters, chunk, cost, turned=False):
     _, rows, width = blocks[0].shape
     return pl.pallas_call(
-        functools.partial(edge_kernel, chunk),
+        functools.partial(edge_kernel, chunk, turned),
         out_shape=jax.ShapeDtypeStruct((2, (GROUP - 1) * rows, width), first.dtype),
         in_specs=[VMEM] * 5 + [ANY] * len(afters),
         out_specs=VMEM,
@@ -196,7 +198,7 @@
 
 
 def attend_kernel(
-    chunk, total_rows, text_one, text_two, text_three, text_four, limit_ref, text_ref, keypos_ref,
+    chunk, turned, total_rows, text_one, text_two, text_three, text_four, limit_ref, text_ref, keypos_ref,
     queries, keys, values, grads, key_one, key_two, key_three, query_one, query_two, query_three,
     edge_ref, query_own, query_to_one, query_to_two, query_to_three, main_ref, far_ref,
     key_all, value_all, query_all, grad_all, key_grad, value_grad, query_out,
@@ -211,16 +213,16 @@
     lanes = columns(place, 0, chunk, width)
     key_all[:edge, :] = edge_ref[0]
     value_all[:edge, :] = edge_ref[1]
-    sources = [(keys.at[:, lanes], values.at[:, lanes], queries.at[:, lanes], grads.at[:, lanes])]
-    for pair, query_pair in ((key_one, query_one), (key_two, query_two), (key_three, query_three)):
-        sources.append((pair.at[0], pair.at[1], query_pair.at[0], query_pair.at[1]))
-    for slot, away in enumerate(aways()):
-        start = pl.multiple_of(lax.rem(place + GROUP - away, GROUP) * rows, rows)
-        key, value, query, grad = sources[slot]
-        key_all[pl.ds(edge + start, rows), :] = key[...]
-        value_all[pl.ds(edge + start, rows), :] = value[...]
-        query_all[pl.ds(start, rows), :] = query[...]
-        grad_all[pl.ds(start, rows), :] = grad[...]
+    for order, pairs, targets, offset in (
+        (aways(turned), (key_one, key_two, key_three), (key_all, value_all), edge),
+        (aways(), (query_one, query_two, query_three), (query_all, grad_all), 0),
+    ):
+        owns = (keys, values) if offset else (queries, grads)
+        for slot, away in enumerate(order):
+            start = pl.multiple_of(lax.rem(place + GROUP - away, GROUP) * rows, rows)
+            for part, target in enumerate(targets):
+                block = owns[part][:, lanes] if slot == 0 else pairs[slot - 1][part]
+                target[pl.ds(offset + start, rows), :] = block
     for block in range(GROUP):
         at = slice(block * rows, (block + 1) * rows)
         window = slice(block * rows, block * rows + span)
@@ -281,13 +283,13 @@
         block[...] = query_out[pl.ds(pl.multiple_of(index * rows, rows), rows), :]
 
 
-def attend(texts, marks, arrays, key_blocks, query_blocks, edge, chunk, total_rows):
+def attend(texts, marks, arrays, key_blocks, query_blocks, edge, chunk, turned, total_rows):
     _, rows, width = key_blocks[0].shape
     heads = width // HEAD
     keys = (2 * GROUP - 1) * rows
     pairs = heads * GROUP * rows * STEPS * rows
     return pl.pallas_call(
-        functools.partial(attend_kernel, chunk, total_rows),
+        functools.partial(attend_kernel, chunk, turned, total_rows),
         out_shape=(
             *[jax.ShapeDtypeStruct((rows, width), jnp.bfloat16)] * GROUP,
             jax.ShapeDtypeStruct((2, GROUP * rows, width), jnp.bfloat16),
@@ -429,11 +431,12 @@
     cycle_size = lax.axis_size("ctx")
     samples = lax.axis_size("dp")
 
-    def swap(value, slot):
+    def swap(value, slot, turned):
         pairs = []
         for sample in range(samples):
             core = sample % 2
-            away = (1 + 2 * core, 3 - 2 * core, 2)[slot]
+            order = (1 + 2 * core, 3 - 2 * core, 2)
+            away = (order[-1:] + order[:-1])[slot] if turned else order[slot]
             for source in range(cycle_size):
                 target = source - source % GROUP + (source + away) % GROUP
                 pairs.append((sample * cycle_size + source, sample * cycle_size + target))
@@ -443,8 +446,8 @@
         pairs = [(source, (source + rows * GROUP) % cycle_size) for source in range(cycle_size)]
         return lax.ppermute(value, "ctx", pairs)
 
-    def swapped(messages):
-        return [swap(message, slot) for slot, message in enumerate(messages)]
+    def swapped(messages, turned=False):
+        return [swap(message, slot, turned) for slot, message in enumerate(messages)]
 
     first_messages, text = first_pack(key_rows, value_rows, lengths, image_flags)
     texts = [text] + [
@@ -455,8 +458,8 @@
 
     key_packs, query_packs, edges = [None] * CHUNKS, [None] * CHUNKS, [None] * CHUNKS
     key_packs[0] = first_messages
-    key_packs[1] = pack(key_rows, value_rows, text, 1)
-    key_blocks = [swapped(messages) for messages in key_packs]
+    key_packs[1] = pack(key_rows, value_rows, text, 1, True)
+    key_blocks = [swapped(messages, chunk == 1) for chunk, messages in enumerate(key_packs)]
     edges[0] = make_edge(
         key_rows, value_rows, key_blocks[0], (*texts[1:], key_packs[1][0]), 0, EDGE_COST[0]
     )
@@ -466,7 +469,7 @@
         after = query_packs[index][0]
     marks = sides(lengths, image_flags, after, row_count // 2, cycle_size)
     edges[1] = make_edge(
-        key_rows, value_rows, key_blocks[1], (marks[1],), 1, EDGE_COST[1]
+        key_rows, value_rows, key_blocks[1], (marks[1],), 1, EDGE_COST[1], True
     )
     query_blocks = [swapped(messages) for messages in query_packs]
     edges = [next_row(edge, 1) for edge in edges]
@@ -475,7 +478,7 @@
     for chunk in range(CHUNKS):
         *query_grads, main, far = attend(
             texts, marks, arrays,
-            key_blocks[chunk], query_blocks[chunk], edges[chunk], chunk, total_rows,
+            key_blocks[chunk], query_blocks[chunk], edges[chunk], chunk, chunk == 1, total_rows,
         )
         halves.append((query_grads, main, next_row(far, -1)))
     (first_queries, main, far), (second_queries, last_main, last_far) = halves

time: 86.4 us -> 86.9 us (level)
  starting transfers between devices: 47.3 us -> 48.9 us
  waiting for transfers between devices: 21.2 us -> 20.1 us
    ppermute x4, waiting for transfers between devices: 8.87 us -> 7.26 us  [next_row(): return lax.ppermute(value, 'ctx', pairs)]
    ppermute x21, starting transfers between devices: 31.9 us -> 33 us  [swap(): return lax.ppermute(value, ('dp', 'ctx'), pairs)]
  transfers between devices with their start and end apart: 28 -> 28, of which waited for: 10 -> 9; matrix products, arithmetic and copies ran while one was open for 0% -> 0% of each run, Pallas kernels for 15% -> 15%
where the time goes in v9:
time: 86.9 us; the launch traced here: 86.7 us
  starting transfers between devices  48.9 us (56%)
  waiting for transfers between devices  20.1 us (23%)
  Pallas kernels  16 us (18%)
  between operations  0.99 us (1%)
    ppermute x21, starting transfers between devices, swap(): return lax.ppermute(value, ('dp', 'ctx'), pairs)  33 us
    ppermute x4, starting transfers between devices, next_row(): return lax.ppermute(value, 'ctx', pairs)  13.2 us
    ppermute x21, waiting for transfers between devices, swap(): return lax.ppermute(value, ('dp', 'ctx'), pairs)  12 us
    pallas_call x2, Pallas kernels, attend(): pl.pallas_call(functools.partial(attend_kernel, chunk, turned, total_rows...  10.6 us
    ppermute x4, waiting for transfers between devices, next_row(): return lax.ppermute(value, 'ctx', pairs)  7.26 us
    ppermute x3, starting transfers between devices, shards(): lax.ppermute(text, 'dp', [(source, (source + away) % samples) for source...  2.73 us
    pallas_call x1, Pallas kernels, first_pack(): pl.pallas_call(first_pack_kernel, out_shape=(message,) * (GROUP - 1) + (j...  2.15 us
  transfers between devices with their start and end apart: 28, of which 9 were waited for; matrix products, arithmetic and copies ran while one was open for 0% of the time, Pallas kernels for 15%

profile of v9, /device:TPU:0, one launch (start us, length us, event | category | flops | bytes accessed | tf_op | source)
XLA Modules:
  0.0 86.7 jit_solution(951915529815116442)
XLA Ops:
  0.7 2.1 %first_pack.1 = (bf16[2,192,256]{2,1,0:T(8,128)(2,1)}, bf16[2,192,256]{2,1,0:T(8,128)(2,1)}, bf16[2,192,256]{2,1,0:T(8,128)(2,1)}, f32[1,32]{1,0:T(1,128)}) custom-call(bf16[192,2048]{1,0:T(8,128)(2,1)} %bitcast.7, bf16[192,2048]{1,0:T(8,128)(2,1)} %bitcast.13, s32[1,32]{1,0:T(1,128)} %lengths_ref.1, s32[1,32]{1,0:T(1,128)} %flags_ref.1), custom_call_target="tpu_custom_call" | custom-call | bytes 1179648 | tf_op jit(solution)/shard_map/first_pack/pallas_call | solution.py:82
  2.8 1.7 %collective-permute-start.3 = (bf16[2,192,256]{2,1,0:T(8,128)(2,1)}, bf16[2,192,256]{2,1,0:T(8,128)(2,1)S(1)}, u32[]{:S(2)}, u32[]{:S(2)}) collective-permute-start(bf16[2,192,256]{2,1,0:T(8,128)(2,1)} %get-tuple-element.45), channel_id=1, source_target_pairs={{0,1},{1,2},{2,3},{3,0},{4,5},{5,6},{6,7},{7,4},{8,9},{9,10},{10,1... | collective-permute-start | bytes 589832 | tf_op jit(solution)/shard_map/ppermute | solution.py:443
  4.5 1.6 %collective-permute-start.4 = (bf16[2,192,256]{2,1,0:T(8,128)(2,1)}, bf16[2,192,256]{2,1,0:T(8,128)(2,1)S(1)}, u32[]{:S(2)}, u32[]{:S(2)}) collective-permute-start(bf16[2,192,256]{2,1,0:T(8,128)(2,1)} %get-tuple-element.46), channel_id=1, source_target_pairs={{0,3},{1,0},{2,1},{3,2},{4,7},{5,4},{6,5},{7,6},{8,11},{9,8},{10,9... | collective-permute-start | bytes 589832 | tf_op jit(solution)/shard_map/ppermute | solution.py:443
  6.1 2.1 %collective-permute-start.5 = (bf16[2,192,256]{2,1,0:T(8,128)(2,1)}, bf16[2,192,256]{2,1,0:T(8,128)(2,1)S(1)}, u32[]{:S(2)}, u32[]{:S(2)}) collective-permute-start(bf16[2,192,256]{2,1,0:T(8,128)(2,1)} %get-tuple-element.47), channel_id=1, source_target_pairs={{0,2},{1,3},{2,0},{3,1},{4,6},{5,7},{6,4},{7,5},{8,10},{9,11},{10,... | collective-permute-start | bytes 589832 | tf_op jit(solution)/shard_map/ppermute | solution.py:443
  8.3 1.4 %collective-permute-start.1 = (f32[1,32]{1,0:T(1,128)S(1)}, f32[1,32]{1,0:T(1,128)S(1)}, u32[]{:S(2)}, u32[]{:S(2)}) collective-permute-start(f32[1,32]{1,0:T(1,128)S(1)} %copy-done.6), channel_id=1, source_target_pairs={{0,64},{32,96},{64,0},{96,32},{1,65},{33,97},{65,1},{97,33},{2,66}... | collective-permute-start | bytes 392 | tf_op jit(solution)/shard_map/ppermute | solution.py:454
  9.8 1.2 %collective-permute-start = (f32[1,32]{1,0:T(1,128)S(1)}, f32[1,32]{1,0:T(1,128)S(1)}, u32[]{:S(2)}, u32[]{:S(2)}) collective-permute-start(f32[1,32]{1,0:T(1,128)S(1)} %copy-done.6), channel_id=1, source_target_pairs={{0,32},{32,64},{64,96},{96,0},{1,33},{33,65},{65,97},{97,1},{2,34}... | collective-permute-start | bytes 392 | tf_op jit(solution)/shard_map/ppermute | solution.py:454
  11.8 1.9 %collective-permute-start.15 = (bf16[2,192,256]{2,1,0:T(8,128)(2,1)S(1)}, bf16[2,192,256]{2,1,0:T(8,128)(2,1)S(1)}, u32[]{:S(2)}, u32[]{:S(2)}) collective-permute-start(bf16[2,192,256]{2,1,0:T(8,128)(2,1)S(1)} %get-tuple-element.62), channel_id=1, source_target_pairs={{0,1},{1,2},{2,3},{3,0},{4,5},{5,6},{6,7},{7,4},{8,9},{9,10},{10,1... | collective-permute-start | bytes 589832 | tf_op jit(solution)/shard_map/ppermute | solution.py:443
  13.7 1.3 %collective-permute-start.16 = (bf16[2,192,256]{2,1,0:T(8,128)(2,1)S(1)}, bf16[2,192,256]{2,1,0:T(8,128)(2,1)S(1)}, u32[]{:S(2)}, u32[]{:S(2)}) collective-permute-start(bf16[2,192,256]{2,1,0:T(8,128)(2,1)S(1)} %get-tuple-element.63), channel_id=1, source_target_pairs={{0,3},{1,0},{2,1},{3,2},{4,7},{5,4},{6,5},{7,6},{8,11},{9,8},{10,9... | collective-permute-start | bytes 589832 | tf_op jit(solution)/shard_map/ppermute | solution.py:443
  15.1 1.7 %collective-permute-start.14 = (bf16[2,192,256]{2,1,0:T(8,128)(2,1)S(1)}, bf16[2,192,256]{2,1,0:T(8,128)(2,1)S(1)}, u32[]{:S(2)}, u32[]{:S(2)}) collective-permute-start(bf16[2,192,256]{2,1,0:T(8,128)(2,1)S(1)} %get-tuple-element.48.refs_3_), channel_id=1, source_target_pairs={{0,2},{1,3},{2,0},{3,1},{4,6},{5,7},{6,4},{7,5},{8,10},{9,11},{10,... | collective-permute-start | bytes 589832 | tf_op jit(solution)/shard_map/ppermute | solution.py:443
  17.6 3.1 %collective-permute-start.9 = (bf16[2,576,256]{2,1,0:T(8,128)(2,1)S(1)}, bf16[2,576,256]{2,1,0:T(8,128)(2,1)S(1)}, u32[]{:S(2)}, u32[]{:S(2)}) collective-permute-start(bf16[2,576,256]{2,1,0:T(8,128)(2,1)S(1)} %edge.2.after), channel_id=1, source_target_pairs={{0,4},{1,5},{2,6},{3,7},{4,8},{5,9},{6,10},{7,11},{8,12},{9,13},{1... | collective-permute-start | bytes 1769480 | tf_op jit(solution)/shard_map/ppermute | solution.py:447
  22.9 2.4 %collective-permute-start.7 = (bf16[2,192,256]{2,1,0:T(8,128)(2,1)S(1)}, bf16[2,192,256]{2,1,0:T(8,128)(2,1)S(1)}, u32[]{:S(2)}, u32[]{:S(2)}) collective-permute-start(bf16[2,192,256]{2,1,0:T(8,128)(2,1)S(1)} %get-tuple-element.54), channel_id=1, source_target_pairs={{0,3},{1,0},{2,1},{3,2},{4,7},{5,4},{6,5},{7,6},{8,11},{9,8},{10,9... | collective-permute-start | bytes 589832 | tf_op jit(solution)/shard_map/ppermute | solution.py:443
  25.5 3.2 %collective-permute-start.20 = (bf16[2,576,256]{2,1,0:T(8,128)(2,1)S(1)}, bf16[2,576,256]{2,1,0:T(8,128)(2,1)S(1)}, u32[]{:S(2)}, u32[]{:S(2)}) collective-permute-start(bf16[2,576,256]{2,1,0:T(8,128)(2,1)S(1)} %edge.3), channel_id=1, source_target_pairs={{0,4},{1,5},{2,6},{3,7},{4,8},{5,9},{6,10},{7,11},{8,12},{9,13},{1... | collective-permute-start | bytes 1769480 | tf_op jit(solution)/shard_map/ppermute | solution.py:447
  28.7 2.9 %collective-permute-done.7.query_two = bf16[2,192,256]{2,1,0:T(8,128)(2,1)S(1)} collective-permute-done((bf16[2,192,256]{2,1,0:T(8,128)(2,1)S(1)}, bf16[2,192,256]{2,1,0:T(8,128)(2,1)S(1)}, u32[]{:S(2)}, u32[]{:S(2)}) %collective-permute-start.7) | collective-permute-done | bytes 196640 | tf_op jit(solution)/shard_map/ppermute | solution.py:443
  32.5 1.3 %collective-permute-done.8.query_three = bf16[2,192,256]{2,1,0:T(8,128)(2,1)S(1)} collective-permute-done((bf16[2,192,256]{2,1,0:T(8,128)(2,1)S(1)}, bf16[2,192,256]{2,1,0:T(8,128)(2,1)S(1)}, u32[]{:S(2)}, u32[]{:S(2)}) %collective-permute-start.8) | collective-permute-done | bytes 196640 | tf_op jit(solution)/shard_map/ppermute | solution.py:443
  33.8 1.7 %collective-permute-start.18 = (bf16[2,192,256]{2,1,0:T(8,128)(2,1)S(1)}, bf16[2,192,256]{2,1,0:T(8,128)(2,1)S(1)}, u32[]{:S(2)}, u32[]{:S(2)}) collective-permute-start(bf16[2,192,256]{2,1,0:T(8,128)(2,1)S(1)} %get-tuple-element.64), channel_id=1, source_target_pairs={{0,3},{1,0},{2,1},{3,2},{4,7},{5,4},{6,5},{7,6},{8,11},{9,8},{10,9... | collective-permute-start | bytes 589832 | tf_op jit(solution)/shard_map/ppermute | solution.py:443
  35.5 1.7 %collective-permute-start.19 = (bf16[2,192,256]{2,1,0:T(8,128)(2,1)S(1)}, bf16[2,192,256]{2,1,0:T(8,128)(2,1)S(1)}, u32[]{:S(2)}, u32[]{:S(2)}) collective-permute-start(bf16[2,192,256]{2,1,0:T(8,128)(2,1)S(1)} %get-tuple-element.65), channel_id=1, source_target_pairs={{0,2},{1,3},{2,0},{3,1},{4,6},{5,7},{6,4},{7,5},{8,10},{9,11},{10,... | collective-permute-start | bytes 589832 | tf_op jit(solution)/shard_map/ppermute | solution.py:443
  37.2 1.3 %collective-permute-done.9.edge_ref = bf16[2,576,256]{2,1,0:T(8,128)(2,1)S(1)} collective-permute-done((bf16[2,576,256]{2,1,0:T(8,128)(2,1)S(1)}, bf16[2,576,256]{2,1,0:T(8,128)(2,1)S(1)}, u32[]{:S(2)}, u32[]{:S(2)}) %collective-permute-start.9) | collective-permute-done | bytes 589856 | tf_op jit(solution)/shard_map/ppermute | solution.py:447
  38.4 5.3 %attend.2 = (bf16[192,256]{1,0:T(8,128)(2,1)S(1)}, bf16[192,256]{1,0:T(8,128)(2,1)S(1)}, bf16[192,256]{1,0:T(8,128)(2,1)S(1)}, bf16[192,256]{1,0:T(8,128)(2,1)S(...) custom-call(f32[1,32]{1,0:T(1,128)S(1)} %copy-done.6, ...), custom_call_target="tpu_custom_call" | custom-call | flops 4499999744 | tf_op jit(solution)/shard_map/attend/pallas_call | solution.py:291
  43.7 4.4 %collective-permute-start.13 = (bf16[2,576,256]{2,1,0:T(8,128)(2,1)S(1)}, bf16[2,576,256]{2,1,0:T(8,128)(2,1)S(1)}, u32[]{:S(2)}, u32[]{:S(2)}) collective-permute-start(bf16[2,576,256]{2,1,0:T(8,128)(2,1)S(1)} %get-tuple-element.61), channel_id=1, source_target_pairs={{0,28},{1,29},{2,30},{3,31},{4,0},{5,1},{6,2},{7,3},{8,4},{9,5},{1... | collective-permute-start | bytes 1769480 | tf_op jit(solution)/shard_map/ppermute | solution.py:447
  49.0 2.4 %collective-permute-start.11 = (bf16[192,256]{1,0:T(8,128)(2,1)S(1)}, bf16[192,256]{1,0:T(8,128)(2,1)S(1)}, u32[]{:S(2)}, u32[]{:S(2)}) collective-permute-start(bf16[192,256]{1,0:T(8,128)(2,1)S(1)} %get-tuple-element.58), channel_id=1, source_target_pairs={{0,3},{1,0},{2,1},{3,2},{4,7},{5,4},{6,5},{7,6},{8,11},{9,8},{10,9... | collective-permute-start | bytes 294920 | tf_op jit(solution)/shard_map/ppermute | solution.py:443
  51.4 2.3 %collective-permute-start.12 = (bf16[192,256]{1,0:T(8,128)(2,1)S(1)}, bf16[192,256]{1,0:T(8,128)(2,1)S(1)}, u32[]{:S(2)}, u32[]{:S(2)}) collective-permute-start(bf16[192,256]{1,0:T(8,128)(2,1)S(1)} %get-tuple-element.59), channel_id=1, source_target_pairs={{0,2},{1,3},{2,0},{3,1},{4,6},{5,7},{6,4},{7,5},{8,10},{9,11},{10,... | collective-permute-start | bytes 294920 | tf_op jit(solution)/shard_map/ppermute | solution.py:443
  53.7 5.3 %attend.3 = (bf16[192,256]{1,0:T(8,128)(2,1)S(1)}, bf16[192,256]{1,0:T(8,128)(2,1)S(1)}, bf16[192,256]{1,0:T(8,128)(2,1)S(1)}, bf16[192,256]{1,0:T(8,128)(2,1)S(...) custom-call(f32[1,32]{1,0:T(1,128)S(1)} %copy-done.6, ...), custom_call_target="tpu_custom_call" | custom-call | flops 4499999744 | tf_op jit(solution)/shard_map/attend/pallas_call | solution.py:291
  59.0 2.5 %collective-permute-start.24 = (bf16[2,576,256]{2,1,0:T(8,128)(2,1)S(1)}, bf16[2,576,256]{2,1,0:T(8,128)(2,1)S(1)}, u32[]{:S(2)}, u32[]{:S(2)}) collective-permute-start(bf16[2,576,256]{2,1,0:T(8,128)(2,1)S(1)} %get-tuple-element.76), channel_id=1, source_target_pairs={{0,28},{1,29},{2,30},{3,31},{4,0},{5,1},{6,2},{7,3},{8,4},{9,5},{1... | collective-permute-start | bytes 1769480 | tf_op jit(solution)/shard_map/ppermute | solution.py:447
  61.7 1.4 %collective-permute-start.21 = (bf16[3,192,256]{2,1,0:T(8,128)(2,1)S(1)}, bf16[3,192,256]{2,1,0:T(8,128)(2,1)S(1)}, u32[]{:S(2)}, u32[]{:S(2)}) collective-permute-start(bf16[3,192,256]{2,1,0:T(8,128)(2,1)S(1)} %get-tuple-element.71), channel_id=1, source_target_pairs={{0,1},{1,2},{2,3},{3,0},{4,5},{5,6},{6,7},{7,4},{8,9},{9,10},{10,1... | collective-permute-start | bytes 884744 | tf_op jit(solution)/shard_map/ppermute | solution.py:443
  63.1 1.9 %collective-permute-start.22 = (bf16[3,192,256]{2,1,0:T(8,128)(2,1)S(1)}, bf16[3,192,256]{2,1,0:T(8,128)(2,1)S(1)}, u32[]{:S(2)}, u32[]{:S(2)}) collective-permute-start(bf16[3,192,256]{2,1,0:T(8,128)(2,1)S(1)} %get-tuple-element.72), channel_id=1, source_target_pairs={{0,3},{1,0},{2,1},{3,2},{4,7},{5,4},{6,5},{7,6},{8,11},{9,8},{10,9... | collective-permute-start | bytes 884744 | tf_op jit(solution)/shard_map/ppermute | solution.py:443
  65.0 1.8 %collective-permute-start.23 = (bf16[3,192,256]{2,1,0:T(8,128)(2,1)S(1)}, bf16[3,192,256]{2,1,0:T(8,128)(2,1)S(1)}, u32[]{:S(2)}, u32[]{:S(2)}) collective-permute-start(bf16[3,192,256]{2,1,0:T(8,128)(2,1)S(1)} %get-tuple-element.73), channel_id=1, source_target_pairs={{0,2},{1,3},{2,0},{3,1},{4,6},{5,7},{6,4},{7,5},{8,10},{9,11},{10,... | collective-permute-start | bytes 884744 | tf_op jit(solution)/shard_map/ppermute | solution.py:443
  66.8 6.0 %collective-permute-done.24.far_ref = bf16[2,576,256]{2,1,0:T(8,128)(2,1)S(1)} collective-permute-done((bf16[2,576,256]{2,1,0:T(8,128)(2,1)S(1)}, bf16[2,576,256]{2,1,0:T(8,128)(2,1)S(1)}, u32[]{:S(2)}, u32[]{:S(2)}) %collective-permute-start.24) | collective-permute-done | bytes 589856 | tf_op jit(solution)/shard_map/ppermute | solution.py:447
  73.0 1.8 %collective-permute-start.25 = (bf16[2,192,256]{2,1,0:T(8,128)(2,1)S(1)}, bf16[2,192,256]{2,1,0:T(8,128)(2,1)S(1)}, u32[]{:S(2)}, u32[]{:S(2)}) collective-permute-start(bf16[2,192,256]{2,1,0:T(8,128)(2,1)S(1)} %get-tuple-element.78), channel_id=1, source_target_pairs={{0,1},{1,2},{2,3},{3,0},{4,5},{5,6},{6,7},{7,4},{8,9},{9,10},{10,1... | collective-permute-start | bytes 589832 | tf_op jit(solution)/shard_map/ppermute | solution.py:443
  74.8 1.5 %collective-permute-start.26 = (bf16[2,192,256]{2,1,0:T(8,128)(2,1)S(1)}, bf16[2,192,256]{2,1,0:T(8,128)(2,1)S(1)}, u32[]{:S(2)}, u32[]{:S(2)}) collective-permute-start(bf16[2,192,256]{2,1,0:T(8,128)(2,1)S(1)} %get-tuple-element.79), channel_id=1, source_target_pairs={{0,3},{1,0},{2,1},{3,2},{4,7},{5,4},{6,5},{7,6},{8,11},{9,8},{10,9... | collective-permute-start | bytes 589832 | tf_op jit(solution)/shard_map/ppermute | solution.py:443
  76.3 1.1 %collective-permute-start.27 = (bf16[2,192,256]{2,1,0:T(8,128)(2,1)S(1)}, bf16[2,192,256]{2,1,0:T(8,128)(2,1)S(1)}, u32[]{:S(2)}, u32[]{:S(2)}) collective-permute-start(bf16[2,192,256]{2,1,0:T(8,128)(2,1)S(1)} %get-tuple-element.80), channel_id=1, source_target_pairs={{0,2},{1,3},{2,0},{3,1},{4,6},{5,7},{6,4},{7,5},{8,10},{9,11},{10,... | collective-permute-start | bytes 589832 | tf_op jit(solution)/shard_map/ppermute | solution.py:443
  78.0 1.3 %early.1 = (bf16[192,2048]{1,0:T(8,128)(2,1)}, bf16[192,2048]{1,0:T(8,128)(2,1)}, bf16[192,2048]{1,0:T(8,128)(2,1)}) custom-call(bf16[192,256]{1,0:T(8,128)(2,1)S(1)} %get-tuple-element.56.refs_0_, bf16[192,256]{1,0:T(8,128)(2,1)S(1)} %collective-permute-done.10.refs_4_.refs_1_, bf16[192,256]{1,0:T(8,128)(2,1)S(1)} %collective-permute-done.11.refs_5_.refs_2_, ...), custom_call_target="tpu_custom_call" | custom-call | bytes 2359296 | tf_op jit(solution)/shard_map/early/pallas_call | solution.py:404
  79.3 6.3 %collective-permute-done.25.refs_1_ = bf16[2,192,256]{2,1,0:T(8,128)(2,1)S(1)} collective-permute-done((bf16[2,192,256]{2,1,0:T(8,128)(2,1)S(1)}, bf16[2,192,256]{2,1,0:T(8,128)(2,1)S(1)}, u32[]{:S(2)}, u32[]{:S(2)}) %collective-permute-start.25) | collective-permute-done | bytes 196640 | tf_op jit(solution)/shard_map/ppermute | solution.py:443
  (51 shorter events, 7.9 us)
Async XLA Ops:
  0.6 9.1 %copy-start = (bf16[1,192,2048]{2,1,0:T(8,128)(2,1)S(1)}, bf16[1,192,2048]{2,1,0:T(8,128)(2,1)}, u32[]{:S(2)}) copy-start(bf16[1,192,2048]{2,1,0:T(8,128)(2,1)} %param.7) | copy-start | bytes 2359300
  0.6 9.0 %copy-start.1 = (bf16[1,192,2048]{2,1,0:T(8,128)(2,1)S(1)}, bf16[1,192,2048]{2,1,0:T(8,128)(2,1)}, u32[]{:S(2)}) copy-start(bf16[1,192,2048]{2,1,0:T(8,128)(2,1)} %param.8) | copy-start | bytes 2359300
  2.8 12.3 %collective-permute-start.3 = (bf16[2,192,256]{2,1,0:T(8,128)(2,1)}, bf16[2,192,256]{2,1,0:T(8,128)(2,1)S(1)}, u32[]{:S(2)}, u32[]{:S(2)}) collective-permute-start(bf16[2,192,256]{2,1,0:T(8,128)(2,1)} %get-tuple-element.45), channel_id=1, source_target_pairs={{0,1},{1,2},{2,3},{3,0},{4,5},{5,6},{6,7},{7,4},{8,9},{9,10},{10,1... | collective-permute-start | bytes 589832 | tf_op jit(solution)/shard_map/ppermute | solution.py:443
  4.5 12.2 %collective-permute-start.4 = (bf16[2,192,256]{2,1,0:T(8,128)(2,1)}, bf16[2,192,256]{2,1,0:T(8,128)(2,1)S(1)}, u32[]{:S(2)}, u32[]{:S(2)}) collective-permute-start(bf16[2,192,256]{2,1,0:T(8,128)(2,1)} %get-tuple-element.46), channel_id=1, source_target_pairs={{0,3},{1,0},{2,1},{3,2},{4,7},{5,4},{6,5},{7,6},{8,11},{9,8},{10,9... | collective-permute-start | bytes 589832 | tf_op jit(solution)/shard_map/ppermute | solution.py:443
  6.1 11.4 %collective-permute-start.5 = (bf16[2,192,256]{2,1,0:T(8,128)(2,1)}, bf16[2,192,256]{2,1,0:T(8,128)(2,1)S(1)}, u32[]{:S(2)}, u32[]{:S(2)}) collective-permute-start(bf16[2,192,256]{2,1,0:T(8,128)(2,1)} %get-tuple-element.47), channel_id=1, source_target_pairs={{0,2},{1,3},{2,0},{3,1},{4,6},{5,7},{6,4},{7,5},{8,10},{9,11},{10,... | collective-permute-start | bytes 589832 | tf_op jit(solution)/shard_map/ppermute | solution.py:443
  8.2 1.6 %collective-permute-start.2 = (f32[1,32]{1,0:T(1,128)S(1)}, f32[1,32]{1,0:T(1,128)S(1)}, u32[]{:S(2)}, u32[]{:S(2)}) collective-permute-start(f32[1,32]{1,0:T(1,128)S(1)} %copy-done.6), channel_id=1, source_target_pairs={{0,96},{32,0},{64,32},{96,64},{1,97},{33,1},{65,33},{97,65},{2,98}... | collective-permute-start | bytes 392 | tf_op jit(solution)/shard_map/ppermute | solution.py:454
  8.3 3.5 %collective-permute-start.1 = (f32[1,32]{1,0:T(1,128)S(1)}, f32[1,32]{1,0:T(1,128)S(1)}, u32[]{:S(2)}, u32[]{:S(2)}) collective-permute-start(f32[1,32]{1,0:T(1,128)S(1)} %copy-done.6), channel_id=1, source_target_pairs={{0,64},{32,96},{64,0},{96,32},{1,65},{33,97},{65,1},{97,33},{2,66}... | collective-permute-start | bytes 392 | tf_op jit(solution)/shard_map/ppermute | solution.py:454
  9.8 3.9 %collective-permute-start = (f32[1,32]{1,0:T(1,128)S(1)}, f32[1,32]{1,0:T(1,128)S(1)}, u32[]{:S(2)}, u32[]{:S(2)}) collective-permute-start(f32[1,32]{1,0:T(1,128)S(1)} %copy-done.6), channel_id=1, source_target_pairs={{0,32},{32,64},{64,96},{96,0},{1,33},{33,65},{65,97},{97,1},{2,34}... | collective-permute-start | bytes 392 | tf_op jit(solution)/shard_map/ppermute | solution.py:454
  11.8 11.1 %collective-permute-start.15 = (bf16[2,192,256]{2,1,0:T(8,128)(2,1)S(1)}, bf16[2,192,256]{2,1,0:T(8,128)(2,1)S(1)}, u32[]{:S(2)}, u32[]{:S(2)}) collective-permute-start(bf16[2,192,256]{2,1,0:T(8,128)(2,1)S(1)} %get-tuple-element.62), channel_id=1, source_target_pairs={{0,1},{1,2},{2,3},{3,0},{4,5},{5,6},{6,7},{7,4},{8,9},{9,10},{10,1... | collective-permute-start | bytes 589832 | tf_op jit(solution)/shard_map/ppermute | solution.py:443
  13.7 11.6 %collective-permute-start.16 = (bf16[2,192,256]{2,1,0:T(8,128)(2,1)S(1)}, bf16[2,192,256]{2,1,0:T(8,128)(2,1)S(1)}, u32[]{:S(2)}, u32[]{:S(2)}) collective-permute-start(bf16[2,192,256]{2,1,0:T(8,128)(2,1)S(1)} %get-tuple-element.63), channel_id=1, source_target_pairs={{0,3},{1,0},{2,1},{3,2},{4,7},{5,4},{6,5},{7,6},{8,11},{9,8},{10,9... | collective-permute-start | bytes 589832 | tf_op jit(solution)/shard_map/ppermute | solution.py:443
  15.1 5.7 %copy-start.2 = (bf16[1,192,2048]{2,1,0:T(8,128)(2,1)S(1)}, bf16[1,192,2048]{2,1,0:T(8,128)(2,1)}, u32[]{:S(2)}) copy-start(bf16[1,192,2048]{2,1,0:T(8,128)(2,1)} %param.6) | copy-start | bytes 2359300
  15.1 5.7 %copy-start.3 = (bf16[1,192,2048]{2,1,0:T(8,128)(2,1)S(1)}, bf16[1,192,2048]{2,1,0:T(8,128)(2,1)}, u32[]{:S(2)}) copy-start(bf16[1,192,2048]{2,1,0:T(8,128)(2,1)} %param.9) | copy-start | bytes 2359300
  15.1 10.3 %collective-permute-start.14 = (bf16[2,192,256]{2,1,0:T(8,128)(2,1)S(1)}, bf16[2,192,256]{2,1,0:T(8,128)(2,1)S(1)}, u32[]{:S(2)}, u32[]{:S(2)}) collective-permute-start(bf16[2,192,256]{2,1,0:T(8,128)(2,1)S(1)} %get-tuple-element.48.refs_3_), channel_id=1, source_target_pairs={{0,2},{1,3},{2,0},{3,1},{4,6},{5,7},{6,4},{7,5},{8,10},{9,11},{10,... | collective-permute-start | bytes 589832 | tf_op jit(solution)/shard_map/ppermute | solution.py:443
  17.6 20.8 %collective-permute-start.9 = (bf16[2,576,256]{2,1,0:T(8,128)(2,1)S(1)}, bf16[2,576,256]{2,1,0:T(8,128)(2,1)S(1)}, u32[]{:S(2)}, u32[]{:S(2)}) collective-permute-start(bf16[2,576,256]{2,1,0:T(8,128)(2,1)S(1)} %edge.2.after), channel_id=1, source_target_pairs={{0,4},{1,5},{2,6},{3,7},{4,8},{5,9},{6,10},{7,11},{8,12},{9,13},{1... | collective-permute-start | bytes 1769480 | tf_op jit(solution)/shard_map/ppermute | solution.py:447
  20.8 14.6 %collective-permute-start.6 = (bf16[2,192,256]{2,1,0:T(8,128)(2,1)S(1)}, bf16[2,192,256]{2,1,0:T(8,128)(2,1)S(1)}, u32[]{:S(2)}, u32[]{:S(2)}) collective-permute-start(bf16[2,192,256]{2,1,0:T(8,128)(2,1)S(1)} %get-tuple-element.49.after), channel_id=1, source_target_pairs={{0,1},{1,2},{2,3},{3,0},{4,5},{5,6},{6,7},{7,4},{8,9},{9,10},{10,1... | collective-permute-start | bytes 589832 | tf_op jit(solution)/shard_map/ppermute | solution.py:443
  22.9 8.7 %collective-permute-start.7 = (bf16[2,192,256]{2,1,0:T(8,128)(2,1)S(1)}, bf16[2,192,256]{2,1,0:T(8,128)(2,1)S(1)}, u32[]{:S(2)}, u32[]{:S(2)}) collective-permute-start(bf16[2,192,256]{2,1,0:T(8,128)(2,1)S(1)} %get-tuple-element.54), channel_id=1, source_target_pairs={{0,3},{1,0},{2,1},{3,2},{4,7},{5,4},{6,5},{7,6},{8,11},{9,8},{10,9... | collective-permute-start | bytes 589832 | tf_op jit(solution)/shard_map/ppermute | solution.py:443
  25.3 8.5 %collective-permute-start.8 = (bf16[2,192,256]{2,1,0:T(8,128)(2,1)S(1)}, bf16[2,192,256]{2,1,0:T(8,128)(2,1)S(1)}, u32[]{:S(2)}, u32[]{:S(2)}) collective-permute-start(bf16[2,192,256]{2,1,0:T(8,128)(2,1)S(1)} %get-tuple-element.55), channel_id=1, source_target_pairs={{0,2},{1,3},{2,0},{3,1},{4,6},{5,7},{6,4},{7,5},{8,10},{9,11},{10,... | collective-permute-start | bytes 589832 | tf_op jit(solution)/shard_map/ppermute | solution.py:443
  25.5 28.2 %collective-permute-start.20 = (bf16[2,576,256]{2,1,0:T(8,128)(2,1)S(1)}, bf16[2,576,256]{2,1,0:T(8,128)(2,1)S(1)}, u32[]{:S(2)}, u32[]{:S(2)}) collective-permute-start(bf16[2,576,256]{2,1,0:T(8,128)(2,1)S(1)} %edge.3), channel_id=1, source_target_pairs={{0,4},{1,5},{2,6},{3,7},{4,8},{5,9},{6,10},{7,11},{8,12},{9,13},{1... | collective-permute-start | bytes 1769480 | tf_op jit(solution)/shard_map/ppermute | solution.py:447
  31.6 19.8 %collective-permute-start.17 = (bf16[2,192,256]{2,1,0:T(8,128)(2,1)S(1)}, bf16[2,192,256]{2,1,0:T(8,128)(2,1)S(1)}, u32[]{:S(2)}, u32[]{:S(2)}) collective-permute-start(bf16[2,192,256]{2,1,0:T(8,128)(2,1)S(1)} %get-tuple-element.50.after), channel_id=1, source_target_pairs={{0,1},{1,2},{2,3},{3,0},{4,5},{5,6},{6,7},{7,4},{8,9},{9,10},{10,1... | collective-permute-start | bytes 589832 | tf_op jit(solution)/shard_map/ppermute | solution.py:443
  33.8 14.3 %collective-permute-start.18 = (bf16[2,192,256]{2,1,0:T(8,128)(2,1)S(1)}, bf16[2,192,256]{2,1,0:T(8,128)(2,1)S(1)}, u32[]{:S(2)}, u32[]{:S(2)}) collective-permute-start(bf16[2,192,256]{2,1,0:T(8,128)(2,1)S(1)} %get-tuple-element.64), channel_id=1, source_target_pairs={{0,3},{1,0},{2,1},{3,2},{4,7},{5,4},{6,5},{7,6},{8,11},{9,8},{10,9... | collective-permute-start | bytes 589832 | tf_op jit(solution)/shard_map/ppermute | solution.py:443
  35.5 13.5 %collective-permute-start.19 = (bf16[2,192,256]{2,1,0:T(8,128)(2,1)S(1)}, bf16[2,192,256]{2,1,0:T(8,128)(2,1)S(1)}, u32[]{:S(2)}, u32[]{:S(2)}) collective-permute-start(bf16[2,192,256]{2,1,0:T(8,128)(2,1)S(1)} %get-tuple-element.65), channel_id=1, source_target_pairs={{0,2},{1,3},{2,0},{3,1},{4,6},{5,7},{6,4},{7,5},{8,10},{9,11},{10,... | collective-permute-start | bytes 589832 | tf_op jit(solution)/shard_map/ppermute | solution.py:443
  43.7 17.8 %collective-permute-start.13 = (bf16[2,576,256]{2,1,0:T(8,128)(2,1)S(1)}, bf16[2,576,256]{2,1,0:T(8,128)(2,1)S(1)}, u32[]{:S(2)}, u32[]{:S(2)}) collective-permute-start(bf16[2,576,256]{2,1,0:T(8,128)(2,1)S(1)} %get-tuple-element.61), channel_id=1, source_target_pairs={{0,28},{1,29},{2,30},{3,31},{4,0},{5,1},{6,2},{7,3},{8,4},{9,5},{1... | collective-permute-start | bytes 1769480 | tf_op jit(solution)/shard_map/ppermute | solution.py:447
  48.1 13.4 %collective-permute-start.10 = (bf16[192,256]{1,0:T(8,128)(2,1)S(1)}, bf16[192,256]{1,0:T(8,128)(2,1)S(1)}, u32[]{:S(2)}, u32[]{:S(2)}) collective-permute-start(bf16[192,256]{1,0:T(8,128)(2,1)S(1)} %get-tuple-element.57), channel_id=1, source_target_pairs={{0,1},{1,2},{2,3},{3,0},{4,5},{5,6},{6,7},{7,4},{8,9},{9,10},{10,1... | collective-permute-start | bytes 294920 | tf_op jit(solution)/shard_map/ppermute | solution.py:443
  49.0 12.5 %collective-permute-start.11 = (bf16[192,256]{1,0:T(8,128)(2,1)S(1)}, bf16[192,256]{1,0:T(8,128)(2,1)S(1)}, u32[]{:S(2)}, u32[]{:S(2)}) collective-permute-start(bf16[192,256]{1,0:T(8,128)(2,1)S(1)} %get-tuple-element.58), channel_id=1, source_target_pairs={{0,3},{1,0},{2,1},{3,2},{4,7},{5,4},{6,5},{7,6},{8,11},{9,8},{10,9... | collective-permute-start | bytes 294920 | tf_op jit(solution)/shard_map/ppermute | solution.py:443
  51.4 10.1 %collective-permute-start.12 = (bf16[192,256]{1,0:T(8,128)(2,1)S(1)}, bf16[192,256]{1,0:T(8,128)(2,1)S(1)}, u32[]{:S(2)}, u32[]{:S(2)}) collective-permute-start(bf16[192,256]{1,0:T(8,128)(2,1)S(1)} %get-tuple-element.59), channel_id=1, source_target_pairs={{0,2},{1,3},{2,0},{3,1},{4,6},{5,7},{6,4},{7,5},{8,10},{9,11},{10,... | collective-permute-start | bytes 294920 | tf_op jit(solution)/shard_map/ppermute | solution.py:443
  59.0 13.8 %collective-permute-start.24 = (bf16[2,576,256]{2,1,0:T(8,128)(2,1)S(1)}, bf16[2,576,256]{2,1,0:T(8,128)(2,1)S(1)}, u32[]{:S(2)}, u32[]{:S(2)}) collective-permute-start(bf16[2,576,256]{2,1,0:T(8,128)(2,1)S(1)} %get-tuple-element.76), channel_id=1, source_target_pairs={{0,28},{1,29},{2,30},{3,31},{4,0},{5,1},{6,2},{7,3},{8,4},{9,5},{1... | collective-permute-start | bytes 1769480 | tf_op jit(solution)/shard_map/ppermute | solution.py:447
  61.7 14.6 %collective-permute-start.21 = (bf16[3,192,256]{2,1,0:T(8,128)(2,1)S(1)}, bf16[3,192,256]{2,1,0:T(8,128)(2,1)S(1)}, u32[]{:S(2)}, u32[]{:S(2)}) collective-permute-start(bf16[3,192,256]{2,1,0:T(8,128)(2,1)S(1)} %get-tuple-element.71), channel_id=1, source_target_pairs={{0,1},{1,2},{2,3},{3,0},{4,5},{5,6},{6,7},{7,4},{8,9},{9,10},{10,1... | collective-permute-start | bytes 884744 | tf_op jit(solution)/shard_map/ppermute | solution.py:443
  63.1 14.3 %collective-permute-start.22 = (bf16[3,192,256]{2,1,0:T(8,128)(2,1)S(1)}, bf16[3,192,256]{2,1,0:T(8,128)(2,1)S(1)}, u32[]{:S(2)}, u32[]{:S(2)}) collective-permute-start(bf16[3,192,256]{2,1,0:T(8,128)(2,1)S(1)} %get-tuple-element.72), channel_id=1, source_target_pairs={{0,3},{1,0},{2,1},{3,2},{4,7},{5,4},{6,5},{7,6},{8,11},{9,8},{10,9... | collective-permute-start | bytes 884744 | tf_op jit(solution)/shard_map/ppermute | solution.py:443
  65.0 13.0 %collective-permute-start.23 = (bf16[3,192,256]{2,1,0:T(8,128)(2,1)S(1)}, bf16[3,192,256]{2,1,0:T(8,128)(2,1)S(1)}, u32[]{:S(2)}, u32[]{:S(2)}) collective-permute-start(bf16[3,192,256]{2,1,0:T(8,128)(2,1)S(1)} %get-tuple-element.73), channel_id=1, source_target_pairs={{0,2},{1,3},{2,0},{3,1},{4,6},{5,7},{6,4},{7,5},{8,10},{9,11},{10,... | collective-permute-start | bytes 884744 | tf_op jit(solution)/shard_map/ppermute | solution.py:443
  73.0 12.6 %collective-permute-start.25 = (bf16[2,192,256]{2,1,0:T(8,128)(2,1)S(1)}, bf16[2,192,256]{2,1,0:T(8,128)(2,1)S(1)}, u32[]{:S(2)}, u32[]{:S(2)}) collective-permute-start(bf16[2,192,256]{2,1,0:T(8,128)(2,1)S(1)} %get-tuple-element.78), channel_id=1, source_target_pairs={{0,1},{1,2},{2,3},{3,0},{4,5},{5,6},{6,7},{7,4},{8,9},{9,10},{10,1... | collective-permute-start | bytes 589832 | tf_op jit(solution)/shard_map/ppermute | solution.py:443
  74.8 10.8 %collective-permute-start.26 = (bf16[2,192,256]{2,1,0:T(8,128)(2,1)S(1)}, bf16[2,192,256]{2,1,0:T(8,128)(2,1)S(1)}, u32[]{:S(2)}, u32[]{:S(2)}) collective-permute-start(bf16[2,192,256]{2,1,0:T(8,128)(2,1)S(1)} %get-tuple-element.79), channel_id=1, source_target_pairs={{0,3},{1,0},{2,1},{3,2},{4,7},{5,4},{6,5},{7,6},{8,11},{9,8},{10,9... | collective-permute-start | bytes 589832 | tf_op jit(solution)/shard_map/ppermute | solution.py:443
  76.3 9.3 %collective-permute-start.27 = (bf16[2,192,256]{2,1,0:T(8,128)(2,1)S(1)}, bf16[2,192,256]{2,1,0:T(8,128)(2,1)S(1)}, u32[]{:S(2)}, u32[]{:S(2)}) collective-permute-start(bf16[2,192,256]{2,1,0:T(8,128)(2,1)S(1)} %get-tuple-element.80), channel_id=1, source_target_pairs={{0,2},{1,3},{2,0},{3,1},{4,6},{5,7},{6,4},{7,5},{8,10},{9,11},{10,... | collective-permute-start | bytes 589832 | tf_op jit(solution)/shard_map/ppermute | solution.py:443
  (3 other events, 3.4 us)

commit v10 on v7

--- a/solution.py
+++ b/solution.py
@@ -255,7 +255,10 @@
             dscore = (prob * (dprob - delta)).astype(jnp.bfloat16)
             prob_half = prob.astype(jnp.bfloat16)
             query_out[at, lanes] = (
-                jnp.dot(dscore, key, preferred_element_type=jnp.float32) * scale
+                lax.dot_general(
+                    key, dscore, (((0,), (1,)), ((), ())), preferred_element_type=jnp.float32
+                ).T
+                * scale
             ).astype(jnp.bfloat16)
             for kind, (left, right, held, scaling) in enumerate(
                 ((dscore, query, key_grad, scale), (prob_half, grad, value_grad, 1.0))

time: 86.4 us -> 87 us (level)
  Pallas kernels: 16 us -> 17.4 us
    pallas_call x2, Pallas kernels: 10.6 us -> 11.9 us  [attend(): pl.pallas_call(functools.partial(attend_kernel, chunk, total_rows), out_s...]
    ppermute x4, waiting for transfers between devices: 8.87 us -> 7.7 us  [next_row(): return lax.ppermute(value, 'ctx', pairs)]
  transfers between devices with their start and end apart: 28 -> 28, of which waited for: 10 -> 8; matrix products, arithmetic and copies ran while one was open for 0% -> 0% of each run, Pallas kernels for 15% -> 16%
where the time goes in v10:
time: 87 us; the launch traced here: 86.9 us
  starting transfers between devices  47.1 us (54%)
  waiting for transfers between devices  20.8 us (24%)
  Pallas kernels  17.4 us (20%)
  between operations  1.01 us (1%)
    ppermute x21, starting transfers between devices, swap(): return lax.ppermute(value, ('dp', 'ctx'), pairs)  32.5 us
    ppermute x21, waiting for transfers between devices, swap(): return lax.ppermute(value, ('dp', 'ctx'), pairs)  12.3 us
    pallas_call x2, Pallas kernels, attend(): pl.pallas_call(functools.partial(attend_kernel, chunk, total_rows), out_s...  11.9 us
    ppermute x4, starting transfers between devices, next_row(): return lax.ppermute(value, 'ctx', pairs)  11.9 us
    ppermute x4, waiting for transfers between devices, next_row(): return lax.ppermute(value, 'ctx', pairs)  7.7 us
    ppermute x3, starting transfers between devices, shards(): lax.ppermute(text, 'dp', [(source, (source + away) % samples) for source...  2.73 us
    pallas_call x1, Pallas kernels, first_pack(): pl.pallas_call(first_pack_kernel, out_shape=(message,) * (GROUP - 1) + (j...  2.15 us
  transfers between devices with their start and end apart: 28, of which 8 were waited for; matrix products, arithmetic and copies ran while one was open for 0% of the time, Pallas kernels for 16%

profile of v10, /device:TPU:0, one launch (start us, length us, event | category | flops | bytes accessed | tf_op | source)
XLA Modules:
  0.0 86.9 jit_solution(5072633949070329081)
XLA Ops:
  0.7 2.1 %first_pack.1 = (bf16[2,192,256]{2,1,0:T(8,128)(2,1)}, bf16[2,192,256]{2,1,0:T(8,128)(2,1)}, bf16[2,192,256]{2,1,0:T(8,128)(2,1)}, f32[1,32]{1,0:T(1,128)}) custom-call(bf16[192,2048]{1,0:T(8,128)(2,1)} %bitcast.7, bf16[192,2048]{1,0:T(8,128)(2,1)} %bitcast.13, s32[1,32]{1,0:T(1,128)} %lengths_ref.1, s32[1,32]{1,0:T(1,128)} %flags_ref.1), custom_call_target="tpu_custom_call" | custom-call | bytes 1179648 | tf_op jit(solution)/shard_map/first_pack/pallas_call | solution.py:80
  2.8 1.7 %collective-permute-start.3 = (bf16[2,192,256]{2,1,0:T(8,128)(2,1)}, bf16[2,192,256]{2,1,0:T(8,128)(2,1)S(1)}, u32[]{:S(2)}, u32[]{:S(2)}) collective-permute-start(bf16[2,192,256]{2,1,0:T(8,128)(2,1)} %get-tuple-element.45), channel_id=1, source_target_pairs={{0,1},{1,2},{2,3},{3,0},{4,5},{5,6},{6,7},{7,4},{8,9},{9,10},{10,1... | collective-permute-start | bytes 589832 | tf_op jit(solution)/shard_map/ppermute | solution.py:443
  4.5 1.6 %collective-permute-start.4 = (bf16[2,192,256]{2,1,0:T(8,128)(2,1)}, bf16[2,192,256]{2,1,0:T(8,128)(2,1)S(1)}, u32[]{:S(2)}, u32[]{:S(2)}) collective-permute-start(bf16[2,192,256]{2,1,0:T(8,128)(2,1)} %get-tuple-element.46), channel_id=1, source_target_pairs={{0,3},{1,0},{2,1},{3,2},{4,7},{5,4},{6,5},{7,6},{8,11},{9,8},{10,9... | collective-permute-start | bytes 589832 | tf_op jit(solution)/shard_map/ppermute | solution.py:443
  6.1 2.1 %collective-permute-start.5 = (bf16[2,192,256]{2,1,0:T(8,128)(2,1)}, bf16[2,192,256]{2,1,0:T(8,128)(2,1)S(1)}, u32[]{:S(2)}, u32[]{:S(2)}) collective-permute-start(bf16[2,192,256]{2,1,0:T(8,128)(2,1)} %get-tuple-element.47), channel_id=1, source_target_pairs={{0,2},{1,3},{2,0},{3,1},{4,6},{5,7},{6,4},{7,5},{8,10},{9,11},{10,... | collective-permute-start | bytes 589832 | tf_op jit(solution)/shard_map/ppermute | solution.py:443
  8.3 1.4 %collective-permute-start.1 = (f32[1,32]{1,0:T(1,128)S(1)}, f32[1,32]{1,0:T(1,128)S(1)}, u32[]{:S(2)}, u32[]{:S(2)}) collective-permute-start(f32[1,32]{1,0:T(1,128)S(1)} %copy-done.6), channel_id=1, source_target_pairs={{0,64},{32,96},{64,0},{96,32},{1,65},{33,97},{65,1},{97,33},{2,66}... | collective-permute-start | bytes 392 | tf_op jit(solution)/shard_map/ppermute | solution.py:454
  9.8 1.2 %collective-permute-start = (f32[1,32]{1,0:T(1,128)S(1)}, f32[1,32]{1,0:T(1,128)S(1)}, u32[]{:S(2)}, u32[]{:S(2)}) collective-permute-start(f32[1,32]{1,0:T(1,128)S(1)} %copy-done.6), channel_id=1, source_target_pairs={{0,32},{32,64},{64,96},{96,0},{1,33},{33,65},{65,97},{97,1},{2,34}... | collective-permute-start | bytes 392 | tf_op jit(solution)/shard_map/ppermute | solution.py:454
  11.8 2.0 %collective-permute-start.15 = (bf16[2,192,256]{2,1,0:T(8,128)(2,1)S(1)}, bf16[2,192,256]{2,1,0:T(8,128)(2,1)S(1)}, u32[]{:S(2)}, u32[]{:S(2)}) collective-permute-start(bf16[2,192,256]{2,1,0:T(8,128)(2,1)S(1)} %get-tuple-element.62), channel_id=1, source_target_pairs={{0,3},{1,0},{2,1},{3,2},{4,7},{5,4},{6,5},{7,6},{8,11},{9,8},{10,9... | collective-permute-start | bytes 589832 | tf_op jit(solution)/shard_map/ppermute | solution.py:443
  13.8 2.0 %collective-permute-start.16 = (bf16[2,192,256]{2,1,0:T(8,128)(2,1)S(1)}, bf16[2,192,256]{2,1,0:T(8,128)(2,1)S(1)}, u32[]{:S(2)}, u32[]{:S(2)}) collective-permute-start(bf16[2,192,256]{2,1,0:T(8,128)(2,1)S(1)} %get-tuple-element.63), channel_id=1, source_target_pairs={{0,2},{1,3},{2,0},{3,1},{4,6},{5,7},{6,4},{7,5},{8,10},{9,11},{10,... | collective-permute-start | bytes 589832 | tf_op jit(solution)/shard_map/ppermute | solution.py:443
  15.8 1.8 %collective-permute-done.5.three.key_three = bf16[2,192,256]{2,1,0:T(8,128)(2,1)S(1)} collective-permute-done((bf16[2,192,256]{2,1,0:T(8,128)(2,1)}, bf16[2,192,256]{2,1,0:T(8,128)(2,1)S(1)}, u32[]{:S(2)}, u32[]{:S(2)}) %collective-permute-start.5) | collective-permute-done | bytes 196640 | tf_op jit(solution)/shard_map/ppermute | solution.py:443
  17.6 3.1 %collective-permute-start.9 = (bf16[2,576,256]{2,1,0:T(8,128)(2,1)S(1)}, bf16[2,576,256]{2,1,0:T(8,128)(2,1)S(1)}, u32[]{:S(2)}, u32[]{:S(2)}) collective-permute-start(bf16[2,576,256]{2,1,0:T(8,128)(2,1)S(1)} %edge.2.after), channel_id=1, source_target_pairs={{0,4},{1,5},{2,6},{3,7},{4,8},{5,9},{6,10},{7,11},{8,12},{9,13},{1... | collective-permute-start | bytes 1769480 | tf_op jit(solution)/shard_map/ppermute | solution.py:447
  22.1 4.0 %collective-permute-start.7 = (bf16[2,192,256]{2,1,0:T(8,128)(2,1)S(1)}, bf16[2,192,256]{2,1,0:T(8,128)(2,1)S(1)}, u32[]{:S(2)}, u32[]{:S(2)}) collective-permute-start(bf16[2,192,256]{2,1,0:T(8,128)(2,1)S(1)} %get-tuple-element.54), channel_id=1, source_target_pairs={{0,3},{1,0},{2,1},{3,2},{4,7},{5,4},{6,5},{7,6},{8,11},{9,8},{10,9... | collective-permute-start | bytes 589832 | tf_op jit(solution)/shard_map/ppermute | solution.py:443
  26.1 1.7 %collective-permute-start.8 = (bf16[2,192,256]{2,1,0:T(8,128)(2,1)S(1)}, bf16[2,192,256]{2,1,0:T(8,128)(2,1)S(1)}, u32[]{:S(2)}, u32[]{:S(2)}) collective-permute-start(bf16[2,192,256]{2,1,0:T(8,128)(2,1)S(1)} %get-tuple-element.55), channel_id=1, source_target_pairs={{0,2},{1,3},{2,0},{3,1},{4,6},{5,7},{6,4},{7,5},{8,10},{9,11},{10,... | collective-permute-start | bytes 589832 | tf_op jit(solution)/shard_map/ppermute | solution.py:443
  27.8 2.6 %collective-permute-start.20 = (bf16[2,576,256]{2,1,0:T(8,128)(2,1)S(1)}, bf16[2,576,256]{2,1,0:T(8,128)(2,1)S(1)}, u32[]{:S(2)}, u32[]{:S(2)}) collective-permute-start(bf16[2,576,256]{2,1,0:T(8,128)(2,1)S(1)} %edge.3), channel_id=1, source_target_pairs={{0,4},{1,5},{2,6},{3,7},{4,8},{5,9},{6,10},{7,11},{8,12},{9,13},{1... | collective-permute-start | bytes 1769480 | tf_op jit(solution)/shard_map/ppermute | solution.py:447
  30.4 1.5 %collective-permute-done.7.query_two = bf16[2,192,256]{2,1,0:T(8,128)(2,1)S(1)} collective-permute-done((bf16[2,192,256]{2,1,0:T(8,128)(2,1)S(1)}, bf16[2,192,256]{2,1,0:T(8,128)(2,1)S(1)}, u32[]{:S(2)}, u32[]{:S(2)}) %collective-permute-start.7) | collective-permute-done | bytes 196640 | tf_op jit(solution)/shard_map/ppermute | solution.py:443
  31.8 1.3 %collective-permute-start.17 = (bf16[2,192,256]{2,1,0:T(8,128)(2,1)S(1)}, bf16[2,192,256]{2,1,0:T(8,128)(2,1)S(1)}, u32[]{:S(2)}, u32[]{:S(2)}) collective-permute-start(bf16[2,192,256]{2,1,0:T(8,128)(2,1)S(1)} %get-tuple-element.50.after), channel_id=1, source_target_pairs={{0,1},{1,2},{2,3},{3,0},{4,5},{5,6},{6,7},{7,4},{8,9},{9,10},{10,1... | collective-permute-start | bytes 589832 | tf_op jit(solution)/shard_map/ppermute | solution.py:443
  33.8 1.8 %collective-permute-start.18 = (bf16[2,192,256]{2,1,0:T(8,128)(2,1)S(1)}, bf16[2,192,256]{2,1,0:T(8,128)(2,1)S(1)}, u32[]{:S(2)}, u32[]{:S(2)}) collective-permute-start(bf16[2,192,256]{2,1,0:T(8,128)(2,1)S(1)} %get-tuple-element.64), channel_id=1, source_target_pairs={{0,3},{1,0},{2,1},{3,2},{4,7},{5,4},{6,5},{7,6},{8,11},{9,8},{10,9... | collective-permute-start | bytes 589832 | tf_op jit(solution)/shard_map/ppermute | solution.py:443
  35.7 1.9 %collective-permute-start.19 = (bf16[2,192,256]{2,1,0:T(8,128)(2,1)S(1)}, bf16[2,192,256]{2,1,0:T(8,128)(2,1)S(1)}, u32[]{:S(2)}, u32[]{:S(2)}) collective-permute-start(bf16[2,192,256]{2,1,0:T(8,128)(2,1)S(1)} %get-tuple-element.65), channel_id=1, source_target_pairs={{0,2},{1,3},{2,0},{3,1},{4,6},{5,7},{6,4},{7,5},{8,10},{9,11},{10,... | collective-permute-start | bytes 589832 | tf_op jit(solution)/shard_map/ppermute | solution.py:443
  38.4 5.9 %attend.2 = (bf16[192,256]{1,0:T(8,128)(2,1)S(1)}, bf16[192,256]{1,0:T(8,128)(2,1)S(1)}, bf16[192,256]{1,0:T(8,128)(2,1)S(1)}, bf16[192,256]{1,0:T(8,128)(2,1)S(...) custom-call(f32[1,32]{1,0:T(1,128)S(1)} %copy-done.6, ...), custom_call_target="tpu_custom_call" | custom-call | flops 4499999744 | tf_op jit(solution)/shard_map/attend/pallas_call | solution.py:292
  44.4 6.1 %collective-permute-start.13 = (bf16[2,576,256]{2,1,0:T(8,128)(2,1)S(1)}, bf16[2,576,256]{2,1,0:T(8,128)(2,1)S(1)}, u32[]{:S(2)}, u32[]{:S(2)}) collective-permute-start(bf16[2,576,256]{2,1,0:T(8,128)(2,1)S(1)} %get-tuple-element.61), channel_id=1, source_target_pairs={{0,28},{1,29},{2,30},{3,31},{4,0},{5,1},{6,2},{7,3},{8,4},{9,5},{1... | collective-permute-start | bytes 1769480 | tf_op jit(solution)/shard_map/ppermute | solution.py:447
  51.2 2.5 %collective-permute-start.11 = (bf16[192,256]{1,0:T(8,128)(2,1)S(1)}, bf16[192,256]{1,0:T(8,128)(2,1)S(1)}, u32[]{:S(2)}, u32[]{:S(2)}) collective-permute-start(bf16[192,256]{1,0:T(8,128)(2,1)S(1)} %get-tuple-element.58), channel_id=1, source_target_pairs={{0,3},{1,0},{2,1},{3,2},{4,7},{5,4},{6,5},{7,6},{8,11},{9,8},{10,9... | collective-permute-start | bytes 294920 | tf_op jit(solution)/shard_map/ppermute | solution.py:443
  53.7 0.9 collective-permute-start.12
  54.5 5.9 %attend.3 = (bf16[192,256]{1,0:T(8,128)(2,1)S(1)}, bf16[192,256]{1,0:T(8,128)(2,1)S(1)}, bf16[192,256]{1,0:T(8,128)(2,1)S(1)}, bf16[192,256]{1,0:T(8,128)(2,1)S(...) custom-call(f32[1,32]{1,0:T(1,128)S(1)} %copy-done.6, ...), custom_call_target="tpu_custom_call" | custom-call | flops 4499999744 | tf_op jit(solution)/shard_map/attend/pallas_call | solution.py:292
  60.9 1.1 %collective-permute-start.21 = (bf16[3,192,256]{2,1,0:T(8,128)(2,1)S(1)}, bf16[3,192,256]{2,1,0:T(8,128)(2,1)S(1)}, u32[]{:S(2)}, u32[]{:S(2)}) collective-permute-start(bf16[3,192,256]{2,1,0:T(8,128)(2,1)S(1)} %get-tuple-element.71), channel_id=1, source_target_pairs={{0,1},{1,2},{2,3},{3,0},{4,5},{5,6},{6,7},{7,4},{8,9},{9,10},{10,1... | collective-permute-start | bytes 884744 | tf_op jit(solution)/shard_map/ppermute | solution.py:443
  62.0 2.2 %collective-permute-start.22 = (bf16[3,192,256]{2,1,0:T(8,128)(2,1)S(1)}, bf16[3,192,256]{2,1,0:T(8,128)(2,1)S(1)}, u32[]{:S(2)}, u32[]{:S(2)}) collective-permute-start(bf16[3,192,256]{2,1,0:T(8,128)(2,1)S(1)} %get-tuple-element.72), channel_id=1, source_target_pairs={{0,3},{1,0},{2,1},{3,2},{4,7},{5,4},{6,5},{7,6},{8,11},{9,8},{10,9... | collective-permute-start | bytes 884744 | tf_op jit(solution)/shard_map/ppermute | solution.py:443
  64.2 1.6 %collective-permute-start.23 = (bf16[3,192,256]{2,1,0:T(8,128)(2,1)S(1)}, bf16[3,192,256]{2,1,0:T(8,128)(2,1)S(1)}, u32[]{:S(2)}, u32[]{:S(2)}) collective-permute-start(bf16[3,192,256]{2,1,0:T(8,128)(2,1)S(1)} %get-tuple-element.73), channel_id=1, source_target_pairs={{0,2},{1,3},{2,0},{3,1},{4,6},{5,7},{6,4},{7,5},{8,10},{9,11},{10,... | collective-permute-start | bytes 884744 | tf_op jit(solution)/shard_map/ppermute | solution.py:443
  65.7 6.9 %collective-permute-done.24.far_ref = bf16[2,576,256]{2,1,0:T(8,128)(2,1)S(1)} collective-permute-done((bf16[2,576,256]{2,1,0:T(8,128)(2,1)S(1)}, bf16[2,576,256]{2,1,0:T(8,128)(2,1)S(1)}, u32[]{:S(2)}, u32[]{:S(2)}) %collective-permute-start.24) | collective-permute-done | bytes 589856 | tf_op jit(solution)/shard_map/ppermute | solution.py:447
  72.8 1.1 %collective-permute-start.25 = (bf16[2,192,256]{2,1,0:T(8,128)(2,1)S(1)}, bf16[2,192,256]{2,1,0:T(8,128)(2,1)S(1)}, u32[]{:S(2)}, u32[]{:S(2)}) collective-permute-start(bf16[2,192,256]{2,1,0:T(8,128)(2,1)S(1)} %get-tuple-element.78), channel_id=1, source_target_pairs={{0,1},{1,2},{2,3},{3,0},{4,5},{5,6},{6,7},{7,4},{8,9},{9,10},{10,1... | collective-permute-start | bytes 589832 | tf_op jit(solution)/shard_map/ppermute | solution.py:443
  74.0 2.2 %collective-permute-start.26 = (bf16[2,192,256]{2,1,0:T(8,128)(2,1)S(1)}, bf16[2,192,256]{2,1,0:T(8,128)(2,1)S(1)}, u32[]{:S(2)}, u32[]{:S(2)}) collective-permute-start(bf16[2,192,256]{2,1,0:T(8,128)(2,1)S(1)} %get-tuple-element.79), channel_id=1, source_target_pairs={{0,3},{1,0},{2,1},{3,2},{4,7},{5,4},{6,5},{7,6},{8,11},{9,8},{10,9... | collective-permute-start | bytes 589832 | tf_op jit(solution)/shard_map/ppermute | solution.py:443
  76.1 2.0 %collective-permute-done.21.refs_5_ = bf16[3,192,256]{2,1,0:T(8,128)(2,1)S(1)} collective-permute-done((bf16[3,192,256]{2,1,0:T(8,128)(2,1)S(1)}, bf16[3,192,256]{2,1,0:T(8,128)(2,1)S(1)}, u32[]{:S(2)}, u32[]{:S(2)}) %collective-permute-start.21) | collective-permute-done | bytes 294944 | tf_op jit(solution)/shard_map/ppermute | solution.py:443
  78.1 1.3 %early.1 = (bf16[192,2048]{1,0:T(8,128)(2,1)}, bf16[192,2048]{1,0:T(8,128)(2,1)}, bf16[192,2048]{1,0:T(8,128)(2,1)}) custom-call(bf16[192,256]{1,0:T(8,128)(2,1)S(1)} %get-tuple-element.56.refs_0_, bf16[192,256]{1,0:T(8,128)(2,1)S(1)} %collective-permute-done.10.refs_4_.refs_1_, bf16[192,256]{1,0:T(8,128)(2,1)S(1)} %collective-permute-done.11.refs_5_.refs_2_, ...), custom_call_target="tpu_custom_call" | custom-call | bytes 2359296 | tf_op jit(solution)/shard_map/early/pallas_call | solution.py:405
  79.4 6.3 %collective-permute-done.25.refs_1_ = bf16[2,192,256]{2,1,0:T(8,128)(2,1)S(1)} collective-permute-done((bf16[2,192,256]{2,1,0:T(8,128)(2,1)S(1)}, bf16[2,192,256]{2,1,0:T(8,128)(2,1)S(1)}, u32[]{:S(2)}, u32[]{:S(2)}) %collective-permute-start.25) | collective-permute-done | bytes 196640 | tf_op jit(solution)/shard_map/ppermute | solution.py:443
  85.8 0.9 %late.1 = (bf16[192,2048]{1,0:T(8,128)(2,1)}, bf16[192,2048]{1,0:T(8,128)(2,1)}) custom-call(bf16[2,192,256]{2,1,0:T(8,128)(2,1)S(1)} %get-tuple-element.77.refs_0_, bf16[2,192,256]{2,1,0:T(8,128)(2,1)S(1)} %collective-permute-done.25.refs_1_, ...), custom_call_target="tpu_custom_call", output_to_operand_aliasing={{0}: (4, {}), {1}: (5, {})} | custom-call | bytes 2359296 | tf_op jit(solution)/shard_map/late/pallas_call | solution.py:415
  (51 shorter events, 5.3 us)
Async XLA Ops:
  0.6 9.1 %copy-start = (bf16[1,192,2048]{2,1,0:T(8,128)(2,1)S(1)}, bf16[1,192,2048]{2,1,0:T(8,128)(2,1)}, u32[]{:S(2)}) copy-start(bf16[1,192,2048]{2,1,0:T(8,128)(2,1)} %param.7) | copy-start | bytes 2359300
  0.6 9.0 %copy-start.1 = (bf16[1,192,2048]{2,1,0:T(8,128)(2,1)S(1)}, bf16[1,192,2048]{2,1,0:T(8,128)(2,1)}, u32[]{:S(2)}) copy-start(bf16[1,192,2048]{2,1,0:T(8,128)(2,1)} %param.8) | copy-start | bytes 2359300
  2.8 13.0 %collective-permute-start.3 = (bf16[2,192,256]{2,1,0:T(8,128)(2,1)}, bf16[2,192,256]{2,1,0:T(8,128)(2,1)S(1)}, u32[]{:S(2)}, u32[]{:S(2)}) collective-permute-start(bf16[2,192,256]{2,1,0:T(8,128)(2,1)} %get-tuple-element.45), channel_id=1, source_target_pairs={{0,1},{1,2},{2,3},{3,0},{4,5},{5,6},{6,7},{7,4},{8,9},{9,10},{10,1... | collective-permute-start | bytes 589832 | tf_op jit(solution)/shard_map/ppermute | solution.py:443
  4.5 11.3 %collective-permute-start.4 = (bf16[2,192,256]{2,1,0:T(8,128)(2,1)}, bf16[2,192,256]{2,1,0:T(8,128)(2,1)S(1)}, u32[]{:S(2)}, u32[]{:S(2)}) collective-permute-start(bf16[2,192,256]{2,1,0:T(8,128)(2,1)} %get-tuple-element.46), channel_id=1, source_target_pairs={{0,3},{1,0},{2,1},{3,2},{4,7},{5,4},{6,5},{7,6},{8,11},{9,8},{10,9... | collective-permute-start | bytes 589832 | tf_op jit(solution)/shard_map/ppermute | solution.py:443
  6.1 11.4 %collective-permute-start.5 = (bf16[2,192,256]{2,1,0:T(8,128)(2,1)}, bf16[2,192,256]{2,1,0:T(8,128)(2,1)S(1)}, u32[]{:S(2)}, u32[]{:S(2)}) collective-permute-start(bf16[2,192,256]{2,1,0:T(8,128)(2,1)} %get-tuple-element.47), channel_id=1, source_target_pairs={{0,2},{1,3},{2,0},{3,1},{4,6},{5,7},{6,4},{7,5},{8,10},{9,11},{10,... | collective-permute-start | bytes 589832 | tf_op jit(solution)/shard_map/ppermute | solution.py:443
  8.2 1.6 %collective-permute-start.2 = (f32[1,32]{1,0:T(1,128)S(1)}, f32[1,32]{1,0:T(1,128)S(1)}, u32[]{:S(2)}, u32[]{:S(2)}) collective-permute-start(f32[1,32]{1,0:T(1,128)S(1)} %copy-done.6), channel_id=1, source_target_pairs={{0,96},{32,0},{64,32},{96,64},{1,97},{33,1},{65,33},{97,65},{2,98}... | collective-permute-start | bytes 392 | tf_op jit(solution)/shard_map/ppermute | solution.py:454
  8.3 3.5 %collective-permute-start.1 = (f32[1,32]{1,0:T(1,128)S(1)}, f32[1,32]{1,0:T(1,128)S(1)}, u32[]{:S(2)}, u32[]{:S(2)}) collective-permute-start(f32[1,32]{1,0:T(1,128)S(1)} %copy-done.6), channel_id=1, source_target_pairs={{0,64},{32,96},{64,0},{96,32},{1,65},{33,97},{65,1},{97,33},{2,66}... | collective-permute-start | bytes 392 | tf_op jit(solution)/shard_map/ppermute | solution.py:454
  9.8 4.0 %collective-permute-start = (f32[1,32]{1,0:T(1,128)S(1)}, f32[1,32]{1,0:T(1,128)S(1)}, u32[]{:S(2)}, u32[]{:S(2)}) collective-permute-start(f32[1,32]{1,0:T(1,128)S(1)} %copy-done.6), channel_id=1, source_target_pairs={{0,32},{32,64},{64,96},{96,0},{1,33},{33,65},{65,97},{97,1},{2,34}... | collective-permute-start | bytes 392 | tf_op jit(solution)/shard_map/ppermute | solution.py:454
  11.8 10.2 %collective-permute-start.15 = (bf16[2,192,256]{2,1,0:T(8,128)(2,1)S(1)}, bf16[2,192,256]{2,1,0:T(8,128)(2,1)S(1)}, u32[]{:S(2)}, u32[]{:S(2)}) collective-permute-start(bf16[2,192,256]{2,1,0:T(8,128)(2,1)S(1)} %get-tuple-element.62), channel_id=1, source_target_pairs={{0,3},{1,0},{2,1},{3,2},{4,7},{5,4},{6,5},{7,6},{8,11},{9,8},{10,9... | collective-permute-start | bytes 589832 | tf_op jit(solution)/shard_map/ppermute | solution.py:443
  13.8 12.3 %collective-permute-start.16 = (bf16[2,192,256]{2,1,0:T(8,128)(2,1)S(1)}, bf16[2,192,256]{2,1,0:T(8,128)(2,1)S(1)}, u32[]{:S(2)}, u32[]{:S(2)}) collective-permute-start(bf16[2,192,256]{2,1,0:T(8,128)(2,1)S(1)} %get-tuple-element.63), channel_id=1, source_target_pairs={{0,2},{1,3},{2,0},{3,1},{4,6},{5,7},{6,4},{7,5},{8,10},{9,11},{10,... | collective-permute-start | bytes 589832 | tf_op jit(solution)/shard_map/ppermute | solution.py:443
  15.8 4.9 %copy-start.2 = (bf16[1,192,2048]{2,1,0:T(8,128)(2,1)S(1)}, bf16[1,192,2048]{2,1,0:T(8,128)(2,1)}, u32[]{:S(2)}) copy-start(bf16[1,192,2048]{2,1,0:T(8,128)(2,1)} %param.6) | copy-start | bytes 2359300
  15.8 4.9 %copy-start.3 = (bf16[1,192,2048]{2,1,0:T(8,128)(2,1)S(1)}, bf16[1,192,2048]{2,1,0:T(8,128)(2,1)}, u32[]{:S(2)}) copy-start(bf16[1,192,2048]{2,1,0:T(8,128)(2,1)} %param.9) | copy-start | bytes 2359300
  15.8 12.0 %collective-permute-start.14 = (bf16[2,192,256]{2,1,0:T(8,128)(2,1)S(1)}, bf16[2,192,256]{2,1,0:T(8,128)(2,1)S(1)}, u32[]{:S(2)}, u32[]{:S(2)}) collective-permute-start(bf16[2,192,256]{2,1,0:T(8,128)(2,1)S(1)} %get-tuple-element.48.refs_3_), channel_id=1, source_target_pairs={{0,1},{1,2},{2,3},{3,0},{4,5},{5,6},{6,7},{7,4},{8,9},{9,10},{10,1... | collective-permute-start | bytes 589832 | tf_op jit(solution)/shard_map/ppermute | solution.py:443
  17.6 20.8 %collective-permute-start.9 = (bf16[2,576,256]{2,1,0:T(8,128)(2,1)S(1)}, bf16[2,576,256]{2,1,0:T(8,128)(2,1)S(1)}, u32[]{:S(2)}, u32[]{:S(2)}) collective-permute-start(bf16[2,576,256]{2,1,0:T(8,128)(2,1)S(1)} %edge.2.after), channel_id=1, source_target_pairs={{0,4},{1,5},{2,6},{3,7},{4,8},{5,9},{6,10},{7,11},{8,12},{9,13},{1... | collective-permute-start | bytes 1769480 | tf_op jit(solution)/shard_map/ppermute | solution.py:447
  20.8 14.9 %collective-permute-start.6 = (bf16[2,192,256]{2,1,0:T(8,128)(2,1)S(1)}, bf16[2,192,256]{2,1,0:T(8,128)(2,1)S(1)}, u32[]{:S(2)}, u32[]{:S(2)}) collective-permute-start(bf16[2,192,256]{2,1,0:T(8,128)(2,1)S(1)} %get-tuple-element.49.after), channel_id=1, source_target_pairs={{0,1},{1,2},{2,3},{3,0},{4,5},{5,6},{6,7},{7,4},{8,9},{9,10},{10,1... | collective-permute-start | bytes 589832 | tf_op jit(solution)/shard_map/ppermute | solution.py:443
  22.1 9.8 %collective-permute-start.7 = (bf16[2,192,256]{2,1,0:T(8,128)(2,1)S(1)}, bf16[2,192,256]{2,1,0:T(8,128)(2,1)S(1)}, u32[]{:S(2)}, u32[]{:S(2)}) collective-permute-start(bf16[2,192,256]{2,1,0:T(8,128)(2,1)S(1)} %get-tuple-element.54), channel_id=1, source_target_pairs={{0,3},{1,0},{2,1},{3,2},{4,7},{5,4},{6,5},{7,6},{8,11},{9,8},{10,9... | collective-permute-start | bytes 589832 | tf_op jit(solution)/shard_map/ppermute | solution.py:443
  26.1 7.8 %collective-permute-start.8 = (bf16[2,192,256]{2,1,0:T(8,128)(2,1)S(1)}, bf16[2,192,256]{2,1,0:T(8,128)(2,1)S(1)}, u32[]{:S(2)}, u32[]{:S(2)}) collective-permute-start(bf16[2,192,256]{2,1,0:T(8,128)(2,1)S(1)} %get-tuple-element.55), channel_id=1, source_target_pairs={{0,2},{1,3},{2,0},{3,1},{4,6},{5,7},{6,4},{7,5},{8,10},{9,11},{10,... | collective-permute-start | bytes 589832 | tf_op jit(solution)/shard_map/ppermute | solution.py:443
  27.8 26.7 %collective-permute-start.20 = (bf16[2,576,256]{2,1,0:T(8,128)(2,1)S(1)}, bf16[2,576,256]{2,1,0:T(8,128)(2,1)S(1)}, u32[]{:S(2)}, u32[]{:S(2)}) collective-permute-start(bf16[2,576,256]{2,1,0:T(8,128)(2,1)S(1)} %edge.3), channel_id=1, source_target_pairs={{0,4},{1,5},{2,6},{3,7},{4,8},{5,9},{6,10},{7,11},{8,12},{9,13},{1... | collective-permute-start | bytes 1769480 | tf_op jit(solution)/shard_map/ppermute | solution.py:447
  31.8 21.8 %collective-permute-start.17 = (bf16[2,192,256]{2,1,0:T(8,128)(2,1)S(1)}, bf16[2,192,256]{2,1,0:T(8,128)(2,1)S(1)}, u32[]{:S(2)}, u32[]{:S(2)}) collective-permute-start(bf16[2,192,256]{2,1,0:T(8,128)(2,1)S(1)} %get-tuple-element.50.after), channel_id=1, source_target_pairs={{0,1},{1,2},{2,3},{3,0},{4,5},{5,6},{6,7},{7,4},{8,9},{9,10},{10,1... | collective-permute-start | bytes 589832 | tf_op jit(solution)/shard_map/ppermute | solution.py:443
  33.8 16.6 %collective-permute-start.18 = (bf16[2,192,256]{2,1,0:T(8,128)(2,1)S(1)}, bf16[2,192,256]{2,1,0:T(8,128)(2,1)S(1)}, u32[]{:S(2)}, u32[]{:S(2)}) collective-permute-start(bf16[2,192,256]{2,1,0:T(8,128)(2,1)S(1)} %get-tuple-element.64), channel_id=1, source_target_pairs={{0,3},{1,0},{2,1},{3,2},{4,7},{5,4},{6,5},{7,6},{8,11},{9,8},{10,9... | collective-permute-start | bytes 589832 | tf_op jit(solution)/shard_map/ppermute | solution.py:443
  35.7 15.5 %collective-permute-start.19 = (bf16[2,192,256]{2,1,0:T(8,128)(2,1)S(1)}, bf16[2,192,256]{2,1,0:T(8,128)(2,1)S(1)}, u32[]{:S(2)}, u32[]{:S(2)}) collective-permute-start(bf16[2,192,256]{2,1,0:T(8,128)(2,1)S(1)} %get-tuple-element.65), channel_id=1, source_target_pairs={{0,2},{1,3},{2,0},{3,1},{4,6},{5,7},{6,4},{7,5},{8,10},{9,11},{10,... | collective-permute-start | bytes 589832 | tf_op jit(solution)/shard_map/ppermute | solution.py:443
  44.4 16.3 %collective-permute-start.13 = (bf16[2,576,256]{2,1,0:T(8,128)(2,1)S(1)}, bf16[2,576,256]{2,1,0:T(8,128)(2,1)S(1)}, u32[]{:S(2)}, u32[]{:S(2)}) collective-permute-start(bf16[2,576,256]{2,1,0:T(8,128)(2,1)S(1)} %get-tuple-element.61), channel_id=1, source_target_pairs={{0,28},{1,29},{2,30},{3,31},{4,0},{5,1},{6,2},{7,3},{8,4},{9,5},{1... | collective-permute-start | bytes 1769480 | tf_op jit(solution)/shard_map/ppermute | solution.py:447
  50.4 10.2 %collective-permute-start.10 = (bf16[192,256]{1,0:T(8,128)(2,1)S(1)}, bf16[192,256]{1,0:T(8,128)(2,1)S(1)}, u32[]{:S(2)}, u32[]{:S(2)}) collective-permute-start(bf16[192,256]{1,0:T(8,128)(2,1)S(1)} %get-tuple-element.57), channel_id=1, source_target_pairs={{0,1},{1,2},{2,3},{3,0},{4,5},{5,6},{6,7},{7,4},{8,9},{9,10},{10,1... | collective-permute-start | bytes 294920 | tf_op jit(solution)/shard_map/ppermute | solution.py:443
  51.2 9.4 %collective-permute-start.11 = (bf16[192,256]{1,0:T(8,128)(2,1)S(1)}, bf16[192,256]{1,0:T(8,128)(2,1)S(1)}, u32[]{:S(2)}, u32[]{:S(2)}) collective-permute-start(bf16[192,256]{1,0:T(8,128)(2,1)S(1)} %get-tuple-element.58), channel_id=1, source_target_pairs={{0,3},{1,0},{2,1},{3,2},{4,7},{5,4},{6,5},{7,6},{8,11},{9,8},{10,9... | collective-permute-start | bytes 294920 | tf_op jit(solution)/shard_map/ppermute | solution.py:443
  53.7 7.0 %collective-permute-start.12 = (bf16[192,256]{1,0:T(8,128)(2,1)S(1)}, bf16[192,256]{1,0:T(8,128)(2,1)S(1)}, u32[]{:S(2)}, u32[]{:S(2)}) collective-permute-start(bf16[192,256]{1,0:T(8,128)(2,1)S(1)} %get-tuple-element.59), channel_id=1, source_target_pairs={{0,2},{1,3},{2,0},{3,1},{4,6},{5,7},{6,4},{7,5},{8,10},{9,11},{10,... | collective-permute-start | bytes 294920 | tf_op jit(solution)/shard_map/ppermute | solution.py:443
  60.5 12.1 %collective-permute-start.24 = (bf16[2,576,256]{2,1,0:T(8,128)(2,1)S(1)}, bf16[2,576,256]{2,1,0:T(8,128)(2,1)S(1)}, u32[]{:S(2)}, u32[]{:S(2)}) collective-permute-start(bf16[2,576,256]{2,1,0:T(8,128)(2,1)S(1)} %get-tuple-element.76), channel_id=1, source_target_pairs={{0,28},{1,29},{2,30},{3,31},{4,0},{5,1},{6,2},{7,3},{8,4},{9,5},{1... | collective-permute-start | bytes 1769480 | tf_op jit(solution)/shard_map/ppermute | solution.py:447
  60.9 17.3 %collective-permute-start.21 = (bf16[3,192,256]{2,1,0:T(8,128)(2,1)S(1)}, bf16[3,192,256]{2,1,0:T(8,128)(2,1)S(1)}, u32[]{:S(2)}, u32[]{:S(2)}) collective-permute-start(bf16[3,192,256]{2,1,0:T(8,128)(2,1)S(1)} %get-tuple-element.71), channel_id=1, source_target_pairs={{0,1},{1,2},{2,3},{3,0},{4,5},{5,6},{6,7},{7,4},{8,9},{9,10},{10,1... | collective-permute-start | bytes 884744 | tf_op jit(solution)/shard_map/ppermute | solution.py:443
  62.0 16.2 %collective-permute-start.22 = (bf16[3,192,256]{2,1,0:T(8,128)(2,1)S(1)}, bf16[3,192,256]{2,1,0:T(8,128)(2,1)S(1)}, u32[]{:S(2)}, u32[]{:S(2)}) collective-permute-start(bf16[3,192,256]{2,1,0:T(8,128)(2,1)S(1)} %get-tuple-element.72), channel_id=1, source_target_pairs={{0,3},{1,0},{2,1},{3,2},{4,7},{5,4},{6,5},{7,6},{8,11},{9,8},{10,9... | collective-permute-start | bytes 884744 | tf_op jit(solution)/shard_map/ppermute | solution.py:443
  64.2 14.0 %collective-permute-start.23 = (bf16[3,192,256]{2,1,0:T(8,128)(2,1)S(1)}, bf16[3,192,256]{2,1,0:T(8,128)(2,1)S(1)}, u32[]{:S(2)}, u32[]{:S(2)}) collective-permute-start(bf16[3,192,256]{2,1,0:T(8,128)(2,1)S(1)} %get-tuple-element.73), channel_id=1, source_target_pairs={{0,2},{1,3},{2,0},{3,1},{4,6},{5,7},{6,4},{7,5},{8,10},{9,11},{10,... | collective-permute-start | bytes 884744 | tf_op jit(solution)/shard_map/ppermute | solution.py:443
  72.8 13.0 %collective-permute-start.25 = (bf16[2,192,256]{2,1,0:T(8,128)(2,1)S(1)}, bf16[2,192,256]{2,1,0:T(8,128)(2,1)S(1)}, u32[]{:S(2)}, u32[]{:S(2)}) collective-permute-start(bf16[2,192,256]{2,1,0:T(8,128)(2,1)S(1)} %get-tuple-element.78), channel_id=1, source_target_pairs={{0,1},{1,2},{2,3},{3,0},{4,5},{5,6},{6,7},{7,4},{8,9},{9,10},{10,1... | collective-permute-start | bytes 589832 | tf_op jit(solution)/shard_map/ppermute | solution.py:443
  74.0 11.8 %collective-permute-start.26 = (bf16[2,192,256]{2,1,0:T(8,128)(2,1)S(1)}, bf16[2,192,256]{2,1,0:T(8,128)(2,1)S(1)}, u32[]{:S(2)}, u32[]{:S(2)}) collective-permute-start(bf16[2,192,256]{2,1,0:T(8,128)(2,1)S(1)} %get-tuple-element.79), channel_id=1, source_target_pairs={{0,3},{1,0},{2,1},{3,2},{4,7},{5,4},{6,5},{7,6},{8,11},{9,8},{10,9... | collective-permute-start | bytes 589832 | tf_op jit(solution)/shard_map/ppermute | solution.py:443
  78.1 7.6 %collective-permute-start.27 = (bf16[2,192,256]{2,1,0:T(8,128)(2,1)S(1)}, bf16[2,192,256]{2,1,0:T(8,128)(2,1)S(1)}, u32[]{:S(2)}, u32[]{:S(2)}) collective-permute-start(bf16[2,192,256]{2,1,0:T(8,128)(2,1)S(1)} %get-tuple-element.80), channel_id=1, source_target_pairs={{0,2},{1,3},{2,0},{3,1},{4,6},{5,7},{6,4},{7,5},{8,10},{9,11},{10,... | collective-permute-start | bytes 589832 | tf_op jit(solution)/shard_map/ppermute | solution.py:443
  (3 other events, 3.4 us)

commit v11 on v7

--- a/solution.py
+++ b/solution.py
@@ -16,7 +16,7 @@
 VMEM = pl.BlockSpec(memory_space=pltpu.VMEM)
 ANY = pl.BlockSpec(memory_space=pl.ANY)
 LARGE = pltpu.CompilerParams(vmem_limit_bytes=60 * 1024 * 1024)
-EDGE_COST = (0, 6000000000)
+EDGE_COST = (0, 3000000000)
 SETTLE_COST = 3000000000
 SMALL = pltpu.CompilerParams(vmem_limit_bytes=10 * 1024 * 1024)
 

time: 86.4 us -> 91.5 us (1.059)
  starting transfers between devices: 47.3 us -> 52.3 us
    ppermute x4, waiting for transfers between devices: 8.87 us -> 3.24 us  [next_row(): return lax.ppermute(value, 'ctx', pairs)]
    ppermute x21, starting transfers between devices: 31.9 us -> 37.1 us  [swap(): return lax.ppermute(value, ('dp', 'ctx'), pairs)]
    ppermute x21, waiting for transfers between devices: 11.6 us -> 16.1 us  [swap(): return lax.ppermute(value, ('dp', 'ctx'), pairs)]
  transfers between devices with their start and end apart: 28 -> 28, of which waited for: 10 -> 8; matrix products, arithmetic and copies ran while one was open for 0% -> 0% of each run, Pallas kernels for 15% -> 14%
where the time goes in v11:
time: 91.5 us; the launch traced here: 91.1 us
  starting transfers between devices  52.3 us (57%)
  waiting for transfers between devices  21 us (23%)
  Pallas kernels  16.1 us (18%)
  between operations  0.99 us (1%)
    ppermute x21, starting transfers between devices, swap(): return lax.ppermute(value, ('dp', 'ctx'), pairs)  37.1 us
    ppermute x21, waiting for transfers between devices, swap(): return lax.ppermute(value, ('dp', 'ctx'), pairs)  16.1 us
    ppermute x4, starting transfers between devices, next_row(): return lax.ppermute(value, 'ctx', pairs)  12.4 us
    pallas_call x2, Pallas kernels, attend(): pl.pallas_call(functools.partial(attend_kernel, chunk, total_rows), out_s...  10.6 us
    ppermute x4, waiting for transfers between devices, next_row(): return lax.ppermute(value, 'ctx', pairs)  3.24 us
    ppermute x3, starting transfers between devices, shards(): lax.ppermute(text, 'dp', [(source, (source + away) % samples) for source...  2.83 us
    pallas_call x1, Pallas kernels, first_pack(): pl.pallas_call(first_pack_kernel, out_shape=(message,) * (GROUP - 1) + (j...  2.15 us
  transfers between devices with their start and end apart: 28, of which 8 were waited for; matrix products, arithmetic and copies ran while one was open for 0% of the time, Pallas kernels for 14%

profile of v11, /device:TPU:0, one launch (start us, length us, event | category | flops | bytes accessed | tf_op | source)
XLA Modules:
  0.0 91.1 jit_solution(11189435897686923062)
XLA Ops:
  0.7 2.1 %first_pack.1 = (bf16[2,192,256]{2,1,0:T(8,128)(2,1)}, bf16[2,192,256]{2,1,0:T(8,128)(2,1)}, bf16[2,192,256]{2,1,0:T(8,128)(2,1)}, f32[1,32]{1,0:T(1,128)}) custom-call(bf16[192,2048]{1,0:T(8,128)(2,1)} %bitcast.7, bf16[192,2048]{1,0:T(8,128)(2,1)} %bitcast.13, s32[1,32]{1,0:T(1,128)} %lengths_ref.1, s32[1,32]{1,0:T(1,128)} %flags_ref.1), custom_call_target="tpu_custom_call" | custom-call | bytes 1179648 | tf_op jit(solution)/shard_map/first_pack/pallas_call | solution.py:80
  2.8 1.7 %collective-permute-start.3 = (bf16[2,192,256]{2,1,0:T(8,128)(2,1)}, bf16[2,192,256]{2,1,0:T(8,128)(2,1)S(1)}, u32[]{:S(2)}, u32[]{:S(2)}) collective-permute-start(bf16[2,192,256]{2,1,0:T(8,128)(2,1)} %get-tuple-element.45), channel_id=1, source_target_pairs={{0,1},{1,2},{2,3},{3,0},{4,5},{5,6},{6,7},{7,4},{8,9},{9,10},{10,1... | collective-permute-start | bytes 589832 | tf_op jit(solution)/shard_map/ppermute | solution.py:440
  4.5 1.6 %collective-permute-start.4 = (bf16[2,192,256]{2,1,0:T(8,128)(2,1)}, bf16[2,192,256]{2,1,0:T(8,128)(2,1)S(1)}, u32[]{:S(2)}, u32[]{:S(2)}) collective-permute-start(bf16[2,192,256]{2,1,0:T(8,128)(2,1)} %get-tuple-element.46), channel_id=1, source_target_pairs={{0,3},{1,0},{2,1},{3,2},{4,7},{5,4},{6,5},{7,6},{8,11},{9,8},{10,9... | collective-permute-start | bytes 589832 | tf_op jit(solution)/shard_map/ppermute | solution.py:440
  6.1 2.1 %collective-permute-start.5 = (bf16[2,192,256]{2,1,0:T(8,128)(2,1)}, bf16[2,192,256]{2,1,0:T(8,128)(2,1)S(1)}, u32[]{:S(2)}, u32[]{:S(2)}) collective-permute-start(bf16[2,192,256]{2,1,0:T(8,128)(2,1)} %get-tuple-element.47), channel_id=1, source_target_pairs={{0,2},{1,3},{2,0},{3,1},{4,6},{5,7},{6,4},{7,5},{8,10},{9,11},{10,... | collective-permute-start | bytes 589832 | tf_op jit(solution)/shard_map/ppermute | solution.py:440
  8.3 1.4 %collective-permute-start.1 = (f32[1,32]{1,0:T(1,128)S(1)}, f32[1,32]{1,0:T(1,128)S(1)}, u32[]{:S(2)}, u32[]{:S(2)}) collective-permute-start(f32[1,32]{1,0:T(1,128)S(1)} %copy-done.6), channel_id=1, source_target_pairs={{0,64},{32,96},{64,0},{96,32},{1,65},{33,97},{65,1},{97,33},{2,66}... | collective-permute-start | bytes 392 | tf_op jit(solution)/shard_map/ppermute | solution.py:451
  9.7 1.3 %collective-permute-start = (f32[1,32]{1,0:T(1,128)S(1)}, f32[1,32]{1,0:T(1,128)S(1)}, u32[]{:S(2)}, u32[]{:S(2)}) collective-permute-start(f32[1,32]{1,0:T(1,128)S(1)} %copy-done.6), channel_id=1, source_target_pairs={{0,32},{32,64},{64,96},{96,0},{1,33},{33,65},{65,97},{97,1},{2,34}... | collective-permute-start | bytes 392 | tf_op jit(solution)/shard_map/ppermute | solution.py:451
  11.8 0.9 %collective-permute-done.refs_0_.text_two = f32[1,32]{1,0:T(1,128)S(1)} collective-permute-done((f32[1,32]{1,0:T(1,128)S(1)}, f32[1,32]{1,0:T(1,128)S(1)}, u32[]{:S(2)}, u32[]{:S(2)}) %collective-permute-start) | collective-permute-done | bytes 160 | tf_op jit(solution)/shard_map/ppermute | solution.py:451
  12.8 1.9 %collective-permute-done.4.two.key_two = bf16[2,192,256]{2,1,0:T(8,128)(2,1)S(1)} collective-permute-done((bf16[2,192,256]{2,1,0:T(8,128)(2,1)}, bf16[2,192,256]{2,1,0:T(8,128)(2,1)S(1)}, u32[]{:S(2)}, u32[]{:S(2)}) %collective-permute-start.4) | collective-permute-done | bytes 196640 | tf_op jit(solution)/shard_map/ppermute | solution.py:440
  14.7 2.2 %collective-permute-done.5.three.key_three = bf16[2,192,256]{2,1,0:T(8,128)(2,1)S(1)} collective-permute-done((bf16[2,192,256]{2,1,0:T(8,128)(2,1)}, bf16[2,192,256]{2,1,0:T(8,128)(2,1)S(1)}, u32[]{:S(2)}, u32[]{:S(2)}) %collective-permute-start.5) | collective-permute-done | bytes 196640 | tf_op jit(solution)/shard_map/ppermute | solution.py:440
  17.0 3.1 %collective-permute-start.9 = (bf16[2,576,256]{2,1,0:T(8,128)(2,1)S(1)}, bf16[2,576,256]{2,1,0:T(8,128)(2,1)S(1)}, u32[]{:S(2)}, u32[]{:S(2)}) collective-permute-start(bf16[2,576,256]{2,1,0:T(8,128)(2,1)S(1)} %edge.2.after), channel_id=1, source_target_pairs={{0,4},{1,5},{2,6},{3,7},{4,8},{5,9},{6,10},{7,11},{8,12},{9,13},{1... | collective-permute-start | bytes 1769480 | tf_op jit(solution)/shard_map/ppermute | solution.py:444
  20.1 1.4 %collective-permute-start.15 = (bf16[2,192,256]{2,1,0:T(8,128)(2,1)S(1)}, bf16[2,192,256]{2,1,0:T(8,128)(2,1)S(1)}, u32[]{:S(2)}, u32[]{:S(2)}) collective-permute-start(bf16[2,192,256]{2,1,0:T(8,128)(2,1)S(1)} %get-tuple-element.62), channel_id=1, source_target_pairs={{0,3},{1,0},{2,1},{3,2},{4,7},{5,4},{6,5},{7,6},{8,11},{9,8},{10,9... | collective-permute-start | bytes 589832 | tf_op jit(solution)/shard_map/ppermute | solution.py:440
  22.6 2.5 %collective-permute-start.6 = (bf16[2,192,256]{2,1,0:T(8,128)(2,1)S(1)}, bf16[2,192,256]{2,1,0:T(8,128)(2,1)S(1)}, u32[]{:S(2)}, u32[]{:S(2)}) collective-permute-start(bf16[2,192,256]{2,1,0:T(8,128)(2,1)S(1)} %get-tuple-element.49.after), channel_id=1, source_target_pairs={{0,1},{1,2},{2,3},{3,0},{4,5},{5,6},{6,7},{7,4},{8,9},{9,10},{10,1... | collective-permute-start | bytes 589832 | tf_op jit(solution)/shard_map/ppermute | solution.py:440
  26.2 3.5 %collective-permute-done.15.two.key_two = bf16[2,192,256]{2,1,0:T(8,128)(2,1)S(1)} collective-permute-done((bf16[2,192,256]{2,1,0:T(8,128)(2,1)S(1)}, bf16[2,192,256]{2,1,0:T(8,128)(2,1)S(1)}, u32[]{:S(2)}, u32[]{:S(2)}) %collective-permute-start.15) | collective-permute-done | bytes 196640 | tf_op jit(solution)/shard_map/ppermute | solution.py:440
  29.7 4.2 %collective-permute-start.7 = (bf16[2,192,256]{2,1,0:T(8,128)(2,1)S(1)}, bf16[2,192,256]{2,1,0:T(8,128)(2,1)S(1)}, u32[]{:S(2)}, u32[]{:S(2)}) collective-permute-start(bf16[2,192,256]{2,1,0:T(8,128)(2,1)S(1)} %get-tuple-element.54), channel_id=1, source_target_pairs={{0,3},{1,0},{2,1},{3,2},{4,7},{5,4},{6,5},{7,6},{8,11},{9,8},{10,9... | collective-permute-start | bytes 589832 | tf_op jit(solution)/shard_map/ppermute | solution.py:440
  34.0 1.9 %collective-permute-start.20 = (bf16[2,576,256]{2,1,0:T(8,128)(2,1)S(1)}, bf16[2,576,256]{2,1,0:T(8,128)(2,1)S(1)}, u32[]{:S(2)}, u32[]{:S(2)}) collective-permute-start(bf16[2,576,256]{2,1,0:T(8,128)(2,1)S(1)} %edge.3), channel_id=1, source_target_pairs={{0,4},{1,5},{2,6},{3,7},{4,8},{5,9},{6,10},{7,11},{8,12},{9,13},{1... | collective-permute-start | bytes 1769480 | tf_op jit(solution)/shard_map/ppermute | solution.py:444
  35.9 6.0 %collective-permute-done.7.query_two = bf16[2,192,256]{2,1,0:T(8,128)(2,1)S(1)} collective-permute-done((bf16[2,192,256]{2,1,0:T(8,128)(2,1)S(1)}, bf16[2,192,256]{2,1,0:T(8,128)(2,1)S(1)}, u32[]{:S(2)}, u32[]{:S(2)}) %collective-permute-start.7) | collective-permute-done | bytes 196640 | tf_op jit(solution)/shard_map/ppermute | solution.py:440
  42.0 3.7 %collective-permute-start.18 = (bf16[2,192,256]{2,1,0:T(8,128)(2,1)S(1)}, bf16[2,192,256]{2,1,0:T(8,128)(2,1)S(1)}, u32[]{:S(2)}, u32[]{:S(2)}) collective-permute-start(bf16[2,192,256]{2,1,0:T(8,128)(2,1)S(1)} %get-tuple-element.64), channel_id=1, source_target_pairs={{0,3},{1,0},{2,1},{3,2},{4,7},{5,4},{6,5},{7,6},{8,11},{9,8},{10,9... | collective-permute-start | bytes 589832 | tf_op jit(solution)/shard_map/ppermute | solution.py:440
  45.7 1.7 %collective-permute-start.19 = (bf16[2,192,256]{2,1,0:T(8,128)(2,1)S(1)}, bf16[2,192,256]{2,1,0:T(8,128)(2,1)S(1)}, u32[]{:S(2)}, u32[]{:S(2)}) collective-permute-start(bf16[2,192,256]{2,1,0:T(8,128)(2,1)S(1)} %get-tuple-element.65), channel_id=1, source_target_pairs={{0,2},{1,3},{2,0},{3,1},{4,6},{5,7},{6,4},{7,5},{8,10},{9,11},{10,... | collective-permute-start | bytes 589832 | tf_op jit(solution)/shard_map/ppermute | solution.py:440
  47.4 5.3 %attend.2 = (bf16[192,256]{1,0:T(8,128)(2,1)S(1)}, bf16[192,256]{1,0:T(8,128)(2,1)S(1)}, bf16[192,256]{1,0:T(8,128)(2,1)S(1)}, bf16[192,256]{1,0:T(8,128)(2,1)S(...) custom-call(f32[1,32]{1,0:T(1,128)S(1)} %copy-done.6, ...), custom_call_target="tpu_custom_call" | custom-call | flops 4499999744 | tf_op jit(solution)/shard_map/attend/pallas_call | solution.py:289
  52.7 3.6 %collective-permute-start.13 = (bf16[2,576,256]{2,1,0:T(8,128)(2,1)S(1)}, bf16[2,576,256]{2,1,0:T(8,128)(2,1)S(1)}, u32[]{:S(2)}, u32[]{:S(2)}) collective-permute-start(bf16[2,576,256]{2,1,0:T(8,128)(2,1)S(1)} %get-tuple-element.61), channel_id=1, source_target_pairs={{0,28},{1,29},{2,30},{3,31},{4,0},{5,1},{6,2},{7,3},{8,4},{9,5},{1... | collective-permute-start | bytes 1769480 | tf_op jit(solution)/shard_map/ppermute | solution.py:444
  56.3 1.2 %collective-permute-start.10 = (bf16[192,256]{1,0:T(8,128)(2,1)S(1)}, bf16[192,256]{1,0:T(8,128)(2,1)S(1)}, u32[]{:S(2)}, u32[]{:S(2)}) collective-permute-start(bf16[192,256]{1,0:T(8,128)(2,1)S(1)} %get-tuple-element.57), channel_id=1, source_target_pairs={{0,1},{1,2},{2,3},{3,0},{4,5},{5,6},{6,7},{7,4},{8,9},{9,10},{10,1... | collective-permute-start | bytes 294920 | tf_op jit(solution)/shard_map/ppermute | solution.py:440
  57.5 2.1 %collective-permute-start.11 = (bf16[192,256]{1,0:T(8,128)(2,1)S(1)}, bf16[192,256]{1,0:T(8,128)(2,1)S(1)}, u32[]{:S(2)}, u32[]{:S(2)}) collective-permute-start(bf16[192,256]{1,0:T(8,128)(2,1)S(1)} %get-tuple-element.58), channel_id=1, source_target_pairs={{0,3},{1,0},{2,1},{3,2},{4,7},{5,4},{6,5},{7,6},{8,11},{9,8},{10,9... | collective-permute-start | bytes 294920 | tf_op jit(solution)/shard_map/ppermute | solution.py:440
  60.2 5.3 %attend.3 = (bf16[192,256]{1,0:T(8,128)(2,1)S(1)}, bf16[192,256]{1,0:T(8,128)(2,1)S(1)}, bf16[192,256]{1,0:T(8,128)(2,1)S(1)}, bf16[192,256]{1,0:T(8,128)(2,1)S(...) custom-call(f32[1,32]{1,0:T(1,128)S(1)} %copy-done.6, ...), custom_call_target="tpu_custom_call" | custom-call | flops 4499999744 | tf_op jit(solution)/shard_map/attend/pallas_call | solution.py:289
  65.5 3.7 %collective-permute-start.24 = (bf16[2,576,256]{2,1,0:T(8,128)(2,1)S(1)}, bf16[2,576,256]{2,1,0:T(8,128)(2,1)S(1)}, u32[]{:S(2)}, u32[]{:S(2)}) collective-permute-start(bf16[2,576,256]{2,1,0:T(8,128)(2,1)S(1)} %get-tuple-element.76), channel_id=1, source_target_pairs={{0,28},{1,29},{2,30},{3,31},{4,0},{5,1},{6,2},{7,3},{8,4},{9,5},{1... | collective-permute-start | bytes 1769480 | tf_op jit(solution)/shard_map/ppermute | solution.py:444
  69.9 2.9 %collective-permute-start.22 = (bf16[3,192,256]{2,1,0:T(8,128)(2,1)S(1)}, bf16[3,192,256]{2,1,0:T(8,128)(2,1)S(1)}, u32[]{:S(2)}, u32[]{:S(2)}) collective-permute-start(bf16[3,192,256]{2,1,0:T(8,128)(2,1)S(1)} %get-tuple-element.72), channel_id=1, source_target_pairs={{0,3},{1,0},{2,1},{3,2},{4,7},{5,4},{6,5},{7,6},{8,11},{9,8},{10,9... | collective-permute-start | bytes 884744 | tf_op jit(solution)/shard_map/ppermute | solution.py:440
  72.8 1.7 %collective-permute-start.23 = (bf16[3,192,256]{2,1,0:T(8,128)(2,1)S(1)}, bf16[3,192,256]{2,1,0:T(8,128)(2,1)S(1)}, u32[]{:S(2)}, u32[]{:S(2)}) collective-permute-start(bf16[3,192,256]{2,1,0:T(8,128)(2,1)S(1)} %get-tuple-element.73), channel_id=1, source_target_pairs={{0,2},{1,3},{2,0},{3,1},{4,6},{5,7},{6,4},{7,5},{8,10},{9,11},{10,... | collective-permute-start | bytes 884744 | tf_op jit(solution)/shard_map/ppermute | solution.py:440
  74.5 3.2 %collective-permute-done.24.far_ref = bf16[2,576,256]{2,1,0:T(8,128)(2,1)S(1)} collective-permute-done((bf16[2,576,256]{2,1,0:T(8,128)(2,1)S(1)}, bf16[2,576,256]{2,1,0:T(8,128)(2,1)S(1)}, u32[]{:S(2)}, u32[]{:S(2)}) %collective-permute-start.24) | collective-permute-done | bytes 589856 | tf_op jit(solution)/shard_map/ppermute | solution.py:444
  78.2 3.0 %collective-permute-start.26 = (bf16[2,192,256]{2,1,0:T(8,128)(2,1)S(1)}, bf16[2,192,256]{2,1,0:T(8,128)(2,1)S(1)}, u32[]{:S(2)}, u32[]{:S(2)}) collective-permute-start(bf16[2,192,256]{2,1,0:T(8,128)(2,1)S(1)} %get-tuple-element.79), channel_id=1, source_target_pairs={{0,3},{1,0},{2,1},{3,2},{4,7},{5,4},{6,5},{7,6},{8,11},{9,8},{10,9... | collective-permute-start | bytes 589832 | tf_op jit(solution)/shard_map/ppermute | solution.py:440
  81.2 5.1 %collective-permute-start.27 = (bf16[2,192,256]{2,1,0:T(8,128)(2,1)S(1)}, bf16[2,192,256]{2,1,0:T(8,128)(2,1)S(1)}, u32[]{:S(2)}, u32[]{:S(2)}) collective-permute-start(bf16[2,192,256]{2,1,0:T(8,128)(2,1)S(1)} %get-tuple-element.80), channel_id=1, source_target_pairs={{0,2},{1,3},{2,0},{3,1},{4,6},{5,7},{6,4},{7,5},{8,10},{9,11},{10,... | collective-permute-start | bytes 589832 | tf_op jit(solution)/shard_map/ppermute | solution.py:440
  86.3 1.3 %early.1 = (bf16[192,2048]{1,0:T(8,128)(2,1)}, bf16[192,2048]{1,0:T(8,128)(2,1)}, bf16[192,2048]{1,0:T(8,128)(2,1)}) custom-call(bf16[192,256]{1,0:T(8,128)(2,1)S(1)} %get-tuple-element.56.refs_0_, bf16[192,256]{1,0:T(8,128)(2,1)S(1)} %collective-permute-done.10.refs_4_.refs_1_, bf16[192,256]{1,0:T(8,128)(2,1)S(1)} %collective-permute-done.11.refs_5_.refs_2_, ...), custom_call_target="tpu_custom_call" | custom-call | bytes 2359296 | tf_op jit(solution)/shard_map/early/pallas_call | solution.py:402
  87.6 2.3 %collective-permute-done.27.refs_3_ = bf16[2,192,256]{2,1,0:T(8,128)(2,1)S(1)} collective-permute-done((bf16[2,192,256]{2,1,0:T(8,128)(2,1)S(1)}, bf16[2,192,256]{2,1,0:T(8,128)(2,1)S(1)}, u32[]{:S(2)}, u32[]{:S(2)}) %collective-permute-start.27) | collective-permute-done | bytes 196640 | tf_op jit(solution)/shard_map/ppermute | solution.py:440
  89.9 0.9 %late.1 = (bf16[192,2048]{1,0:T(8,128)(2,1)}, bf16[192,2048]{1,0:T(8,128)(2,1)}) custom-call(bf16[2,192,256]{2,1,0:T(8,128)(2,1)S(1)} %get-tuple-element.77.refs_0_, bf16[2,192,256]{2,1,0:T(8,128)(2,1)S(1)} %collective-permute-done.25.refs_1_, ...), custom_call_target="tpu_custom_call", output_to_operand_aliasing={{0}: (4, {}), {1}: (5, {})} | custom-call | bytes 2359296 | tf_op jit(solution)/shard_map/late/pallas_call | solution.py:412
  (51 shorter events, 5.1 us)
Async XLA Ops:
  0.6 10.4 %copy-start = (bf16[1,192,2048]{2,1,0:T(8,128)(2,1)S(1)}, bf16[1,192,2048]{2,1,0:T(8,128)(2,1)}, u32[]{:S(2)}) copy-start(bf16[1,192,2048]{2,1,0:T(8,128)(2,1)} %param.7) | copy-start | bytes 2359300
  0.6 10.4 %copy-start.1 = (bf16[1,192,2048]{2,1,0:T(8,128)(2,1)S(1)}, bf16[1,192,2048]{2,1,0:T(8,128)(2,1)}, u32[]{:S(2)}) copy-start(bf16[1,192,2048]{2,1,0:T(8,128)(2,1)} %param.8) | copy-start | bytes 2359300
  2.8 10.0 %collective-permute-start.3 = (bf16[2,192,256]{2,1,0:T(8,128)(2,1)}, bf16[2,192,256]{2,1,0:T(8,128)(2,1)S(1)}, u32[]{:S(2)}, u32[]{:S(2)}) collective-permute-start(bf16[2,192,256]{2,1,0:T(8,128)(2,1)} %get-tuple-element.45), channel_id=1, source_target_pairs={{0,1},{1,2},{2,3},{3,0},{4,5},{5,6},{6,7},{7,4},{8,9},{9,10},{10,1... | collective-permute-start | bytes 589832 | tf_op jit(solution)/shard_map/ppermute | solution.py:440
  4.5 10.2 %collective-permute-start.4 = (bf16[2,192,256]{2,1,0:T(8,128)(2,1)}, bf16[2,192,256]{2,1,0:T(8,128)(2,1)S(1)}, u32[]{:S(2)}, u32[]{:S(2)}) collective-permute-start(bf16[2,192,256]{2,1,0:T(8,128)(2,1)} %get-tuple-element.46), channel_id=1, source_target_pairs={{0,3},{1,0},{2,1},{3,2},{4,7},{5,4},{6,5},{7,6},{8,11},{9,8},{10,9... | collective-permute-start | bytes 589832 | tf_op jit(solution)/shard_map/ppermute | solution.py:440
  6.1 10.8 %collective-permute-start.5 = (bf16[2,192,256]{2,1,0:T(8,128)(2,1)}, bf16[2,192,256]{2,1,0:T(8,128)(2,1)S(1)}, u32[]{:S(2)}, u32[]{:S(2)}) collective-permute-start(bf16[2,192,256]{2,1,0:T(8,128)(2,1)} %get-tuple-element.47), channel_id=1, source_target_pairs={{0,2},{1,3},{2,0},{3,1},{4,6},{5,7},{6,4},{7,5},{8,10},{9,11},{10,... | collective-permute-start | bytes 589832 | tf_op jit(solution)/shard_map/ppermute | solution.py:440
  8.2 1.5 %collective-permute-start.2 = (f32[1,32]{1,0:T(1,128)S(1)}, f32[1,32]{1,0:T(1,128)S(1)}, u32[]{:S(2)}, u32[]{:S(2)}) collective-permute-start(f32[1,32]{1,0:T(1,128)S(1)} %copy-done.6), channel_id=1, source_target_pairs={{0,96},{32,0},{64,32},{96,64},{1,97},{33,1},{65,33},{97,65},{2,98}... | collective-permute-start | bytes 392 | tf_op jit(solution)/shard_map/ppermute | solution.py:451
  8.3 3.5 %collective-permute-start.1 = (f32[1,32]{1,0:T(1,128)S(1)}, f32[1,32]{1,0:T(1,128)S(1)}, u32[]{:S(2)}, u32[]{:S(2)}) collective-permute-start(f32[1,32]{1,0:T(1,128)S(1)} %copy-done.6), channel_id=1, source_target_pairs={{0,64},{32,96},{64,0},{96,32},{1,65},{33,97},{65,1},{97,33},{2,66}... | collective-permute-start | bytes 392 | tf_op jit(solution)/shard_map/ppermute | solution.py:451
  9.7 3.1 %collective-permute-start = (f32[1,32]{1,0:T(1,128)S(1)}, f32[1,32]{1,0:T(1,128)S(1)}, u32[]{:S(2)}, u32[]{:S(2)}) collective-permute-start(f32[1,32]{1,0:T(1,128)S(1)} %copy-done.6), channel_id=1, source_target_pairs={{0,32},{32,64},{64,96},{96,0},{1,33},{33,65},{65,97},{97,1},{2,34}... | collective-permute-start | bytes 392 | tf_op jit(solution)/shard_map/ppermute | solution.py:451
  16.9 5.6 %copy-start.2 = (bf16[1,192,2048]{2,1,0:T(8,128)(2,1)S(1)}, bf16[1,192,2048]{2,1,0:T(8,128)(2,1)}, u32[]{:S(2)}) copy-start(bf16[1,192,2048]{2,1,0:T(8,128)(2,1)} %param.6) | copy-start | bytes 2359300
  16.9 5.6 %copy-start.3 = (bf16[1,192,2048]{2,1,0:T(8,128)(2,1)S(1)}, bf16[1,192,2048]{2,1,0:T(8,128)(2,1)}, u32[]{:S(2)}) copy-start(bf16[1,192,2048]{2,1,0:T(8,128)(2,1)} %param.9) | copy-start | bytes 2359300
  17.0 30.4 %collective-permute-start.9 = (bf16[2,576,256]{2,1,0:T(8,128)(2,1)S(1)}, bf16[2,576,256]{2,1,0:T(8,128)(2,1)S(1)}, u32[]{:S(2)}, u32[]{:S(2)}) collective-permute-start(bf16[2,576,256]{2,1,0:T(8,128)(2,1)S(1)} %edge.2.after), channel_id=1, source_target_pairs={{0,4},{1,5},{2,6},{3,7},{4,8},{5,9},{6,10},{7,11},{8,12},{9,13},{1... | collective-permute-start | bytes 1769480 | tf_op jit(solution)/shard_map/ppermute | solution.py:444
  20.1 9.6 %collective-permute-start.15 = (bf16[2,192,256]{2,1,0:T(8,128)(2,1)S(1)}, bf16[2,192,256]{2,1,0:T(8,128)(2,1)S(1)}, u32[]{:S(2)}, u32[]{:S(2)}) collective-permute-start(bf16[2,192,256]{2,1,0:T(8,128)(2,1)S(1)} %get-tuple-element.62), channel_id=1, source_target_pairs={{0,3},{1,0},{2,1},{3,2},{4,7},{5,4},{6,5},{7,6},{8,11},{9,8},{10,9... | collective-permute-start | bytes 589832 | tf_op jit(solution)/shard_map/ppermute | solution.py:440
  21.4 12.5 %collective-permute-start.16 = (bf16[2,192,256]{2,1,0:T(8,128)(2,1)S(1)}, bf16[2,192,256]{2,1,0:T(8,128)(2,1)S(1)}, u32[]{:S(2)}, u32[]{:S(2)}) collective-permute-start(bf16[2,192,256]{2,1,0:T(8,128)(2,1)S(1)} %get-tuple-element.63), channel_id=1, source_target_pairs={{0,2},{1,3},{2,0},{3,1},{4,6},{5,7},{6,4},{7,5},{8,10},{9,11},{10,... | collective-permute-start | bytes 589832 | tf_op jit(solution)/shard_map/ppermute | solution.py:440
  22.0 12.0 %collective-permute-start.14 = (bf16[2,192,256]{2,1,0:T(8,128)(2,1)S(1)}, bf16[2,192,256]{2,1,0:T(8,128)(2,1)S(1)}, u32[]{:S(2)}, u32[]{:S(2)}) collective-permute-start(bf16[2,192,256]{2,1,0:T(8,128)(2,1)S(1)} %get-tuple-element.48.refs_3_), channel_id=1, source_target_pairs={{0,1},{1,2},{2,3},{3,0},{4,5},{5,6},{6,7},{7,4},{8,9},{9,10},{10,1... | collective-permute-start | bytes 589832 | tf_op jit(solution)/shard_map/ppermute | solution.py:440
  22.6 23.1 %collective-permute-start.6 = (bf16[2,192,256]{2,1,0:T(8,128)(2,1)S(1)}, bf16[2,192,256]{2,1,0:T(8,128)(2,1)S(1)}, u32[]{:S(2)}, u32[]{:S(2)}) collective-permute-start(bf16[2,192,256]{2,1,0:T(8,128)(2,1)S(1)} %get-tuple-element.49.after), channel_id=1, source_target_pairs={{0,1},{1,2},{2,3},{3,0},{4,5},{5,6},{6,7},{7,4},{8,9},{9,10},{10,1... | collective-permute-start | bytes 589832 | tf_op jit(solution)/shard_map/ppermute | solution.py:440
  29.7 12.3 %collective-permute-start.7 = (bf16[2,192,256]{2,1,0:T(8,128)(2,1)S(1)}, bf16[2,192,256]{2,1,0:T(8,128)(2,1)S(1)}, u32[]{:S(2)}, u32[]{:S(2)}) collective-permute-start(bf16[2,192,256]{2,1,0:T(8,128)(2,1)S(1)} %get-tuple-element.54), channel_id=1, source_target_pairs={{0,3},{1,0},{2,1},{3,2},{4,7},{5,4},{6,5},{7,6},{8,11},{9,8},{10,9... | collective-permute-start | bytes 589832 | tf_op jit(solution)/shard_map/ppermute | solution.py:440
  33.9 8.1 %collective-permute-start.8 = (bf16[2,192,256]{2,1,0:T(8,128)(2,1)S(1)}, bf16[2,192,256]{2,1,0:T(8,128)(2,1)S(1)}, u32[]{:S(2)}, u32[]{:S(2)}) collective-permute-start(bf16[2,192,256]{2,1,0:T(8,128)(2,1)S(1)} %get-tuple-element.55), channel_id=1, source_target_pairs={{0,2},{1,3},{2,0},{3,1},{4,6},{5,7},{6,4},{7,5},{8,10},{9,11},{10,... | collective-permute-start | bytes 589832 | tf_op jit(solution)/shard_map/ppermute | solution.py:440
  34.0 26.2 %collective-permute-start.20 = (bf16[2,576,256]{2,1,0:T(8,128)(2,1)S(1)}, bf16[2,576,256]{2,1,0:T(8,128)(2,1)S(1)}, u32[]{:S(2)}, u32[]{:S(2)}) collective-permute-start(bf16[2,576,256]{2,1,0:T(8,128)(2,1)S(1)} %edge.3), channel_id=1, source_target_pairs={{0,4},{1,5},{2,6},{3,7},{4,8},{5,9},{6,10},{7,11},{8,12},{9,13},{1... | collective-permute-start | bytes 1769480 | tf_op jit(solution)/shard_map/ppermute | solution.py:444
  42.0 17.6 %collective-permute-start.17 = (bf16[2,192,256]{2,1,0:T(8,128)(2,1)S(1)}, bf16[2,192,256]{2,1,0:T(8,128)(2,1)S(1)}, u32[]{:S(2)}, u32[]{:S(2)}) collective-permute-start(bf16[2,192,256]{2,1,0:T(8,128)(2,1)S(1)} %get-tuple-element.50.after), channel_id=1, source_target_pairs={{0,1},{1,2},{2,3},{3,0},{4,5},{5,6},{6,7},{7,4},{8,9},{9,10},{10,1... | collective-permute-start | bytes 589832 | tf_op jit(solution)/shard_map/ppermute | solution.py:440
  42.0 14.3 %collective-permute-start.18 = (bf16[2,192,256]{2,1,0:T(8,128)(2,1)S(1)}, bf16[2,192,256]{2,1,0:T(8,128)(2,1)S(1)}, u32[]{:S(2)}, u32[]{:S(2)}) collective-permute-start(bf16[2,192,256]{2,1,0:T(8,128)(2,1)S(1)} %get-tuple-element.64), channel_id=1, source_target_pairs={{0,3},{1,0},{2,1},{3,2},{4,7},{5,4},{6,5},{7,6},{8,11},{9,8},{10,9... | collective-permute-start | bytes 589832 | tf_op jit(solution)/shard_map/ppermute | solution.py:440
  45.7 11.8 %collective-permute-start.19 = (bf16[2,192,256]{2,1,0:T(8,128)(2,1)S(1)}, bf16[2,192,256]{2,1,0:T(8,128)(2,1)S(1)}, u32[]{:S(2)}, u32[]{:S(2)}) collective-permute-start(bf16[2,192,256]{2,1,0:T(8,128)(2,1)S(1)} %get-tuple-element.65), channel_id=1, source_target_pairs={{0,2},{1,3},{2,0},{3,1},{4,6},{5,7},{6,4},{7,5},{8,10},{9,11},{10,... | collective-permute-start | bytes 589832 | tf_op jit(solution)/shard_map/ppermute | solution.py:440
  52.7 16.5 %collective-permute-start.13 = (bf16[2,576,256]{2,1,0:T(8,128)(2,1)S(1)}, bf16[2,576,256]{2,1,0:T(8,128)(2,1)S(1)}, u32[]{:S(2)}, u32[]{:S(2)}) collective-permute-start(bf16[2,576,256]{2,1,0:T(8,128)(2,1)S(1)} %get-tuple-element.61), channel_id=1, source_target_pairs={{0,28},{1,29},{2,30},{3,31},{4,0},{5,1},{6,2},{7,3},{8,4},{9,5},{1... | collective-permute-start | bytes 1769480 | tf_op jit(solution)/shard_map/ppermute | solution.py:444
  56.3 12.9 %collective-permute-start.10 = (bf16[192,256]{1,0:T(8,128)(2,1)S(1)}, bf16[192,256]{1,0:T(8,128)(2,1)S(1)}, u32[]{:S(2)}, u32[]{:S(2)}) collective-permute-start(bf16[192,256]{1,0:T(8,128)(2,1)S(1)} %get-tuple-element.57), channel_id=1, source_target_pairs={{0,1},{1,2},{2,3},{3,0},{4,5},{5,6},{6,7},{7,4},{8,9},{9,10},{10,1... | collective-permute-start | bytes 294920 | tf_op jit(solution)/shard_map/ppermute | solution.py:440
  57.5 11.7 %collective-permute-start.11 = (bf16[192,256]{1,0:T(8,128)(2,1)S(1)}, bf16[192,256]{1,0:T(8,128)(2,1)S(1)}, u32[]{:S(2)}, u32[]{:S(2)}) collective-permute-start(bf16[192,256]{1,0:T(8,128)(2,1)S(1)} %get-tuple-element.58), channel_id=1, source_target_pairs={{0,3},{1,0},{2,1},{3,2},{4,7},{5,4},{6,5},{7,6},{8,11},{9,8},{10,9... | collective-permute-start | bytes 294920 | tf_op jit(solution)/shard_map/ppermute | solution.py:440
  59.6 9.7 %collective-permute-start.12 = (bf16[192,256]{1,0:T(8,128)(2,1)S(1)}, bf16[192,256]{1,0:T(8,128)(2,1)S(1)}, u32[]{:S(2)}, u32[]{:S(2)}) collective-permute-start(bf16[192,256]{1,0:T(8,128)(2,1)S(1)} %get-tuple-element.59), channel_id=1, source_target_pairs={{0,2},{1,3},{2,0},{3,1},{4,6},{5,7},{6,4},{7,5},{8,10},{9,11},{10,... | collective-permute-start | bytes 294920 | tf_op jit(solution)/shard_map/ppermute | solution.py:440
  65.5 12.2 %collective-permute-start.24 = (bf16[2,576,256]{2,1,0:T(8,128)(2,1)S(1)}, bf16[2,576,256]{2,1,0:T(8,128)(2,1)S(1)}, u32[]{:S(2)}, u32[]{:S(2)}) collective-permute-start(bf16[2,576,256]{2,1,0:T(8,128)(2,1)S(1)} %get-tuple-element.76), channel_id=1, source_target_pairs={{0,28},{1,29},{2,30},{3,31},{4,0},{5,1},{6,2},{7,3},{8,4},{9,5},{1... | collective-permute-start | bytes 1769480 | tf_op jit(solution)/shard_map/ppermute | solution.py:444
  69.5 11.8 %collective-permute-start.21 = (bf16[3,192,256]{2,1,0:T(8,128)(2,1)S(1)}, bf16[3,192,256]{2,1,0:T(8,128)(2,1)S(1)}, u32[]{:S(2)}, u32[]{:S(2)}) collective-permute-start(bf16[3,192,256]{2,1,0:T(8,128)(2,1)S(1)} %get-tuple-element.71), channel_id=1, source_target_pairs={{0,1},{1,2},{2,3},{3,0},{4,5},{5,6},{6,7},{7,4},{8,9},{9,10},{10,1... | collective-permute-start | bytes 884744 | tf_op jit(solution)/shard_map/ppermute | solution.py:440
  69.9 16.4 %collective-permute-start.22 = (bf16[3,192,256]{2,1,0:T(8,128)(2,1)S(1)}, bf16[3,192,256]{2,1,0:T(8,128)(2,1)S(1)}, u32[]{:S(2)}, u32[]{:S(2)}) collective-permute-start(bf16[3,192,256]{2,1,0:T(8,128)(2,1)S(1)} %get-tuple-element.72), channel_id=1, source_target_pairs={{0,3},{1,0},{2,1},{3,2},{4,7},{5,4},{6,5},{7,6},{8,11},{9,8},{10,9... | collective-permute-start | bytes 884744 | tf_op jit(solution)/shard_map/ppermute | solution.py:440
  72.8 13.5 %collective-permute-start.23 = (bf16[3,192,256]{2,1,0:T(8,128)(2,1)S(1)}, bf16[3,192,256]{2,1,0:T(8,128)(2,1)S(1)}, u32[]{:S(2)}, u32[]{:S(2)}) collective-permute-start(bf16[3,192,256]{2,1,0:T(8,128)(2,1)S(1)} %get-tuple-element.73), channel_id=1, source_target_pairs={{0,2},{1,3},{2,0},{3,1},{4,6},{5,7},{6,4},{7,5},{8,10},{9,11},{10,... | collective-permute-start | bytes 884744 | tf_op jit(solution)/shard_map/ppermute | solution.py:440
  77.9 9.7 %collective-permute-start.25 = (bf16[2,192,256]{2,1,0:T(8,128)(2,1)S(1)}, bf16[2,192,256]{2,1,0:T(8,128)(2,1)S(1)}, u32[]{:S(2)}, u32[]{:S(2)}) collective-permute-start(bf16[2,192,256]{2,1,0:T(8,128)(2,1)S(1)} %get-tuple-element.78), channel_id=1, source_target_pairs={{0,1},{1,2},{2,3},{3,0},{4,5},{5,6},{6,7},{7,4},{8,9},{9,10},{10,1... | collective-permute-start | bytes 589832 | tf_op jit(solution)/shard_map/ppermute | solution.py:440
  78.2 9.4 %collective-permute-start.26 = (bf16[2,192,256]{2,1,0:T(8,128)(2,1)S(1)}, bf16[2,192,256]{2,1,0:T(8,128)(2,1)S(1)}, u32[]{:S(2)}, u32[]{:S(2)}) collective-permute-start(bf16[2,192,256]{2,1,0:T(8,128)(2,1)S(1)} %get-tuple-element.79), channel_id=1, source_target_pairs={{0,3},{1,0},{2,1},{3,2},{4,7},{5,4},{6,5},{7,6},{8,11},{9,8},{10,9... | collective-permute-start | bytes 589832 | tf_op jit(solution)/shard_map/ppermute | solution.py:440
  81.2 8.7 %collective-permute-start.27 = (bf16[2,192,256]{2,1,0:T(8,128)(2,1)S(1)}, bf16[2,192,256]{2,1,0:T(8,128)(2,1)S(1)}, u32[]{:S(2)}, u32[]{:S(2)}) collective-permute-start(bf16[2,192,256]{2,1,0:T(8,128)(2,1)S(1)} %get-tuple-element.80), channel_id=1, source_target_pairs={{0,2},{1,3},{2,0},{3,1},{4,6},{5,7},{6,4},{7,5},{8,10},{9,11},{10,... | collective-permute-start | bytes 589832 | tf_op jit(solution)/shard_map/ppermute | solution.py:440
  (3 other events, 3.4 us)

commit v12 on v7

--- a/solution.py
+++ b/solution.py
@@ -39,23 +39,32 @@
         message[1] = second[:, lanes]
 
 
-def first_pack_kernel(first, second, lengths, flags, one, two, three, text, held, sems):
+def first_pack_kernel(first, second, lengths, flags, one, two, three, text, staged, held, sems):
     width = one.shape[2]
     place = lax.rem(lax.axis_index("ctx"), GROUP)
-    copies = []
-    for away, message in zip(aways()[1:], (one, two, three)):
+    inward, outward = [], []
+    for slot, (away, message) in enumerate(zip(aways()[1:], (one, two, three))):
         lanes = columns(place, away, 0, width)
         for part, source in enumerate((first, second)):
-            copies.append(
-                pltpu.make_async_copy(source.at[:, lanes], message.at[part], sems.at[len(copies)])
+            inward.append(
+                pltpu.make_async_copy(
+                    source.at[:, lanes], staged.at[slot, part], sems.at[len(inward)]
+                )
             )
+        outward.append(pltpu.make_async_copy(staged.at[slot], message, sems.at[8 + slot]))
     for part, source in enumerate((lengths, flags)):
-        copies.append(pltpu.make_async_copy(source, held.at[part], sems.at[len(copies)]))
-    for copy in copies:
+        inward.append(pltpu.make_async_copy(source, held.at[part], sems.at[len(inward)]))
+    for copy in inward:
         copy.start()
-    for copy in copies:
+    for slot, copy in enumerate(outward):
+        inward[2 * slot].wait()
+        inward[2 * slot + 1].wait()
+        copy.start()
+    for copy in inward[6:]:
         copy.wait()
     text[...] = (held[0] * (1 - held[1])).astype(jnp.float32)
+    for copy in outward:
+        copy.wait()
 
 
 def pack(first, second, after, chunk):
@@ -81,10 +90,11 @@
         first_pack_kernel,
         out_shape=(message,) * (GROUP - 1) + (jax.ShapeDtypeStruct(lengths.shape, jnp.float32),),
         in_specs=[ANY, ANY, ANY, ANY],
-        out_specs=(VMEM,) * GROUP,
+        out_specs=(ANY,) * (GROUP - 1) + (VMEM,),
         scratch_shapes=[
+            pltpu.VMEM((GROUP - 1, 2, rows, width), first.dtype),
             pltpu.VMEM((2, *lengths.shape), lengths.dtype),
-            pltpu.SemaphoreType.DMA((2 * GROUP,)),
+            pltpu.SemaphoreType.DMA((2 * GROUP + 3,)),
         ],
         compiler_params=LARGE,
         cost_estimate=pl.CostEstimate(flops=0, bytes_accessed=12 * rows * width * 2, transcendentals=0),

time: 86.4 us -> 86.9 us (level)
  no operation moved by 1% of the time
where the time goes in v12:
time: 86.9 us; the launch traced here: 86.7 us
  starting transfers between devices  47.3 us (54%)
  waiting for transfers between devices  21.3 us (25%)
  Pallas kernels  16.5 us (19%)
  between operations  1.01 us (1%)
    ppermute x21, starting transfers between devices, swap(): return lax.ppermute(value, ('dp', 'ctx'), pairs)  31.8 us
    ppermute x4, starting transfers between devices, next_row(): return lax.ppermute(value, 'ctx', pairs)  12.7 us
    ppermute x21, waiting for transfers between devices, swap(): return lax.ppermute(value, ('dp', 'ctx'), pairs)  11.6 us
    pallas_call x2, Pallas kernels, attend(): pl.pallas_call(functools.partial(attend_kernel, chunk, total_rows), out_s...  10.6 us
    ppermute x4, waiting for transfers between devices, next_row(): return lax.ppermute(value, 'ctx', pairs)  8.86 us
    ppermute x3, starting transfers between devices, shards(): lax.ppermute(text, 'dp', [(source, (source + away) % samples) for source...  2.73 us
    pallas_call x1, Pallas kernels, first_pack(): pl.pallas_call(first_pack_kernel, out_shape=(message,) * (GROUP - 1) + (j...  2.61 us
  transfers between devices with their start and end apart: 28, of which 10 were waited for; matrix products, arithmetic and copies ran while one was open for 0% of the time, Pallas kernels for 15%

profile of v12, /device:TPU:0, one launch (start us, length us, event | category | flops | bytes accessed | tf_op | source)
XLA Modules:
  0.0 86.7 jit_solution(2562130450593870494)
XLA Ops:
  0.7 2.6 %first_pack.1 = (bf16[2,192,256]{2,1,0:T(8,128)(2,1)}, bf16[2,192,256]{2,1,0:T(8,128)(2,1)}, bf16[2,192,256]{2,1,0:T(8,128)(2,1)}, f32[1,32]{1,0:T(1,128)}) custom-call(bf16[192,2048]{1,0:T(8,128)(2,1)} %bitcast.7, bf16[192,2048]{1,0:T(8,128)(2,1)} %bitcast.13, s32[1,32]{1,0:T(1,128)} %lengths_ref.1, s32[1,32]{1,0:T(1,128)} %flags_ref.1), custom_call_target="tpu_custom_call" | custom-call | bytes 1179648 | tf_op jit(solution)/shard_map/first_pack/pallas_call | solution.py:89
  3.3 1.7 %collective-permute-start.3 = (bf16[2,192,256]{2,1,0:T(8,128)(2,1)}, bf16[2,192,256]{2,1,0:T(8,128)(2,1)S(1)}, u32[]{:S(2)}, u32[]{:S(2)}) collective-permute-start(bf16[2,192,256]{2,1,0:T(8,128)(2,1)} %get-tuple-element.45), channel_id=1, source_target_pairs={{0,1},{1,2},{2,3},{3,0},{4,5},{5,6},{6,7},{7,4},{8,9},{9,10},{10,1... | collective-permute-start | bytes 589832 | tf_op jit(solution)/shard_map/ppermute | solution.py:450
  5.0 1.6 %collective-permute-start.4 = (bf16[2,192,256]{2,1,0:T(8,128)(2,1)}, bf16[2,192,256]{2,1,0:T(8,128)(2,1)S(1)}, u32[]{:S(2)}, u32[]{:S(2)}) collective-permute-start(bf16[2,192,256]{2,1,0:T(8,128)(2,1)} %get-tuple-element.46), channel_id=1, source_target_pairs={{0,3},{1,0},{2,1},{3,2},{4,7},{5,4},{6,5},{7,6},{8,11},{9,8},{10,9... | collective-permute-start | bytes 589832 | tf_op jit(solution)/shard_map/ppermute | solution.py:450
  6.6 2.1 %collective-permute-start.5 = (bf16[2,192,256]{2,1,0:T(8,128)(2,1)}, bf16[2,192,256]{2,1,0:T(8,128)(2,1)S(1)}, u32[]{:S(2)}, u32[]{:S(2)}) collective-permute-start(bf16[2,192,256]{2,1,0:T(8,128)(2,1)} %get-tuple-element.47), channel_id=1, source_target_pairs={{0,2},{1,3},{2,0},{3,1},{4,6},{5,7},{6,4},{7,5},{8,10},{9,11},{10,... | collective-permute-start | bytes 589832 | tf_op jit(solution)/shard_map/ppermute | solution.py:450
  8.7 1.4 %collective-permute-start.1 = (f32[1,32]{1,0:T(1,128)S(1)}, f32[1,32]{1,0:T(1,128)S(1)}, u32[]{:S(2)}, u32[]{:S(2)}) collective-permute-start(f32[1,32]{1,0:T(1,128)S(1)} %copy-done.6), channel_id=1, source_target_pairs={{0,64},{32,96},{64,0},{96,32},{1,65},{33,97},{65,1},{97,33},{2,66}... | collective-permute-start | bytes 392 | tf_op jit(solution)/shard_map/ppermute | solution.py:461
  10.2 1.2 %collective-permute-start = (f32[1,32]{1,0:T(1,128)S(1)}, f32[1,32]{1,0:T(1,128)S(1)}, u32[]{:S(2)}, u32[]{:S(2)}) collective-permute-start(f32[1,32]{1,0:T(1,128)S(1)} %copy-done.6), channel_id=1, source_target_pairs={{0,32},{32,64},{64,96},{96,0},{1,33},{33,65},{65,97},{97,1},{2,34}... | collective-permute-start | bytes 392 | tf_op jit(solution)/shard_map/ppermute | solution.py:461
  12.3 2.0 %collective-permute-start.15 = (bf16[2,192,256]{2,1,0:T(8,128)(2,1)S(1)}, bf16[2,192,256]{2,1,0:T(8,128)(2,1)S(1)}, u32[]{:S(2)}, u32[]{:S(2)}) collective-permute-start(bf16[2,192,256]{2,1,0:T(8,128)(2,1)S(1)} %get-tuple-element.62), channel_id=1, source_target_pairs={{0,3},{1,0},{2,1},{3,2},{4,7},{5,4},{6,5},{7,6},{8,11},{9,8},{10,9... | collective-permute-start | bytes 589832 | tf_op jit(solution)/shard_map/ppermute | solution.py:450
  14.3 2.0 %collective-permute-start.16 = (bf16[2,192,256]{2,1,0:T(8,128)(2,1)S(1)}, bf16[2,192,256]{2,1,0:T(8,128)(2,1)S(1)}, u32[]{:S(2)}, u32[]{:S(2)}) collective-permute-start(bf16[2,192,256]{2,1,0:T(8,128)(2,1)S(1)} %get-tuple-element.63), channel_id=1, source_target_pairs={{0,2},{1,3},{2,0},{3,1},{4,6},{5,7},{6,4},{7,5},{8,10},{9,11},{10,... | collective-permute-start | bytes 589832 | tf_op jit(solution)/shard_map/ppermute | solution.py:450
  16.3 1.8 %collective-permute-done.5.three.key_three = bf16[2,192,256]{2,1,0:T(8,128)(2,1)S(1)} collective-permute-done((bf16[2,192,256]{2,1,0:T(8,128)(2,1)}, bf16[2,192,256]{2,1,0:T(8,128)(2,1)S(1)}, u32[]{:S(2)}, u32[]{:S(2)}) %collective-permute-start.5) | collective-permute-done | bytes 196640 | tf_op jit(solution)/shard_map/ppermute | solution.py:450
  18.1 3.1 %collective-permute-start.9 = (bf16[2,576,256]{2,1,0:T(8,128)(2,1)S(1)}, bf16[2,576,256]{2,1,0:T(8,128)(2,1)S(1)}, u32[]{:S(2)}, u32[]{:S(2)}) collective-permute-start(bf16[2,576,256]{2,1,0:T(8,128)(2,1)S(1)} %edge.2.after), channel_id=1, source_target_pairs={{0,4},{1,5},{2,6},{3,7},{4,8},{5,9},{6,10},{7,11},{8,12},{9,13},{1... | collective-permute-start | bytes 1769480 | tf_op jit(solution)/shard_map/ppermute | solution.py:454
  22.5 4.0 %collective-permute-start.7 = (bf16[2,192,256]{2,1,0:T(8,128)(2,1)S(1)}, bf16[2,192,256]{2,1,0:T(8,128)(2,1)S(1)}, u32[]{:S(2)}, u32[]{:S(2)}) collective-permute-start(bf16[2,192,256]{2,1,0:T(8,128)(2,1)S(1)} %get-tuple-element.54), channel_id=1, source_target_pairs={{0,3},{1,0},{2,1},{3,2},{4,7},{5,4},{6,5},{7,6},{8,11},{9,8},{10,9... | collective-permute-start | bytes 589832 | tf_op jit(solution)/shard_map/ppermute | solution.py:450
  26.5 1.7 %collective-permute-start.8 = (bf16[2,192,256]{2,1,0:T(8,128)(2,1)S(1)}, bf16[2,192,256]{2,1,0:T(8,128)(2,1)S(1)}, u32[]{:S(2)}, u32[]{:S(2)}) collective-permute-start(bf16[2,192,256]{2,1,0:T(8,128)(2,1)S(1)} %get-tuple-element.55), channel_id=1, source_target_pairs={{0,2},{1,3},{2,0},{3,1},{4,6},{5,7},{6,4},{7,5},{8,10},{9,11},{10,... | collective-permute-start | bytes 589832 | tf_op jit(solution)/shard_map/ppermute | solution.py:450
  28.3 2.6 %collective-permute-start.20 = (bf16[2,576,256]{2,1,0:T(8,128)(2,1)S(1)}, bf16[2,576,256]{2,1,0:T(8,128)(2,1)S(1)}, u32[]{:S(2)}, u32[]{:S(2)}) collective-permute-start(bf16[2,576,256]{2,1,0:T(8,128)(2,1)S(1)} %edge.3), channel_id=1, source_target_pairs={{0,4},{1,5},{2,6},{3,7},{4,8},{5,9},{6,10},{7,11},{8,12},{9,13},{1... | collective-permute-start | bytes 1769480 | tf_op jit(solution)/shard_map/ppermute | solution.py:454
  30.8 1.5 %collective-permute-done.7.query_two = bf16[2,192,256]{2,1,0:T(8,128)(2,1)S(1)} collective-permute-done((bf16[2,192,256]{2,1,0:T(8,128)(2,1)S(1)}, bf16[2,192,256]{2,1,0:T(8,128)(2,1)S(1)}, u32[]{:S(2)}, u32[]{:S(2)}) %collective-permute-start.7) | collective-permute-done | bytes 196640 | tf_op jit(solution)/shard_map/ppermute | solution.py:450
  32.3 1.3 %collective-permute-start.17 = (bf16[2,192,256]{2,1,0:T(8,128)(2,1)S(1)}, bf16[2,192,256]{2,1,0:T(8,128)(2,1)S(1)}, u32[]{:S(2)}, u32[]{:S(2)}) collective-permute-start(bf16[2,192,256]{2,1,0:T(8,128)(2,1)S(1)} %get-tuple-element.50.after), channel_id=1, source_target_pairs={{0,1},{1,2},{2,3},{3,0},{4,5},{5,6},{6,7},{7,4},{8,9},{9,10},{10,1... | collective-permute-start | bytes 589832 | tf_op jit(solution)/shard_map/ppermute | solution.py:450
  34.3 1.8 %collective-permute-start.18 = (bf16[2,192,256]{2,1,0:T(8,128)(2,1)S(1)}, bf16[2,192,256]{2,1,0:T(8,128)(2,1)S(1)}, u32[]{:S(2)}, u32[]{:S(2)}) collective-permute-start(bf16[2,192,256]{2,1,0:T(8,128)(2,1)S(1)} %get-tuple-element.64), channel_id=1, source_target_pairs={{0,3},{1,0},{2,1},{3,2},{4,7},{5,4},{6,5},{7,6},{8,11},{9,8},{10,9... | collective-permute-start | bytes 589832 | tf_op jit(solution)/shard_map/ppermute | solution.py:450
  36.1 1.9 %collective-permute-start.19 = (bf16[2,192,256]{2,1,0:T(8,128)(2,1)S(1)}, bf16[2,192,256]{2,1,0:T(8,128)(2,1)S(1)}, u32[]{:S(2)}, u32[]{:S(2)}) collective-permute-start(bf16[2,192,256]{2,1,0:T(8,128)(2,1)S(1)} %get-tuple-element.65), channel_id=1, source_target_pairs={{0,2},{1,3},{2,0},{3,1},{4,6},{5,7},{6,4},{7,5},{8,10},{9,11},{10,... | collective-permute-start | bytes 589832 | tf_op jit(solution)/shard_map/ppermute | solution.py:450
  38.1 0.8 collective-permute-done.9.edge_ref
  38.9 5.3 %attend.2 = (bf16[192,256]{1,0:T(8,128)(2,1)S(1)}, bf16[192,256]{1,0:T(8,128)(2,1)S(1)}, bf16[192,256]{1,0:T(8,128)(2,1)S(1)}, bf16[192,256]{1,0:T(8,128)(2,1)S(...) custom-call(f32[1,32]{1,0:T(1,128)S(1)} %copy-done.6, ...), custom_call_target="tpu_custom_call" | custom-call | flops 4499999744 | tf_op jit(solution)/shard_map/attend/pallas_call | solution.py:299
  44.2 6.0 %collective-permute-start.13 = (bf16[2,576,256]{2,1,0:T(8,128)(2,1)S(1)}, bf16[2,576,256]{2,1,0:T(8,128)(2,1)S(1)}, u32[]{:S(2)}, u32[]{:S(2)}) collective-permute-start(bf16[2,576,256]{2,1,0:T(8,128)(2,1)S(1)} %get-tuple-element.61), channel_id=1, source_target_pairs={{0,28},{1,29},{2,30},{3,31},{4,0},{5,1},{6,2},{7,3},{8,4},{9,5},{1... | collective-permute-start | bytes 1769480 | tf_op jit(solution)/shard_map/ppermute | solution.py:454
  51.0 2.5 %collective-permute-start.11 = (bf16[192,256]{1,0:T(8,128)(2,1)S(1)}, bf16[192,256]{1,0:T(8,128)(2,1)S(1)}, u32[]{:S(2)}, u32[]{:S(2)}) collective-permute-start(bf16[192,256]{1,0:T(8,128)(2,1)S(1)} %get-tuple-element.58), channel_id=1, source_target_pairs={{0,3},{1,0},{2,1},{3,2},{4,7},{5,4},{6,5},{7,6},{8,11},{9,8},{10,9... | collective-permute-start | bytes 294920 | tf_op jit(solution)/shard_map/ppermute | solution.py:450
  53.5 0.9 collective-permute-start.12
  54.4 5.3 %attend.3 = (bf16[192,256]{1,0:T(8,128)(2,1)S(1)}, bf16[192,256]{1,0:T(8,128)(2,1)S(1)}, bf16[192,256]{1,0:T(8,128)(2,1)S(1)}, bf16[192,256]{1,0:T(8,128)(2,1)S(...) custom-call(f32[1,32]{1,0:T(1,128)S(1)} %copy-done.6, ...), custom_call_target="tpu_custom_call" | custom-call | flops 4499999744 | tf_op jit(solution)/shard_map/attend/pallas_call | solution.py:299
  59.7 1.0 %collective-permute-start.24 = (bf16[2,576,256]{2,1,0:T(8,128)(2,1)S(1)}, bf16[2,576,256]{2,1,0:T(8,128)(2,1)S(1)}, u32[]{:S(2)}, u32[]{:S(2)}) collective-permute-start(bf16[2,576,256]{2,1,0:T(8,128)(2,1)S(1)} %get-tuple-element.76), channel_id=1, source_target_pairs={{0,28},{1,29},{2,30},{3,31},{4,0},{5,1},{6,2},{7,3},{8,4},{9,5},{1... | collective-permute-start | bytes 1769480 | tf_op jit(solution)/shard_map/ppermute | solution.py:454
  60.7 0.9 %collective-permute-done.13.far_ref = bf16[2,576,256]{2,1,0:T(8,128)(2,1)S(1)} collective-permute-done((bf16[2,576,256]{2,1,0:T(8,128)(2,1)S(1)}, bf16[2,576,256]{2,1,0:T(8,128)(2,1)S(1)}, u32[]{:S(2)}, u32[]{:S(2)}) %collective-permute-start.13) | collective-permute-done | bytes 589856 | tf_op jit(solution)/shard_map/ppermute | solution.py:454
  61.9 3.2 %collective-permute-start.22 = (bf16[3,192,256]{2,1,0:T(8,128)(2,1)S(1)}, bf16[3,192,256]{2,1,0:T(8,128)(2,1)S(1)}, u32[]{:S(2)}, u32[]{:S(2)}) collective-permute-start(bf16[3,192,256]{2,1,0:T(8,128)(2,1)S(1)} %get-tuple-element.72), channel_id=1, source_target_pairs={{0,3},{1,0},{2,1},{3,2},{4,7},{5,4},{6,5},{7,6},{8,11},{9,8},{10,9... | collective-permute-start | bytes 884744 | tf_op jit(solution)/shard_map/ppermute | solution.py:450
  65.1 0.8 collective-permute-start.23
  65.9 7.1 %collective-permute-done.24.far_ref = bf16[2,576,256]{2,1,0:T(8,128)(2,1)S(1)} collective-permute-done((bf16[2,576,256]{2,1,0:T(8,128)(2,1)S(1)}, bf16[2,576,256]{2,1,0:T(8,128)(2,1)S(1)}, u32[]{:S(2)}, u32[]{:S(2)}) %collective-permute-start.24) | collective-permute-done | bytes 589856 | tf_op jit(solution)/shard_map/ppermute | solution.py:454
  73.8 2.8 %collective-permute-start.26 = (bf16[2,192,256]{2,1,0:T(8,128)(2,1)S(1)}, bf16[2,192,256]{2,1,0:T(8,128)(2,1)S(1)}, u32[]{:S(2)}, u32[]{:S(2)}) collective-permute-start(bf16[2,192,256]{2,1,0:T(8,128)(2,1)S(1)} %get-tuple-element.79), channel_id=1, source_target_pairs={{0,3},{1,0},{2,1},{3,2},{4,7},{5,4},{6,5},{7,6},{8,11},{9,8},{10,9... | collective-permute-start | bytes 589832 | tf_op jit(solution)/shard_map/ppermute | solution.py:450
  77.9 1.3 %early.1 = (bf16[192,2048]{1,0:T(8,128)(2,1)}, bf16[192,2048]{1,0:T(8,128)(2,1)}, bf16[192,2048]{1,0:T(8,128)(2,1)}) custom-call(bf16[192,256]{1,0:T(8,128)(2,1)S(1)} %get-tuple-element.56.refs_0_, bf16[192,256]{1,0:T(8,128)(2,1)S(1)} %collective-permute-done.10.refs_4_.refs_1_, bf16[192,256]{1,0:T(8,128)(2,1)S(1)} %collective-permute-done.11.refs_5_.refs_2_, ...), custom_call_target="tpu_custom_call" | custom-call | bytes 2359296 | tf_op jit(solution)/shard_map/early/pallas_call | solution.py:412
  79.1 6.5 %collective-permute-done.25.refs_1_ = bf16[2,192,256]{2,1,0:T(8,128)(2,1)S(1)} collective-permute-done((bf16[2,192,256]{2,1,0:T(8,128)(2,1)S(1)}, bf16[2,192,256]{2,1,0:T(8,128)(2,1)S(1)}, u32[]{:S(2)}, u32[]{:S(2)}) %collective-permute-start.25) | collective-permute-done | bytes 196640 | tf_op jit(solution)/shard_map/ppermute | solution.py:450
  85.6 0.9 %late.1 = (bf16[192,2048]{1,0:T(8,128)(2,1)}, bf16[192,2048]{1,0:T(8,128)(2,1)}) custom-call(bf16[2,192,256]{2,1,0:T(8,128)(2,1)S(1)} %get-tuple-element.77.refs_0_, bf16[2,192,256]{2,1,0:T(8,128)(2,1)S(1)} %collective-permute-done.25.refs_1_, ...), custom_call_target="tpu_custom_call", output_to_operand_aliasing={{0}: (4, {}), {1}: (5, {})} | custom-call | bytes 2359296 | tf_op jit(solution)/shard_map/late/pallas_call | solution.py:422
  (51 shorter events, 6.2 us)
Async XLA Ops:
  0.6 9.5 %copy-start = (bf16[1,192,2048]{2,1,0:T(8,128)(2,1)S(1)}, bf16[1,192,2048]{2,1,0:T(8,128)(2,1)}, u32[]{:S(2)}) copy-start(bf16[1,192,2048]{2,1,0:T(8,128)(2,1)} %param.7) | copy-start | bytes 2359300
  0.6 9.5 %copy-start.1 = (bf16[1,192,2048]{2,1,0:T(8,128)(2,1)S(1)}, bf16[1,192,2048]{2,1,0:T(8,128)(2,1)}, u32[]{:S(2)}) copy-start(bf16[1,192,2048]{2,1,0:T(8,128)(2,1)} %param.8) | copy-start | bytes 2359300
  3.3 13.0 %collective-permute-start.3 = (bf16[2,192,256]{2,1,0:T(8,128)(2,1)}, bf16[2,192,256]{2,1,0:T(8,128)(2,1)S(1)}, u32[]{:S(2)}, u32[]{:S(2)}) collective-permute-start(bf16[2,192,256]{2,1,0:T(8,128)(2,1)} %get-tuple-element.45), channel_id=1, source_target_pairs={{0,1},{1,2},{2,3},{3,0},{4,5},{5,6},{6,7},{7,4},{8,9},{9,10},{10,1... | collective-permute-start | bytes 589832 | tf_op jit(solution)/shard_map/ppermute | solution.py:450
  5.0 11.3 %collective-permute-start.4 = (bf16[2,192,256]{2,1,0:T(8,128)(2,1)}, bf16[2,192,256]{2,1,0:T(8,128)(2,1)S(1)}, u32[]{:S(2)}, u32[]{:S(2)}) collective-permute-start(bf16[2,192,256]{2,1,0:T(8,128)(2,1)} %get-tuple-element.46), channel_id=1, source_target_pairs={{0,3},{1,0},{2,1},{3,2},{4,7},{5,4},{6,5},{7,6},{8,11},{9,8},{10,9... | collective-permute-start | bytes 589832 | tf_op jit(solution)/shard_map/ppermute | solution.py:450
  6.6 11.4 %collective-permute-start.5 = (bf16[2,192,256]{2,1,0:T(8,128)(2,1)}, bf16[2,192,256]{2,1,0:T(8,128)(2,1)S(1)}, u32[]{:S(2)}, u32[]{:S(2)}) collective-permute-start(bf16[2,192,256]{2,1,0:T(8,128)(2,1)} %get-tuple-element.47), channel_id=1, source_target_pairs={{0,2},{1,3},{2,0},{3,1},{4,6},{5,7},{6,4},{7,5},{8,10},{9,11},{10,... | collective-permute-start | bytes 589832 | tf_op jit(solution)/shard_map/ppermute | solution.py:450
  8.6 1.6 %collective-permute-start.2 = (f32[1,32]{1,0:T(1,128)S(1)}, f32[1,32]{1,0:T(1,128)S(1)}, u32[]{:S(2)}, u32[]{:S(2)}) collective-permute-start(f32[1,32]{1,0:T(1,128)S(1)} %copy-done.6), channel_id=1, source_target_pairs={{0,96},{32,0},{64,32},{96,64},{1,97},{33,1},{65,33},{97,65},{2,98}... | collective-permute-start | bytes 392 | tf_op jit(solution)/shard_map/ppermute | solution.py:461
  8.7 3.5 %collective-permute-start.1 = (f32[1,32]{1,0:T(1,128)S(1)}, f32[1,32]{1,0:T(1,128)S(1)}, u32[]{:S(2)}, u32[]{:S(2)}) collective-permute-start(f32[1,32]{1,0:T(1,128)S(1)} %copy-done.6), channel_id=1, source_target_pairs={{0,64},{32,96},{64,0},{96,32},{1,65},{33,97},{65,1},{97,33},{2,66}... | collective-permute-start | bytes 392 | tf_op jit(solution)/shard_map/ppermute | solution.py:461
  10.2 4.0 %collective-permute-start = (f32[1,32]{1,0:T(1,128)S(1)}, f32[1,32]{1,0:T(1,128)S(1)}, u32[]{:S(2)}, u32[]{:S(2)}) collective-permute-start(f32[1,32]{1,0:T(1,128)S(1)} %copy-done.6), channel_id=1, source_target_pairs={{0,32},{32,64},{64,96},{96,0},{1,33},{33,65},{65,97},{97,1},{2,34}... | collective-permute-start | bytes 392 | tf_op jit(solution)/shard_map/ppermute | solution.py:461
  12.3 10.2 %collective-permute-start.15 = (bf16[2,192,256]{2,1,0:T(8,128)(2,1)S(1)}, bf16[2,192,256]{2,1,0:T(8,128)(2,1)S(1)}, u32[]{:S(2)}, u32[]{:S(2)}) collective-permute-start(bf16[2,192,256]{2,1,0:T(8,128)(2,1)S(1)} %get-tuple-element.62), channel_id=1, source_target_pairs={{0,3},{1,0},{2,1},{3,2},{4,7},{5,4},{6,5},{7,6},{8,11},{9,8},{10,9... | collective-permute-start | bytes 589832 | tf_op jit(solution)/shard_map/ppermute | solution.py:450
  14.3 12.3 %collective-permute-start.16 = (bf16[2,192,256]{2,1,0:T(8,128)(2,1)S(1)}, bf16[2,192,256]{2,1,0:T(8,128)(2,1)S(1)}, u32[]{:S(2)}, u32[]{:S(2)}) collective-permute-start(bf16[2,192,256]{2,1,0:T(8,128)(2,1)S(1)} %get-tuple-element.63), channel_id=1, source_target_pairs={{0,2},{1,3},{2,0},{3,1},{4,6},{5,7},{6,4},{7,5},{8,10},{9,11},{10,... | collective-permute-start | bytes 589832 | tf_op jit(solution)/shard_map/ppermute | solution.py:450
  16.2 4.9 %copy-start.2 = (bf16[1,192,2048]{2,1,0:T(8,128)(2,1)S(1)}, bf16[1,192,2048]{2,1,0:T(8,128)(2,1)}, u32[]{:S(2)}) copy-start(bf16[1,192,2048]{2,1,0:T(8,128)(2,1)} %param.6) | copy-start | bytes 2359300
  16.2 4.9 %copy-start.3 = (bf16[1,192,2048]{2,1,0:T(8,128)(2,1)S(1)}, bf16[1,192,2048]{2,1,0:T(8,128)(2,1)}, u32[]{:S(2)}) copy-start(bf16[1,192,2048]{2,1,0:T(8,128)(2,1)} %param.9) | copy-start | bytes 2359300
  16.2 12.0 %collective-permute-start.14 = (bf16[2,192,256]{2,1,0:T(8,128)(2,1)S(1)}, bf16[2,192,256]{2,1,0:T(8,128)(2,1)S(1)}, u32[]{:S(2)}, u32[]{:S(2)}) collective-permute-start(bf16[2,192,256]{2,1,0:T(8,128)(2,1)S(1)} %get-tuple-element.48.refs_3_), channel_id=1, source_target_pairs={{0,1},{1,2},{2,3},{3,0},{4,5},{5,6},{6,7},{7,4},{8,9},{9,10},{10,1... | collective-permute-start | bytes 589832 | tf_op jit(solution)/shard_map/ppermute | solution.py:450
  18.1 20.8 %collective-permute-start.9 = (bf16[2,576,256]{2,1,0:T(8,128)(2,1)S(1)}, bf16[2,576,256]{2,1,0:T(8,128)(2,1)S(1)}, u32[]{:S(2)}, u32[]{:S(2)}) collective-permute-start(bf16[2,576,256]{2,1,0:T(8,128)(2,1)S(1)} %edge.2.after), channel_id=1, source_target_pairs={{0,4},{1,5},{2,6},{3,7},{4,8},{5,9},{6,10},{7,11},{8,12},{9,13},{1... | collective-permute-start | bytes 1769480 | tf_op jit(solution)/shard_map/ppermute | solution.py:454
  21.3 14.9 %collective-permute-start.6 = (bf16[2,192,256]{2,1,0:T(8,128)(2,1)S(1)}, bf16[2,192,256]{2,1,0:T(8,128)(2,1)S(1)}, u32[]{:S(2)}, u32[]{:S(2)}) collective-permute-start(bf16[2,192,256]{2,1,0:T(8,128)(2,1)S(1)} %get-tuple-element.49.after), channel_id=1, source_target_pairs={{0,1},{1,2},{2,3},{3,0},{4,5},{5,6},{6,7},{7,4},{8,9},{9,10},{10,1... | collective-permute-start | bytes 589832 | tf_op jit(solution)/shard_map/ppermute | solution.py:450
  22.5 9.8 %collective-permute-start.7 = (bf16[2,192,256]{2,1,0:T(8,128)(2,1)S(1)}, bf16[2,192,256]{2,1,0:T(8,128)(2,1)S(1)}, u32[]{:S(2)}, u32[]{:S(2)}) collective-permute-start(bf16[2,192,256]{2,1,0:T(8,128)(2,1)S(1)} %get-tuple-element.54), channel_id=1, source_target_pairs={{0,3},{1,0},{2,1},{3,2},{4,7},{5,4},{6,5},{7,6},{8,11},{9,8},{10,9... | collective-permute-start | bytes 589832 | tf_op jit(solution)/shard_map/ppermute | solution.py:450
  26.5 7.8 %collective-permute-start.8 = (bf16[2,192,256]{2,1,0:T(8,128)(2,1)S(1)}, bf16[2,192,256]{2,1,0:T(8,128)(2,1)S(1)}, u32[]{:S(2)}, u32[]{:S(2)}) collective-permute-start(bf16[2,192,256]{2,1,0:T(8,128)(2,1)S(1)} %get-tuple-element.55), channel_id=1, source_target_pairs={{0,2},{1,3},{2,0},{3,1},{4,6},{5,7},{6,4},{7,5},{8,10},{9,11},{10,... | collective-permute-start | bytes 589832 | tf_op jit(solution)/shard_map/ppermute | solution.py:450
  28.3 26.1 %collective-permute-start.20 = (bf16[2,576,256]{2,1,0:T(8,128)(2,1)S(1)}, bf16[2,576,256]{2,1,0:T(8,128)(2,1)S(1)}, u32[]{:S(2)}, u32[]{:S(2)}) collective-permute-start(bf16[2,576,256]{2,1,0:T(8,128)(2,1)S(1)} %edge.3), channel_id=1, source_target_pairs={{0,4},{1,5},{2,6},{3,7},{4,8},{5,9},{6,10},{7,11},{8,12},{9,13},{1... | collective-permute-start | bytes 1769480 | tf_op jit(solution)/shard_map/ppermute | solution.py:454
  32.3 21.2 %collective-permute-start.17 = (bf16[2,192,256]{2,1,0:T(8,128)(2,1)S(1)}, bf16[2,192,256]{2,1,0:T(8,128)(2,1)S(1)}, u32[]{:S(2)}, u32[]{:S(2)}) collective-permute-start(bf16[2,192,256]{2,1,0:T(8,128)(2,1)S(1)} %get-tuple-element.50.after), channel_id=1, source_target_pairs={{0,1},{1,2},{2,3},{3,0},{4,5},{5,6},{6,7},{7,4},{8,9},{9,10},{10,1... | collective-permute-start | bytes 589832 | tf_op jit(solution)/shard_map/ppermute | solution.py:450
  34.3 15.9 %collective-permute-start.18 = (bf16[2,192,256]{2,1,0:T(8,128)(2,1)S(1)}, bf16[2,192,256]{2,1,0:T(8,128)(2,1)S(1)}, u32[]{:S(2)}, u32[]{:S(2)}) collective-permute-start(bf16[2,192,256]{2,1,0:T(8,128)(2,1)S(1)} %get-tuple-element.64), channel_id=1, source_target_pairs={{0,3},{1,0},{2,1},{3,2},{4,7},{5,4},{6,5},{7,6},{8,11},{9,8},{10,9... | collective-permute-start | bytes 589832 | tf_op jit(solution)/shard_map/ppermute | solution.py:450
  36.1 14.8 %collective-permute-start.19 = (bf16[2,192,256]{2,1,0:T(8,128)(2,1)S(1)}, bf16[2,192,256]{2,1,0:T(8,128)(2,1)S(1)}, u32[]{:S(2)}, u32[]{:S(2)}) collective-permute-start(bf16[2,192,256]{2,1,0:T(8,128)(2,1)S(1)} %get-tuple-element.65), channel_id=1, source_target_pairs={{0,2},{1,3},{2,0},{3,1},{4,6},{5,7},{6,4},{7,5},{8,10},{9,11},{10,... | collective-permute-start | bytes 589832 | tf_op jit(solution)/shard_map/ppermute | solution.py:450
  44.2 17.4 %collective-permute-start.13 = (bf16[2,576,256]{2,1,0:T(8,128)(2,1)S(1)}, bf16[2,576,256]{2,1,0:T(8,128)(2,1)S(1)}, u32[]{:S(2)}, u32[]{:S(2)}) collective-permute-start(bf16[2,576,256]{2,1,0:T(8,128)(2,1)S(1)} %get-tuple-element.61), channel_id=1, source_target_pairs={{0,28},{1,29},{2,30},{3,31},{4,0},{5,1},{6,2},{7,3},{8,4},{9,5},{1... | collective-permute-start | bytes 1769480 | tf_op jit(solution)/shard_map/ppermute | solution.py:454
  50.2 10.4 %collective-permute-start.10 = (bf16[192,256]{1,0:T(8,128)(2,1)S(1)}, bf16[192,256]{1,0:T(8,128)(2,1)S(1)}, u32[]{:S(2)}, u32[]{:S(2)}) collective-permute-start(bf16[192,256]{1,0:T(8,128)(2,1)S(1)} %get-tuple-element.57), channel_id=1, source_target_pairs={{0,1},{1,2},{2,3},{3,0},{4,5},{5,6},{6,7},{7,4},{8,9},{9,10},{10,1... | collective-permute-start | bytes 294920 | tf_op jit(solution)/shard_map/ppermute | solution.py:450
  51.0 9.7 %collective-permute-start.11 = (bf16[192,256]{1,0:T(8,128)(2,1)S(1)}, bf16[192,256]{1,0:T(8,128)(2,1)S(1)}, u32[]{:S(2)}, u32[]{:S(2)}) collective-permute-start(bf16[192,256]{1,0:T(8,128)(2,1)S(1)} %get-tuple-element.58), channel_id=1, source_target_pairs={{0,3},{1,0},{2,1},{3,2},{4,7},{5,4},{6,5},{7,6},{8,11},{9,8},{10,9... | collective-permute-start | bytes 294920 | tf_op jit(solution)/shard_map/ppermute | solution.py:450
  53.5 7.2 %collective-permute-start.12 = (bf16[192,256]{1,0:T(8,128)(2,1)S(1)}, bf16[192,256]{1,0:T(8,128)(2,1)S(1)}, u32[]{:S(2)}, u32[]{:S(2)}) collective-permute-start(bf16[192,256]{1,0:T(8,128)(2,1)S(1)} %get-tuple-element.59), channel_id=1, source_target_pairs={{0,2},{1,3},{2,0},{3,1},{4,6},{5,7},{6,4},{7,5},{8,10},{9,11},{10,... | collective-permute-start | bytes 294920 | tf_op jit(solution)/shard_map/ppermute | solution.py:450
  59.7 13.4 %collective-permute-start.24 = (bf16[2,576,256]{2,1,0:T(8,128)(2,1)S(1)}, bf16[2,576,256]{2,1,0:T(8,128)(2,1)S(1)}, u32[]{:S(2)}, u32[]{:S(2)}) collective-permute-start(bf16[2,576,256]{2,1,0:T(8,128)(2,1)S(1)} %get-tuple-element.76), channel_id=1, source_target_pairs={{0,28},{1,29},{2,30},{3,31},{4,0},{5,1},{6,2},{7,3},{8,4},{9,5},{1... | collective-permute-start | bytes 1769480 | tf_op jit(solution)/shard_map/ppermute | solution.py:454
  61.8 15.2 %collective-permute-start.21 = (bf16[3,192,256]{2,1,0:T(8,128)(2,1)S(1)}, bf16[3,192,256]{2,1,0:T(8,128)(2,1)S(1)}, u32[]{:S(2)}, u32[]{:S(2)}) collective-permute-start(bf16[3,192,256]{2,1,0:T(8,128)(2,1)S(1)} %get-tuple-element.71), channel_id=1, source_target_pairs={{0,1},{1,2},{2,3},{3,0},{4,5},{5,6},{6,7},{7,4},{8,9},{9,10},{10,1... | collective-permute-start | bytes 884744 | tf_op jit(solution)/shard_map/ppermute | solution.py:450
  61.9 15.2 %collective-permute-start.22 = (bf16[3,192,256]{2,1,0:T(8,128)(2,1)S(1)}, bf16[3,192,256]{2,1,0:T(8,128)(2,1)S(1)}, u32[]{:S(2)}, u32[]{:S(2)}) collective-permute-start(bf16[3,192,256]{2,1,0:T(8,128)(2,1)S(1)} %get-tuple-element.72), channel_id=1, source_target_pairs={{0,3},{1,0},{2,1},{3,2},{4,7},{5,4},{6,5},{7,6},{8,11},{9,8},{10,9... | collective-permute-start | bytes 884744 | tf_op jit(solution)/shard_map/ppermute | solution.py:450
  65.1 12.8 %collective-permute-start.23 = (bf16[3,192,256]{2,1,0:T(8,128)(2,1)S(1)}, bf16[3,192,256]{2,1,0:T(8,128)(2,1)S(1)}, u32[]{:S(2)}, u32[]{:S(2)}) collective-permute-start(bf16[3,192,256]{2,1,0:T(8,128)(2,1)S(1)} %get-tuple-element.73), channel_id=1, source_target_pairs={{0,2},{1,3},{2,0},{3,1},{4,6},{5,7},{6,4},{7,5},{8,10},{9,11},{10,... | collective-permute-start | bytes 884744 | tf_op jit(solution)/shard_map/ppermute | solution.py:450
  73.2 12.4 %collective-permute-start.25 = (bf16[2,192,256]{2,1,0:T(8,128)(2,1)S(1)}, bf16[2,192,256]{2,1,0:T(8,128)(2,1)S(1)}, u32[]{:S(2)}, u32[]{:S(2)}) collective-permute-start(bf16[2,192,256]{2,1,0:T(8,128)(2,1)S(1)} %get-tuple-element.78), channel_id=1, source_target_pairs={{0,1},{1,2},{2,3},{3,0},{4,5},{5,6},{6,7},{7,4},{8,9},{9,10},{10,1... | collective-permute-start | bytes 589832 | tf_op jit(solution)/shard_map/ppermute | solution.py:450
  73.8 11.8 %collective-permute-start.26 = (bf16[2,192,256]{2,1,0:T(8,128)(2,1)S(1)}, bf16[2,192,256]{2,1,0:T(8,128)(2,1)S(1)}, u32[]{:S(2)}, u32[]{:S(2)}) collective-permute-start(bf16[2,192,256]{2,1,0:T(8,128)(2,1)S(1)} %get-tuple-element.79), channel_id=1, source_target_pairs={{0,3},{1,0},{2,1},{3,2},{4,7},{5,4},{6,5},{7,6},{8,11},{9,8},{10,9... | collective-permute-start | bytes 589832 | tf_op jit(solution)/shard_map/ppermute | solution.py:450
  77.0 8.6 %collective-permute-start.27 = (bf16[2,192,256]{2,1,0:T(8,128)(2,1)S(1)}, bf16[2,192,256]{2,1,0:T(8,128)(2,1)S(1)}, u32[]{:S(2)}, u32[]{:S(2)}) collective-permute-start(bf16[2,192,256]{2,1,0:T(8,128)(2,1)S(1)} %get-tuple-element.80), channel_id=1, source_target_pairs={{0,2},{1,3},{2,0},{3,1},{4,6},{5,7},{6,4},{7,5},{8,10},{9,11},{10,... | collective-permute-start | bytes 589832 | tf_op jit(solution)/shard_map/ppermute | solution.py:450
  (3 other events, 3.4 us)
